TPU v7x, 32 devices: a whole 2x2x4 slice. The times are simulated.
32 devices in a mesh: dp: 16 (over z, y, x), tensor: 2 (over core).
Axes of the slice: x: 2, y: 2, z: 4, core: 2. Of those that a mesh axis runs over, the one named last changes fastest.
Arguments:
- block_in: float32 [4096, 768], P(('dp', 'tensor')), may hold values from -6 to 6
- seq_lengths: int32 [16, 4], P('dp'), may hold values from 1 to 160, 256 in all within a row
- routes: int32 [4096, 2], P('dp'), may hold values from 0 to 7, all different within a row; in each aligned block of 256 rows (0 to 255, 256 to 511, ...) at most 128 rows name the same one
- w_query: bfloat16 [768, 768], P('dp', 'tensor'), may hold values from -0.21875 to 0.21875
- w_key: bfloat16 [768, 768], P('dp', 'tensor'), may hold values from -0.21875 to 0.21875
- w_value: bfloat16 [768, 768], P('dp', 'tensor'), may hold values from -0.21875 to 0.21875
- w_out_proj: bfloat16 [768, 768], P('tensor', 'dp'), may hold values from -0.875 to 0.875
- router: bfloat16 [768, 8], P('dp'), may hold values from -0.15625 to 0.15625
- gain_attn: bfloat16 [768], P('dp'), may hold values from 0.099609375 to 1.8984375
- gain_moe: bfloat16 [768], P('dp'), may hold values from 0.099609375 to 1.8984375
- expert_in: bfloat16 [16, 768, 1536], P('dp', None, 'tensor'), may hold values from -0.21875 to 0.21875
- expert_out: bfloat16 [16, 1536, 768], P('dp', 'tensor'), may hold values from -0.109375 to 0.109375
- cotangent: float32 [4096, 768], P('dp'), may hold values from -6 to 6
Outputs:
- block_out: float32 [4096, 768], P(('dp', 'tensor'))
- grad_in: float32 [4096, 768], P(('dp', 'tensor'))
- grad_query: float32 [768, 768], P('dp', 'tensor')
- grad_key: float32 [768, 768], P('dp', 'tensor')
- grad_value: float32 [768, 768], P('dp', 'tensor')
- grad_out_proj: float32 [768, 768], P('tensor', 'dp')
- grad_router: float32 [768, 8], P(('dp', 'tensor'))
- grad_gain_attn: float32 [768], P(('dp', 'tensor'))
- grad_gain_moe: float32 [768], P(('dp', 'tensor'))
- grad_expert_in: float32 [16, 768, 1536], P('dp', None, 'tensor')
- grad_expert_out: float32 [16, 1536, 768], P('dp', 'tensor')
Inputs may be any that keep to these rules, and one draw needn't show every extreme that they name: `seq_lengths`: each group's 4 lengths sum to 256, and the largest is exactly 160. A token names 2 different experts. Among the 256 tokens of one group no expert is named by more than 128 routes, a bound that some block reaches.
All inputs are finite; a program needn't handle non-finite values.
Results may differ from a plain program's by a relative error of at most 0.015.
Values may be sent and summed in bfloat16 or wider, within the bound.
No kernel may reach another device: no remote copies, remote signals or barrier semaphores. Data moves between devices by JAX's collectives and lax.ppermute only.
A program may use at most 128 MiB of HBM per device.

v0:
```python
import jax
import jax.numpy as jnp
from jax import lax
from jax.sharding import PartitionSpec as P

HEAD_DIM = 64


EPSILON = 1e-06
NEGATIVE = -1e30
PRECISE = lax.Precision.HIGHEST


def contract_rows(left_side, right_side):
    return lax.dot_general(
        left_side, right_side, (((0,), (0,)), ((), ())), preferred_element_type=jnp.float32
    )


def contract_cols(left_side, right_side):
    return lax.dot_general(
        left_side, right_side, (((1,), (1,)), ((), ())), preferred_element_type=jnp.float32
    )


def segment_ids(lengths, row_count):
    seq_ends = jnp.cumsum(lengths)
    places = jnp.arange(row_count, dtype=jnp.int32)
    return jnp.sum((places[:, None] >= seq_ends[None, :]).astype(jnp.int32), axis=1)


def masked_scores(queries, key_rows, start_row, seg_id):
    row_count = queries.shape[0]
    scores = jnp.einsum(
        "qhd,khd->hqk", queries, key_rows, preferred_element_type=jnp.float32
    ) * queries.shape[2] ** (-0.5)
    query_pos = start_row + jnp.arange(row_count, dtype=jnp.int32)
    key_pos = jnp.arange(key_rows.shape[0], dtype=jnp.int32)
    allowed = (seg_id[:, None] == seg_id[None, :]) & (query_pos[:, None] >= key_pos[None, :])
    return jnp.where(allowed[None], scores, NEGATIVE)


def both_owners(per_expert, dp_count):
    experts, capacity, width = per_expert.shape
    return jnp.broadcast_to(per_expert[:, None], (experts, 2, capacity, width)).reshape(
        dp_count, capacity, width
    )


def pair_total(received, experts):
    dp_count, capacity, width = received.shape
    return jnp.sum(
        received.reshape(experts, 2, capacity, width).astype(jnp.float32), axis=1
    ).reshape(experts * capacity, width)


def local(
    block_in,
    seq_lengths,
    routes,
    w_query,
    w_key,
    w_value,
    w_out_proj,
    router,
    gain_attn,
    gain_moe,
    expert_in,
    expert_out,
    cotangent,
):
    dp_count = lax.axis_size("dp")
    tensor_count = lax.axis_size("tensor")
    own_index = lax.axis_index("tensor")
    tok_rows, model_width = block_in.shape
    group_rows, top_count = routes.shape
    experts = router.shape[1]
    capacity = 2 * top_count * group_rows // experts
    gain_share = model_width // (dp_count * tensor_count)
    query_full, key_full, value_full, proj_full, router_full, gain_one, gain_two = (
        lax.all_gather(w_query, "dp", axis=0, tiled=True),
        lax.all_gather(w_key, "dp", axis=0, tiled=True),
        lax.all_gather(w_value, "dp", axis=0, tiled=True),
        lax.all_gather(w_out_proj, "dp", axis=1, tiled=True),
        lax.all_gather(router, "dp", axis=0, tiled=True),
        lax.all_gather(gain_attn, "dp", axis=0, tiled=True),
        lax.all_gather(gain_moe, "dp", axis=0, tiled=True),
    )
    head_count = query_full.shape[1] // HEAD_DIM
    seg_id = segment_ids(seq_lengths[0], group_rows)
    score_scale = HEAD_DIM ** (-0.5)
    rows_all = lax.all_gather(block_in, "tensor", axis=0, tiled=True)
    inv_one = lax.rsqrt(jnp.mean(rows_all * rows_all, axis=1, keepdims=True) + EPSILON)
    normed_one = rows_all * inv_one
    h_one = (normed_one * gain_one.astype(jnp.float32)).astype(jnp.bfloat16)
    queries = (
        jnp.dot(h_one, query_full, preferred_element_type=jnp.float32)
        .astype(jnp.bfloat16)
        .reshape(group_rows, head_count, HEAD_DIM)
    )
    key_rows = (
        jnp.dot(h_one, key_full, preferred_element_type=jnp.float32)
        .astype(jnp.bfloat16)
        .reshape(group_rows, head_count, HEAD_DIM)
    )
    value_rows = (
        jnp.dot(h_one, value_full, preferred_element_type=jnp.float32)
        .astype(jnp.bfloat16)
        .reshape(group_rows, head_count, HEAD_DIM)
    )
    block_rows = min(512, group_rows)
    start_row = 0
    scores = masked_scores(queries, key_rows, start_row, seg_id)
    row_peak = jnp.max(scores, axis=-1, keepdims=True)
    exp_terms = jnp.exp(scores - row_peak)
    row_total = jnp.sum(exp_terms, axis=-1, keepdims=True)
    prob_low = (exp_terms / row_total).astype(jnp.bfloat16)
    block_outs = jnp.einsum(
        "hqk,khd->qhd", prob_low, value_rows, preferred_element_type=jnp.float32
    )
    block_lses = [row_peak + jnp.log(row_total)]
    mixed_rows = block_outs.reshape(group_rows, head_count * HEAD_DIM).astype(jnp.bfloat16)
    attn_own = lax.psum_scatter(
        jnp.dot(mixed_rows, proj_full, preferred_element_type=jnp.float32),
        "tensor",
        scatter_dimension=0,
        tiled=True,
    )
    residual = block_in + attn_own
    inv_two = lax.rsqrt(jnp.mean(residual * residual, axis=1, keepdims=True) + EPSILON)
    normed_two = residual * inv_two
    gain_two_f = gain_two.astype(jnp.float32)
    h_two = (normed_two * gain_two_f).astype(jnp.bfloat16)
    h_all = lax.all_gather(h_two, "tensor", axis=0, tiled=True)
    h_all_f = h_all.astype(jnp.float32)
    router_f = router_full.astype(jnp.float32)
    logits = jnp.dot(h_all_f, router_f, precision=PRECISE)
    picks = routes[:, :, None] == jnp.arange(experts, dtype=jnp.int32)[None, None, :]
    chosen = jnp.sum(jnp.where(picks, logits[:, None, :], 0.0), axis=2)
    gate_values = jax.nn.softmax(chosen, axis=1)
    flat_routes = routes.reshape(-1)
    expert_hits = (flat_routes[:, None] == jnp.arange(experts, dtype=jnp.int32)[None, :]).astype(
        jnp.int32
    )
    expert_rank = jnp.cumsum(expert_hits, axis=0) - 1
    slot_place = flat_routes * capacity + jnp.sum(expert_hits * expert_rank, axis=1)
    pair_count = group_rows * top_count
    slot_table = (
        jnp.full((experts * capacity,), pair_count, dtype=jnp.int32)
        .at[slot_place]
        .set(jnp.arange(pair_count, dtype=jnp.int32))
    )
    padded_rows = jnp.concatenate([h_all, jnp.zeros((1, model_width), jnp.bfloat16)], axis=0)
    outgoing = both_owners(
        padded_rows[slot_table // top_count].reshape(experts, capacity, model_width), dp_count
    )
    incoming = lax.all_to_all(outgoing, "dp", split_axis=0, concat_axis=0, tiled=True).reshape(
        dp_count * capacity, model_width
    )
    first_weight = expert_in[0]
    second_weight = expert_out[0]
    pre_act = jnp.dot(incoming, first_weight, preferred_element_type=jnp.float32)
    hidden = jax.nn.gelu(pre_act).astype(jnp.bfloat16)
    produced = jnp.dot(hidden, second_weight, preferred_element_type=jnp.float32).astype(
        jnp.bfloat16
    )
    returned = lax.all_to_all(
        produced.reshape(dp_count, capacity, model_width),
        "dp",
        split_axis=0,
        concat_axis=0,
        tiled=True,
    )
    returned_rows = pair_total(returned, experts)[slot_place].reshape(
        group_rows, top_count, model_width
    )
    expert_part = jnp.sum(gate_values[:, :, None] * returned_rows, axis=1)
    expert_sum = lax.psum_scatter(
        expert_part.astype(jnp.bfloat16), "tensor", scatter_dimension=0, tiled=True
    ).astype(jnp.float32)
    block_out = residual + expert_sum
    own_grad = lax.dynamic_slice_in_dim(cotangent, own_index * tok_rows, tok_rows, 0)
    gate_grad = jnp.sum(cotangent[:, None, :] * returned_rows, axis=2)
    slot_grad = (
        (gate_values[:, :, None] * cotangent[:, None, :])
        .astype(jnp.bfloat16)
        .reshape(pair_count, model_width)
    )
    padded_grad = jnp.concatenate([slot_grad, jnp.zeros((1, model_width), jnp.bfloat16)], axis=0)
    grad_outgoing = both_owners(
        padded_grad[slot_table].reshape(experts, capacity, model_width), dp_count
    )
    arrived = lax.all_to_all(grad_outgoing, "dp", split_axis=0, concat_axis=0, tiled=True).reshape(
        dp_count * capacity, model_width
    )
    grad_second = contract_rows(hidden, arrived)
    grad_hidden = contract_cols(arrived, second_weight)
    unused_value, gelu_back = jax.vjp(jax.nn.gelu, pre_act)
    grad_pre = gelu_back(grad_hidden)[0].astype(jnp.bfloat16)
    grad_first = contract_rows(incoming, grad_pre)
    grad_rows = contract_cols(grad_pre, first_weight).astype(jnp.bfloat16)
    sent_back = lax.all_to_all(
        grad_rows.reshape(dp_count, capacity, model_width),
        "dp",
        split_axis=0,
        concat_axis=0,
        tiled=True,
    )
    grad_pairs = pair_total(sent_back, experts)[slot_place].reshape(
        group_rows, top_count, model_width
    )
    expert_grad = jnp.sum(grad_pairs, axis=1)
    chosen_grad = gate_values * (
        gate_grad - jnp.sum(gate_values * gate_grad, axis=1, keepdims=True)
    )
    logit_grad = jnp.sum(jnp.where(picks, chosen_grad[:, :, None], 0.0), axis=1)
    h_grad_part = expert_grad + lax.dot_general(
        logit_grad, router_f, (((1,), (1,)), ((), ())), precision=PRECISE
    )
    router_part = lax.dot_general(h_all_f, logit_grad, (((0,), (0,)), ((), ())), precision=PRECISE)
    h_grad = lax.psum_scatter(
        h_grad_part.astype(jnp.bfloat16), "tensor", scatter_dimension=0, tiled=True
    ).astype(jnp.float32)
    gain_two_part = jnp.sum(h_grad * normed_two, axis=0)
    scaled_two = h_grad * gain_two_f
    resid_grad = own_grad + inv_two * (
        scaled_two - normed_two * jnp.mean(scaled_two * normed_two, axis=1, keepdims=True)
    )
    attn_grad = lax.all_gather(resid_grad.astype(jnp.bfloat16), "tensor", axis=0, tiled=True)
    grad_proj = contract_rows(mixed_rows, attn_grad)
    mixed_grad = (
        contract_cols(attn_grad, proj_full)
        .astype(jnp.bfloat16)
        .reshape(group_rows, head_count, HEAD_DIM)
    )
    query_grads = []
    key_acc = jnp.zeros((group_rows, head_count, HEAD_DIM), jnp.float32)
    value_acc = jnp.zeros((group_rows, head_count, HEAD_DIM), jnp.float32)
    for block_index, start_row in enumerate(range(0, group_rows, block_rows)):
        scores = masked_scores(queries, key_rows, start_row, seg_id)
        prob_rows = jnp.exp(scores - block_lses[block_index])
        prob_grad = jnp.einsum(
            "qhd,khd->hqk", mixed_grad, value_rows, preferred_element_type=jnp.float32
        )
        row_carry = jnp.sum(prob_grad * prob_rows, axis=-1, keepdims=True)
        score_grad = (prob_rows * (prob_grad - row_carry)).astype(jnp.bfloat16)
        query_grads.append(
            jnp.einsum("hqk,khd->qhd", score_grad, key_rows, preferred_element_type=jnp.float32)
            * score_scale
        )
        key_acc = (
            jnp.einsum("hqk,qhd->khd", score_grad, queries, preferred_element_type=jnp.float32)
            * score_scale
        )
        value_acc = jnp.einsum(
            "hqk,qhd->khd",
            prob_rows.astype(jnp.bfloat16),
            mixed_grad,
            preferred_element_type=jnp.float32,
        )
    inner_width = head_count * HEAD_DIM
    query_grad = query_grads[0].reshape(group_rows, inner_width).astype(jnp.bfloat16)
    key_grad = key_acc.reshape(group_rows, inner_width).astype(jnp.bfloat16)
    value_grad = value_acc.reshape(group_rows, inner_width).astype(jnp.bfloat16)
    grad_q_part = contract_rows(h_one, query_grad)
    grad_k_part = contract_rows(h_one, key_grad)
    grad_v_part = contract_rows(h_one, value_grad)
    one_grad_part = (
        contract_cols(query_grad, query_full)
        + contract_cols(key_grad, key_full)
        + contract_cols(value_grad, value_full)
    )
    gain_one_part = jnp.sum(one_grad_part * normed_one, axis=0)
    one_grad, gain_one_sum, gain_two_sum, router_sum = (
        lax.psum_scatter(
            one_grad_part.astype(jnp.bfloat16), "tensor", scatter_dimension=0, tiled=True
        ).astype(jnp.float32),
        lax.psum_scatter(
            gain_one_part.reshape(dp_count, tensor_count, gain_share).astype(jnp.bfloat16),
            "tensor",
            scatter_dimension=1,
            tiled=True,
        ).astype(jnp.float32),
        lax.psum_scatter(
            gain_two_part.reshape(dp_count, tensor_count, gain_share).astype(jnp.bfloat16),
            "tensor",
            scatter_dimension=1,
            tiled=True,
        ).astype(jnp.float32),
        lax.psum_scatter(
            router_part.reshape(dp_count, tensor_count, gain_share, experts).astype(jnp.bfloat16),
            "tensor",
            scatter_dimension=1,
            tiled=True,
        ).astype(jnp.float32),
    )
    own_normed = lax.dynamic_slice_in_dim(normed_one, own_index * tok_rows, tok_rows, 0)
    own_inv = lax.dynamic_slice_in_dim(inv_one, own_index * tok_rows, tok_rows, 0)
    scaled_one = one_grad * gain_one.astype(jnp.float32)
    grad_in = resid_grad + own_inv * (
        scaled_one - own_normed * jnp.mean(scaled_one * own_normed, axis=1, keepdims=True)
    )
    grad_query, grad_key, grad_value, grad_out_proj, gain_one_grad, gain_two_grad, router_grad = (
        lax.psum_scatter(grad_q_part, "dp", scatter_dimension=0, tiled=True),
        lax.psum_scatter(grad_k_part, "dp", scatter_dimension=0, tiled=True),
        lax.psum_scatter(grad_v_part, "dp", scatter_dimension=0, tiled=True),
        lax.psum_scatter(grad_proj, "dp", scatter_dimension=1, tiled=True),
        lax.psum_scatter(gain_one_sum, "dp", scatter_dimension=0, tiled=True),
        lax.psum_scatter(gain_two_sum, "dp", scatter_dimension=0, tiled=True),
        lax.psum_scatter(router_sum, "dp", scatter_dimension=0, tiled=True),
    )
    return (
        block_out,
        grad_in,
        grad_query,
        grad_key,
        grad_value,
        grad_out_proj,
        router_grad.reshape(gain_share, experts),
        gain_one_grad.reshape(gain_share),
        gain_two_grad.reshape(gain_share),
        grad_first[None],
        grad_second[None],
    )


def solution(mesh):
    in_specs = (
        P(("dp", "tensor"), None),
        P("dp", None),
        P("dp", None),
        P("dp", "tensor"),
        P("dp", "tensor"),
        P("dp", "tensor"),
        P("tensor", "dp"),
        P("dp", None),
        P("dp"),
        P("dp"),
        P("dp", None, "tensor"),
        P("dp", "tensor", None),
        P("dp", None),
    )
    out_specs = (
        P(("dp", "tensor"), None),
        P(("dp", "tensor"), None),
        P("dp", "tensor"),
        P("dp", "tensor"),
        P("dp", "tensor"),
        P("tensor", "dp"),
        P(("dp", "tensor"), None),
        P(("dp", "tensor")),
        P(("dp", "tensor")),
        P("dp", None, "tensor"),
        P("dp", "tensor", None),
    )
    return jax.shard_map(local, mesh=mesh, in_specs=in_specs, out_specs=out_specs, check_vma=False)
```

profile of v0, /device:TPU:0, one launch (start us, length us, event | category | flops | bytes accessed | tf_op | source)
XLA Modules:
  0.0 1180.9 jit_solution(11799272457879546801)
XLA Ops:
  11.9 43.5 %all-reduce.9 = (bf16[768]{0:T(1024)(128)(2,1)S(1)}, bf16[768]{0:T(1024)(128)(2,1)S(1)}) all-reduce(bf16[768]{0:T(1024)(128)(2,1)S(1)} %dynamic-update-slice, bf16[768]{0:T(1024)(128)(2,1)S(1)} %dynamic-update-slice.1), channel_id=1, replica_groups=mesh['dp'=16,'tensor'=2] {'dp'}, use_global_device_ids=true, to_apply=%add.2 | all-reduce | flops 1536 | bytes 6144
  56.2 39.1 %all_gather.33 = bf16[768,384]{1,0:T(8,128)(2,1)S(1)} all-gather(bf16[48,384]{1,0:T(8,128)(2,1)} %param.16), channel_id=1, replica_groups=mesh['dp'=16,'tensor'=2] {'dp'}, dimensions={0}, use_global_device_ids=true | all-gather | bytes 626688 | tf_op jit(solution)/shard_map/all_gather | solution.py:81
  95.3 40.9 %all_gather.34 = bf16[768,384]{1,0:T(8,128)(2,1)S(1)} all-gather(bf16[48,384]{1,0:T(8,128)(2,1)} %param.17), channel_id=1, replica_groups=mesh['dp'=16,'tensor'=2] {'dp'}, dimensions={0}, use_global_device_ids=true | all-gather | bytes 626688 | tf_op jit(solution)/shard_map/all_gather | solution.py:82
  136.2 42.0 %all_gather.32 = bf16[768,384]{1,0:T(8,128)(2,1)} all-gather(bf16[48,384]{1,0:T(8,128)(2,1)} %param.18), channel_id=1, replica_groups=mesh['dp'=16,'tensor'=2] {'dp'}, dimensions={0}, use_global_device_ids=true | all-gather | bytes 626688 | tf_op jit(solution)/shard_map/all_gather | solution.py:83
  178.2 40.5 %all_gather.35 = bf16[384,768]{0,1:T(8,128)(2,1)S(1)} all-gather(bf16[384,48]{0,1:T(8,128)(2,1)} %param.19), channel_id=1, replica_groups=mesh['dp'=16,'tensor'=2] {'dp'}, dimensions={1}, use_global_device_ids=true | all-gather | bytes 626688 | tf_op jit(solution)/shard_map/all_gather | solution.py:84
  238.3 5.2 gather_fusion
  246.9 6.6 all-to-all-start
  253.6 87.1 %all-gather = bf16[16,48,8]{1,2,0:T(8,128)(2,1)S(1)} all-gather(bf16[1,48,8]{1,2,0:T(8,128)(2,1)S(1)} %bitcast.159), channel_id=1, replica_groups=mesh['dp'=16,'tensor'=2] {'dp'}, dimensions={0}, use_global_device_ids=true | all-gather | bytes 13056 | tf_op jit(solution)/shard_map/all_gather | solution.py:85
  349.5 5.2 gather_fusion.2
  358.2 13.8 %all-to-all-start.2 = ((bf16[16,128,768]{2,1,0:T(8,128)(2,1)}), bf16[16,128,768]{2,1,0:T(8,128)(2,1)}, u32[]{:S(2)}, u32[]{:S(2)}) async-start(bf16[16,128,768]{2,1,0:T(8,128)(2,1)} %bitcast.132), calls=%async_computation.4 | async-start | bytes 6291456 | tf_op jit(solution)/shard_map/all_to_all | solution.py:193
  384.4 42.6 %all-to-all-done.2 = bf16[16,128,768]{2,1,0:T(8,128)(2,1)} async-done(((bf16[16,128,768]{2,1,0:T(8,128)(2,1)}), bf16[16,128,768]{2,1,0:T(8,128)(2,1)}, u32[]{:S(2)}, u32[]{:S(2)}) %all-to-all-start.2) | async-done | bytes 3145760 | tf_op jit(solution)/shard_map/all_to_all | solution.py:193
  427.0 14.4 %all-to-all-start.1 = ((bf16[16,128,768]{2,1,0:T(8,128)(2,1)}), bf16[16,128,768]{2,1,0:T(8,128)(2,1)}, u32[]{:S(2)}, u32[]{:S(2)}) async-start(bf16[16,128,768]{2,1,0:T(8,128)(2,1)} %bitcast.136), calls=%async_computation.2 | async-start | bytes 6291456 | tf_op jit(solution)/shard_map/all_to_all | solution.py:167
  441.4 9.7 fusion.6
  456.8 44.7 %all-to-all-done.1 = bf16[16,128,768]{2,1,0:T(8,128)(2,1)} async-done(((bf16[16,128,768]{2,1,0:T(8,128)(2,1)}), bf16[16,128,768]{2,1,0:T(8,128)(2,1)}, u32[]{:S(2)}, u32[]{:S(2)}) %all-to-all-start.1) | async-done | bytes 3145760 | tf_op jit(solution)/shard_map/all_to_all | solution.py:167
  501.6 14.0 %all-to-all-start.3 = ((bf16[16,128,768]{2,1,0:T(8,128)(2,1)}), bf16[16,128,768]{2,1,0:T(8,128)(2,1)}, u32[]{:S(2)}, u32[]{:S(2)}) async-start(bf16[16,128,768]{2,1,0:T(8,128)(2,1)} %bitcast.24), calls=%async_computation.5 | async-start | bytes 6291456 | tf_op jit(solution)/shard_map/all_to_all | solution.py:202
  528.8 47.4 %all-to-all-done.3 = bf16[16,128,768]{2,1,0:T(8,128)(2,1)} async-done(((bf16[16,128,768]{2,1,0:T(8,128)(2,1)}), bf16[16,128,768]{2,1,0:T(8,128)(2,1)}, u32[]{:S(2)}, u32[]{:S(2)}) %all-to-all-start.3) | async-done | bytes 3145760 | tf_op jit(solution)/shard_map/all_to_all | solution.py:202
  589.7 16.3 %reduce-scatter.16.cloned.1.call-done = bf16[128,768]{1,0:T(8,128)(2,1)} async-done(((bf16[256,768]{1,0:T(8,128)(2,1)}), bf16[128,768]{1,0:T(8,128)(2,1)}) %reduce-scatter.16.cloned.1.call-update) | async-done | bytes 196624 | tf_op jit(solution)/shard_map/reduce_scatter | solution.py:221
  630.8 6.9 convolution_bitcast_fusion.1
  637.8 8.5 convolution_bitcast_fusion
  653.0 78.8 %all-reduce.8 = (f32[16,1,24,8]{2,3,1,0:T(8,128)}, f32[16,1,24]{2,1,0:T(1,128)S(1)}, f32[16,1,24]{2,1,0:T(1,128)S(1)}) all-reduce(f32[16,1,24,8]{2,3,1,0:T(8,128)S(1)} %dynamic-slice_convert_fusion, f32[16,1,24]{2,1,0:T(1,128)S(1)} %bitcast.155, f32[16,1,24]{2,1,0:T(1,128)S(1)} %bitcast.154), channel_id=11, replica_groups=mesh['dp'=16,'tensor'=2] {'dp'}, use_global_device_ids=true, to_apply=%region_32.33.clone | all-reduce | flops 3840 | bytes 30720
  738.0 51.7 %reduce-scatter.26.cloned.1.call-done = f32[384,48]{0,1:T(8,128)} async-done(((f32[384,768]{0,1:T(8,128)}), f32[384,48]{0,1:T(8,128)}) %reduce-scatter.26.cloned.1.call-update) | async-done | bytes 73744 | tf_op jit(solution)/shard_map/reduce_scatter | solution.py:307
  789.7 128.0 %reduce-scatter.24.cloned.1.call-done = f32[48,384]{1,0:T(8,128)} async-done(((f32[768,384]{1,0:T(8,128)}), f32[48,384]{1,0:T(8,128)}) %reduce-scatter.24.cloned.1.call-update) | async-done | bytes 73744 | tf_op jit(solution)/shard_map/reduce_scatter | solution.py:306
  917.7 128.0 %reduce-scatter.22.cloned.1.call-done = f32[48,384]{1,0:T(8,128)} async-done(((f32[768,384]{1,0:T(8,128)}), f32[48,384]{1,0:T(8,128)}) %reduce-scatter.22.cloned.1.call-update) | async-done | bytes 73744 | tf_op jit(solution)/shard_map/reduce_scatter | solution.py:305
  1045.7 127.9 %reduce-scatter.20.cloned.1.call-done = f32[48,384]{1,0:T(8,128)} async-done(((f32[768,384]{1,0:T(8,128)}), f32[48,384]{1,0:T(8,128)}) %reduce-scatter.20.cloned.1.call-update) | async-done | bytes 73744 | tf_op jit(solution)/shard_map/reduce_scatter | solution.py:304
  (257 shorter events, 121.7 us)
Async XLA Ops:
  7.2 372.1 %copy-start = (bf16[1,768,768]{2,1,0:T(8,128)(2,1)S(1)}, bf16[1,768,768]{2,1,0:T(8,128)(2,1)}, u32[]{:S(2)}) copy-start(bf16[1,768,768]{2,1,0:T(8,128)(2,1)} %param.24) | copy-start | bytes 3538948
  7.2 227.1 %reduce-scatter.12.cloned.1.call-start = ((), (), s32[]{:S(2)}) async-start(), calls=%async_computation.14 | async-start | bytes 1179648 | tf_op jit(solution)/shard_map/reduce_scatter | solution.py:123
  55.4 167.1 %copy-start.37 = (f32[768]{0:T(1024)}, f32[768]{0:T(1024)S(1)}, u32[]{:S(2)}) copy-start(f32[768]{0:T(1024)S(1)} %convert_element_type.153) | copy-start | bytes 9220
  95.3 127.8 %copy-start.13 = (bf16[768,384]{1,0:T(8,128)(2,1)}, bf16[768,384]{1,0:T(8,128)(2,1)S(1)}, u32[]{:S(2)}) copy-start(bf16[768,384]{1,0:T(8,128)(2,1)S(1)} %all_gather.33) | copy-start | bytes 1769476
  238.3 107.4 %copy-start.11 = (bf16[256,768]{1,0:T(8,128)(2,1)}, bf16[256,768]{1,0:T(8,128)(2,1)S(1)}, u32[]{:S(2)}) copy-start(bf16[256,768]{1,0:T(8,128)(2,1)S(1)} %all_gather.37) | copy-start | bytes 1179652
  246.9 107.8 %all-to-all-start = ((bf16[16,128,768]{2,1,0:T(8,128)(2,1)}), bf16[16,128,768]{2,1,0:T(8,128)(2,1)}, u32[]{:S(2)}, u32[]{:S(2)}) async-start(bf16[16,128,768]{2,1,0:T(8,128)(2,1)} %bitcast.131), calls=%async_computation.1 | async-start | bytes 6291456 | tf_op jit(solution)/shard_map/all_to_all | solution.py:157
  358.2 68.8 %all-to-all-start.2 = ((bf16[16,128,768]{2,1,0:T(8,128)(2,1)}), bf16[16,128,768]{2,1,0:T(8,128)(2,1)}, u32[]{:S(2)}, u32[]{:S(2)}) async-start(bf16[16,128,768]{2,1,0:T(8,128)(2,1)} %bitcast.132), calls=%async_computation.4 | async-start | bytes 6291456 | tf_op jit(solution)/shard_map/all_to_all | solution.py:193
  427.0 74.5 %all-to-all-start.1 = ((bf16[16,128,768]{2,1,0:T(8,128)(2,1)}), bf16[16,128,768]{2,1,0:T(8,128)(2,1)}, u32[]{:S(2)}, u32[]{:S(2)}) async-start(bf16[16,128,768]{2,1,0:T(8,128)(2,1)} %bitcast.136), calls=%async_computation.2 | async-start | bytes 6291456 | tf_op jit(solution)/shard_map/all_to_all | solution.py:167
  501.6 74.7 %all-to-all-start.3 = ((bf16[16,128,768]{2,1,0:T(8,128)(2,1)}), bf16[16,128,768]{2,1,0:T(8,128)(2,1)}, u32[]{:S(2)}, u32[]{:S(2)}) async-start(bf16[16,128,768]{2,1,0:T(8,128)(2,1)} %bitcast.24), calls=%async_computation.5 | async-start | bytes 6291456 | tf_op jit(solution)/shard_map/all_to_all | solution.py:202
  515.6 90.3 %reduce-scatter.16.cloned.1.call-start = ((), (), s32[]{:S(2)}) async-start(), calls=%async_computation.16 | async-start | bytes 589824 | tf_op jit(solution)/shard_map/reduce_scatter | solution.py:221
  589.6 62.1 %reduce-scatter.30.cloned.1.call-start = ((), (), s32[]{:S(2)}) async-start(), calls=%async_computation.23 | async-start | bytes 12288 | tf_op jit(solution)/shard_map/reduce_scatter | solution.py:284
  616.9 35.5 %reduce-scatter.28.cloned.1.call-start = ((), (), s32[]{:S(2)}) async-start(), calls=%async_computation.22 | async-start | bytes 12288 | tf_op jit(solution)/shard_map/reduce_scatter | solution.py:278
  621.0 113.8 %reduce-scatter.18.cloned.1.call-start = ((), (), s32[]{:S(2)}) async-start(), calls=%async_computation.17 | async-start | bytes 589824 | tf_op jit(solution)/shard_map/reduce_scatter | solution.py:275
  621.6 114.3 %reduce-scatter.14.cloned.1.call-start = ((), (), s32[]{:S(2)}) async-start(), calls=%async_computation.15 | async-start | bytes 589824 | tf_op jit(solution)/shard_map/reduce_scatter | solution.py:178
  622.2 167.6 %reduce-scatter.26.cloned.1.call-start = ((), (), s32[]{:S(2)}) async-start(), calls=%async_computation.21 | async-start | bytes 1253376 | tf_op jit(solution)/shard_map/reduce_scatter | solution.py:307
  624.6 293.1 %reduce-scatter.24.cloned.1.call-start = ((), (), s32[]{:S(2)}) async-start(), calls=%async_computation.20 | async-start | bytes 1253376 | tf_op jit(solution)/shard_map/reduce_scatter | solution.py:306
  626.2 419.6 %reduce-scatter.22.cloned.1.call-start = ((), (), s32[]{:S(2)}) async-start(), calls=%async_computation.19 | async-start | bytes 1253376 | tf_op jit(solution)/shard_map/reduce_scatter | solution.py:305
  627.7 545.9 %reduce-scatter.20.cloned.1.call-start = ((), (), s32[]{:S(2)}) async-start(), calls=%async_computation.18 | async-start | bytes 1253376 | tf_op jit(solution)/shard_map/reduce_scatter | solution.py:304
  637.7 97.1 %copy-start.38 = (f32[768]{0:T(1024)S(1)}, f32[768]{0:T(1024)}, u32[]{:S(2)}) copy-start(f32[768]{0:T(1024)} %copy-done.37) | copy-start | bytes 9220
  637.7 98.2 %copy-start.10 = (f32[256,768]{1,0:T(8,128)S(1)}, f32[256,768]{1,0:T(8,128)}, u32[]{:S(2)}) copy-start(f32[256,768]{1,0:T(8,128)} %param.25) | copy-start | bytes 2359300
  637.7 98.2 %copy-start.18 = (bf16[128,768]{1,0:T(8,128)(2,1)S(1)}, bf16[128,768]{1,0:T(8,128)(2,1)}, u32[]{:S(2)}) copy-start(bf16[128,768]{1,0:T(8,128)(2,1)} %reduce-scatter.16.cloned.1.call-done) | copy-start | bytes 589828
  637.7 98.2 %copy-start.49 = (f32[128]{0:T(128)S(1)}, f32[128]{0:T(128)}, u32[]{:S(2)}) copy-start(f32[128]{0:T(128)} %copy-done.47) | copy-start | bytes 1540
  637.8 98.2 %copy-start.53 = (f32[128]{0:T(128)S(1)}, f32[128]{0:T(128)}, u32[]{:S(2)}) copy-start(f32[128]{0:T(128)} %copy-done.52) | copy-start | bytes 1540
  637.8 535.8 %copy-start.1 = (bf16[1,768,768]{2,1,0:T(8,128)(2,1)S(1)}, bf16[1,768,768]{2,1,0:T(8,128)(2,1)}, u32[]{:S(2)}) copy-start(bf16[1,768,768]{2,1,0:T(8,128)(2,1)} %param.24) | copy-start | bytes 3538948
  (49 other events, 448.2 us)
Sparse Core Ops, SparseCore 0:
  229.6 4.3 reduce-scatter.11
  589.7 16.1 reduce-scatter.15
  617.0 8.5 reduce-scatter.29
  627.6 8.5 reduce-scatter.27
  638.9 8.9 reduce-scatter.17
  650.6 8.9 reduce-scatter.13
  664.9 124.7 reduce-scatter.25
  795.1 122.6 reduce-scatter.23
  923.1 122.6 reduce-scatter.21
  1050.9 122.6 reduce-scatter.19
where the time goes:
time: 1190 us; the launch traced here: 1180 us
  waiting for transfers between devices  588 us (49%)
  blocking collectives  382 us (32%)
  matrix products  62.2 us (5%)
  local copies, waits for them, and re-layouts  54 us (5%)
  starting transfers between devices  49.8 us (4%)
  other arithmetic  28.7 us (2%)
  between operations  16.2 us (1%)
    reduce_scatter x1, waiting for transfers between devices, local(): lax.psum_scatter(grad_v_part, 'dp', scatter_dimension=0, tiled=True)  128 us
    reduce_scatter x1, waiting for transfers between devices, local(): lax.psum_scatter(grad_k_part, 'dp', scatter_dimension=0, tiled=True)  128 us
    reduce_scatter x1, waiting for transfers between devices, local(): lax.psum_scatter(grad_q_part, 'dp', scatter_dimension=0, tiled=True)  128 us
    unnamed x3, blocking collectives  126 us
    all_gather x1, blocking collectives, local(): lax.all_gather(router, 'dp', axis=0, tiled=True)  87.1 us
    reduce_scatter x1, waiting for transfers between devices, local(): lax.psum_scatter(grad_proj, 'dp', scatter_dimension=1, tiled=True)  51.7 us
    all_to_all x1, waiting for transfers between devices, local(): lax.all_to_all(grad_rows.reshape(dp_count, capacity, model_width), 'dp',...  47.4 us
    all_to_all x1, waiting for transfers between devices, local(): lax.all_to_all(produced.reshape(dp_count, capacity, model_width), 'dp', s...  44.7 us
  transfers between devices with their start and end apart: 14, of which 8 were waited for; matrix products, arithmetic and copies ran while one was open for 8% of the time, Pallas kernels for 0%

commit v1 on v0

v1 whole, which is shorter than its diff:
```python
import jax
import jax.numpy as jnp
from jax import lax
from jax.sharding import PartitionSpec as P

HEAD_DIM = 64
LANES = 128


EPSILON = 1e-06
NEGATIVE = -1e30
PRECISE = lax.Precision.HIGHEST
LOW = jnp.bfloat16
FULL = jnp.float32


def dot(left_side, right_side):
    return jnp.dot(left_side, right_side, preferred_element_type=FULL)


def contract_rows(left_side, right_side):
    return lax.dot_general(
        left_side, right_side, (((0,), (0,)), ((), ())), preferred_element_type=FULL
    )


def contract_cols(left_side, right_side):
    return lax.dot_general(
        left_side, right_side, (((1,), (1,)), ((), ())), preferred_element_type=FULL
    )


def segment_ids(lengths, row_count):
    seq_ends = jnp.cumsum(lengths)
    places = jnp.arange(row_count, dtype=jnp.int32)
    return jnp.sum((places[:, None] >= seq_ends[None, :]).astype(jnp.int32), axis=1)


def swap(values):
    return lax.ppermute(values, "tensor", [(0, 1), (1, 0)])


def bit_orders():
    bits = lax.axis_size("dp").bit_length() - 1
    falling = list(range(bits - 1, -1, -1))
    return falling, falling[:-2] + [falling[-1], falling[-2]]


def partners(bit):
    return [(i, i ^ (1 << bit)) for i in range(lax.axis_size("dp"))]


def gather_dp(shard, order):
    bits, own = len(order), lax.axis_index("dp")
    block = shard.reshape((1,) * bits + shard.shape)
    for bit in order:
        other = lax.ppermute(block, "dp", partners(bit))
        axis = bits - 1 - bit
        upper = ((own >> bit) & 1) == 1
        block = jnp.where(
            upper,
            jnp.concatenate([other, block], axis=axis),
            jnp.concatenate([block, other], axis=axis),
        )
    return block.reshape(shard.shape[0] << bits, shard.shape[1])


def reduce_dp(partial, order):
    bits, own = len(order), lax.axis_index("dp")
    rows, width = partial.shape[0] >> len(order), partial.shape[1]
    block = partial.reshape((2,) * bits + (rows, width))
    for bit in order:
        axis, place = bits - 1 - bit, (own >> bit) & 1
        given = lax.dynamic_index_in_dim(block, 1 - place, axis, keepdims=True).astype(LOW)
        kept = lax.dynamic_index_in_dim(block, place, axis, keepdims=True)
        block = kept.astype(FULL) + lax.ppermute(given, "dp", partners(bit)).astype(FULL)
    return block.reshape(rows, width)


def trade(values):
    return lax.all_to_all(values, "dp", split_axis=0, concat_axis=0, tiled=True)


def local(
    block_in,
    seq_lengths,
    routes,
    w_query,
    w_key,
    w_value,
    w_out_proj,
    router,
    gain_attn,
    gain_moe,
    expert_in,
    expert_out,
    cotangent,
):
    dp_count = lax.axis_size("dp")
    core = lax.axis_index("tensor")
    tok_rows, model_width = block_in.shape
    group_rows, top_count = routes.shape
    experts = router.shape[1]
    owners = dp_count // experts
    half_cap = top_count * group_rows // experts
    slots = dp_count * half_cap
    inner_width = w_query.shape[1]
    head_count = inner_width // HEAD_DIM
    order_a, order_b = bit_orders()

    extra_width = -(-(2 + experts) // LANES) * LANES
    extra = jnp.concatenate(
        [
            gain_attn[:, None],
            gain_moe[:, None],
            router,
            jnp.zeros((router.shape[0], extra_width - 2 - experts), LOW),
        ],
        axis=1,
    )
    qk_full = gather_dp(jnp.concatenate([w_query, w_key], axis=1), order_a)
    ve_full = gather_dp(jnp.concatenate([w_value, extra], axis=1), order_b)
    proj_back = gather_dp(w_out_proj.T, order_b)
    qkv_full = jnp.concatenate([qk_full, ve_full[:, :inner_width]], axis=1)
    gain_one = ve_full[:, inner_width].astype(FULL)[None, :]
    gain_two = ve_full[:, inner_width + 1].astype(FULL)[None, :]
    router_full = ve_full[:, inner_width + 2 : inner_width + 2 + experts]

    hits = jnp.any(
        routes[:, :, None] == jnp.arange(experts, dtype=jnp.int32)[None, None, :], axis=1
    )
    places = jnp.arange(group_rows, dtype=jnp.int32)
    earlier = (places[:, None] > places[None, :]).astype(LOW)
    rank = dot(earlier, hits.astype(LOW)).astype(jnp.int32)
    slot_of = jnp.where(hits, rank, -1).T
    hits_t = slot_of >= 0
    slot_ids = core * half_cap + jnp.arange(half_cap, dtype=jnp.int32)
    in_slot = slot_of[:, None, :] == slot_ids[None, :, None]
    dispatch = (
        jnp.broadcast_to(in_slot[:, None], (experts, owners, half_cap, group_rows))
        .astype(LOW)
        .reshape(slots, group_rows)
    )

    def send_rows(token_rows):
        picked = dot(dispatch, token_rows).astype(LOW)
        return trade(picked.reshape(dp_count, half_cap, model_width)).reshape(slots, model_width)

    def both_halves(own):
        return jnp.concatenate([own, swap(own)], axis=0)

    cot_rows = both_halves(send_rows(cotangent.astype(LOW)))

    seg_id = segment_ids(seq_lengths[0], group_rows)
    score_scale = HEAD_DIM ** (-0.5)
    rows_all = lax.all_gather(block_in, "tensor", axis=0, tiled=True)
    inv_one = lax.rsqrt(jnp.mean(rows_all * rows_all, axis=1, keepdims=True) + EPSILON)
    normed_one = rows_all * inv_one
    h_one = (normed_one * gain_one).astype(LOW)
    qkv = dot(h_one, qkv_full).astype(LOW).reshape(group_rows, 3, head_count, HEAD_DIM)
    queries, key_rows, value_rows = qkv[:, 0], qkv[:, 1], qkv[:, 2]
    scores = jnp.einsum("qhd,khd->hqk", queries, key_rows, preferred_element_type=FULL) * score_scale
    allowed = (seg_id[:, None] == seg_id[None, :]) & (places[:, None] >= places[None, :])
    scores = jnp.where(allowed[None], scores, NEGATIVE)
    exp_terms = jnp.exp(scores - jnp.max(scores, axis=-1, keepdims=True))
    probs = exp_terms / jnp.sum(exp_terms, axis=-1, keepdims=True)
    prob_low = probs.astype(LOW)
    mixed_rows = (
        jnp.einsum("hqk,khd->qhd", prob_low, value_rows, preferred_element_type=FULL)
        .reshape(group_rows, inner_width)
        .astype(LOW)
    )
    attn_part = contract_cols(mixed_rows, proj_back)
    residual = rows_all + (attn_part + swap(attn_part))
    inv_two = lax.rsqrt(jnp.mean(residual * residual, axis=1, keepdims=True) + EPSILON)
    normed_two = residual * inv_two
    h_two = (normed_two * gain_two).astype(LOW)

    logits = lax.dot_general(
        router_full, h_two, (((0,), (1,)), ((), ())), preferred_element_type=FULL
    )
    peak = jnp.max(jnp.where(hits_t, logits, NEGATIVE), axis=0, keepdims=True)
    gate_terms = jnp.where(hits_t, jnp.exp(jnp.where(hits_t, logits - peak, 0.0)), 0.0)
    gates = gate_terms / jnp.sum(gate_terms, axis=0, keepdims=True)
    slot_gates = jnp.sum(jnp.where(in_slot, gates[:, None, :], 0.0), axis=2)
    gate_rows = jnp.broadcast_to(slot_gates[:, None], (experts, owners, half_cap)).reshape(
        dp_count, half_cap
    )

    incoming = both_halves(send_rows(h_two))
    gate_col = both_halves(trade(gate_rows).reshape(slots, 1))
    first_weight = expert_in[0]
    second_weight = expert_out[0]
    pre_act = dot(incoming, first_weight)
    hidden, gelu_back = jax.vjp(jax.nn.gelu, pre_act)
    hidden = hidden.astype(LOW)
    arrived = (gate_col * cot_rows.astype(FULL)).astype(LOW)
    grad_hidden = contract_cols(arrived, second_weight)
    gated_grad = jnp.sum(hidden.astype(FULL) * grad_hidden, axis=1)
    grad_pre = gelu_back(grad_hidden)[0].astype(LOW)
    given_rows = contract_cols(grad_pre[slots:], first_weight).astype(LOW)
    kept_rows = contract_cols(grad_pre[:slots], first_weight)
    in_rows = (kept_rows + swap(given_rows).astype(FULL)).astype(LOW)
    own_gated = gated_grad[:slots] + swap(gated_grad[slots:])
    back_gated = trade(own_gated.reshape(dp_count, half_cap))
    back_rows = trade(in_rows.reshape(dp_count, half_cap, model_width)).reshape(slots, model_width)

    given_out = (gate_col[slots:] * dot(hidden[slots:], second_weight)).astype(LOW)
    kept_out = gate_col[:slots] * dot(hidden[:slots], second_weight)
    out_rows = (kept_out + swap(given_out).astype(FULL)).astype(LOW)
    back_out = trade(out_rows.reshape(dp_count, half_cap, model_width)).reshape(slots, model_width)
    grad_second = contract_rows(hidden, arrived)
    grad_first = contract_rows(incoming, grad_pre)

    out_part = contract_rows(dispatch, back_out)
    own_start = core * tok_rows
    other_start = (1 - core) * tok_rows

    def rows_at(values, start):
        return lax.dynamic_slice_in_dim(values, start, tok_rows, 0)

    block_out = rows_at(residual, own_start) + (
        rows_at(out_part, own_start) + swap(rows_at(out_part, other_start))
    )

    slot_gated = jnp.sum(back_gated.reshape(experts, owners, half_cap), axis=1)
    gated = jnp.sum(jnp.where(in_slot, slot_gated[:, :, None], 0.0), axis=1)
    logit_grad = jnp.where(hits_t, gated - gates * jnp.sum(gated, axis=0, keepdims=True), 0.0)
    h_grad_part = contract_rows(dispatch, back_rows) + lax.dot_general(
        logit_grad, router_full.astype(FULL), (((0,), (1,)), ((), ())), precision=PRECISE
    )
    router_part = lax.dot_general(
        h_two.astype(FULL), logit_grad, (((0,), (1,)), ((), ())), precision=PRECISE
    )
    h_grad = h_grad_part + swap(h_grad_part)
    gain_two_part = 0.5 * jnp.sum(h_grad * normed_two, axis=0)
    scaled_two = h_grad * gain_two
    resid_grad = cotangent + inv_two * (
        scaled_two - normed_two * jnp.mean(scaled_two * normed_two, axis=1, keepdims=True)
    )
    attn_grad = resid_grad.astype(LOW)

    grad_proj_part = contract_rows(attn_grad, mixed_rows)
    mixed_grad = (
        dot(attn_grad, proj_back).astype(LOW).reshape(group_rows, head_count, HEAD_DIM)
    )
    prob_grad = jnp.einsum("qhd,khd->hqk", mixed_grad, value_rows, preferred_element_type=FULL)
    row_carry = jnp.sum(prob_grad * probs, axis=-1, keepdims=True)
    score_grad = (probs * (prob_grad - row_carry)).astype(LOW)
    query_grad = (
        jnp.einsum("hqk,khd->qhd", score_grad, key_rows, preferred_element_type=FULL) * score_scale
    )
    key_grad = (
        jnp.einsum("hqk,qhd->khd", score_grad, queries, preferred_element_type=FULL) * score_scale
    )
    value_grad = jnp.einsum("hqk,qhd->khd", prob_low, mixed_grad, preferred_element_type=FULL)
    qk_grad = jnp.concatenate(
        [query_grad.reshape(group_rows, inner_width), key_grad.reshape(group_rows, inner_width)],
        axis=1,
    ).astype(LOW)
    v_grad = value_grad.reshape(group_rows, inner_width).astype(LOW)
    grad_qk_part = contract_rows(h_one, qk_grad)
    grad_v_part = contract_rows(h_one, v_grad)
    one_grad_part = contract_cols(qk_grad, qk_full) + contract_cols(v_grad, ve_full[:, :inner_width])
    gain_one_part = jnp.sum(one_grad_part * normed_one, axis=0)
    extra_part = jnp.concatenate(
        [
            gain_one_part[:, None],
            gain_two_part[:, None],
            router_part,
            jnp.zeros((model_width, extra_width - 2 - experts), FULL),
        ],
        axis=1,
    )
    proj_sum = reduce_dp(grad_proj_part, order_b[::-1])
    qk_sum = reduce_dp(grad_qk_part, order_a[::-1])
    ve_sum = reduce_dp(jnp.concatenate([grad_v_part, extra_part], axis=1), order_b[::-1])
    one_grad = rows_at(one_grad_part, own_start) + swap(
        rows_at(one_grad_part, other_start).astype(LOW)
    ).astype(FULL)
    own_normed = rows_at(normed_one, own_start)
    scaled_one = one_grad * gain_one
    grad_in = rows_at(resid_grad, own_start) + rows_at(inv_one, own_start) * (
        scaled_one - own_normed * jnp.mean(scaled_one * own_normed, axis=1, keepdims=True)
    )
    extra_sum = ve_sum[:, inner_width:]
    extra_sum = extra_sum + swap(extra_sum)
    share = extra_sum.shape[0] // 2
    extra_own = lax.dynamic_slice_in_dim(extra_sum, core * share, share, 0)
    return (
        block_out,
        grad_in,
        qk_sum[:, :inner_width],
        qk_sum[:, inner_width:],
        ve_sum[:, :inner_width],
        proj_sum.T,
        extra_own[:, 2 : 2 + experts],
        extra_own[:, 0],
        extra_own[:, 1],
        grad_first[None],
        grad_second[None],
    )


def solution(mesh):
    in_specs = (
        P(("dp", "tensor"), None),
        P("dp", None),
        P("dp", None),
        P("dp", "tensor"),
        P("dp", "tensor"),
        P("dp", "tensor"),
        P("tensor", "dp"),
        P("dp", None),
        P("dp"),
        P("dp"),
        P("dp", None, "tensor"),
        P("dp", "tensor", None),
        P("dp", None),
    )
    out_specs = (
        P(("dp", "tensor"), None),
        P(("dp", "tensor"), None),
        P("dp", "tensor"),
        P("dp", "tensor"),
        P("dp", "tensor"),
        P("tensor", "dp"),
        P(("dp", "tensor"), None),
        P(("dp", "tensor")),
        P(("dp", "tensor")),
        P("dp", None, "tensor"),
        P("dp", "tensor", None),
    )
    return jax.shard_map(local, mesh=mesh, in_specs=in_specs, out_specs=out_specs, check_vma=False)
```

time: 1190 us -> 386 us (0.32)
  waiting for transfers between devices: 588 us -> 171 us
  blocking collectives: 382 us -> 17.1 us
  local copies, waits for them, and re-layouts: 54 us -> 30.5 us
  starting transfers between devices: 49.8 us -> 64.3 us
  between operations: 16.2 us -> 2.15 us
    reduce_scatter x10 -> x0, waiting for transfers between devices: 452 us -> none  [the longest x1 128 us: local(): lax.psum_scatter(grad_v_part, 'dp', scatter_dimension=0, tiled=True)]
    all_gather x7 -> x0, blocking collectives: 254 us -> none  [the longest x1 87.1 us: local(): lax.all_gather(router, 'dp', axis=0, tiled=True)]
    unnamed x3 -> x0, blocking collectives: 126 us -> none
    ppermute x0 -> x35, waiting for transfers between devices: none -> 59.3 us  [the longest x12 35 us: reduce_dp(): lax.ppermute(given, 'dp', partners(bit)).astype(FULL)]
    ppermute x0 -> x35, starting transfers between devices: none -> 34.9 us  [the longest x12 19.7 us: gather_dp(): other = lax.ppermute(block, 'dp', partners(bit))]
    all_to_all x4 -> x5, waiting for transfers between devices: 135 us -> 112 us  [trade(): return lax.all_to_all(values, 'dp', split_axis=0, concat_axis=0, tiled=True)]
    all_to_all x4 -> x5, starting transfers between devices: 48.9 us -> 29.3 us  [trade(): return lax.all_to_all(values, 'dp', split_axis=0, concat_axis=0, tiled=True)]
    gather x4 -> x0, local copies, waits for them, and re-layouts: 15.9 us -> none  [the longest x1 5.21 us: local(): padded_rows[slot_table // top_count].reshape(experts, capacity, model_width)]
  transfers between devices with their start and end apart: 14 -> 40, of which waited for: 8 -> 25; matrix products, arithmetic and copies ran while one was open for 8% -> 18% of each run, Pallas kernels for 0% -> 0%
where the time goes in v1:
time: 386 us; the launch traced here: 379 us
  waiting for transfers between devices  171 us (44%)
  matrix products  72.1 us (19%)
  starting transfers between devices  64.3 us (17%)
  local copies, waits for them, and re-layouts  30.5 us (8%)
  other arithmetic  21.5 us (6%)
  blocking collectives  17.1 us (4%)
    all_to_all x5, waiting for transfers between devices, trade(): return lax.all_to_all(values, 'dp', split_axis=0, concat_axis=0, tiled=True)  112 us
    ppermute x12, waiting for transfers between devices, reduce_dp(): lax.ppermute(given, 'dp', partners(bit)).astype(FULL)  35 us
    all_to_all x5, starting transfers between devices, trade(): return lax.all_to_all(values, 'dp', split_axis=0, concat_axis=0, tiled=True)  29.3 us
    dot_general x7, matrix products, contract_rows(): lax.dot_general(left_side, right_side, (((0,), (0,)), ((), ())), preferre...  22.1 us
    dot_general x6, matrix products, contract_cols(): lax.dot_general(left_side, right_side, (((1,), (1,)), ((), ())), preferre...  20.7 us
    ppermute x12, starting transfers between devices, gather_dp(): other = lax.ppermute(block, 'dp', partners(bit))  19.7 us
    dot_general x8, matrix products, dot(): return jnp.dot(left_side, right_side, preferred_element_type=FULL)  19.2 us
    ppermute x12, waiting for transfers between devices, gather_dp(): other = lax.ppermute(block, 'dp', partners(bit))  18.2 us
  transfers between devices with their start and end apart: 40, of which 25 were waited for; matrix products, arithmetic and copies ran while one was open for 18% of the time, Pallas kernels for 0%

profile of v1, /device:TPU:0, one launch (start us, length us, event | category | flops | bytes accessed | tf_op | source)
XLA Modules:
  0.0 378.9 jit_solution(3107508370623559279)
XLA Ops:
  3.9 4.1 %collective-permute-start = (bf16[1,1,1,1,48,512]{5,4,0,3,2,1:T(8,128)(2,1)S(1)}, bf16[1,1,1,1,48,512]{5,4,0,3,2,1:T(8,128)(2,1)S(1)}, u32[]{:S(2)}, u32[]{:S(2)}) collective-permute-start(bf16[1,1,1,1,48,512]{5,4,0,3,2,1:T(8,128)(2,1)S(1)} %bitcast.276), channel_id=1, source_target_pairs={{0,16},{2,18},{4,20},{6,22},{8,24},{10,26},{12,28},{14,30},{16,0},... | collective-permute-start | bytes 147464 | tf_op jit(solution)/shard_map/ppermute | solution.py:57
  33.5 4.6 %collective-permute-done.6 = bf16[2,2,1,1,48,768]{5,4,3,2,1,0:T(8,128)(2,1)} collective-permute-done((bf16[2,2,1,1,48,768]{5,4,3,2,1,0:T(8,128)(2,1)}, bf16[2,2,1,1,48,768]{5,4,3,2,1,0:T(8,128)(2,1)}, u32[]{:S(2)}, u32[]{:S(2)}) %collective-permute-start.6) | collective-permute-done | bytes 294944 | tf_op jit(solution)/shard_map/ppermute | solution.py:57
  45.6 5.6 %collective-permute-done.3 = bf16[2,2,1,2,48,512]{5,4,3,2,1,0:T(8,128)(2,1)} collective-permute-done((bf16[2,2,1,2,48,512]{5,4,3,2,1,0:T(8,128)(2,1)S(1)}, bf16[2,2,1,2,48,512]{5,4,3,2,1,0:T(8,128)(2,1)}, u32[]{:S(2)}, u32[]{:S(2)}) %collective-permute-start.3) | collective-permute-done | bytes 393248 | tf_op jit(solution)/shard_map/ppermute | solution.py:57
  71.3 4.4 %all-to-all-start.1 = ((bf16[16,64,768]{2,1,0:T(8,128)(2,1)}), bf16[16,64,768]{2,1,0:T(8,128)(2,1)}, u32[]{:S(2)}, u32[]{:S(2)}) async-start(bf16[16,64,768]{2,1,0:T(8,128)(2,1)} %bitcast.248), calls=%async_computation.1 | async-start | bytes 3145728 | tf_op jit(solution)/shard_map/all_to_all | solution.py:81
  78.6 31.4 %all-to-all-done.1 = bf16[16,64,768]{2,1,0:T(8,128)(2,1)} async-done(((bf16[16,64,768]{2,1,0:T(8,128)(2,1)}), bf16[16,64,768]{2,1,0:T(8,128)(2,1)}, u32[]{:S(2)}, u32[]{:S(2)}) %all-to-all-start.1) | async-done | bytes 1572896 | tf_op jit(solution)/shard_map/all_to_all | solution.py:81
  110.0 8.5 %all-to-all-start.3 = ((bf16[16,64,768]{2,1,0:T(8,128)(2,1)}), bf16[16,64,768]{2,1,0:T(8,128)(2,1)}, u32[]{:S(2)}, u32[]{:S(2)}) async-start(bf16[16,64,768]{2,1,0:T(8,128)(2,1)} %bitcast.247), calls=%async_computation.3 | async-start | bytes 3145728 | tf_op jit(solution)/shard_map/all_to_all | solution.py:81
  118.6 33.8 %all-to-all-done.3 = bf16[16,64,768]{2,1,0:T(8,128)(2,1)} async-done(((bf16[16,64,768]{2,1,0:T(8,128)(2,1)}), bf16[16,64,768]{2,1,0:T(8,128)(2,1)}, u32[]{:S(2)}, u32[]{:S(2)}) %all-to-all-start.3) | async-done | bytes 1572896 | tf_op jit(solution)/shard_map/all_to_all | solution.py:81
  153.1 14.6 %all_to_all.38 = f32[16,1,64]{2,1,0:T(1,128)S(1)} all-to-all(f32[16,1,64]{2,1,0:T(1,128)S(1)} %bitcast.297), channel_id=1, replica_groups=mesh['dp'=16,'tensor'=2] {'dp'}, dimensions={0} | all-to-all | bytes 8192 | tf_op jit(solution)/shard_map/all_to_all | solution.py:81
  168.9 5.0 %fusion.9 = f32[2048,768]{0,1:T(8,128)S(1)} fusion(bf16[1024,768]{1,0:T(8,128)(2,1)} %collective-permute-done.13, bf16[1024,768]{1,0:T(8,128)(2,1)} %bitcast.59, bf16[1,768,768]{2,1,0:T(8,128)(2,1)} %param.23), kind=kOutput, calls=%fused_computation.19 | convolution fusion | flops 2422210560 | bytes 10616832 | tf_op jit(solution)/shard_map/dot_general | solution.py:18
  174.0 10.2 %multiply_reduce_fusion = (f32[2048]{0:T(1024)S(1)}, bf16[2048,768]{0,1:T(8,128)(2,1)}, bf16[2048,768]{0,1:T(8,128)(2,1)S(1)}) fusion(f32[2048,768]{0,1:T(8,128)S(1)} %fusion.9, bf16[1,768,768]{2,1,0:T(8,128)(2,1)S(1)} %copy-done, bf16[1024,768]{1,0:T(8,128)(2,1)} %collective-permute-done.17, bf16[1024,768]{1,0:T(8,128)(2,1)} %bitcast.67, ...), kind=kOutput, calls=%fused_computation.10 | convolution fusion | flops 2464675840 | bytes 16924672 | tf_op jit(solution)/shard_map/dot_general | solution.py:28
  194.2 4.8 %add_convert_fusion = bf16[1024,768]{1,0:T(8,128)(2,1)} fusion(bf16[1024,768]{1,0:T(8,128)(2,1)} %collective-permute-done.18, bf16[2048,768]{0,1:T(8,128)(2,1)} %copy-done.47, bf16[1,768,768]{2,1,0:T(8,128)(2,1)} %param.23), kind=kOutput, calls=%fused_computation.14 | convolution fusion | flops 1210318848 | bytes 5898240 | tf_op jit(solution)/shard_map/dot_general | solution.py:28
  201.4 4.6 %all-to-all-start.4 = ((bf16[16,64,768]{2,1,0:T(8,128)(2,1)}), bf16[16,64,768]{2,1,0:T(8,128)(2,1)}, u32[]{:S(2)}, u32[]{:S(2)}) async-start(bf16[16,64,768]{2,1,0:T(8,128)(2,1)} %bitcast.264), calls=%async_computation.4 | async-start | bytes 3145728 | tf_op jit(solution)/shard_map/all_to_all | solution.py:81
  206.0 4.0 %multiply_convert_fusion.2 = bf16[1024,768]{1,0:T(8,128)(2,1)} fusion(f32[1024]{0:T(1024)S(1)} %bitcast.300, bf16[1,768,768]{2,1,0:T(8,128)(2,1)S(1)} %copy-done, bf16[2048,768]{0,1:T(8,128)(2,1)} %get-tuple-element.88), kind=kOutput, calls=%fused_computation.16 | convolution fusion | flops 1209532416 | bytes 4329472 | tf_op jit(solution)/shard_map/dot_general | solution.py:18
  217.1 23.2 %all-to-all-done.4 = bf16[16,64,768]{2,1,0:T(8,128)(2,1)} async-done(((bf16[16,64,768]{2,1,0:T(8,128)(2,1)}), bf16[16,64,768]{2,1,0:T(8,128)(2,1)}, u32[]{:S(2)}, u32[]{:S(2)}) %all-to-all-start.4) | async-done | bytes 1572896 | tf_op jit(solution)/shard_map/all_to_all | solution.py:81
  240.3 8.3 %all-to-all-start.2 = ((bf16[16,64,768]{2,1,0:T(8,128)(2,1)}), bf16[16,64,768]{2,1,0:T(8,128)(2,1)}, u32[]{:S(2)}, u32[]{:S(2)}) async-start(bf16[16,64,768]{2,1,0:T(8,128)(2,1)} %bitcast.249), calls=%async_computation.2 | async-start | bytes 3145728 | tf_op jit(solution)/shard_map/all_to_all | solution.py:81
  250.2 7.0 %convolution_bitcast_fusion = f32[1,768,768]{2,1,0:T(8,128)} fusion(bf16[2048,768]{0,1:T(8,128)(2,1)} %get-tuple-element.88, bf16[1024,768]{1,0:T(8,128)(2,1)} %collective-permute-done.17, bf16[1024,768]{1,0:T(8,128)(2,1)} %bitcast.67, f32[2048]{0:T(1024)S(1)} %bitcast.299), kind=kOutput, calls=%fused_computation.23 | convolution fusion | flops 2425356288 | bytes 8658944 | tf_op jit(solution)/shard_map/dot_general | solution.py:22
  260.9 21.1 %all-to-all-done.2 = bf16[16,64,768]{2,1,0:T(8,128)(2,1)} async-done(((bf16[16,64,768]{2,1,0:T(8,128)(2,1)}), bf16[16,64,768]{2,1,0:T(8,128)(2,1)}, u32[]{:S(2)}, u32[]{:S(2)}) %all-to-all-start.2) | async-done | bytes 1572896 | tf_op jit(solution)/shard_map/all_to_all | solution.py:81
  284.4 6.0 %fusion.13 = f32[1,768,768]{2,1,0:T(8,128)} fusion(bf16[2048,768]{0,1:T(8,128)(2,1)S(1)} %copy-done.48, bf16[1024,768]{1,0:T(8,128)(2,1)} %collective-permute-done.13, bf16[1024,768]{1,0:T(8,128)(2,1)} %bitcast.59), kind=kOutput, calls=%fused_computation.24 | convolution fusion | flops 2422210560 | bytes 8650752 | tf_op jit(solution)/shard_map/dot_general | solution.py:22
  312.0 3.9 %concatenate.627 = f32[2,2,2,2,48,512]{5,4,3,2,1,0:T(8,128)} concatenate(f32[2,2,2,2,48,384]{5,4,3,2,1,0:T(8,128)} %fusion.87, f32[2,2,2,2,48,1]{5,4,3,2,1,0:T(8,128)} %concatenate.628, f32[2,2,2,2,48,1]{5,4,3,2,1,0:T(8,128)} %mul.298, f32[2,2,2,2,48,8]{5,4,3,2,1,0:T(8,128)} %bitcast.266, f32[2,2,2,2,48,118]{5,4,3,2,1,0:T(8,128)} %broadcast_in_dim.119), dimensions={5} | concatenate | bytes 3145728 | tf_op jit(solution)/shard_map/concatenate | solution.py:277
  327.6 9.2 %collective-permute-done.30 = bf16[2,2,1,2,48,384]{5,4,3,2,1,0:T(8,128)(2,1)S(1)} collective-permute-done((bf16[2,2,1,2,48,384]{5,4,3,2,1,0:T(8,128)(2,1)S(1)}, bf16[2,2,1,2,48,384]{5,4,3,2,1,0:T(8,128)(2,1)S(1)}, u32[]{:S(2)}, u32[]{:S(2)}) %collective-permute-start.30) | collective-permute-done | bytes 294944 | tf_op jit(solution)/shard_map/ppermute | solution.py:76
  338.7 5.5 %collective-permute-done.31 = bf16[2,2,1,1,48,384]{5,4,3,2,1,0:T(8,128)(2,1)S(1)} collective-permute-done((bf16[2,2,1,1,48,384]{5,4,3,2,1,0:T(8,128)(2,1)S(1)}, bf16[2,2,1,1,48,384]{5,4,3,2,1,0:T(8,128)(2,1)S(1)}, u32[]{:S(2)}, u32[]{:S(2)}) %collective-permute-start.31) | collective-permute-done | bytes 147488 | tf_op jit(solution)/shard_map/ppermute | solution.py:76
  344.3 3.9 %collective-permute-start.32 = (bf16[2,1,1,1,48,384]{5,4,3,2,1,0:T(8,128)(2,1)S(1)}, bf16[2,1,1,1,48,384]{5,4,3,2,1,0:T(8,128)(2,1)S(1)}, u32[]{:S(2)}, u32[]{:S(2)}) collective-permute-start(bf16[2,1,1,1,48,384]{5,4,3,2,1,0:T(8,128)(2,1)S(1)} %dynamic-slice_convert_fusion.9), channel_id=1, source_target_pairs={{0,8},{2,10},{4,12},{6,14},{8,0},{10,2},{12,4},{14,6},{16,24},{18,... | collective-permute-start | bytes 221192 | tf_op jit(solution)/shard_map/ppermute | solution.py:76
  367.2 4.1 %collective-permute-done.24 = bf16[2,1,1,1,48,768]{5,4,3,2,1,0:T(8,128)(2,1)S(1)} collective-permute-done((bf16[2,1,1,1,48,768]{5,4,3,2,1,0:T(8,128)(2,1)S(1)}, bf16[2,1,1,1,48,768]{5,4,3,2,1,0:T(8,128)(2,1)S(1)}, u32[]{:S(2)}, u32[]{:S(2)}) %collective-permute-start.24) | collective-permute-done | bytes 147488 | tf_op jit(solution)/shard_map/ppermute | solution.py:76
  372.2 5.6 %collective-permute-done.25 = bf16[1,1,1,1,48,768]{5,4,3,2,1,0:T(8,128)(2,1)S(1)} collective-permute-done((bf16[1,1,1,1,48,768]{5,4,3,2,1,0:T(8,128)(2,1)S(1)}, bf16[1,1,1,1,48,768]{5,4,3,2,1,0:T(8,128)(2,1)S(1)}, u32[]{:S(2)}, u32[]{:S(2)}) %collective-permute-start.25) | collective-permute-done | bytes 73760 | tf_op jit(solution)/shard_map/ppermute | solution.py:76
  (295 shorter events, 143.3 us)
Async XLA Ops:
  3.9 14.6 %collective-permute-start = (bf16[1,1,1,1,48,512]{5,4,0,3,2,1:T(8,128)(2,1)S(1)}, bf16[1,1,1,1,48,512]{5,4,0,3,2,1:T(8,128)(2,1)S(1)}, u32[]{:S(2)}, u32[]{:S(2)}) collective-permute-start(bf16[1,1,1,1,48,512]{5,4,0,3,2,1:T(8,128)(2,1)S(1)} %bitcast.276), channel_id=1, source_target_pairs={{0,16},{2,18},{4,20},{6,22},{8,24},{10,26},{12,28},{14,30},{16,0},... | collective-permute-start | bytes 147464 | tf_op jit(solution)/shard_map/ppermute | solution.py:57
  9.6 10.1 %collective-permute-start.4 = (bf16[1,1,1,1,48,768]{5,4,0,3,2,1:T(8,128)(2,1)S(1)}, bf16[1,1,1,1,48,768]{5,4,0,3,2,1:T(8,128)(2,1)S(1)}, u32[]{:S(2)}, u32[]{:S(2)}) collective-permute-start(bf16[1,1,1,1,48,768]{5,4,0,3,2,1:T(8,128)(2,1)S(1)} %bitcast.268), channel_id=1, source_target_pairs={{0,16},{2,18},{4,20},{6,22},{8,24},{10,26},{12,28},{14,30},{16,0},... | collective-permute-start | bytes 221192 | tf_op jit(solution)/shard_map/ppermute | solution.py:57
  9.6 7.8 %collective-permute-start.8 = (bf16[1,1,1,1,48,384]{5,4,0,3,2,1:T(8,128)(2,1)}, bf16[1,1,1,1,48,384]{5,4,0,3,2,1:T(8,128)(2,1)S(1)}, u32[]{:S(2)}, u32[]{:S(2)}) collective-permute-start(bf16[1,1,1,1,48,384]{5,4,0,3,2,1:T(8,128)(2,1)} %bitcast.286), channel_id=1, source_target_pairs={{0,16},{2,18},{4,20},{6,22},{8,24},{10,26},{12,28},{14,30},{16,0},... | collective-permute-start | bytes 110600 | tf_op jit(solution)/shard_map/ppermute | solution.py:57
  19.7 7.4 %collective-permute-start.5 = (bf16[2,1,1,1,48,768]{5,4,0,3,2,1:T(8,128)(2,1)S(1)}, bf16[2,1,1,1,48,768]{5,4,0,3,2,1:T(8,128)(2,1)S(1)}, u32[]{:S(2)}, u32[]{:S(2)}) collective-permute-start(bf16[2,1,1,1,48,768]{5,4,0,3,2,1:T(8,128)(2,1)S(1)} %fusion.51), channel_id=1, source_target_pairs={{0,8},{2,10},{4,12},{6,14},{8,0},{10,2},{12,4},{14,6},{16,24},{18,... | collective-permute-start | bytes 442376 | tf_op jit(solution)/shard_map/ppermute | solution.py:57
  24.6 7.2 %collective-permute-start.2 = (bf16[2,2,1,1,48,512]{5,4,3,2,1,0:T(8,128)(2,1)S(1)}, bf16[2,2,1,1,48,512]{5,4,3,2,1,0:T(8,128)(2,1)S(1)}, u32[]{:S(2)}, u32[]{:S(2)}) collective-permute-start(bf16[2,2,1,1,48,512]{5,4,3,2,1,0:T(8,128)(2,1)S(1)} %copy.207), channel_id=1, source_target_pairs={{0,2},{2,0},{4,6},{6,4},{8,10},{10,8},{12,14},{14,12},{16,18},{18,... | collective-permute-start | bytes 589832 | tf_op jit(solution)/shard_map/ppermute | solution.py:57
  27.8 10.3 %collective-permute-start.6 = (bf16[2,2,1,1,48,768]{5,4,3,2,1,0:T(8,128)(2,1)}, bf16[2,2,1,1,48,768]{5,4,3,2,1,0:T(8,128)(2,1)}, u32[]{:S(2)}, u32[]{:S(2)}) collective-permute-start(bf16[2,2,1,1,48,768]{5,4,3,2,1,0:T(8,128)(2,1)} %copy.214), channel_id=1, source_target_pairs={{0,4},{2,6},{4,0},{6,2},{8,12},{10,14},{12,8},{14,10},{16,20},{18,... | collective-permute-start | bytes 884744 | tf_op jit(solution)/shard_map/ppermute | solution.py:57
  29.4 15.0 %collective-permute-start.11 = (bf16[2,2,1,2,48,384]{5,4,3,2,1,0:T(8,128)(2,1)S(1)}, bf16[2,2,1,2,48,384]{5,4,3,2,1,0:T(8,128)(2,1)}, u32[]{:S(2)}, u32[]{:S(2)}) collective-permute-start(bf16[2,2,1,2,48,384]{5,4,3,2,1,0:T(8,128)(2,1)S(1)} %maximum_select_fusion.7), channel_id=1, source_target_pairs={{0,4},{2,6},{4,0},{6,2},{8,12},{10,14},{12,8},{14,10},{16,20},{18,... | collective-permute-start | bytes 884744 | tf_op jit(solution)/shard_map/ppermute | solution.py:57
  31.9 19.4 %collective-permute-start.3 = (bf16[2,2,1,2,48,512]{5,4,3,2,1,0:T(8,128)(2,1)S(1)}, bf16[2,2,1,2,48,512]{5,4,3,2,1,0:T(8,128)(2,1)}, u32[]{:S(2)}, u32[]{:S(2)}) collective-permute-start(bf16[2,2,1,2,48,512]{5,4,3,2,1,0:T(8,128)(2,1)S(1)} %maximum_select_fusion.4), channel_id=1, source_target_pairs={{0,4},{2,6},{4,0},{6,2},{8,12},{10,14},{12,8},{14,10},{16,20},{18,... | collective-permute-start | bytes 1179656 | tf_op jit(solution)/shard_map/ppermute | solution.py:57
  39.2 15.0 %collective-permute-start.7 = (bf16[2,2,2,1,48,768]{5,4,3,2,1,0:T(8,128)(2,1)S(1)}, bf16[2,2,2,1,48,768]{5,4,3,2,1,0:T(8,128)(2,1)S(1)}, u32[]{:S(2)}, u32[]{:S(2)}) collective-permute-start(bf16[2,2,2,1,48,768]{5,4,3,2,1,0:T(8,128)(2,1)S(1)} %maximum_select_fusion.2), channel_id=1, source_target_pairs={{0,2},{2,0},{4,6},{6,4},{8,10},{10,8},{12,14},{14,12},{16,18},{18,... | collective-permute-start | bytes 1769480 | tf_op jit(solution)/shard_map/ppermute | solution.py:57
  71.3 38.7 %all-to-all-start.1 = ((bf16[16,64,768]{2,1,0:T(8,128)(2,1)}), bf16[16,64,768]{2,1,0:T(8,128)(2,1)}, u32[]{:S(2)}, u32[]{:S(2)}) async-start(bf16[16,64,768]{2,1,0:T(8,128)(2,1)} %bitcast.248), calls=%async_computation.1 | async-start | bytes 3145728 | tf_op jit(solution)/shard_map/all_to_all | solution.py:81
  110.0 42.4 %all-to-all-start.3 = ((bf16[16,64,768]{2,1,0:T(8,128)(2,1)}), bf16[16,64,768]{2,1,0:T(8,128)(2,1)}, u32[]{:S(2)}, u32[]{:S(2)}) async-start(bf16[16,64,768]{2,1,0:T(8,128)(2,1)} %bitcast.247), calls=%async_computation.3 | async-start | bytes 3145728 | tf_op jit(solution)/shard_map/all_to_all | solution.py:81
  118.5 50.4 %collective-permute-start.13 = (bf16[1024,768]{1,0:T(8,128)(2,1)}, bf16[1024,768]{1,0:T(8,128)(2,1)}, u32[]{:S(2)}, u32[]{:S(2)}) collective-permute-start(bf16[1024,768]{1,0:T(8,128)(2,1)} %bitcast.59), channel_id=1, source_target_pairs={{0,1},{1,0},{2,3},{3,2},{4,5},{5,4},{6,7},{7,6},{8,9},{9,8},{10,11... | collective-permute-start | bytes 4718600 | tf_op jit(solution)/shard_map/ppermute | solution.py:40
  152.4 21.6 %collective-permute-start.17 = (bf16[1024,768]{1,0:T(8,128)(2,1)}, bf16[1024,768]{1,0:T(8,128)(2,1)}, u32[]{:S(2)}, u32[]{:S(2)}) collective-permute-start(bf16[1024,768]{1,0:T(8,128)(2,1)} %bitcast.67), channel_id=1, source_target_pairs={{0,1},{1,0},{2,3},{3,2},{4,5},{5,4},{6,7},{7,6},{8,9},{9,8},{10,11... | collective-permute-start | bytes 4718600 | tf_op jit(solution)/shard_map/ppermute | solution.py:40
  186.8 7.4 %collective-permute-start.18 = (bf16[1024,768]{1,0:T(8,128)(2,1)}, bf16[1024,768]{1,0:T(8,128)(2,1)}, u32[]{:S(2)}, u32[]{:S(2)}) collective-permute-start(bf16[1024,768]{1,0:T(8,128)(2,1)} %convolution_convert_fusion.1), channel_id=1, source_target_pairs={{0,1},{1,0},{2,3},{3,2},{4,5},{5,4},{6,7},{7,6},{8,9},{9,8},{10,11... | collective-permute-start | bytes 4718600 | tf_op jit(solution)/shard_map/ppermute | solution.py:40
  190.7 10.7 %all-to-all-start.5 = ((f32[16,1,64]{2,1,0:T(1,128)}), f32[16,1,64]{2,1,0:T(1,128)S(1)}, u32[]{:S(2)}, u32[]{:S(2)}) async-start(f32[16,1,64]{2,1,0:T(1,128)} %all_to_all.30), calls=%async_computation.5 | async-start | bytes 16384 | tf_op jit(solution)/shard_map/all_to_all | solution.py:81
  201.4 38.9 %all-to-all-start.4 = ((bf16[16,64,768]{2,1,0:T(8,128)(2,1)}), bf16[16,64,768]{2,1,0:T(8,128)(2,1)}, u32[]{:S(2)}, u32[]{:S(2)}) async-start(bf16[16,64,768]{2,1,0:T(8,128)(2,1)} %bitcast.264), calls=%async_computation.4 | async-start | bytes 3145728 | tf_op jit(solution)/shard_map/all_to_all | solution.py:81
  240.3 41.6 %all-to-all-start.2 = ((bf16[16,64,768]{2,1,0:T(8,128)(2,1)}), bf16[16,64,768]{2,1,0:T(8,128)(2,1)}, u32[]{:S(2)}, u32[]{:S(2)}) async-start(bf16[16,64,768]{2,1,0:T(8,128)(2,1)} %bitcast.249), calls=%async_computation.2 | async-start | bytes 3145728 | tf_op jit(solution)/shard_map/all_to_all | solution.py:81
  260.8 31.8 %collective-permute-start.20 = (f32[256,768]{1,0:T(8,128)S(1)}, f32[256,768]{1,0:T(8,128)}, u32[]{:S(2)}, u32[]{:S(2)}) collective-permute-start(f32[256,768]{1,0:T(8,128)S(1)} %convolution_add_fusion.1), channel_id=1, source_target_pairs={{0,1},{1,0},{2,3},{3,2},{4,5},{5,4},{6,7},{7,6},{8,9},{9,8},{10,11... | collective-permute-start | bytes 2359304 | tf_op jit(solution)/shard_map/ppermute | solution.py:40
  284.3 7.4 %collective-permute-start.16 = (f32[128,768]{1,0:T(8,128)S(1)}, f32[128,768]{1,0:T(8,128)S(1)}, u32[]{:S(2)}, u32[]{:S(2)}) collective-permute-start(f32[128,768]{1,0:T(8,128)S(1)} %constant_dynamic-slice_fusion), channel_id=1, source_target_pairs={{0,1},{1,0},{2,3},{3,2},{4,5},{5,4},{6,7},{7,6},{8,9},{9,8},{10,11... | collective-permute-start | bytes 1179656 | tf_op jit(solution)/shard_map/ppermute | solution.py:40
  317.8 19.8 %collective-permute-start.26 = (bf16[2,2,1,2,48,512]{5,4,3,2,1,0:T(8,128)(2,1)}, bf16[2,2,1,2,48,512]{5,4,3,2,1,0:T(8,128)(2,1)}, u32[]{:S(2)}, u32[]{:S(2)}) collective-permute-start(bf16[2,2,1,2,48,512]{5,4,3,2,1,0:T(8,128)(2,1)} %dynamic-slice_convert_fusion.1), channel_id=1, source_target_pairs={{0,4},{2,6},{4,0},{6,2},{8,12},{10,14},{12,8},{14,10},{16,20},{18,... | collective-permute-start | bytes 1179656 | tf_op jit(solution)/shard_map/ppermute | solution.py:76
  325.3 11.4 %collective-permute-start.30 = (bf16[2,2,1,2,48,384]{5,4,3,2,1,0:T(8,128)(2,1)S(1)}, bf16[2,2,1,2,48,384]{5,4,3,2,1,0:T(8,128)(2,1)S(1)}, u32[]{:S(2)}, u32[]{:S(2)}) collective-permute-start(bf16[2,2,1,2,48,384]{5,4,3,2,1,0:T(8,128)(2,1)S(1)} %dynamic-slice_convert_fusion.2), channel_id=1, source_target_pairs={{0,4},{2,6},{4,0},{6,2},{8,12},{10,14},{12,8},{14,10},{16,20},{18,... | collective-permute-start | bytes 884744 | tf_op jit(solution)/shard_map/ppermute | solution.py:76
  325.8 28.7 %collective-permute-start.22 = (bf16[2,2,2,1,48,768]{5,4,3,2,1,0:T(8,128)(2,1)S(1)}, bf16[2,2,2,1,48,768]{5,4,3,2,1,0:T(8,128)(2,1)S(1)}, u32[]{:S(2)}, u32[]{:S(2)}) collective-permute-start(bf16[2,2,2,1,48,768]{5,4,3,2,1,0:T(8,128)(2,1)S(1)} %dynamic-slice_convert_fusion), channel_id=1, source_target_pairs={{0,2},{2,0},{4,6},{6,4},{8,10},{10,8},{12,14},{14,12},{16,18},{18,... | collective-permute-start | bytes 1769480 | tf_op jit(solution)/shard_map/ppermute | solution.py:76
  336.9 7.4 %collective-permute-start.31 = (bf16[2,2,1,1,48,384]{5,4,3,2,1,0:T(8,128)(2,1)S(1)}, bf16[2,2,1,1,48,384]{5,4,3,2,1,0:T(8,128)(2,1)S(1)}, u32[]{:S(2)}, u32[]{:S(2)}) collective-permute-start(bf16[2,2,1,1,48,384]{5,4,3,2,1,0:T(8,128)(2,1)S(1)} %dynamic-slice_convert_fusion.6), channel_id=1, source_target_pairs={{0,2},{2,0},{4,6},{6,4},{8,10},{10,8},{12,14},{14,12},{16,18},{18,... | collective-permute-start | bytes 442376 | tf_op jit(solution)/shard_map/ppermute | solution.py:76
  354.7 10.3 %collective-permute-start.23 = (bf16[2,2,1,1,48,768]{5,4,3,2,1,0:T(8,128)(2,1)S(1)}, bf16[2,2,1,1,48,768]{5,4,3,2,1,0:T(8,128)(2,1)S(1)}, u32[]{:S(2)}, u32[]{:S(2)}) collective-permute-start(bf16[2,2,1,1,48,768]{5,4,3,2,1,0:T(8,128)(2,1)S(1)} %dynamic-slice_convert_fusion.3), channel_id=1, source_target_pairs={{0,4},{2,6},{4,0},{6,2},{8,12},{10,14},{12,8},{14,10},{16,20},{18,... | collective-permute-start | bytes 884744 | tf_op jit(solution)/shard_map/ppermute | solution.py:76
  (65 other events, 795.9 us)

commit v2 on v1

v2 whole, which is shorter than its diff:
```python
import math

import jax
import jax.numpy as jnp
from jax import lax
from jax.experimental import pallas as pl
from jax.experimental.pallas import tpu as pltpu
from jax.sharding import PartitionSpec as P

HEAD_DIM = 64
LANES = 128


EPSILON = 1e-06
NEGATIVE = -1e30
VMEM_BYTES = 48 * 1024 * 1024
EXTRA_ROWS = 16
LOW = jnp.bfloat16
FULL = jnp.float32


def dot(left_side, right_side):
    return jnp.dot(left_side, right_side, preferred_element_type=FULL)


def contract_rows(left_side, right_side):
    return lax.dot_general(
        left_side, right_side, (((0,), (0,)), ((), ())), preferred_element_type=FULL
    )


def contract_cols(left_side, right_side):
    return lax.dot_general(
        left_side, right_side, (((1,), (1,)), ((), ())), preferred_element_type=FULL
    )


def split_low(values):
    high = values.astype(LOW)
    return high, (values - high.astype(FULL)).astype(LOW)


def iota(shape, axis):
    return lax.broadcasted_iota(jnp.int32, shape, axis)


def swap(values):
    return lax.ppermute(values, "tensor", [(0, 1), (1, 0)])


def bit_orders():
    bits = lax.axis_size("dp").bit_length() - 1
    falling = list(range(bits - 1, -1, -1))
    return falling, falling[:-2] + [falling[-1], falling[-2]]


def partners(bit):
    return [(i, i ^ (1 << bit)) for i in range(lax.axis_size("dp"))]


def double(block, bit, bits):
    other = lax.ppermute(block, "dp", partners(bit))
    axis = bits - 1 - bit
    upper = ((lax.axis_index("dp") >> bit) & 1) == 1
    return jnp.where(
        upper,
        jnp.concatenate([other, block], axis=axis),
        jnp.concatenate([block, other], axis=axis),
    )


def halve(block, bit, bits):
    axis, place = bits - 1 - bit, (lax.axis_index("dp") >> bit) & 1
    given = lax.dynamic_index_in_dim(block, 1 - place, axis, keepdims=True).astype(LOW)
    kept = lax.dynamic_index_in_dim(block, place, axis, keepdims=True)
    return kept.astype(FULL) + lax.ppermute(given, "dp", partners(bit)).astype(FULL)


def trade(values):
    return lax.all_to_all(values, "dp", split_axis=0, concat_axis=0, tiled=True)


def call(kernel, out_shape, *operands, flops=0, smem=()):
    moved = sum(x.size * x.dtype.itemsize for x in (*operands, *out_shape))
    return pl.pallas_call(
        kernel,
        out_shape=out_shape,
        in_specs=[
            pl.BlockSpec(memory_space=pltpu.SMEM if i in smem else pltpu.VMEM)
            for i in range(len(operands))
        ],
        out_specs=[pl.BlockSpec(memory_space=pltpu.VMEM) for _ in out_shape],
        compiler_params=pltpu.CompilerParams(vmem_limit_bytes=VMEM_BYTES),
        cost_estimate=pl.CostEstimate(flops=flops, bytes_accessed=moved, transcendentals=0),
    )(*operands)


def inverse_rms(rows):
    return lax.rsqrt(jnp.mean(rows * rows, axis=1, keepdims=True) + EPSILON)


GELU_SCALE = math.sqrt(2.0 / math.pi)
GELU_CUBE = 0.044715


def attention_kernel(
    len_ref, rows_ref, qk_ref, vx_ref, attn_ref, h_ref, qkv_ref, probs_ref, mixed_ref, ext_ref
):
    group_rows = rows_ref.shape[0]
    inner = qk_ref.shape[1] // 2
    rows = rows_ref[...]
    ext = vx_ref[:, 2 * inner :].astype(FULL).T
    ext_ref[...] = ext
    h_one = (rows * inverse_rms(rows) * ext[0:1, :]).astype(LOW)
    h_ref[...] = h_one
    qkv_ref[:, : 2 * inner] = dot(h_one, qk_ref[...]).astype(LOW)
    qkv_ref[:, 2 * inner :] = dot(h_one, vx_ref[:, :inner]).astype(LOW)
    down, across = iota((group_rows, group_rows), 0), iota((group_rows, group_rows), 1)
    allowed = down >= across
    end = jnp.int32(0)
    for place in range(len_ref.shape[1]):
        end = end + len_ref[0, place]
        allowed = allowed & ((down >= end) == (across >= end))
    low_lanes = iota((group_rows, LANES), 1) < HEAD_DIM
    for pair in range(inner // LANES):
        at = pair * LANES
        queries = qkv_ref[:, at : at + LANES]
        key_rows = qkv_ref[:, inner + at : inner + at + LANES]
        value_rows = qkv_ref[:, 2 * inner + at : 2 * inner + at + LANES]
        outs = []
        for sub in range(2):
            own = low_lanes if sub == 0 else ~low_lanes
            scores = contract_cols(jnp.where(own, queries, jnp.zeros_like(queries)), key_rows)
            scores = jnp.where(allowed, scores * HEAD_DIM ** (-0.5), NEGATIVE)
            terms = jnp.exp(scores - jnp.max(scores, axis=1, keepdims=True))
            probs = terms / jnp.sum(terms, axis=1, keepdims=True)
            probs_ref[2 * pair + sub] = probs
            outs.append(dot(probs.astype(LOW), value_rows))
        mixed_ref[:, at : at + LANES] = jnp.where(low_lanes, outs[0], outs[1]).astype(LOW)
    attn_ref[...] = contract_cols(mixed_ref[...], vx_ref[:, inner : 2 * inner])


def slot_tables(slot_row, base, half):
    experts, group_rows = slot_row.shape
    count, shift = experts * half, half.bit_length() - 1
    of_expert = (iota((count, experts), 0) >> shift) == iota((count, experts), 1)
    wanted = (iota((count, 1), 0) & (half - 1)) + base
    here = dot(of_expert.astype(LOW), slot_row) == wanted.astype(FULL)
    return here, of_expert


def dispatch_kernel(
    base_ref, rows_ref, attn_ref, other_ref, ext_ref, slot_ref, resid_ref, h_ref, gates_ref, send_ref
):
    experts, owners, rows_sent, _ = send_ref.shape
    blocks = rows_ref.shape[1] // LANES
    half = (rows_sent - EXTRA_ROWS) // blocks
    count = experts * half
    residual = rows_ref[...] + (attn_ref[...] + other_ref[...])
    resid_ref[...] = residual
    h_two = (residual * inverse_rms(residual) * ext_ref[1:2, :]).astype(LOW)
    h_ref[...] = h_two
    slot_row = slot_ref[...]
    hits = slot_row >= 0
    all_logits = contract_cols(ext_ref[...].astype(LOW), h_two)
    logits = all_logits[2 : 2 + experts, :]
    peak = jnp.max(jnp.where(hits, logits, NEGATIVE), axis=0, keepdims=True)
    terms = jnp.where(hits, jnp.exp(jnp.where(hits, logits - peak, 0.0)), 0.0)
    gates = terms / jnp.sum(terms, axis=0, keepdims=True)
    gates_ref[...] = gates
    here, of_expert = slot_tables(slot_row, base_ref[0], half)
    one_hot = here.astype(LOW)
    picked = dot(one_hot, h_two).astype(LOW).reshape(experts, half, blocks * LANES)
    high, low = split_low(gates)
    by_expert = contract_cols(one_hot, high) + contract_cols(one_hot, low)
    gate_col = jnp.sum(jnp.where(of_expert, by_expert, 0.0), axis=1, keepdims=True)
    on_lane = iota((count, LANES), 1) == (iota((count, LANES), 0) & (half - 1))
    high_rows, low_rows = [
        contract_rows(of_expert.astype(LOW), jnp.where(on_lane, part.astype(FULL), 0.0).astype(LOW))
        for part in split_low(gate_col)
    ]
    sub = iota((EXTRA_ROWS, LANES), 0)
    for owner in range(owners):
        for block in range(blocks):
            send_ref[:, owner, block * half : (block + 1) * half, :] = picked[
                :, :, block * LANES : (block + 1) * LANES
            ]
        for expert in range(experts):
            send_ref[expert, owner, blocks * half :, :] = jnp.where(
                sub == 0,
                high_rows[expert : expert + 1, :],
                jnp.where(sub == 1, low_rows[expert : expert + 1, :], 0.0),
            ).astype(LOW)


def rows_of(ref, half):
    blocks = (ref.shape[1] - EXTRA_ROWS) // half
    return jnp.concatenate(
        [
            ref[:, at * half : (at + 1) * half, :].reshape(ref.shape[0] * half, LANES)
            for at in range(blocks)
        ],
        axis=1,
    )


def expert_kernel(half, h_ref, cot_ref, first_ref, second_ref, back_ref, hid_ref, pre_ref, out_ref, gate_ref):
    sources = h_ref.shape[0]
    blocks = (h_ref.shape[1] - EXTRA_ROWS) // half
    count, shift = sources * half, half.bit_length() - 1
    extra = h_ref[:, blocks * half :, :].reshape(sources * EXTRA_ROWS, LANES)
    source = iota((count, sources * EXTRA_ROWS), 0) >> shift
    row = iota((count, sources * EXTRA_ROWS), 1)
    two_rows = (row == source * EXTRA_ROWS) | (row == source * EXTRA_ROWS + 1)
    on_lane = iota((count, LANES), 1) == (iota((count, LANES), 0) & (half - 1))
    gate_lanes = dot(two_rows.astype(LOW), extra)
    gate = jnp.sum(jnp.where(on_lane, gate_lanes, 0.0), axis=1, keepdims=True)
    gate_ref[...] = jnp.broadcast_to(gate, (count, LANES))
    arrived = (gate * cot_ref[...].reshape(count, blocks * LANES).astype(FULL)).astype(LOW)
    out_ref[...] = arrived
    incoming = rows_of(h_ref, half)
    pre = dot(incoming, first_ref[...])
    grad_hidden = contract_cols(arrived, second_ref[...])
    square = pre * pre
    bend = jnp.tanh(GELU_SCALE * pre * (1.0 + GELU_CUBE * square))
    rise = 0.5 * (1.0 + bend)
    hidden = (pre * rise).astype(LOW)
    hid_ref[...] = hidden
    slope = rise + (0.5 * GELU_SCALE) * pre * (1.0 - bend * bend) * (1.0 + 3.0 * GELU_CUBE * square)
    gated = jnp.sum(hidden.astype(FULL) * grad_hidden, axis=1, keepdims=True)
    grad_pre = (grad_hidden * slope).astype(LOW)
    pre_ref[...] = grad_pre
    grad_rows = contract_cols(grad_pre, first_ref[...]).astype(LOW).reshape(sources, half, blocks * LANES)
    for block in range(blocks):
        back_ref[:, block * half : (block + 1) * half, :] = grad_rows[
            :, :, block * LANES : (block + 1) * LANES
        ]
    source = iota((sources * EXTRA_ROWS, count), 1) >> shift
    row = iota((sources * EXTRA_ROWS, count), 0)
    high, low = [
        jnp.where(on_lane, part.astype(FULL), 0.0).astype(LOW) for part in split_low(gated)
    ]
    rows_back = dot((row == source * EXTRA_ROWS).astype(LOW), high) + dot(
        (row == source * EXTRA_ROWS + 1).astype(LOW), low
    )
    back_ref[:, blocks * half :, :] = rows_back.astype(LOW).reshape(sources, EXTRA_ROWS, LANES)


def expert_rows(h_rows, cot_rows, first_weight, second_weight, half):
    dp_count, rows_sent, _ = h_rows.shape
    width, hidden_width = first_weight.shape
    sources = min(dp_count, 256 // half)
    count = sources * half
    wide = lambda lanes, kind: jax.ShapeDtypeStruct((dp_count * half, lanes), kind)
    rows = lambda lanes: pl.BlockSpec((count, lanes), lambda i: (i, 0))
    block = lambda *shape: pl.BlockSpec((sources, *shape), lambda i: (i, 0, 0))
    whole = lambda array: pl.BlockSpec(array.shape, lambda i: (0, 0))
    return pl.pallas_call(
        lambda *refs: expert_kernel(half, *refs),
        grid=(dp_count // sources,),
        out_shape=[
            jax.ShapeDtypeStruct(h_rows.shape, LOW),
            wide(hidden_width, LOW),
            wide(hidden_width, LOW),
            wide(width, LOW),
            wide(LANES, FULL),
        ],
        in_specs=[
            block(rows_sent, LANES),
            block(half, width),
            whole(first_weight),
            whole(second_weight),
        ],
        out_specs=[
            block(rows_sent, LANES),
            rows(hidden_width),
            rows(hidden_width),
            rows(width),
            rows(LANES),
        ],
        compiler_params=pltpu.CompilerParams(vmem_limit_bytes=VMEM_BYTES),
        cost_estimate=pl.CostEstimate(
            flops=6 * dp_count * half * width * hidden_width,
            bytes_accessed=12 * dp_count * half * width,
            transcendentals=dp_count * half * hidden_width,
        ),
    )(h_rows, cot_rows, first_weight, second_weight)


def weight_kernel(half, h_ref, hid_ref, pre_ref, arr_ref, gate_ref, second_ref, first_in, second_in, out_ref, first_ref, second_out):
    @pl.when(pl.program_id(0) == 0)
    def _():
        first_ref[...] = first_in[...]
        second_out[...] = second_in[...]

    hidden = hid_ref[...]
    produced = dot(hidden, second_ref[...])
    out_ref[...] = (gate_ref[:, 0:1] * produced).astype(LOW)
    first_ref[...] += contract_rows(rows_of(h_ref, half), pre_ref[...])
    second_out[...] += contract_rows(hidden, arr_ref[...])


def expert_weights(h_rows, hidden, grad_pre, arrived, gate, second_weight, first_sum, second_sum, half):
    dp_count, rows_sent, _ = h_rows.shape
    hidden_width, width = second_weight.shape
    sources = min(dp_count, 512 // half)
    count = sources * half
    rows = lambda lanes: pl.BlockSpec((count, lanes), lambda i: (i, 0))
    whole = lambda array: pl.BlockSpec(array.shape, lambda i: (0, 0))
    return pl.pallas_call(
        lambda *refs: weight_kernel(half, *refs),
        grid=(dp_count // sources,),
        out_shape=[
            jax.ShapeDtypeStruct((dp_count * half, width), LOW),
            jax.ShapeDtypeStruct(first_sum.shape, FULL),
            jax.ShapeDtypeStruct(second_sum.shape, FULL),
        ],
        in_specs=[
            pl.BlockSpec((sources, rows_sent, LANES), lambda i: (i, 0, 0)),
            rows(hidden_width),
            rows(hidden_width),
            rows(width),
            rows(LANES),
            whole(second_weight),
            whole(first_sum),
            whole(second_sum),
        ],
        out_specs=[rows(width), whole(first_sum), whole(second_sum)],
        compiler_params=pltpu.CompilerParams(vmem_limit_bytes=VMEM_BYTES),
        cost_estimate=pl.CostEstimate(
            flops=6 * dp_count * half * width * hidden_width,
            bytes_accessed=10 * dp_count * half * width,
            transcendentals=0,
        ),
    )(h_rows, hidden, grad_pre, arrived, gate, second_weight, first_sum, second_sum)


def combine_kernel(base_ref, back_ref, slot_ref, col_ref, gates_ref, ext_ref, h_ref, part_ref, router_ref):
    experts, owners, rows_sent, _ = back_ref.shape
    blocks = h_ref.shape[1] // LANES
    half = (rows_sent - EXTRA_ROWS) // blocks
    count = experts * half
    slot_row = slot_ref[...]
    hits = slot_row >= 0
    here, of_expert = slot_tables(slot_row, base_ref[0], half)
    extra = back_ref[:, :, blocks * half :, :].reshape(experts * owners * EXTRA_ROWS, LANES)
    reach = owners * EXTRA_ROWS
    shift, reach_shift = half.bit_length() - 1, reach.bit_length() - 1
    row = iota((count, experts * reach), 1)
    wanted = (row >> reach_shift) == (iota((count, experts * reach), 0) >> shift)
    wanted = wanted & ((row & (EXTRA_ROWS - 1)) < 2)
    on_lane = iota((count, LANES), 1) == (iota((count, LANES), 0) & (half - 1))
    lanes = dot(wanted.astype(LOW), extra)
    slot_gated = jnp.sum(jnp.where(on_lane, lanes, 0.0), axis=1, keepdims=True)
    high, low = split_low(jnp.where(here, slot_gated, 0.0))
    gated = contract_rows(of_expert.astype(LOW), high) + contract_rows(of_expert.astype(LOW), low)
    gated = jnp.where(hits, gated, 0.0)
    logit_grad = gated - gates_ref[...] * jnp.sum(gated, axis=0, keepdims=True)
    logit_grad = jnp.where(hits, logit_grad, 0.0)
    high, low = split_low(logit_grad)
    router_ref[...] = dot(high, h_ref[...]) + dot(low, h_ref[...])
    router_rows = ext_ref[2 : 2 + experts, :].astype(LOW)
    span = owners * half
    span_shift = span.bit_length() - 1
    total = experts * span
    expand = (iota((experts, total), 1) >> span_shift) == iota((experts, total), 0)
    wanted = (iota((1, total), 1) & (half - 1)) + base_ref[0]
    one_hot = (dot(col_ref[...], expand.astype(LOW)) == wanted.astype(FULL)).astype(LOW)
    for block in range(blocks):
        rows = back_ref[:, :, block * half : (block + 1) * half, :].reshape(total, LANES)
        at = slice(block * LANES, (block + 1) * LANES)
        part_ref[:, at] = (
            dot(one_hot, rows)
            + contract_rows(high, router_rows[:, at])
            + contract_rows(low, router_rows[:, at])
        )


def backward_kernel(
    part_ref, other_ref, cot_ref, resid_ref, rows_ref, ext_ref, qk_ref, vx_ref, h_ref, qkv_ref, probs_ref,
    mixed_ref, router_ref, qk_out, vx_out, one_ref, rgrad_ref, qkg_ref, vg_ref,
):
    group_rows = rows_ref.shape[0]
    inner = qk_ref.shape[1] // 2
    h_grad = part_ref[...] + other_ref[...]
    residual = resid_ref[...]
    inv_two = inverse_rms(residual)
    normed_two = residual * inv_two
    gain_two_row = 0.5 * jnp.sum(h_grad * normed_two, axis=0, keepdims=True)
    scaled = h_grad * ext_ref[1:2, :]
    resid_grad = cot_ref[...] + inv_two * (
        scaled - normed_two * jnp.mean(scaled * normed_two, axis=1, keepdims=True)
    )
    rgrad_ref[...] = resid_grad
    attn_grad = resid_grad.astype(LOW)
    vx_out[:, inner : 2 * inner] = contract_rows(attn_grad, mixed_ref[...]).astype(LOW)
    mixed_grad = dot(attn_grad, vx_ref[:, inner : 2 * inner]).astype(LOW)
    low_lanes = iota((group_rows, LANES), 1) < HEAD_DIM
    for pair in range(inner // LANES):
        at = pair * LANES
        queries = qkv_ref[:, at : at + LANES]
        key_rows = qkv_ref[:, inner + at : inner + at + LANES]
        value_rows = qkv_ref[:, 2 * inner + at : 2 * inner + at + LANES]
        out_grad = mixed_grad[:, at : at + LANES]
        grads = []
        for sub in range(2):
            own = low_lanes if sub == 0 else ~low_lanes
            probs = probs_ref[2 * pair + sub]
            prob_grad = contract_cols(jnp.where(own, out_grad, jnp.zeros_like(out_grad)), value_rows)
            carry = jnp.sum(prob_grad * probs, axis=1, keepdims=True)
            score_grad = (probs * (prob_grad - carry)).astype(LOW)
            grads.append(
                (
                    dot(score_grad, key_rows),
                    contract_rows(score_grad, queries),
                    contract_rows(probs.astype(LOW), out_grad),
                )
            )
        scale = HEAD_DIM ** (-0.5)
        qkg_ref[:, at : at + LANES] = (jnp.where(low_lanes, grads[0][0], grads[1][0]) * scale).astype(LOW)
        qkg_ref[:, inner + at : inner + at + LANES] = (
            jnp.where(low_lanes, grads[0][1], grads[1][1]) * scale
        ).astype(LOW)
        vg_ref[:, at : at + LANES] = jnp.where(low_lanes, grads[0][2], grads[1][2]).astype(LOW)
    h_one = h_ref[...]
    qk_out[...] = contract_rows(h_one, qkg_ref[...]).astype(LOW)
    vx_out[:, :inner] = contract_rows(h_one, vg_ref[...]).astype(LOW)
    one_grad = contract_cols(qkg_ref[...], qk_ref[...]) + contract_cols(vg_ref[...], vx_ref[:, :inner])
    one_ref[...] = one_grad
    rows = rows_ref[...]
    gain_one_row = jnp.sum(one_grad * (rows * inverse_rms(rows)), axis=0, keepdims=True)
    router_rows = router_ref[...]
    sub = iota(router_rows.shape, 0)
    extra = jnp.where(sub == 0, gain_one_row, jnp.where(sub == 1, gain_two_row, router_rows))
    vx_out[:, 2 * inner :] = extra.T.astype(LOW)


def local(
    block_in,
    seq_lengths,
    routes,
    w_query,
    w_key,
    w_value,
    w_out_proj,
    router,
    gain_attn,
    gain_moe,
    expert_in,
    expert_out,
    cotangent,
):
    dp_count = lax.axis_size("dp")
    core = lax.axis_index("tensor")
    tok_rows, width = block_in.shape
    group_rows, top_count = routes.shape
    experts = router.shape[1]
    owners = dp_count // experts
    half = max(EXTRA_ROWS, top_count * group_rows // experts)
    slots = dp_count * half
    rows_sent = half * (width // LANES) + EXTRA_ROWS
    inner = w_query.shape[1]
    bits = dp_count.bit_length() - 1
    order_a, order_b = bit_orders()

    expert_ids = jnp.arange(experts, dtype=jnp.int32)
    hits = jnp.any(routes[:, :, None] == expert_ids[None, None, :], axis=1)
    places = jnp.arange(group_rows, dtype=jnp.int32)
    earlier = (places[:, None] > places[None, :]).astype(LOW)
    slot_col = jnp.where(hits, dot(earlier, hits.astype(LOW)), -1.0).astype(LOW)
    slot_row = slot_col.T
    base = core * half
    slot_ids = (base + jnp.arange(half, dtype=jnp.int32)).astype(LOW)
    in_slot = slot_row[:, None, :] == slot_ids[None, :, None]
    dispatch = (
        jnp.broadcast_to(in_slot[:, None], (experts, owners, half, group_rows))
        .astype(LOW)
        .reshape(slots, group_rows)
    )
    base = base.reshape(1).astype(jnp.int32)
    cot_picked = dot(dispatch, cotangent.astype(LOW)).astype(LOW).reshape(dp_count, half, width)

    extra_width = -(-(2 + experts) // LANES) * LANES
    extra = jnp.concatenate(
        [
            gain_attn[:, None],
            gain_moe[:, None],
            router,
            jnp.zeros((router.shape[0], extra_width - 2 - experts), LOW),
        ],
        axis=1,
    )
    qk_full = jnp.concatenate([w_query, w_key], axis=1)
    vx_full = jnp.concatenate([w_value, w_out_proj.T, extra], axis=1)
    qk_full = qk_full.reshape((1,) * bits + qk_full.shape)
    vx_full = vx_full.reshape((1,) * bits + vx_full.shape)
    for step in range(bits):
        vx_full = double(vx_full, order_b[step], bits)
        qk_full = double(qk_full, order_a[step], bits)
        if step == bits - 3:
            cot_picked, qk_full, vx_full = lax.optimization_barrier((cot_picked, qk_full, vx_full))
    qk_full = qk_full.reshape(width, 2 * inner)
    vx_full = vx_full.reshape(width, 2 * inner + extra_width)
    cot_own = trade(cot_picked)

    rows_all = lax.all_gather(block_in, "tensor", axis=0, tiled=True)
    shape = jax.ShapeDtypeStruct
    attn_part, h_one, qkv, probs, mixed, ext = call(
        attention_kernel,
        [
            shape((group_rows, width), FULL),
            shape((group_rows, width), LOW),
            shape((group_rows, 3 * inner), LOW),
            shape((inner // HEAD_DIM, group_rows, group_rows), FULL),
            shape((group_rows, inner), LOW),
            shape((extra_width, width), FULL),
        ],
        seq_lengths,
        rows_all,
        qk_full,
        vx_full,
        flops=8 * group_rows * width * inner + 4 * group_rows * group_rows * inner,
        smem=(0,),
    )
    attn_part, cot_own = lax.optimization_barrier((attn_part, cot_own))
    cot_other = swap(cot_own)

    residual, h_two, gates, sent = call(
        dispatch_kernel,
        [
            shape((group_rows, width), FULL),
            shape((group_rows, width), LOW),
            shape((experts, group_rows), FULL),
            shape((experts, owners, rows_sent, LANES), LOW),
        ],
        base,
        rows_all,
        attn_part,
        swap(attn_part),
        ext,
        slot_row,
        flops=2 * experts * half * group_rows * width,
        smem=(0,),
    )

    h_own = trade(sent.reshape(dp_count, rows_sent, LANES))
    h_other = swap(h_own)
    first_weight = expert_in[0]
    second_weight = expert_out[0]
    back_own, *own_kept = expert_rows(h_own, cot_own, first_weight, second_weight, half)
    back_other, *other_kept = expert_rows(h_other, cot_other, first_weight, second_weight, half)
    back = (back_own.astype(FULL) + swap(back_other).astype(FULL)).astype(LOW)
    back = trade(back)

    zeros = jnp.zeros((width, first_weight.shape[1]), FULL)
    out_other, first_sum, second_sum = expert_weights(
        h_other, *other_kept, second_weight, zeros, zeros.reshape(second_weight.shape), half
    )
    out_own, grad_first, grad_second = expert_weights(
        h_own, *own_kept, second_weight, first_sum, second_sum, half
    )
    out_rows = (out_own.astype(FULL) + swap(out_other).astype(FULL)).astype(LOW)
    out_rows, back = lax.optimization_barrier((out_rows, back))
    back_out = trade(out_rows.reshape(dp_count, half, width)).reshape(slots, width)

    h_part, router_part = call(
        combine_kernel,
        [shape((group_rows, width), FULL), shape((experts, width), FULL)],
        base,
        back.reshape(experts, owners, rows_sent, LANES),
        slot_row,
        slot_col,
        gates,
        ext,
        h_two,
        flops=2 * slots * group_rows * width,
        smem=(0,),
    )
    router_part = jnp.pad(router_part, ((2, extra_width - 2 - experts), (0, 0)))
    qk_part, vx_part, one_part, resid_grad, _, _ = call(
        backward_kernel,
        [
            shape((width, 2 * inner), LOW),
            shape((width, 2 * inner + extra_width), LOW),
            shape((group_rows, width), FULL),
            shape((group_rows, width), FULL),
            shape((group_rows, 2 * inner), LOW),
            shape((group_rows, inner), LOW),
        ],
        h_part,
        swap(h_part),
        cotangent,
        residual,
        rows_all,
        ext,
        qk_full,
        vx_full,
        h_one,
        qkv,
        probs,
        mixed,
        router_part,
        flops=20 * group_rows * width * inner + 12 * group_rows * group_rows * inner,
    )

    own_start = core * tok_rows
    other_start = (1 - core) * tok_rows

    def rows_at(values, start):
        return lax.dynamic_slice_in_dim(values, start, tok_rows, 0)

    one_other = swap(rows_at(one_part, other_start).astype(LOW)).astype(FULL)
    qk_sum = qk_part.reshape((2,) * bits + (width // dp_count, 2 * inner))
    vx_sum = vx_part.reshape((2,) * bits + (width // dp_count, 2 * inner + extra_width))
    for step in range(bits):
        vx_sum = halve(vx_sum, order_b[bits - 1 - step], bits)
        qk_sum = halve(qk_sum, order_a[bits - 1 - step], bits)
        if step == 1:
            vx_sum, qk_sum, back_out = lax.optimization_barrier((vx_sum, qk_sum, back_out))
    qk_sum = qk_sum.reshape(width // dp_count, 2 * inner)
    vx_sum = vx_sum.reshape(width // dp_count, 2 * inner + extra_width)

    out_part = contract_rows(dispatch, back_out)
    block_out = rows_at(residual, own_start) + (
        rows_at(out_part, own_start) + swap(rows_at(out_part, other_start))
    )
    scaled_one = (rows_at(one_part, own_start) + one_other) * ext[0:1, :]
    inv_own = inverse_rms(block_in)
    normed_own = block_in * inv_own
    grad_in = rows_at(resid_grad, own_start) + inv_own * (
        scaled_one - normed_own * jnp.mean(scaled_one * normed_own, axis=1, keepdims=True)
    )
    extra_sum = vx_sum[:, 2 * inner :]
    extra_sum = extra_sum + swap(extra_sum)
    share = extra_sum.shape[0] // 2
    extra_own = lax.dynamic_slice_in_dim(extra_sum, core * share, share, 0)
    return (
        block_out,
        grad_in,
        qk_sum[:, :inner],
        qk_sum[:, inner:],
        vx_sum[:, :inner],
        vx_sum[:, inner : 2 * inner].T,
        extra_own[:, 2 : 2 + experts],
        extra_own[:, 0],
        extra_own[:, 1],
        grad_first[None],
        grad_second[None],
    )


def solution(mesh):
    in_specs = (
        P(("dp", "tensor"), None),
        P("dp", None),
        P("dp", None),
        P("dp", "tensor"),
        P("dp", "tensor"),
        P("dp", "tensor"),
        P("tensor", "dp"),
        P("dp", None),
        P("dp"),
        P("dp"),
        P("dp", None, "tensor"),
        P("dp", "tensor", None),
        P("dp", None),
    )
    out_specs = (
        P(("dp", "tensor"), None),
        P(("dp", "tensor"), None),
        P("dp", "tensor"),
        P("dp", "tensor"),
        P("dp", "tensor"),
        P("tensor", "dp"),
        P(("dp", "tensor"), None),
        P(("dp", "tensor")),
        P(("dp", "tensor")),
        P("dp", None, "tensor"),
        P("dp", "tensor", None),
    )
    return jax.shard_map(local, mesh=mesh, in_specs=in_specs, out_specs=out_specs, check_vma=False)
```

time: 386 us -> 286 us (0.74); the launches traced: 379 us -> 285 us
  waiting for transfers between devices: 171 us -> 93.6 us
  matrix products: 72.1 us -> 3.97 us
  Pallas kernels: 0 us -> 49.7 us
  blocking collectives: 17.1 us -> 49.8 us
  starting transfers between devices: 64.3 us -> 48.7 us
  other arithmetic: 21.5 us -> 9.67 us
    all_to_all x5 -> x3, waiting for transfers between devices: 112 us -> 11.3 us  [trade(): return lax.all_to_all(values, 'dp', split_axis=0, concat_axis=0, tiled=True)]
    pallas_call x0 -> x8, Pallas kernels: none -> 49.7 us  [the longest x2 19.6 us: expert_weights(): pl.pallas_call(lambda *refs: weight_kernel(half, *refs), grid=(dp_count /...]
    all_to_all x1, blocking collectives: 14.6 us -> 47.5 us  [trade(): return lax.all_to_all(values, 'dp', split_axis=0, concat_axis=0, tiled=True)]
    dot_general x14 -> x0, matrix products: 28 us -> none  [the longest x6 20.7 us: contract_cols(): lax.dot_general(left_side, right_side, (((1,), (1,)), ((), ())), preferre...]
    ppermute x24 -> x16, waiting for transfers between devices: 53.2 us -> 73.8 us  [the longest x8 38 us: double(): other = lax.ppermute(block, 'dp', partners(bit))]
    dot_general x7 -> x1, matrix products: 22.1 us -> 2.07 us  [contract_rows(): lax.dot_general(left_side, right_side, (((0,), (0,)), ((), ())), preferre...]
    dot_general x8 -> x2, matrix products: 19.2 us -> 1.9 us  [dot(): return jnp.dot(left_side, right_side, preferred_element_type=FULL)]
    unnamed x101 -> x81, local copies, waits for them, and re-layouts: 5.58 us -> 17.6 us
  transfers between devices with their start and end apart: 40 -> 28, of which waited for: 25 -> 16; matrix products, arithmetic and copies ran while one was open for 18% -> 7% of each run, Pallas kernels for 0% -> 14%
where the time goes in v2:
time: 286 us; the launch traced here: 285 us
  waiting for transfers between devices  93.6 us (33%)
  blocking collectives  49.8 us (17%)
  Pallas kernels  49.7 us (17%)
  starting transfers between devices  48.7 us (17%)
  local copies, waits for them, and re-layouts  28.3 us (10%)
  other arithmetic  9.67 us (3%)
  matrix products  3.97 us (1%)
    all_to_all x1, blocking collectives, trade(): return lax.all_to_all(values, 'dp', split_axis=0, concat_axis=0, tiled=True)  47.5 us
    ppermute x8, waiting for transfers between devices, double(): other = lax.ppermute(block, 'dp', partners(bit))  38 us
    ppermute x8, waiting for transfers between devices, halve(): lax.ppermute(given, 'dp', partners(bit)).astype(FULL)  35.8 us
    pallas_call x2, Pallas kernels, expert_weights(): pl.pallas_call(lambda *refs: weight_kernel(half, *refs), grid=(dp_count /...  19.6 us
    all_to_all x3, starting transfers between devices, trade(): return lax.all_to_all(values, 'dp', split_axis=0, concat_axis=0, tiled=True)  19.5 us
    unnamed x81, local copies, waits for them, and re-layouts  17.6 us
    pallas_call x4, Pallas kernels, call(): pl.pallas_call(kernel, out_shape=out_shape, in_specs=[pl.BlockSpec(memory...  15.9 us
    ppermute x8, starting transfers between devices, halve(): lax.ppermute(given, 'dp', partners(bit)).astype(FULL)  14.8 us
  transfers between devices with their start and end apart: 28, of which 16 were waited for; matrix products, arithmetic and copies ran while one was open for 7% of the time, Pallas kernels for 14%

profile of v2, /device:TPU:0, one launch (start us, length us, event | category | flops | bytes accessed | tf_op | source)
XLA Modules:
  0.0 285.0 jit_solution(277337235685513775)
XLA Ops:
  2.3 4.0 %collective-permute-start = (bf16[1,1,1,1,48,768]{5,4,0,3,2,1:T(8,128)(2,1)S(1)}, bf16[1,1,1,1,48,768]{5,4,0,3,2,1:T(8,128)(2,1)S(1)}, u32[]{:S(2)}, u32[]{:S(2)}) collective-permute-start(bf16[1,1,1,1,48,768]{5,4,0,3,2,1:T(8,128)(2,1)S(1)} %bitcast.62), channel_id=1, source_target_pairs={{0,16},{2,18},{4,20},{6,22},{8,24},{10,26},{12,28},{14,30},{16,0},... | collective-permute-start | bytes 221192 | tf_op jit(solution)/shard_map/ppermute | solution.py:62
  16.6 3.0 %collective-permute-done.1 = bf16[2,1,1,1,48,768]{5,4,0,3,2,1:T(8,128)(2,1)S(1)} collective-permute-done((bf16[2,1,1,1,48,768]{5,4,0,3,2,1:T(8,128)(2,1)S(1)}, bf16[2,1,1,1,48,768]{5,4,0,3,2,1:T(8,128)(2,1)S(1)}, u32[]{:S(2)}, u32[]{:S(2)}) %collective-permute-start.1) | collective-permute-done | bytes 147488 | tf_op jit(solution)/shard_map/ppermute | solution.py:62
  19.7 2.6 collective-permute-done.3
  22.4 6.4 %all-to-all-start = ((bf16[16,64,768]{2,1,0:T(8,128)(2,1)}), bf16[16,64,768]{2,1,0:T(8,128)(2,1)}, u32[]{:S(2)}, u32[]{:S(2)}) async-start(bf16[16,64,768]{2,1,0:T(8,128)(2,1)} %bitcast.3), calls=%async_computation | async-start | bytes 3145728 | tf_op jit(solution)/shard_map/all_to_all | solution.py:80
  32.2 14.8 %collective-permute-done.4 = bf16[2,2,1,1,48,768]{5,4,0,3,2,1:T(8,128)(2,1)S(1)} collective-permute-done((bf16[2,2,1,1,48,768]{5,4,0,3,2,1:T(8,128)(2,1)S(1)}, bf16[2,2,1,1,48,768]{5,4,0,3,2,1:T(8,128)(2,1)S(1)}, u32[]{:S(2)}, u32[]{:S(2)}) %collective-permute-start.4) | collective-permute-done | bytes 294944 | tf_op jit(solution)/shard_map/ppermute | solution.py:62
  47.1 2.9 %collective-permute-start.5 = (bf16[2,2,2,1,48,768]{5,4,0,3,2,1:T(8,128)(2,1)S(1)}, bf16[2,2,2,1,48,768]{5,4,0,3,2,1:T(8,128)(2,1)S(1)}, u32[]{:S(2)}, u32[]{:S(2)}) collective-permute-start(bf16[2,2,2,1,48,768]{5,4,0,3,2,1:T(8,128)(2,1)S(1)} %maximum_select_fusion.3), channel_id=1, source_target_pairs={{0,2},{2,0},{4,6},{6,4},{8,10},{10,8},{12,14},{14,12},{16,18},{18,... | collective-permute-start | bytes 1769480 | tf_op jit(solution)/shard_map/ppermute | solution.py:62
  53.0 15.3 %collective-permute-done.5 = bf16[2,2,2,1,48,768]{5,4,0,3,2,1:T(8,128)(2,1)S(1)} collective-permute-done((bf16[2,2,2,1,48,768]{5,4,0,3,2,1:T(8,128)(2,1)S(1)}, bf16[2,2,2,1,48,768]{5,4,0,3,2,1:T(8,128)(2,1)S(1)}, u32[]{:S(2)}, u32[]{:S(2)}) %collective-permute-start.5) | collective-permute-done | bytes 589856 | tf_op jit(solution)/shard_map/ppermute | solution.py:62
  69.9 3.7 %shard_map.212 = (f32[256,768]{1,0:T(8,128)S(1)}, bf16[256,768]{1,0:T(8,128)(2,1)S(1)}, bf16[256,1152]{1,0:T(8,128)(2,1)S(1)}, f32[6,256,256]{2,1,0:T(8,128)}, b...) custom-call(s32[1,4]{1,0:T(1,128)S(1)} %copy-done.16, f32[256,768]{1,0:T(8,128)S(1)} %all_gather.3.rows_ref, ...), custom_call_target="tpu_custom_call" | custom-call | flops 704643072 | bytes 7274512 | tf_op jit(solution)/shard_map/pallas_call | solution.py:85
  83.4 47.5 %all_to_all.20.refs_0_ = bf16[16,400,128]{2,1,0:T(8,128)(2,1)S(1)} all-to-all(bf16[16,400,128]{2,1,0:T(8,128)(2,1)S(1)} %bitcast.44), channel_id=1, replica_groups=mesh['dp'=16,'tensor'=2] {'dp'}, dimensions={0} | all-to-all | bytes 3276800 | tf_op jit(solution)/shard_map/all_to_all | solution.py:80
  131.4 5.5 %collective-permute-done.10.refs_1_ = bf16[16,64,768]{2,1,0:T(8,128)(2,1)S(1)} collective-permute-done((bf16[16,64,768]{2,1,0:T(8,128)(2,1)}, bf16[16,64,768]{2,1,0:T(8,128)(2,1)S(1)}, u32[]{:S(2)}, u32[]{:S(2)}) %collective-permute-start.10) | collective-permute-done | bytes 1572896 | tf_op jit(solution)/shard_map/ppermute | solution.py:48
  138.5 7.1 %shard_map.215 = (bf16[16,400,128]{2,1,0:T(8,128)(2,1)}, bf16[1024,768]{1,0:T(8,128)(2,1)S(1)}, bf16[1024,768]{1,0:T(8,128)(2,1)S(1)}, bf16[1024,768]{1,0:T(8,128)(2,1)}, f32[1024,128]{1,0:T(8,128)S(1)}) custom-call(bf16[16,400,128]{2,1,0:T(8,128)(2,1)} %copy-done.37, bf16[16,64,768]{2,1,0:T(8,128)(2,1)} %copy-done.38, bf16[768,768]{1,0:T(8,128)(2,1)S(1)} %bitcast.46, ...), custom_call_target="tpu_custom_call" | custom-call | flops 3623878656 | bytes 9437184 | tf_op jit(solution)/shard_map/pallas_call | solution.py:258
  148.9 7.1 %shard_map.214 = (bf16[16,400,128]{2,1,0:T(8,128)(2,1)}, bf16[1024,768]{1,0:T(8,128)(2,1)S(1)}, bf16[1024,768]{1,0:T(8,128)(2,1)S(1)}, bf16[1024,768]{1,0:T(8,128)(2,1)}, f32[1024,128]{1,0:T(8,128)S(1)}) custom-call(bf16[16,400,128]{2,1,0:T(8,128)(2,1)} %copy-done.34, bf16[16,64,768]{2,1,0:T(8,128)(2,1)} %all-to-all-done.refs_1_, ...), custom_call_target="tpu_custom_call" | custom-call | flops 3623878656 | bytes 9437184 | tf_op jit(solution)/shard_map/pallas_call | solution.py:258
  159.1 3.1 %add_convert_fusion = bf16[16,400,128]{2,1,0:T(8,128)(2,1)} fusion(bf16[16,400,128]{2,1,0:T(8,128)(2,1)S(1)} %collective-permute-done.12, bf16[16,400,128]{2,1,0:T(8,128)(2,1)} %get-tuple-element.74), kind=kLoop, calls=%fused_computation | loop fusion | flops 3276800 | bytes 4915200 | tf_op jit(solution)/shard_map/convert_element_type | solution.py:552
  162.2 3.9 %all-to-all-start.2 = ((bf16[16,400,128]{2,1,0:T(8,128)(2,1)}), bf16[16,400,128]{2,1,0:T(8,128)(2,1)S(1)}, u32[]{:S(2)}, u32[]{:S(2)}) async-start(bf16[16,400,128]{2,1,0:T(8,128)(2,1)} %add_convert_fusion), calls=%async_computation.2 | async-start | bytes 3276800 | tf_op jit(solution)/shard_map/all_to_all | solution.py:80
  168.5 9.8 %shard_map.216 = (bf16[1024,768]{1,0:T(8,128)(2,1)S(1)}, f32[768,768]{1,0:T(8,128)}, f32[768,768]{1,0:T(8,128)}) custom-call(bf16[16,400,128]{2,1,0:T(8,128)(2,1)} %copy-done.37, bf16[1024,768]{1,0:T(8,128)(2,1)S(1)} %copy-done.23, bf16[1024,768]{1,0:T(8,128)(2,1)} %copy-done.24, bf16[1024,768]{1,0:T(8,128)(2,1)} %get-tuple-element.68.refs_3_, ...), custom_call_target="tpu_custom_call" | custom-call | flops 3623878656 | bytes 7864320 | tf_op jit(solution)/shard_map/pallas_call | solution.py:310
  178.7 9.7 %shard_map.217 = (bf16[1024,768]{1,0:T(8,128)(2,1)S(1)}, f32[768,768]{1,0:T(8,128)}, f32[768,768]{1,0:T(8,128)}) custom-call(bf16[16,400,128]{2,1,0:T(8,128)(2,1)} %copy-done.34, bf16[1024,768]{1,0:T(8,128)(2,1)S(1)} %copy-done.20, bf16[1024,768]{1,0:T(8,128)(2,1)} %copy-done.21, bf16[1024,768]{1,0:T(8,128)(2,1)} %get-tuple-element.64.refs_3_, ...), custom_call_target="tpu_custom_call" | custom-call | flops 3623878656 | bytes 7864320 | tf_op jit(solution)/shard_map/pallas_call | solution.py:310
  189.9 11.3 %all-to-all-done.2 = bf16[16,400,128]{2,1,0:T(8,128)(2,1)S(1)} async-done(((bf16[16,400,128]{2,1,0:T(8,128)(2,1)}), bf16[16,400,128]{2,1,0:T(8,128)(2,1)S(1)}, u32[]{:S(2)}, u32[]{:S(2)}) %all-to-all-start.2) | async-done | bytes 1638432 | tf_op jit(solution)/shard_map/all_to_all | solution.py:80
  203.4 9.2 %all-to-all-start.3 = ((bf16[16,64,768]{2,1,0:T(8,128)(2,1)}), bf16[16,64,768]{2,1,0:T(8,128)(2,1)}, u32[]{:S(2)}, u32[]{:S(2)}) async-start(bf16[16,64,768]{2,1,0:T(8,128)(2,1)} %bitcast.52), calls=%async_computation.3 | async-start | bytes 3145728 | tf_op jit(solution)/shard_map/all_to_all | solution.py:80
  213.7 9.0 %shard_map.219 = (bf16[768,768]{1,0:T(8,128)(2,1)}, bf16[768,896]{1,0:T(8,128)(2,1)}, f32[256,768]{1,0:T(8,128)S(1)}, f32[256,768]{1,0:T(8,128)S(1)}, bf16[256,7...) custom-call(f32[256,768]{1,0:T(8,128)S(1)} %get-tuple-element.79.part_ref, f32[256,768]{1,0:T(8,128)S(1)} %collective-permute-done.13.other_ref, ...), custom_call_target="tpu_custom_call" | custom-call | flops 1811939328 | bytes 14745600 | tf_op jit(solution)/shard_map/pallas_call | solution.py:85
  228.9 22.7 %collective-permute-done.16 = bf16[2,2,2,1,48,768]{5,4,3,2,1,0:T(8,128)(2,1)S(1)} collective-permute-done((bf16[2,2,2,1,48,768]{5,4,3,2,1,0:T(8,128)(2,1)S(1)}, bf16[2,2,2,1,48,768]{5,4,3,2,1,0:T(8,128)(2,1)S(1)}, u32[]{:S(2)}, u32[]{:S(2)}) %collective-permute-start.16) | collective-permute-done | bytes 589856 | tf_op jit(solution)/shard_map/ppermute | solution.py:76
  256.0 4.6 %collective-permute-done.17 = bf16[2,2,1,1,48,768]{5,4,3,2,1,0:T(8,128)(2,1)S(1)} collective-permute-done((bf16[2,2,1,1,48,768]{5,4,3,2,1,0:T(8,128)(2,1)S(1)}, bf16[2,2,1,1,48,768]{5,4,3,2,1,0:T(8,128)(2,1)S(1)}, u32[]{:S(2)}, u32[]{:S(2)}) %collective-permute-start.17) | collective-permute-done | bytes 294944 | tf_op jit(solution)/shard_map/ppermute | solution.py:76
  260.7 2.7 collective-permute-done.15
  268.5 3.4 %collective-permute-done.20 = bf16[2,1,1,1,48,768]{5,4,3,2,1,0:T(8,128)(2,1)S(1)} collective-permute-done((bf16[2,1,1,1,48,768]{5,4,3,2,1,0:T(8,128)(2,1)S(1)}, bf16[2,1,1,1,48,768]{5,4,3,2,1,0:T(8,128)(2,1)S(1)}, u32[]{:S(2)}, u32[]{:S(2)}) %collective-permute-start.20) | collective-permute-done | bytes 147488 | tf_op jit(solution)/shard_map/ppermute | solution.py:76
  271.9 3.9 %collective-permute-start.21 = (bf16[1,1,1,1,48,768]{5,4,3,2,1,0:T(8,128)(2,1)S(1)}, bf16[1,1,1,1,48,768]{5,4,3,2,1,0:T(8,128)(2,1)S(1)}, u32[]{:S(2)}, u32[]{:S(2)}) collective-permute-start(bf16[1,1,1,1,48,768]{5,4,3,2,1,0:T(8,128)(2,1)S(1)} %dynamic-slice_convert_fusion.6), channel_id=1, source_target_pairs={{0,16},{2,18},{4,20},{6,22},{8,24},{10,26},{12,28},{14,30},{16,0},... | collective-permute-start | bytes 221192 | tf_op jit(solution)/shard_map/ppermute | solution.py:76
  (184 shorter events, 70.5 us)
Async XLA Ops:
  2.3 10.4 %collective-permute-start = (bf16[1,1,1,1,48,768]{5,4,0,3,2,1:T(8,128)(2,1)S(1)}, bf16[1,1,1,1,48,768]{5,4,0,3,2,1:T(8,128)(2,1)S(1)}, u32[]{:S(2)}, u32[]{:S(2)}) collective-permute-start(bf16[1,1,1,1,48,768]{5,4,0,3,2,1:T(8,128)(2,1)S(1)} %bitcast.62), channel_id=1, source_target_pairs={{0,16},{2,18},{4,20},{6,22},{8,24},{10,26},{12,28},{14,30},{16,0},... | collective-permute-start | bytes 221192 | tf_op jit(solution)/shard_map/ppermute | solution.py:62
  9.5 7.0 %collective-permute-start.2 = (bf16[1,1,1,1,48,896]{5,4,0,3,2,1:T(8,128)(2,1)S(1)}, bf16[1,1,1,1,48,896]{5,4,0,3,2,1:T(8,128)(2,1)S(1)}, u32[]{:S(2)}, u32[]{:S(2)}) collective-permute-start(bf16[1,1,1,1,48,896]{5,4,0,3,2,1:T(8,128)(2,1)S(1)} %bitcast.59), channel_id=1, source_target_pairs={{0,16},{2,18},{4,20},{6,22},{8,24},{10,26},{12,28},{14,30},{16,0},... | collective-permute-start | bytes 258056 | tf_op jit(solution)/shard_map/ppermute | solution.py:62
  12.7 6.9 %collective-permute-start.1 = (bf16[2,1,1,1,48,768]{5,4,0,3,2,1:T(8,128)(2,1)S(1)}, bf16[2,1,1,1,48,768]{5,4,0,3,2,1:T(8,128)(2,1)S(1)}, u32[]{:S(2)}, u32[]{:S(2)}) collective-permute-start(bf16[2,1,1,1,48,768]{5,4,0,3,2,1:T(8,128)(2,1)S(1)} %maximum_select_fusion.8), channel_id=1, source_target_pairs={{0,8},{2,10},{4,12},{6,14},{8,0},{10,2},{12,4},{14,6},{16,24},{18,... | collective-permute-start | bytes 442376 | tf_op jit(solution)/shard_map/ppermute | solution.py:62
  22.4 55.2 %all-to-all-start = ((bf16[16,64,768]{2,1,0:T(8,128)(2,1)}), bf16[16,64,768]{2,1,0:T(8,128)(2,1)}, u32[]{:S(2)}, u32[]{:S(2)}) async-start(bf16[16,64,768]{2,1,0:T(8,128)(2,1)} %bitcast.3), calls=%async_computation | async-start | bytes 3145728 | tf_op jit(solution)/shard_map/all_to_all | solution.py:80
  28.8 18.2 %collective-permute-start.4 = (bf16[2,2,1,1,48,768]{5,4,0,3,2,1:T(8,128)(2,1)S(1)}, bf16[2,2,1,1,48,768]{5,4,0,3,2,1:T(8,128)(2,1)S(1)}, u32[]{:S(2)}, u32[]{:S(2)}) collective-permute-start(bf16[2,2,1,1,48,768]{5,4,0,3,2,1:T(8,128)(2,1)S(1)} %maximum_select_fusion.5), channel_id=1, source_target_pairs={{0,4},{2,6},{4,0},{6,2},{8,12},{10,14},{12,8},{14,10},{16,20},{18,... | collective-permute-start | bytes 884744 | tf_op jit(solution)/shard_map/ppermute | solution.py:62
  30.8 19.2 %collective-permute-start.6 = (bf16[2,2,1,1,48,896]{5,4,0,3,2,1:T(8,128)(2,1)S(1)}, bf16[2,2,1,1,48,896]{5,4,0,3,2,1:T(8,128)(2,1)S(1)}, u32[]{:S(2)}, u32[]{:S(2)}) collective-permute-start(bf16[2,2,1,1,48,896]{5,4,0,3,2,1:T(8,128)(2,1)S(1)} %maximum_select_fusion.4), channel_id=1, source_target_pairs={{0,2},{2,0},{4,6},{6,4},{8,10},{10,8},{12,14},{14,12},{16,18},{18,... | collective-permute-start | bytes 1032200 | tf_op jit(solution)/shard_map/ppermute | solution.py:62
  47.1 21.2 %collective-permute-start.5 = (bf16[2,2,2,1,48,768]{5,4,0,3,2,1:T(8,128)(2,1)S(1)}, bf16[2,2,2,1,48,768]{5,4,0,3,2,1:T(8,128)(2,1)S(1)}, u32[]{:S(2)}, u32[]{:S(2)}) collective-permute-start(bf16[2,2,2,1,48,768]{5,4,0,3,2,1:T(8,128)(2,1)S(1)} %maximum_select_fusion.3), channel_id=1, source_target_pairs={{0,2},{2,0},{4,6},{6,4},{8,10},{10,8},{12,14},{14,12},{16,18},{18,... | collective-permute-start | bytes 1769480 | tf_op jit(solution)/shard_map/ppermute | solution.py:62
  50.1 18.9 %collective-permute-start.7 = (bf16[2,2,1,2,48,896]{5,4,0,3,2,1:T(8,128)(2,1)S(1)}, bf16[2,2,1,2,48,896]{5,4,0,3,2,1:T(8,128)(2,1)S(1)}, u32[]{:S(2)}, u32[]{:S(2)}) collective-permute-start(bf16[2,2,1,2,48,896]{5,4,0,3,2,1:T(8,128)(2,1)S(1)} %maximum_select_fusion.2), channel_id=1, source_target_pairs={{0,4},{2,6},{4,0},{6,2},{8,12},{10,14},{12,8},{14,10},{16,20},{18,... | collective-permute-start | bytes 2064392 | tf_op jit(solution)/shard_map/ppermute | solution.py:62
  130.9 6.0 %collective-permute-start.9 = (bf16[16,400,128]{2,1,0:T(8,128)(2,1)S(1)}, bf16[16,400,128]{2,1,0:T(8,128)(2,1)S(1)}, u32[]{:S(2)}, u32[]{:S(2)}) collective-permute-start(bf16[16,400,128]{2,1,0:T(8,128)(2,1)S(1)} %all_to_all.20.refs_0_), channel_id=1, source_target_pairs={{0,1},{1,0},{2,3},{3,2},{4,5},{5,4},{6,7},{7,6},{8,9},{9,8},{10,11... | collective-permute-start | bytes 4915208 | tf_op jit(solution)/shard_map/ppermute | solution.py:48
  130.9 6.0 %collective-permute-start.10 = (bf16[16,64,768]{2,1,0:T(8,128)(2,1)}, bf16[16,64,768]{2,1,0:T(8,128)(2,1)S(1)}, u32[]{:S(2)}, u32[]{:S(2)}) collective-permute-start(bf16[16,64,768]{2,1,0:T(8,128)(2,1)} %all-to-all-done.refs_1_), channel_id=1, source_target_pairs={{0,1},{1,0},{2,3},{3,2},{4,5},{5,4},{6,7},{7,6},{8,9},{9,8},{10,11... | collective-permute-start | bytes 4718600 | tf_op jit(solution)/shard_map/ppermute | solution.py:48
  148.7 10.3 %collective-permute-start.12 = (bf16[16,400,128]{2,1,0:T(8,128)(2,1)}, bf16[16,400,128]{2,1,0:T(8,128)(2,1)S(1)}, u32[]{:S(2)}, u32[]{:S(2)}) collective-permute-start(bf16[16,400,128]{2,1,0:T(8,128)(2,1)} %get-tuple-element.75), channel_id=1, source_target_pairs={{0,1},{1,0},{2,3},{3,2},{4,5},{5,4},{6,7},{7,6},{8,9},{9,8},{10,11... | collective-permute-start | bytes 4915208 | tf_op jit(solution)/shard_map/ppermute | solution.py:48
  162.2 39.1 %all-to-all-start.2 = ((bf16[16,400,128]{2,1,0:T(8,128)(2,1)}), bf16[16,400,128]{2,1,0:T(8,128)(2,1)S(1)}, u32[]{:S(2)}, u32[]{:S(2)}) async-start(bf16[16,400,128]{2,1,0:T(8,128)(2,1)} %add_convert_fusion), calls=%async_computation.2 | async-start | bytes 3276800 | tf_op jit(solution)/shard_map/all_to_all | solution.py:80
  178.3 10.1 %collective-permute-start.11 = (bf16[1024,768]{1,0:T(8,128)(2,1)S(1)}, bf16[1024,768]{1,0:T(8,128)(2,1)S(1)}, u32[]{:S(2)}, u32[]{:S(2)}) collective-permute-start(bf16[1024,768]{1,0:T(8,128)(2,1)S(1)} %get-tuple-element.73), channel_id=1, source_target_pairs={{0,1},{1,0},{2,3},{3,2},{4,5},{5,4},{6,7},{7,6},{8,9},{9,8},{10,11... | collective-permute-start | bytes 4718600 | tf_op jit(solution)/shard_map/ppermute | solution.py:48
  203.3 10.4 %collective-permute-start.13 = (f32[256,768]{1,0:T(8,128)S(1)}, f32[256,768]{1,0:T(8,128)S(1)}, u32[]{:S(2)}, u32[]{:S(2)}) collective-permute-start(f32[256,768]{1,0:T(8,128)S(1)} %get-tuple-element.79.part_ref), channel_id=1, source_target_pairs={{0,1},{1,0},{2,3},{3,2},{4,5},{5,4},{6,7},{7,6},{8,9},{9,8},{10,11... | collective-permute-start | bytes 2359304 | tf_op jit(solution)/shard_map/ppermute | solution.py:48
  203.4 60.0 %all-to-all-start.3 = ((bf16[16,64,768]{2,1,0:T(8,128)(2,1)}), bf16[16,64,768]{2,1,0:T(8,128)(2,1)}, u32[]{:S(2)}, u32[]{:S(2)}) async-start(bf16[16,64,768]{2,1,0:T(8,128)(2,1)} %bitcast.52), calls=%async_computation.3 | async-start | bytes 3145728 | tf_op jit(solution)/shard_map/all_to_all | solution.py:80
  222.8 5.9 %collective-permute-start.19 = (bf16[128,768]{1,0:T(8,128)(2,1)S(1)}, bf16[128,768]{1,0:T(8,128)(2,1)S(1)}, u32[]{:S(2)}, u32[]{:S(2)}) collective-permute-start(bf16[128,768]{1,0:T(8,128)(2,1)S(1)} %dynamic-slice_convert_fusion.2), channel_id=1, source_target_pairs={{0,1},{1,0},{2,3},{3,2},{4,5},{5,4},{6,7},{7,6},{8,9},{9,8},{10,11... | collective-permute-start | bytes 589832 | tf_op jit(solution)/shard_map/ppermute | solution.py:48
  224.2 27.4 %collective-permute-start.16 = (bf16[2,2,2,1,48,768]{5,4,3,2,1,0:T(8,128)(2,1)S(1)}, bf16[2,2,2,1,48,768]{5,4,3,2,1,0:T(8,128)(2,1)S(1)}, u32[]{:S(2)}, u32[]{:S(2)}) collective-permute-start(bf16[2,2,2,1,48,768]{5,4,3,2,1,0:T(8,128)(2,1)S(1)} %constant_dynamic-slice_fusion.1), channel_id=1, source_target_pairs={{0,2},{2,0},{4,6},{6,4},{8,10},{10,8},{12,14},{14,12},{16,18},{18,... | collective-permute-start | bytes 1769480 | tf_op jit(solution)/shard_map/ppermute | solution.py:76
  227.2 26.3 %collective-permute-start.14 = (bf16[2,2,1,2,48,896]{5,4,3,2,1,0:T(8,128)(2,1)S(1)}, bf16[2,2,1,2,48,896]{5,4,3,2,1,0:T(8,128)(2,1)S(1)}, u32[]{:S(2)}, u32[]{:S(2)}) collective-permute-start(bf16[2,2,1,2,48,896]{5,4,3,2,1,0:T(8,128)(2,1)S(1)} %constant_dynamic-slice_fusion.2), channel_id=1, source_target_pairs={{0,4},{2,6},{4,0},{6,2},{8,12},{10,14},{12,8},{14,10},{16,20},{18,... | collective-permute-start | bytes 2064392 | tf_op jit(solution)/shard_map/ppermute | solution.py:76
  251.9 8.7 %collective-permute-start.17 = (bf16[2,2,1,1,48,768]{5,4,3,2,1,0:T(8,128)(2,1)S(1)}, bf16[2,2,1,1,48,768]{5,4,3,2,1,0:T(8,128)(2,1)S(1)}, u32[]{:S(2)}, u32[]{:S(2)}) collective-permute-start(bf16[2,2,1,1,48,768]{5,4,3,2,1,0:T(8,128)(2,1)S(1)} %dynamic-slice_convert_fusion.1), channel_id=1, source_target_pairs={{0,4},{2,6},{4,0},{6,2},{8,12},{10,14},{12,8},{14,10},{16,20},{18,... | collective-permute-start | bytes 884744 | tf_op jit(solution)/shard_map/ppermute | solution.py:76
  253.7 9.6 %collective-permute-start.15 = (bf16[2,2,1,1,48,896]{5,4,3,2,1,0:T(8,128)(2,1)S(1)}, bf16[2,2,1,1,48,896]{5,4,3,2,1,0:T(8,128)(2,1)S(1)}, u32[]{:S(2)}, u32[]{:S(2)}) collective-permute-start(bf16[2,2,1,1,48,896]{5,4,3,2,1,0:T(8,128)(2,1)S(1)} %dynamic-slice_convert_fusion), channel_id=1, source_target_pairs={{0,2},{2,0},{4,6},{6,4},{8,10},{10,8},{12,14},{14,12},{16,18},{18,... | collective-permute-start | bytes 1032200 | tf_op jit(solution)/shard_map/ppermute | solution.py:76
  265.5 6.3 %collective-permute-start.20 = (bf16[2,1,1,1,48,768]{5,4,3,2,1,0:T(8,128)(2,1)S(1)}, bf16[2,1,1,1,48,768]{5,4,3,2,1,0:T(8,128)(2,1)S(1)}, u32[]{:S(2)}, u32[]{:S(2)}) collective-permute-start(bf16[2,1,1,1,48,768]{5,4,3,2,1,0:T(8,128)(2,1)S(1)} %dynamic-slice_convert_fusion.4), channel_id=1, source_target_pairs={{0,8},{2,10},{4,12},{6,14},{8,0},{10,2},{12,4},{14,6},{16,24},{18,... | collective-permute-start | bytes 442376 | tf_op jit(solution)/shard_map/ppermute | solution.py:76
  266.9 8.9 %collective-permute-start.22 = (bf16[2,1,1,1,48,896]{5,4,3,2,1,0:T(8,128)(2,1)S(1)}, bf16[2,1,1,1,48,896]{5,4,3,2,1,0:T(8,128)(2,1)S(1)}, u32[]{:S(2)}, u32[]{:S(2)}) collective-permute-start(bf16[2,1,1,1,48,896]{5,4,3,2,1,0:T(8,128)(2,1)S(1)} %dynamic-slice_convert_fusion.3), channel_id=1, source_target_pairs={{0,8},{2,10},{4,12},{6,14},{8,0},{10,2},{12,4},{14,6},{16,24},{18,... | collective-permute-start | bytes 516104 | tf_op jit(solution)/shard_map/ppermute | solution.py:76
  268.5 15.7 %collective-permute-start.18 = (f32[128,768]{1,0:T(8,128)}, f32[128,768]{1,0:T(8,128)S(1)}, u32[]{:S(2)}, u32[]{:S(2)}) collective-permute-start(f32[128,768]{1,0:T(8,128)} %constant_dynamic-slice_fusion), channel_id=1, source_target_pairs={{0,1},{1,0},{2,3},{3,2},{4,5},{5,4},{6,7},{7,6},{8,9},{9,8},{10,11... | collective-permute-start | bytes 1179656 | tf_op jit(solution)/shard_map/ppermute | solution.py:48
  271.9 7.5 %collective-permute-start.21 = (bf16[1,1,1,1,48,768]{5,4,3,2,1,0:T(8,128)(2,1)S(1)}, bf16[1,1,1,1,48,768]{5,4,3,2,1,0:T(8,128)(2,1)S(1)}, u32[]{:S(2)}, u32[]{:S(2)}) collective-permute-start(bf16[1,1,1,1,48,768]{5,4,3,2,1,0:T(8,128)(2,1)S(1)} %dynamic-slice_convert_fusion.6), channel_id=1, source_target_pairs={{0,16},{2,18},{4,20},{6,22},{8,24},{10,26},{12,28},{14,30},{16,0},... | collective-permute-start | bytes 221192 | tf_op jit(solution)/shard_map/ppermute | solution.py:76
  (43 other events, 422.8 us)

commit v3 on v2

--- a/solution.py
+++ b/solution.py
@@ -13,7 +13,7 @@
 
 EPSILON = 1e-06
 NEGATIVE = -1e30
-VMEM_BYTES = 48 * 1024 * 1024
+MIB = 1024 * 1024
 EXTRA_ROWS = 16
 LOW = jnp.bfloat16
 FULL = jnp.float32
@@ -77,10 +77,23 @@
 
 
 def trade(values):
-    return lax.all_to_all(values, "dp", split_axis=0, concat_axis=0, tiled=True)
-
-
-def call(kernel, out_shape, *operands, flops=0, smem=()):
+    experts, dp_count = values.shape[0], lax.axis_size("dp")
+    owners = dp_count // experts
+    groups = [[owners * e + o for e in range(experts)] for o in range(owners)]
+    return lax.all_to_all(
+        values, "dp", split_axis=0, concat_axis=0, tiled=True, axis_index_groups=groups
+    )
+
+
+def cross(values):
+    return lax.ppermute(values, "dp", partners(0))
+
+
+def add_low(*parts):
+    return sum(part.astype(FULL) for part in parts).astype(LOW)
+
+
+def call(kernel, out_shape, *operands, flops=0, smem=(), limit=20):
     moved = sum(x.size * x.dtype.itemsize for x in (*operands, *out_shape))
     return pl.pallas_call(
         kernel,
@@ -90,7 +103,7 @@
             for i in range(len(operands))
         ],
         out_specs=[pl.BlockSpec(memory_space=pltpu.VMEM) for _ in out_shape],
-        compiler_params=pltpu.CompilerParams(vmem_limit_bytes=VMEM_BYTES),
+        compiler_params=pltpu.CompilerParams(vmem_limit_bytes=limit * MIB),
         cost_estimate=pl.CostEstimate(flops=flops, bytes_accessed=moved, transcendentals=0),
     )(*operands)
 
@@ -152,7 +165,7 @@
 def dispatch_kernel(
     base_ref, rows_ref, attn_ref, other_ref, ext_ref, slot_ref, resid_ref, h_ref, gates_ref, send_ref
 ):
-    experts, owners, rows_sent, _ = send_ref.shape
+    experts, rows_sent, _ = send_ref.shape
     blocks = rows_ref.shape[1] // LANES
     half = (rows_sent - EXTRA_ROWS) // blocks
     count = experts * half
@@ -180,17 +193,16 @@
         for part in split_low(gate_col)
     ]
     sub = iota((EXTRA_ROWS, LANES), 0)
-    for owner in range(owners):
-        for block in range(blocks):
-            send_ref[:, owner, block * half : (block + 1) * half, :] = picked[
-                :, :, block * LANES : (block + 1) * LANES
-            ]
-        for expert in range(experts):
-            send_ref[expert, owner, blocks * half :, :] = jnp.where(
-                sub == 0,
-                high_rows[expert : expert + 1, :],
-                jnp.where(sub == 1, low_rows[expert : expert + 1, :], 0.0),
-            ).astype(LOW)
+    for block in range(blocks):
+        send_ref[:, block * half : (block + 1) * half, :] = picked[
+            :, :, block * LANES : (block + 1) * LANES
+        ]
+    for expert in range(experts):
+        send_ref[expert, blocks * half :, :] = jnp.where(
+            sub == 0,
+            high_rows[expert : expert + 1, :],
+            jnp.where(sub == 1, low_rows[expert : expert + 1, :], 0.0),
+        ).astype(LOW)
 
 
 def rows_of(ref, half):
@@ -204,7 +216,7 @@
     )
 
 
-def expert_kernel(half, h_ref, cot_ref, first_ref, second_ref, back_ref, hid_ref, pre_ref, out_ref, gate_ref):
+def expert_step(half, h_ref, cot_ref, first_ref, second_ref, back_ref, hid_ref, pre_ref, out_ref, gate_ref):
     sources = h_ref.shape[0]
     blocks = (h_ref.shape[1] - EXTRA_ROWS) // half
     count, shift = sources * half, half.bit_length() - 1
@@ -246,105 +258,107 @@
     back_ref[:, blocks * half :, :] = rows_back.astype(LOW).reshape(sources, EXTRA_ROWS, LANES)
 
 
+def part_specs(sources, steps, shapes):
+    maps = (lambda i: (jnp.minimum(i, steps - 1), 0, 0), lambda i: (jnp.maximum(i - steps, 0), 0, 0))
+    return [pl.BlockSpec((sources, *shape), place) for shape in shapes for place in maps]
+
+
+def in_halves(steps, first, second):
+    pl.when(pl.program_id(0) < steps)(first)
+    pl.when(pl.program_id(0) >= steps)(second)
+
+
+def whole(array):
+    return pl.BlockSpec(array.shape, lambda i: (0,) * array.ndim, pipeline_mode=pl.Buffered(1))
+
+
 def expert_rows(h_rows, cot_rows, first_weight, second_weight, half):
-    dp_count, rows_sent, _ = h_rows.shape
+    experts, rows_sent, _ = h_rows[0].shape
     width, hidden_width = first_weight.shape
-    sources = min(dp_count, 256 // half)
-    count = sources * half
-    wide = lambda lanes, kind: jax.ShapeDtypeStruct((dp_count * half, lanes), kind)
-    rows = lambda lanes: pl.BlockSpec((count, lanes), lambda i: (i, 0))
-    block = lambda *shape: pl.BlockSpec((sources, *shape), lambda i: (i, 0, 0))
-    whole = lambda array: pl.BlockSpec(array.shape, lambda i: (0, 0))
+    sources = min(experts, 256 // half)
+    count, steps = sources * half, experts // sources
+    total = 2 * experts * half
+
+    def kernel(h_a, h_b, cot_a, cot_b, first_ref, second_ref, back_a, back_b, *kept):
+        in_halves(
+            steps,
+            lambda: expert_step(half, h_a, cot_a, first_ref, second_ref, back_a, *kept),
+            lambda: expert_step(half, h_b, cot_b, first_ref, second_ref, back_b, *kept),
+        )
+
+    lanes = ((hidden_width, LOW), (hidden_width, LOW), (width, LOW), (LANES, FULL))
+    back_a, back_b, *kept = pl.pallas_call(
+        kernel,
+        grid=(2 * steps,),
+        out_shape=[jax.ShapeDtypeStruct(h_rows[0].shape, LOW)] * 2
+        + [jax.ShapeDtypeStruct((total, n), kind) for n, kind in lanes],
+        in_specs=part_specs(sources, steps, [(rows_sent, LANES), (half, width)])
+        + [whole(first_weight), whole(second_weight)],
+        out_specs=part_specs(sources, steps, [(rows_sent, LANES)])
+        + [pl.BlockSpec((count, n), lambda i: (i, 0)) for n, _ in lanes],
+        compiler_params=pltpu.CompilerParams(vmem_limit_bytes=24 * MIB),
+        cost_estimate=pl.CostEstimate(
+            flops=6 * total * width * hidden_width,
+            bytes_accessed=12 * total * width,
+            transcendentals=total * hidden_width,
+        ),
+    )(*h_rows, *cot_rows, first_weight, second_weight)
+    return back_a, back_b, kept
+
+
+def expert_weights(h_rows, kept, second_weight, sums, half):
+    experts, rows_sent, _ = h_rows[0].shape
+    hidden_width, width = second_weight.shape
+    sources = min(experts, 256 // half)
+    count, steps = sources * half, experts // sources
+    total = 2 * experts * half
+
+    def kernel(h_a, h_b, hid_ref, pre_ref, arr_ref, gate_ref, second_ref, *refs):
+        out_a, out_b, grad_first, grad_second = refs[-4:]
+
+        @pl.when(pl.program_id(0) == 0)
+        def _():
+            for at, grad in enumerate((grad_first, grad_second)):
+                grad[...] = refs[at][...] if sums else jnp.zeros(grad.shape, FULL)
+
+        def step(h_ref, out_ref):
+            hidden = hid_ref[...]
+            produced = dot(hidden, second_ref[...])
+            out_ref[...] = (gate_ref[:, 0:1] * produced).astype(LOW).reshape(out_ref.shape)
+            grad_first[...] += contract_rows(rows_of(h_ref, half), pre_ref[...])
+            grad_second[...] += contract_rows(hidden, arr_ref[...])
+
+        in_halves(steps, lambda: step(h_a, out_a), lambda: step(h_b, out_b))
+
+    shape = jax.ShapeDtypeStruct
+    grads = [shape((width, hidden_width), FULL), shape((hidden_width, width), FULL)]
     return pl.pallas_call(
-        lambda *refs: expert_kernel(half, *refs),
-        grid=(dp_count // sources,),
-        out_shape=[
-            jax.ShapeDtypeStruct(h_rows.shape, LOW),
-            wide(hidden_width, LOW),
-            wide(hidden_width, LOW),
-            wide(width, LOW),
-            wide(LANES, FULL),
-        ],
-        in_specs=[
-            block(rows_sent, LANES),
-            block(half, width),
-            whole(first_weight),
-            whole(second_weight),
-        ],
-        out_specs=[
-            block(rows_sent, LANES),
-            rows(hidden_width),
-            rows(hidden_width),
-            rows(width),
-            rows(LANES),
-        ],
-        compiler_params=pltpu.CompilerParams(vmem_limit_bytes=VMEM_BYTES),
+        kernel,
+        grid=(2 * steps,),
+        out_shape=[shape((experts, half, width), LOW)] * 2 + grads,
+        in_specs=part_specs(sources, steps, [(rows_sent, LANES)])
+        + [pl.BlockSpec((count, x.shape[1]), lambda i: (i, 0)) for x in kept]
+        + [whole(x) for x in (second_weight, *sums)],
+        out_specs=part_specs(sources, steps, [(half, width)]) + [whole(x) for x in grads],
+        compiler_params=pltpu.CompilerParams(vmem_limit_bytes=32 * MIB),
         cost_estimate=pl.CostEstimate(
-            flops=6 * dp_count * half * width * hidden_width,
-            bytes_accessed=12 * dp_count * half * width,
-            transcendentals=dp_count * half * hidden_width,
-        ),
-    )(h_rows, cot_rows, first_weight, second_weight)
-
-
-def weight_kernel(half, h_ref, hid_ref, pre_ref, arr_ref, gate_ref, second_ref, first_in, second_in, out_ref, first_ref, second_out):
-    @pl.when(pl.program_id(0) == 0)
-    def _():
-        first_ref[...] = first_in[...]
-        second_out[...] = second_in[...]
-
-    hidden = hid_ref[...]
-    produced = dot(hidden, second_ref[...])
-    out_ref[...] = (gate_ref[:, 0:1] * produced).astype(LOW)
-    first_ref[...] += contract_rows(rows_of(h_ref, half), pre_ref[...])
-    second_out[...] += contract_rows(hidden, arr_ref[...])
-
-
-def expert_weights(h_rows, hidden, grad_pre, arrived, gate, second_weight, first_sum, second_sum, half):
-    dp_count, rows_sent, _ = h_rows.shape
-    hidden_width, width = second_weight.shape
-    sources = min(dp_count, 512 // half)
-    count = sources * half
-    rows = lambda lanes: pl.BlockSpec((count, lanes), lambda i: (i, 0))
-    whole = lambda array: pl.BlockSpec(array.shape, lambda i: (0, 0))
-    return pl.pallas_call(
-        lambda *refs: weight_kernel(half, *refs),
-        grid=(dp_count // sources,),
-        out_shape=[
-            jax.ShapeDtypeStruct((dp_count * half, width), LOW),
-            jax.ShapeDtypeStruct(first_sum.shape, FULL),
-            jax.ShapeDtypeStruct(second_sum.shape, FULL),
-        ],
-        in_specs=[
-            pl.BlockSpec((sources, rows_sent, LANES), lambda i: (i, 0, 0)),
-            rows(hidden_width),
-            rows(hidden_width),
-            rows(width),
-            rows(LANES),
-            whole(second_weight),
-            whole(first_sum),
-            whole(second_sum),
-        ],
-        out_specs=[rows(width), whole(first_sum), whole(second_sum)],
-        compiler_params=pltpu.CompilerParams(vmem_limit_bytes=VMEM_BYTES),
-        cost_estimate=pl.CostEstimate(
-            flops=6 * dp_count * half * width * hidden_width,
-            bytes_accessed=10 * dp_count * half * width,
+            flops=6 * total * width * hidden_width,
+            bytes_accessed=10 * total * width,
             transcendentals=0,
         ),
-    )(h_rows, hidden, grad_pre, arrived, gate, second_weight, first_sum, second_sum)
+    )(*h_rows, *kept, second_weight, *sums)
 
 
 def combine_kernel(base_ref, back_ref, slot_ref, col_ref, gates_ref, ext_ref, h_ref, part_ref, router_ref):
-    experts, owners, rows_sent, _ = back_ref.shape
+    experts, rows_sent, _ = back_ref.shape
     blocks = h_ref.shape[1] // LANES
     half = (rows_sent - EXTRA_ROWS) // blocks
     count = experts * half
     slot_row = slot_ref[...]
     hits = slot_row >= 0
     here, of_expert = slot_tables(slot_row, base_ref[0], half)
-    extra = back_ref[:, :, blocks * half :, :].reshape(experts * owners * EXTRA_ROWS, LANES)
-    reach = owners * EXTRA_ROWS
+    extra = back_ref[:, blocks * half :, :].reshape(experts * EXTRA_ROWS, LANES)
+    reach = EXTRA_ROWS
     shift, reach_shift = half.bit_length() - 1, reach.bit_length() - 1
     row = iota((count, experts * reach), 1)
     wanted = (row >> reach_shift) == (iota((count, experts * reach), 0) >> shift)
@@ -360,14 +374,11 @@
     high, low = split_low(logit_grad)
     router_ref[...] = dot(high, h_ref[...]) + dot(low, h_ref[...])
     router_rows = ext_ref[2 : 2 + experts, :].astype(LOW)
-    span = owners * half
-    span_shift = span.bit_length() - 1
-    total = experts * span
-    expand = (iota((experts, total), 1) >> span_shift) == iota((experts, total), 0)
-    wanted = (iota((1, total), 1) & (half - 1)) + base_ref[0]
+    expand = (iota((experts, count), 1) >> shift) == iota((experts, count), 0)
+    wanted = (iota((1, count), 1) & (half - 1)) + base_ref[0]
     one_hot = (dot(col_ref[...], expand.astype(LOW)) == wanted.astype(FULL)).astype(LOW)
     for block in range(blocks):
-        rows = back_ref[:, :, block * half : (block + 1) * half, :].reshape(total, LANES)
+        rows = back_ref[:, block * half : (block + 1) * half, :].reshape(count, LANES)
         at = slice(block * LANES, (block + 1) * LANES)
         part_ref[:, at] = (
             dot(one_hot, rows)
@@ -455,9 +466,8 @@
     tok_rows, width = block_in.shape
     group_rows, top_count = routes.shape
     experts = router.shape[1]
-    owners = dp_count // experts
     half = max(EXTRA_ROWS, top_count * group_rows // experts)
-    slots = dp_count * half
+    slots = experts * half
     rows_sent = half * (width // LANES) + EXTRA_ROWS
     inner = w_query.shape[1]
     bits = dp_count.bit_length() - 1
@@ -472,13 +482,9 @@
     base = core * half
     slot_ids = (base + jnp.arange(half, dtype=jnp.int32)).astype(LOW)
     in_slot = slot_row[:, None, :] == slot_ids[None, :, None]
-    dispatch = (
-        jnp.broadcast_to(in_slot[:, None], (experts, owners, half, group_rows))
-        .astype(LOW)
-        .reshape(slots, group_rows)
-    )
+    dispatch = in_slot.astype(LOW).reshape(slots, group_rows)
     base = base.reshape(1).astype(jnp.int32)
-    cot_picked = dot(dispatch, cotangent.astype(LOW)).astype(LOW).reshape(dp_count, half, width)
+    cot_picked = dot(dispatch, cotangent.astype(LOW)).astype(LOW).reshape(experts, half, width)
 
     extra_width = -(-(2 + experts) // LANES) * LANES
     extra = jnp.concatenate(
@@ -497,7 +503,7 @@
     for step in range(bits):
         vx_full = double(vx_full, order_b[step], bits)
         qk_full = double(qk_full, order_a[step], bits)
-        if step == bits - 3:
+        if step == bits - 2:
             cot_picked, qk_full, vx_full = lax.optimization_barrier((cot_picked, qk_full, vx_full))
     qk_full = qk_full.reshape(width, 2 * inner)
     vx_full = vx_full.reshape(width, 2 * inner + extra_width)
@@ -522,16 +528,13 @@
         flops=8 * group_rows * width * inner + 4 * group_rows * group_rows * inner,
         smem=(0,),
     )
-    attn_part, cot_own = lax.optimization_barrier((attn_part, cot_own))
-    cot_other = swap(cot_own)
-
     residual, h_two, gates, sent = call(
         dispatch_kernel,
         [
             shape((group_rows, width), FULL),
             shape((group_rows, width), LOW),
             shape((experts, group_rows), FULL),
-            shape((experts, owners, rows_sent, LANES), LOW),
+            shape((experts, rows_sent, LANES), LOW),
         ],
         base,
         rows_all,
@@ -543,31 +546,35 @@
         smem=(0,),
     )
 
-    h_own = trade(sent.reshape(dp_count, rows_sent, LANES))
-    h_other = swap(h_own)
+    sent, cot_own = lax.optimization_barrier((sent, cot_own))
+    cot_crossed = cross(cot_own)
+    cot_own = (cot_own, swap(cot_own))
+    cot_far = (cot_crossed, swap(cot_crossed))
+    h_own = trade(sent)
+    h_crossed = cross(h_own)
+    h_own = (h_own, swap(h_own))
+    h_far = (h_crossed, swap(h_crossed))
     first_weight = expert_in[0]
     second_weight = expert_out[0]
-    back_own, *own_kept = expert_rows(h_own, cot_own, first_weight, second_weight, half)
-    back_other, *other_kept = expert_rows(h_other, cot_other, first_weight, second_weight, half)
-    back = (back_own.astype(FULL) + swap(back_other).astype(FULL)).astype(LOW)
-    back = trade(back)
-
-    zeros = jnp.zeros((width, first_weight.shape[1]), FULL)
-    out_other, first_sum, second_sum = expert_weights(
-        h_other, *other_kept, second_weight, zeros, zeros.reshape(second_weight.shape), half
-    )
-    out_own, grad_first, grad_second = expert_weights(
-        h_own, *own_kept, second_weight, first_sum, second_sum, half
-    )
-    out_rows = (out_own.astype(FULL) + swap(out_other).astype(FULL)).astype(LOW)
+    own_back, own_given, own_kept = expert_rows(h_own, cot_own, first_weight, second_weight, half)
+    far_back, far_given, far_kept = expert_rows(h_far, cot_far, first_weight, second_weight, half)
+    far_total = cross(add_low(far_back, swap(far_given)))
+    back = trade(add_low(own_back, swap(own_given), far_total))
+
+    far_out, far_given, *sums = expert_weights(h_far, far_kept, second_weight, (), half)
+    own_out, own_given, grad_first, grad_second = expert_weights(
+        h_own, own_kept, second_weight, sums, half
+    )
+    far_total = cross(add_low(far_out, swap(far_given)))
+    out_rows = add_low(own_out, swap(own_given), far_total)
     out_rows, back = lax.optimization_barrier((out_rows, back))
-    back_out = trade(out_rows.reshape(dp_count, half, width)).reshape(slots, width)
+    back_out = trade(out_rows).reshape(slots, width)
 
     h_part, router_part = call(
         combine_kernel,
         [shape((group_rows, width), FULL), shape((experts, width), FULL)],
         base,
-        back.reshape(experts, owners, rows_sent, LANES),
+        back,
         slot_row,
         slot_col,
         gates,

time: 286 us -> 314 us (1.098)
  waiting for transfers between devices: 93.6 us -> 128 us
  local copies, waits for them, and re-layouts: 28.3 us -> 48.9 us
  blocking collectives: 49.8 us -> 34.3 us
  Pallas kernels: 49.7 us -> 38.4 us
    ppermute x0 -> x4, waiting for transfers between devices: none -> 62.1 us  [cross(): return lax.ppermute(values, 'dp', partners(0))]
    unnamed x81 -> x111, local copies, waits for them, and re-layouts: 17.6 us -> 41.1 us
    ppermute x8, waiting for transfers between devices: 38 us -> 21.7 us  [double(): other = lax.ppermute(block, 'dp', partners(bit))]
    all_to_all x1, blocking collectives: 47.5 us -> 31.9 us  [trade(): lax.all_to_all(values, 'dp', split_axis=0, concat_axis=0, tiled=True, axi...]
    all_to_all x3, waiting for transfers between devices: 11.3 us -> 0.01 us  [trade(): lax.all_to_all(values, 'dp', split_axis=0, concat_axis=0, tiled=True, axi...]
    pallas_call x4, Pallas kernels: 33.8 us -> 24.3 us  [the longest x2 12.6 us: expert_weights(): pl.pallas_call(kernel, grid=(2 * steps,), out_shape=[shape((experts, half...]
    ppermute x0 -> x4, starting transfers between devices: none -> 3.23 us  [cross(): return lax.ppermute(values, 'dp', partners(0))]
    ppermute x9 -> x13, waiting for transfers between devices: 8.48 us -> 7.49 us  [swap(): return lax.ppermute(values, 'tensor', [(0, 1), (1, 0)])]
  transfers between devices with their start and end apart: 28 -> 36, of which waited for: 16 -> 23; matrix products, arithmetic and copies ran while one was open for 7% -> 6% of each run, Pallas kernels for 14% -> 9%
where the time goes in v3:
time: 314 us; the launch traced here: 312 us
  waiting for transfers between devices  128 us (41%)
  local copies, waits for them, and re-layouts  48.9 us (16%)
  starting transfers between devices  47.9 us (15%)
  Pallas kernels  38.4 us (12%)
  blocking collectives  34.3 us (11%)
  other arithmetic  11.6 us (4%)
    ppermute x4, waiting for transfers between devices, cross(): return lax.ppermute(values, 'dp', partners(0))  62.1 us
    unnamed x111, local copies, waits for them, and re-layouts  41.1 us
    ppermute x8, waiting for transfers between devices, halve(): lax.ppermute(given, 'dp', partners(bit)).astype(FULL)  36.9 us
    all_to_all x1, blocking collectives, trade(): lax.all_to_all(values, 'dp', split_axis=0, concat_axis=0, tiled=True, axi...  31.9 us
    ppermute x8, waiting for transfers between devices, double(): other = lax.ppermute(block, 'dp', partners(bit))  21.7 us
    all_to_all x3, starting transfers between devices, trade(): lax.all_to_all(values, 'dp', split_axis=0, concat_axis=0, tiled=True, axi...  17.1 us
    pallas_call x4, Pallas kernels, call(): pl.pallas_call(kernel, out_shape=out_shape, in_specs=[pl.BlockSpec(memory...  14.2 us
    ppermute x8, starting transfers between devices, halve(): lax.ppermute(given, 'dp', partners(bit)).astype(FULL)  13.5 us
  transfers between devices with their start and end apart: 36, of which 23 were waited for; matrix products, arithmetic and copies ran while one was open for 6% of the time, Pallas kernels for 9%

profile of v3, /device:TPU:0, one launch (start us, length us, event | category | flops | bytes accessed | tf_op | source)
XLA Modules:
  0.0 312.3 jit_solution(8862070821896093896)
XLA Ops:
  3.9 4.1 %collective-permute-start.3 = (bf16[1,1,1,1,48,896]{5,4,0,1,3,2:T(8,128)(2,1)S(1)}, bf16[1,1,1,1,48,896]{5,4,0,1,3,2:T(8,128)(2,1)S(1)}, u32[]{:S(2)}, u32[]{:S(2)}) collective-permute-start(bf16[1,1,1,1,48,896]{5,4,0,1,3,2:T(8,128)(2,1)S(1)} %bitcast.63), channel_id=1, source_target_pairs={{0,16},{2,18},{4,20},{6,22},{8,24},{10,26},{12,28},{14,30},{16,0},... | collective-permute-start | bytes 258056 | tf_op jit(solution)/shard_map/ppermute | solution.py:62
  12.9 3.1 %collective-permute-done = bf16[1,1,1,1,48,768]{5,4,0,1,3,2:T(8,128)(2,1)S(1)} collective-permute-done((bf16[1,1,1,1,48,768]{5,4,0,1,3,2:T(8,128)(2,1)S(1)}, bf16[1,1,1,1,48,768]{5,4,0,1,3,2:T(8,128)(2,1)S(1)}, u32[]{:S(2)}, u32[]{:S(2)}) %collective-permute-start) | collective-permute-done | bytes 73760 | tf_op jit(solution)/shard_map/ppermute | solution.py:62
  18.3 3.9 %collective-permute-done.1 = bf16[2,1,1,1,48,768]{5,4,0,1,3,2:T(8,128)(2,1)S(1)} collective-permute-done((bf16[2,1,1,1,48,768]{5,4,0,1,3,2:T(8,128)(2,1)S(1)}, bf16[2,1,1,1,48,768]{5,4,0,1,3,2:T(8,128)(2,1)S(1)}, u32[]{:S(2)}, u32[]{:S(2)}) %collective-permute-start.1) | collective-permute-done | bytes 147488 | tf_op jit(solution)/shard_map/ppermute | solution.py:62
  25.7 3.3 %collective-permute-done.2 = bf16[2,2,1,1,48,768]{5,4,0,1,3,2:T(8,128)(2,1)S(1)} collective-permute-done((bf16[2,2,1,1,48,768]{5,4,0,1,3,2:T(8,128)(2,1)S(1)}, bf16[2,2,1,1,48,768]{5,4,0,1,3,2:T(8,128)(2,1)S(1)}, u32[]{:S(2)}, u32[]{:S(2)}) %collective-permute-start.2) | collective-permute-done | bytes 294944 | tf_op jit(solution)/shard_map/ppermute | solution.py:62
  35.3 6.8 %all-to-all-start = ((bf16[8,64,768]{2,1,0:T(8,128)(2,1)}), bf16[8,64,768]{2,1,0:T(8,128)(2,1)}, u32[]{:S(2)}, u32[]{:S(2)}) async-start(bf16[8,64,768]{2,1,0:T(8,128)(2,1)} %bitcast.3), calls=%async_computation | async-start | bytes 1572864 | tf_op jit(solution)/shard_map/all_to_all | solution.py:83
  46.4 7.8 %collective-permute-done.7 = bf16[2,2,1,2,48,896]{5,4,0,1,3,2:T(8,128)(2,1)S(1)} collective-permute-done((bf16[2,2,1,2,48,896]{5,4,0,1,3,2:T(8,128)(2,1)S(1)}, bf16[2,2,1,2,48,896]{5,4,0,1,3,2:T(8,128)(2,1)S(1)}, u32[]{:S(2)}, u32[]{:S(2)}) %collective-permute-start.7) | collective-permute-done | bytes 688160 | tf_op jit(solution)/shard_map/ppermute | solution.py:62
  68.0 31.9 %all_to_all.20.h_a = bf16[8,400,128]{2,1,0:T(8,128)(2,1)S(1)} all-to-all(bf16[8,400,128]{2,1,0:T(8,128)(2,1)} %copy-done.18), channel_id=1, replica_groups={{0,4,8,12,16,20,24,28},{2,6,10,14,18,22,26,30},{1,5,9,13,17,21,25,29},{..., dimensions={0} | all-to-all | bytes 1638400 | tf_op jit(solution)/shard_map/all_to_all | solution.py:83
  102.0 19.2 %collective-permute-done.11.h_a = bf16[8,400,128]{2,1,0:T(8,128)(2,1)S(1)} collective-permute-done((bf16[8,400,128]{2,1,0:T(8,128)(2,1)S(1)}, bf16[8,400,128]{2,1,0:T(8,128)(2,1)S(1)}, u32[]{:S(2)}, u32[]{:S(2)}) %collective-permute-start.11) | collective-permute-done | bytes 819232 | tf_op jit(solution)/shard_map/ppermute | solution.py:89
  121.1 14.6 %collective-permute-done.13.cot_a = bf16[8,64,768]{2,1,0:T(8,128)(2,1)S(1)} collective-permute-done((bf16[8,64,768]{2,1,0:T(8,128)(2,1)}, bf16[8,64,768]{2,1,0:T(8,128)(2,1)S(1)}, u32[]{:S(2)}, u32[]{:S(2)}) %collective-permute-start.13) | collective-permute-done | bytes 786464 | tf_op jit(solution)/shard_map/ppermute | solution.py:89
  140.4 5.2 %shard_map.215 = (bf16[8,400,128]{2,1,0:T(8,128)(2,1)S(1)}, bf16[8,400,128]{2,1,0:T(8,128)(2,1)S(1)}, bf16[1024,768]{1,0:T(8,128)(2,1)S(1)}, bf16[1024,768]{1,0:...) custom-call(bf16[8,400,128]{2,1,0:T(8,128)(2,1)S(1)} %collective-permute-done.11.h_a, ...), custom_call_target="tpu_custom_call" | custom-call | flops 3623878656 | bytes 9437184 | tf_op jit(solution)/shard_map/pallas_call | solution.py:290
  145.8 6.5 %shard_map.214 = (bf16[8,400,128]{2,1,0:T(8,128)(2,1)S(1)}, bf16[8,400,128]{2,1,0:T(8,128)(2,1)S(1)}, bf16[1024,768]{1,0:T(8,128)(2,1)S(1)}, bf16[1024,768]{1,0:...) custom-call(bf16[8,400,128]{2,1,0:T(8,128)(2,1)S(1)} %all_to_all.20.h_a, ...), custom_call_target="tpu_custom_call" | custom-call | flops 3623878656 | bytes 9437184 | tf_op jit(solution)/shard_map/pallas_call | solution.py:290
  156.7 5.6 %shard_map.216 = (bf16[8,64,768]{2,1,0:T(8,128)(2,1)S(1)}, bf16[8,64,768]{2,1,0:T(8,128)(2,1)}, f32[768,768]{1,0:T(8,128)S(1)}, f32[768,768]{1,0:T(8,128)S(1)}) custom-call(bf16[8,400,128]{2,1,0:T(8,128)(2,1)S(1)} %collective-permute-done.11.h_a, bf16[8,400,128]{2,1,0:T(8,128)(2,1)S(1)} %collective-permute-done.12.h_b, ...), custom_call_target="tpu_custom_call" | custom-call | flops 3623878656 | bytes 7864320 | tf_op jit(solution)/shard_map/pallas_call | solution.py:335
  166.4 9.3 %collective-permute-done.20 = bf16[8,400,128]{2,1,0:T(8,128)(2,1)S(1)} collective-permute-done((bf16[8,400,128]{2,1,0:T(8,128)(2,1)S(1)}, bf16[8,400,128]{2,1,0:T(8,128)(2,1)S(1)}, u32[]{:S(2)}, u32[]{:S(2)}) %collective-permute-start.20) | collective-permute-done | bytes 819232 | tf_op jit(solution)/shard_map/ppermute | solution.py:89
  176.9 4.4 %all-to-all-start.2 = ((bf16[8,400,128]{2,1,0:T(8,128)(2,1)}), bf16[8,400,128]{2,1,0:T(8,128)(2,1)}, u32[]{:S(2)}, u32[]{:S(2)}) async-start(bf16[8,400,128]{2,1,0:T(8,128)(2,1)} %add_convert_fusion), calls=%async_computation.2 | async-start | bytes 1638400 | tf_op jit(solution)/shard_map/all_to_all | solution.py:83
  193.5 7.0 %shard_map.217 = (bf16[8,64,768]{2,1,0:T(8,128)(2,1)S(1)}, bf16[8,64,768]{2,1,0:T(8,128)(2,1)S(1)}, f32[768,768]{1,0:T(8,128)}, f32[768,768]{1,0:T(8,128)}) custom-call(bf16[8,400,128]{2,1,0:T(8,128)(2,1)S(1)} %copy-done.17, bf16[8,400,128]{2,1,0:T(8,128)(2,1)S(1)} %copy-done.37, bf16[1024,768]{1,0:T(8,128)(2,1)S(1)} %copy-done.43, ...), custom_call_target="tpu_custom_call" | custom-call | flops 3623878656 | bytes 7864320 | tf_op jit(solution)/shard_map/pallas_call | solution.py:335
  202.8 19.1 %collective-permute-done.17 = bf16[8,64,768]{2,1,0:T(8,128)(2,1)S(1)} collective-permute-done((bf16[8,64,768]{2,1,0:T(8,128)(2,1)S(1)}, bf16[8,64,768]{2,1,0:T(8,128)(2,1)S(1)}, u32[]{:S(2)}, u32[]{:S(2)}) %collective-permute-start.17) | collective-permute-done | bytes 786464 | tf_op jit(solution)/shard_map/ppermute | solution.py:89
  225.1 3.6 %shard_map.218 = (f32[256,768]{1,0:T(8,128)}, f32[8,768]{1,0:T(8,128)S(1)}) custom-call(s32[1]{0:T(128)} %bitcast.base_ref, bf16[8,400,128]{2,1,0:T(8,128)(2,1)} %all-to-all-done.2.back_ref, bf16[8,256]{1,0:T(8,128)(2,1)S(1)} %copy.62.slot_ref, bf16[256,8]{1,0:T(8,128)(2,1)S(1)} %fusion.col_ref, f32[8,256]{1,0:T(8,128)S(1)} %get-tuple-element.85.gates_ref, ...), custom_call_target="tpu_custom_call" | custom-call | flops 201326592 | bytes 2433028 | tf_op jit(solution)/shard_map/pallas_call | solution.py:98
  238.9 6.6 %shard_map.219 = (bf16[768,768]{1,0:T(8,128)(2,1)S(1)}, bf16[768,896]{1,0:T(8,128)(2,1)S(1)}, f32[256,768]{1,0:T(8,128)S(1)}, f32[256,768]{1,0:T(8,128)S(1)}, bf...) custom-call(f32[256,768]{1,0:T(8,128)} %get-tuple-element.87.part_ref, f32[256,768]{1,0:T(8,128)} %collective-permute-done.21.other_ref, ...), custom_call_target="tpu_custom_call" | custom-call | flops 1811939328 | bytes 14745600 | tf_op jit(solution)/shard_map/pallas_call | solution.py:98
  248.9 5.8 %all-to-all-start.3 = ((bf16[8,64,768]{2,1,0:T(8,128)(2,1)}), bf16[8,64,768]{2,1,0:T(8,128)(2,1)S(1)}, u32[]{:S(2)}, u32[]{:S(2)}) async-start(bf16[8,64,768]{2,1,0:T(8,128)(2,1)} %add_convert_fusion.2), calls=%async_computation.3 | async-start | bytes 1572864 | tf_op jit(solution)/shard_map/all_to_all | solution.py:83
  257.1 6.2 %collective-permute-done.24 = bf16[2,2,2,1,48,768]{5,4,3,2,1,0:T(8,128)(2,1)} collective-permute-done((bf16[2,2,2,1,48,768]{5,4,3,2,1,0:T(8,128)(2,1)}, bf16[2,2,2,1,48,768]{5,4,3,2,1,0:T(8,128)(2,1)}, u32[]{:S(2)}, u32[]{:S(2)}) %collective-permute-start.24) | collective-permute-done | bytes 589856 | tf_op jit(solution)/shard_map/ppermute | solution.py:76
  266.2 15.4 %collective-permute-done.22 = bf16[2,2,1,2,48,896]{5,4,3,2,1,0:T(8,128)(2,1)S(1)} collective-permute-done((bf16[2,2,1,2,48,896]{5,4,3,2,1,0:T(8,128)(2,1)S(1)}, bf16[2,2,1,2,48,896]{5,4,3,2,1,0:T(8,128)(2,1)S(1)}, u32[]{:S(2)}, u32[]{:S(2)}) %collective-permute-start.22) | collective-permute-done | bytes 688160 | tf_op jit(solution)/shard_map/ppermute | solution.py:76
  287.3 3.2 %collective-permute-done.23 = bf16[2,2,1,1,48,896]{5,4,3,2,1,0:T(8,128)(2,1)S(1)} collective-permute-done((bf16[2,2,1,1,48,896]{5,4,3,2,1,0:T(8,128)(2,1)S(1)}, bf16[2,2,1,1,48,896]{5,4,3,2,1,0:T(8,128)(2,1)S(1)}, u32[]{:S(2)}, u32[]{:S(2)}) %collective-permute-start.23) | collective-permute-done | bytes 344096 | tf_op jit(solution)/shard_map/ppermute | solution.py:76
  293.3 4.5 %collective-permute-done.28 = bf16[2,1,1,1,48,768]{5,4,3,2,1,0:T(8,128)(2,1)S(1)} collective-permute-done((bf16[2,1,1,1,48,768]{5,4,3,2,1,0:T(8,128)(2,1)S(1)}, bf16[2,1,1,1,48,768]{5,4,3,2,1,0:T(8,128)(2,1)S(1)}, u32[]{:S(2)}, u32[]{:S(2)}) %collective-permute-start.28) | collective-permute-done | bytes 147488 | tf_op jit(solution)/shard_map/ppermute | solution.py:76
  297.9 5.3 %collective-permute-start.29 = (bf16[1,1,1,1,48,768]{5,4,3,2,1,0:T(8,128)(2,1)S(1)}, bf16[1,1,1,1,48,768]{5,4,3,2,1,0:T(8,128)(2,1)S(1)}, u32[]{:S(2)}, u32[]{:S(2)}) collective-permute-start(bf16[1,1,1,1,48,768]{5,4,3,2,1,0:T(8,128)(2,1)S(1)} %dynamic-slice_convert_fusion.6), channel_id=1, source_target_pairs={{0,16},{2,18},{4,20},{6,22},{8,24},{10,26},{12,28},{14,30},{16,0},... | collective-permute-start | bytes 221192 | tf_op jit(solution)/shard_map/ppermute | solution.py:76
  (234 shorter events, 108.8 us)
Async XLA Ops:
  3.9 12.7 %collective-permute-start.3 = (bf16[1,1,1,1,48,896]{5,4,0,1,3,2:T(8,128)(2,1)S(1)}, bf16[1,1,1,1,48,896]{5,4,0,1,3,2:T(8,128)(2,1)S(1)}, u32[]{:S(2)}, u32[]{:S(2)}) collective-permute-start(bf16[1,1,1,1,48,896]{5,4,0,1,3,2:T(8,128)(2,1)S(1)} %bitcast.63), channel_id=1, source_target_pairs={{0,16},{2,18},{4,20},{6,22},{8,24},{10,26},{12,28},{14,30},{16,0},... | collective-permute-start | bytes 258056 | tf_op jit(solution)/shard_map/ppermute | solution.py:62
  24.0 8.1 %collective-permute-start.5 = (bf16[2,2,1,1,48,896]{5,4,0,1,3,2:T(8,128)(2,1)S(1)}, bf16[2,2,1,1,48,896]{5,4,0,1,3,2:T(8,128)(2,1)S(1)}, u32[]{:S(2)}, u32[]{:S(2)}) collective-permute-start(bf16[2,2,1,1,48,896]{5,4,0,1,3,2:T(8,128)(2,1)S(1)} %maximum_select_fusion.4), channel_id=1, source_target_pairs={{0,2},{2,0},{4,6},{6,4},{8,10},{10,8},{12,14},{14,12},{16,18},{18,... | collective-permute-start | bytes 1032200 | tf_op jit(solution)/shard_map/ppermute | solution.py:62
  32.3 12.6 %collective-permute-start.6 = (bf16[2,2,2,1,48,768]{5,4,0,1,3,2:T(8,128)(2,1)S(1)}, bf16[2,2,2,1,48,768]{5,4,0,1,3,2:T(8,128)(2,1)}, u32[]{:S(2)}, u32[]{:S(2)}) collective-permute-start(bf16[2,2,2,1,48,768]{5,4,0,1,3,2:T(8,128)(2,1)S(1)} %maximum_select_fusion.3), channel_id=1, source_target_pairs={{0,2},{2,0},{4,6},{6,4},{8,10},{10,8},{12,14},{14,12},{16,18},{18,... | collective-permute-start | bytes 1769480 | tf_op jit(solution)/shard_map/ppermute | solution.py:62
  33.8 20.4 %collective-permute-start.7 = (bf16[2,2,1,2,48,896]{5,4,0,1,3,2:T(8,128)(2,1)S(1)}, bf16[2,2,1,2,48,896]{5,4,0,1,3,2:T(8,128)(2,1)S(1)}, u32[]{:S(2)}, u32[]{:S(2)}) collective-permute-start(bf16[2,2,1,2,48,896]{5,4,0,1,3,2:T(8,128)(2,1)S(1)} %maximum_select_fusion.2), channel_id=1, source_target_pairs={{0,4},{2,6},{4,0},{6,2},{8,12},{10,14},{12,8},{14,10},{16,20},{18,... | collective-permute-start | bytes 2064392 | tf_op jit(solution)/shard_map/ppermute | solution.py:62
  35.3 32.7 %all-to-all-start = ((bf16[8,64,768]{2,1,0:T(8,128)(2,1)}), bf16[8,64,768]{2,1,0:T(8,128)(2,1)}, u32[]{:S(2)}, u32[]{:S(2)}) async-start(bf16[8,64,768]{2,1,0:T(8,128)(2,1)} %bitcast.3), calls=%async_computation | async-start | bytes 1572864 | tf_op jit(solution)/shard_map/all_to_all | solution.py:83
  99.9 21.2 %collective-permute-start.11 = (bf16[8,400,128]{2,1,0:T(8,128)(2,1)S(1)}, bf16[8,400,128]{2,1,0:T(8,128)(2,1)S(1)}, u32[]{:S(2)}, u32[]{:S(2)}) collective-permute-start(bf16[8,400,128]{2,1,0:T(8,128)(2,1)S(1)} %all_to_all.20.h_a), channel_id=1, source_target_pairs={{0,2},{2,0},{4,6},{6,4},{8,10},{10,8},{12,14},{14,12},{16,18},{18,... | collective-permute-start | bytes 2457608 | tf_op jit(solution)/shard_map/ppermute | solution.py:89
  100.5 35.3 %collective-permute-start.13 = (bf16[8,64,768]{2,1,0:T(8,128)(2,1)}, bf16[8,64,768]{2,1,0:T(8,128)(2,1)S(1)}, u32[]{:S(2)}, u32[]{:S(2)}) collective-permute-start(bf16[8,64,768]{2,1,0:T(8,128)(2,1)} %all-to-all-done.cot_a), channel_id=1, source_target_pairs={{0,2},{2,0},{4,6},{6,4},{8,10},{10,8},{12,14},{14,12},{16,18},{18,... | collective-permute-start | bytes 2359304 | tf_op jit(solution)/shard_map/ppermute | solution.py:89
  121.1 18.0 %collective-permute-start.12 = (bf16[8,400,128]{2,1,0:T(8,128)(2,1)S(1)}, bf16[8,400,128]{2,1,0:T(8,128)(2,1)S(1)}, u32[]{:S(2)}, u32[]{:S(2)}) collective-permute-start(bf16[8,400,128]{2,1,0:T(8,128)(2,1)S(1)} %collective-permute-done.11.h_a), channel_id=1, source_target_pairs={{0,1},{1,0},{2,3},{3,2},{4,5},{5,4},{6,7},{7,6},{8,9},{9,8},{10,11... | collective-permute-start | bytes 2457608 | tf_op jit(solution)/shard_map/ppermute | solution.py:48
  135.7 10.0 %collective-permute-start.10 = (bf16[8,64,768]{2,1,0:T(8,128)(2,1)}, bf16[8,64,768]{2,1,0:T(8,128)(2,1)S(1)}, u32[]{:S(2)}, u32[]{:S(2)}) collective-permute-start(bf16[8,64,768]{2,1,0:T(8,128)(2,1)} %all-to-all-done.cot_a), channel_id=1, source_target_pairs={{0,1},{1,0},{2,3},{3,2},{4,5},{5,4},{6,7},{7,6},{8,9},{9,8},{10,11... | collective-permute-start | bytes 2359304 | tf_op jit(solution)/shard_map/ppermute | solution.py:48
  136.3 9.5 %collective-permute-start.9 = (bf16[8,400,128]{2,1,0:T(8,128)(2,1)S(1)}, bf16[8,400,128]{2,1,0:T(8,128)(2,1)S(1)}, u32[]{:S(2)}, u32[]{:S(2)}) collective-permute-start(bf16[8,400,128]{2,1,0:T(8,128)(2,1)S(1)} %all_to_all.20.h_a), channel_id=1, source_target_pairs={{0,1},{1,0},{2,3},{3,2},{4,5},{5,4},{6,7},{7,6},{8,9},{9,8},{10,11... | collective-permute-start | bytes 2457608 | tf_op jit(solution)/shard_map/ppermute | solution.py:48
  145.6 9.5 %collective-permute-start.19 = (bf16[8,400,128]{2,1,0:T(8,128)(2,1)S(1)}, bf16[8,400,128]{2,1,0:T(8,128)(2,1)S(1)}, u32[]{:S(2)}, u32[]{:S(2)}) collective-permute-start(bf16[8,400,128]{2,1,0:T(8,128)(2,1)S(1)} %get-tuple-element.83), channel_id=1, source_target_pairs={{0,1},{1,0},{2,3},{3,2},{4,5},{5,4},{6,7},{7,6},{8,9},{9,8},{10,11... | collective-permute-start | bytes 2457608 | tf_op jit(solution)/shard_map/ppermute | solution.py:48
  154.7 11.7 %collective-permute-start.18 = (bf16[8,400,128]{2,1,0:T(8,128)(2,1)S(1)}, bf16[8,400,128]{2,1,0:T(8,128)(2,1)S(1)}, u32[]{:S(2)}, u32[]{:S(2)}) collective-permute-start(bf16[8,400,128]{2,1,0:T(8,128)(2,1)S(1)} %get-tuple-element.81), channel_id=1, source_target_pairs={{0,1},{1,0},{2,3},{3,2},{4,5},{5,4},{6,7},{7,6},{8,9},{9,8},{10,11... | collective-permute-start | bytes 2457608 | tf_op jit(solution)/shard_map/ppermute | solution.py:48
  155.3 20.3 %collective-permute-start.20 = (bf16[8,400,128]{2,1,0:T(8,128)(2,1)S(1)}, bf16[8,400,128]{2,1,0:T(8,128)(2,1)S(1)}, u32[]{:S(2)}, u32[]{:S(2)}) collective-permute-start(bf16[8,400,128]{2,1,0:T(8,128)(2,1)S(1)} %add_convert_fusion.1), channel_id=1, source_target_pairs={{0,2},{2,0},{4,6},{6,4},{8,10},{10,8},{12,14},{14,12},{16,18},{18,... | collective-permute-start | bytes 2457608 | tf_op jit(solution)/shard_map/ppermute | solution.py:89
  166.0 34.5 %collective-permute-start.16 = (bf16[8,64,768]{2,1,0:T(8,128)(2,1)}, bf16[8,64,768]{2,1,0:T(8,128)(2,1)}, u32[]{:S(2)}, u32[]{:S(2)}) collective-permute-start(bf16[8,64,768]{2,1,0:T(8,128)(2,1)} %get-tuple-element.79), channel_id=1, source_target_pairs={{0,1},{1,0},{2,3},{3,2},{4,5},{5,4},{6,7},{7,6},{8,9},{9,8},{10,11... | collective-permute-start | bytes 2359304 | tf_op jit(solution)/shard_map/ppermute | solution.py:48
  176.9 46.2 %all-to-all-start.2 = ((bf16[8,400,128]{2,1,0:T(8,128)(2,1)}), bf16[8,400,128]{2,1,0:T(8,128)(2,1)}, u32[]{:S(2)}, u32[]{:S(2)}) async-start(bf16[8,400,128]{2,1,0:T(8,128)(2,1)} %add_convert_fusion), calls=%async_computation.2 | async-start | bytes 1638400 | tf_op jit(solution)/shard_map/all_to_all | solution.py:83
  201.8 20.0 %collective-permute-start.17 = (bf16[8,64,768]{2,1,0:T(8,128)(2,1)S(1)}, bf16[8,64,768]{2,1,0:T(8,128)(2,1)S(1)}, u32[]{:S(2)}, u32[]{:S(2)}) collective-permute-start(bf16[8,64,768]{2,1,0:T(8,128)(2,1)S(1)} %add_convert_fusion.3), channel_id=1, source_target_pairs={{0,2},{2,0},{4,6},{6,4},{8,10},{10,8},{12,14},{14,12},{16,18},{18,... | collective-permute-start | bytes 2359304 | tf_op jit(solution)/shard_map/ppermute | solution.py:89
  247.6 15.7 %collective-permute-start.24 = (bf16[2,2,2,1,48,768]{5,4,3,2,1,0:T(8,128)(2,1)}, bf16[2,2,2,1,48,768]{5,4,3,2,1,0:T(8,128)(2,1)}, u32[]{:S(2)}, u32[]{:S(2)}) collective-permute-start(bf16[2,2,2,1,48,768]{5,4,3,2,1,0:T(8,128)(2,1)} %constant_dynamic-slice_fusion.1), channel_id=1, source_target_pairs={{0,2},{2,0},{4,6},{6,4},{8,10},{10,8},{12,14},{14,12},{16,18},{18,... | collective-permute-start | bytes 1769480 | tf_op jit(solution)/shard_map/ppermute | solution.py:76
  248.9 41.7 %all-to-all-start.3 = ((bf16[8,64,768]{2,1,0:T(8,128)(2,1)}), bf16[8,64,768]{2,1,0:T(8,128)(2,1)S(1)}, u32[]{:S(2)}, u32[]{:S(2)}) async-start(bf16[8,64,768]{2,1,0:T(8,128)(2,1)} %add_convert_fusion.2), calls=%async_computation.3 | async-start | bytes 1572864 | tf_op jit(solution)/shard_map/all_to_all | solution.py:83
  254.8 26.8 %collective-permute-start.22 = (bf16[2,2,1,2,48,896]{5,4,3,2,1,0:T(8,128)(2,1)S(1)}, bf16[2,2,1,2,48,896]{5,4,3,2,1,0:T(8,128)(2,1)S(1)}, u32[]{:S(2)}, u32[]{:S(2)}) collective-permute-start(bf16[2,2,1,2,48,896]{5,4,3,2,1,0:T(8,128)(2,1)S(1)} %constant_dynamic-slice_fusion.2), channel_id=1, source_target_pairs={{0,4},{2,6},{4,0},{6,2},{8,12},{10,14},{12,8},{14,10},{16,20},{18,... | collective-permute-start | bytes 2064392 | tf_op jit(solution)/shard_map/ppermute | solution.py:76
  264.5 22.7 %collective-permute-start.25 = (bf16[2,2,1,1,48,768]{5,4,3,2,1,0:T(8,128)(2,1)S(1)}, bf16[2,2,1,1,48,768]{5,4,3,2,1,0:T(8,128)(2,1)S(1)}, u32[]{:S(2)}, u32[]{:S(2)}) collective-permute-start(bf16[2,2,1,1,48,768]{5,4,3,2,1,0:T(8,128)(2,1)S(1)} %dynamic-slice_convert_fusion.1), channel_id=1, source_target_pairs={{0,4},{2,6},{4,0},{6,2},{8,12},{10,14},{12,8},{14,10},{16,20},{18,... | collective-permute-start | bytes 884744 | tf_op jit(solution)/shard_map/ppermute | solution.py:76
  281.8 8.7 %collective-permute-start.23 = (bf16[2,2,1,1,48,896]{5,4,3,2,1,0:T(8,128)(2,1)S(1)}, bf16[2,2,1,1,48,896]{5,4,3,2,1,0:T(8,128)(2,1)S(1)}, u32[]{:S(2)}, u32[]{:S(2)}) collective-permute-start(bf16[2,2,1,1,48,896]{5,4,3,2,1,0:T(8,128)(2,1)S(1)} %dynamic-slice_convert_fusion), channel_id=1, source_target_pairs={{0,2},{2,0},{4,6},{6,4},{8,10},{10,8},{12,14},{14,12},{16,18},{18,... | collective-permute-start | bytes 1032200 | tf_op jit(solution)/shard_map/ppermute | solution.py:76
  290.6 12.6 %collective-permute-start.30 = (bf16[2,1,1,1,48,896]{5,4,3,2,1,0:T(8,128)(2,1)S(1)}, bf16[2,1,1,1,48,896]{5,4,3,2,1,0:T(8,128)(2,1)S(1)}, u32[]{:S(2)}, u32[]{:S(2)}) collective-permute-start(bf16[2,1,1,1,48,896]{5,4,3,2,1,0:T(8,128)(2,1)S(1)} %dynamic-slice_convert_fusion.3), channel_id=1, source_target_pairs={{0,8},{2,10},{4,12},{6,14},{8,0},{10,2},{12,4},{14,6},{16,24},{18,... | collective-permute-start | bytes 516104 | tf_op jit(solution)/shard_map/ppermute | solution.py:76
  293.2 18.2 %collective-permute-start.26 = (f32[128,768]{1,0:T(8,128)S(1)}, f32[128,768]{1,0:T(8,128)S(1)}, u32[]{:S(2)}, u32[]{:S(2)}) collective-permute-start(f32[128,768]{1,0:T(8,128)S(1)} %constant_dynamic-slice_fusion), channel_id=1, source_target_pairs={{0,1},{1,0},{2,3},{3,2},{4,5},{5,4},{6,7},{7,6},{8,9},{9,8},{10,11... | collective-permute-start | bytes 1179656 | tf_op jit(solution)/shard_map/ppermute | solution.py:48
  297.9 8.5 %collective-permute-start.29 = (bf16[1,1,1,1,48,768]{5,4,3,2,1,0:T(8,128)(2,1)S(1)}, bf16[1,1,1,1,48,768]{5,4,3,2,1,0:T(8,128)(2,1)S(1)}, u32[]{:S(2)}, u32[]{:S(2)}) collective-permute-start(bf16[1,1,1,1,48,768]{5,4,3,2,1,0:T(8,128)(2,1)S(1)} %dynamic-slice_convert_fusion.6), channel_id=1, source_target_pairs={{0,16},{2,18},{4,20},{6,22},{8,24},{10,26},{12,28},{14,30},{16,0},... | collective-permute-start | bytes 221192 | tf_op jit(solution)/shard_map/ppermute | solution.py:76
  (66 other events, 331.3 us)

commit v4 on v3

--- a/solution.py
+++ b/solution.py
@@ -89,12 +89,28 @@
     return lax.ppermute(values, "dp", partners(0))
 
 
+def after(values, *others):
+    return lax.optimization_barrier((values, *others))[0]
+
+
 def add_low(*parts):
     return sum(part.astype(FULL) for part in parts).astype(LOW)
 
 
-def call(kernel, out_shape, *operands, flops=0, smem=(), limit=20):
-    moved = sum(x.size * x.dtype.itemsize for x in (*operands, *out_shape))
+def far(values):
+    return pltpu.with_memory_space_constraint(values, pltpu.HBM)
+
+
+def near_shape(shape, kind):
+    return jax.ShapeDtypeStruct(shape, kind)
+
+
+def far_shape(shape, kind):
+    return pltpu.HBM(shape, kind)
+
+
+def call(kernel, out_shape, *operands, flops=0, smem=(), limit=8):
+    moved = sum(x.size * x.dtype.itemsize for x in operands)
     return pl.pallas_call(
         kernel,
         out_shape=out_shape,
@@ -104,7 +120,7 @@
         ],
         out_specs=[pl.BlockSpec(memory_space=pltpu.VMEM) for _ in out_shape],
         compiler_params=pltpu.CompilerParams(vmem_limit_bytes=limit * MIB),
-        cost_estimate=pl.CostEstimate(flops=flops, bytes_accessed=moved, transcendentals=0),
+        cost_estimate=pl.CostEstimate(flops=flops, bytes_accessed=2 * moved, transcendentals=0),
     )(*operands)
 
 
@@ -117,11 +133,14 @@
 
 
 def attention_kernel(
-    len_ref, rows_ref, qk_ref, vx_ref, attn_ref, h_ref, qkv_ref, probs_ref, mixed_ref, ext_ref
+    len_ref, rows_ref, qk_ref, vx_ref, attn_ref, ext_ref, h_ref, qkv_ref, probs_ref, mixed_ref, rows_out, qk_out, vx_out
 ):
     group_rows = rows_ref.shape[0]
     inner = qk_ref.shape[1] // 2
     rows = rows_ref[...]
+    rows_out[...] = rows
+    qk_out[...] = qk_ref[...]
+    vx_out[...] = vx_ref[...]
     ext = vx_ref[:, 2 * inner :].astype(FULL).T
     ext_ref[...] = ext
     h_one = (rows * inverse_rms(rows) * ext[0:1, :]).astype(LOW)
@@ -216,7 +235,12 @@
     )
 
 
-def expert_step(half, h_ref, cot_ref, first_ref, second_ref, back_ref, hid_ref, pre_ref, out_ref, gate_ref):
+def gated_cot(gate, cot_ref):
+    sources, half, width = cot_ref.shape
+    return (gate * cot_ref[...].reshape(sources * half, width).astype(FULL)).astype(LOW)
+
+
+def expert_step(half, h_ref, cot_ref, first_ref, second_ref, back_ref, hid_ref, pre_ref, gate_ref):
     sources = h_ref.shape[0]
     blocks = (h_ref.shape[1] - EXTRA_ROWS) // half
     count, shift = sources * half, half.bit_length() - 1
@@ -228,8 +252,7 @@
     gate_lanes = dot(two_rows.astype(LOW), extra)
     gate = jnp.sum(jnp.where(on_lane, gate_lanes, 0.0), axis=1, keepdims=True)
     gate_ref[...] = jnp.broadcast_to(gate, (count, LANES))
-    arrived = (gate * cot_ref[...].reshape(count, blocks * LANES).astype(FULL)).astype(LOW)
-    out_ref[...] = arrived
+    arrived = gated_cot(gate, cot_ref)
     incoming = rows_of(h_ref, half)
     pre = dot(incoming, first_ref[...])
     grad_hidden = contract_cols(arrived, second_ref[...])
@@ -269,7 +292,8 @@
 
 
 def whole(array):
-    return pl.BlockSpec(array.shape, lambda i: (0,) * array.ndim, pipeline_mode=pl.Buffered(1))
+    rank = len(array.shape)
+    return pl.BlockSpec(array.shape, lambda i: (0,) * rank, pipeline_mode=pl.Buffered(1))
 
 
 def expert_rows(h_rows, cot_rows, first_weight, second_weight, half):
@@ -286,34 +310,34 @@
             lambda: expert_step(half, h_b, cot_b, first_ref, second_ref, back_b, *kept),
         )
 
-    lanes = ((hidden_width, LOW), (hidden_width, LOW), (width, LOW), (LANES, FULL))
+    lanes = ((hidden_width, LOW), (hidden_width, LOW), (LANES, FULL))
     back_a, back_b, *kept = pl.pallas_call(
         kernel,
         grid=(2 * steps,),
-        out_shape=[jax.ShapeDtypeStruct(h_rows[0].shape, LOW)] * 2
-        + [jax.ShapeDtypeStruct((total, n), kind) for n, kind in lanes],
+        out_shape=[near_shape(h_rows[0].shape, LOW)] * 2
+        + [far_shape((total, n), kind) for n, kind in lanes],
         in_specs=part_specs(sources, steps, [(rows_sent, LANES), (half, width)])
         + [whole(first_weight), whole(second_weight)],
         out_specs=part_specs(sources, steps, [(rows_sent, LANES)])
         + [pl.BlockSpec((count, n), lambda i: (i, 0)) for n, _ in lanes],
-        compiler_params=pltpu.CompilerParams(vmem_limit_bytes=24 * MIB),
+        compiler_params=pltpu.CompilerParams(vmem_limit_bytes=16 * MIB),
         cost_estimate=pl.CostEstimate(
             flops=6 * total * width * hidden_width,
             bytes_accessed=12 * total * width,
             transcendentals=total * hidden_width,
         ),
-    )(*h_rows, *cot_rows, first_weight, second_weight)
+    )(*h_rows, *cot_rows, far(first_weight), far(second_weight))
     return back_a, back_b, kept
 
 
-def expert_weights(h_rows, kept, second_weight, sums, half):
+def expert_weights(h_rows, cot_rows, kept, second_weight, sums, half):
     experts, rows_sent, _ = h_rows[0].shape
     hidden_width, width = second_weight.shape
     sources = min(experts, 256 // half)
     count, steps = sources * half, experts // sources
     total = 2 * experts * half
 
-    def kernel(h_a, h_b, hid_ref, pre_ref, arr_ref, gate_ref, second_ref, *refs):
+    def kernel(h_a, h_b, cot_a, cot_b, hid_ref, pre_ref, gate_ref, second_ref, *refs):
         out_a, out_b, grad_first, grad_second = refs[-4:]
 
         @pl.when(pl.program_id(0) == 0)
@@ -321,32 +345,31 @@
             for at, grad in enumerate((grad_first, grad_second)):
                 grad[...] = refs[at][...] if sums else jnp.zeros(grad.shape, FULL)
 
-        def step(h_ref, out_ref):
-            hidden = hid_ref[...]
+        def step(h_ref, cot_ref, out_ref):
+            hidden, gate = hid_ref[...], gate_ref[:, 0:1]
             produced = dot(hidden, second_ref[...])
-            out_ref[...] = (gate_ref[:, 0:1] * produced).astype(LOW).reshape(out_ref.shape)
+            out_ref[...] = (gate * produced).astype(LOW).reshape(out_ref.shape)
             grad_first[...] += contract_rows(rows_of(h_ref, half), pre_ref[...])
-            grad_second[...] += contract_rows(hidden, arr_ref[...])
-
-        in_halves(steps, lambda: step(h_a, out_a), lambda: step(h_b, out_b))
-
-    shape = jax.ShapeDtypeStruct
-    grads = [shape((width, hidden_width), FULL), shape((hidden_width, width), FULL)]
+            grad_second[...] += contract_rows(hidden, gated_cot(gate, cot_ref))
+
+        in_halves(steps, lambda: step(h_a, cot_a, out_a), lambda: step(h_b, cot_b, out_b))
+
+    grads = [far_shape((width, hidden_width), FULL), far_shape((hidden_width, width), FULL)]
     return pl.pallas_call(
         kernel,
         grid=(2 * steps,),
-        out_shape=[shape((experts, half, width), LOW)] * 2 + grads,
-        in_specs=part_specs(sources, steps, [(rows_sent, LANES)])
+        out_shape=[near_shape((experts, half, width), LOW)] * 2 + grads,
+        in_specs=part_specs(sources, steps, [(rows_sent, LANES), (half, width)])
         + [pl.BlockSpec((count, x.shape[1]), lambda i: (i, 0)) for x in kept]
         + [whole(x) for x in (second_weight, *sums)],
         out_specs=part_specs(sources, steps, [(half, width)]) + [whole(x) for x in grads],
-        compiler_params=pltpu.CompilerParams(vmem_limit_bytes=32 * MIB),
+        compiler_params=pltpu.CompilerParams(vmem_limit_bytes=24 * MIB),
         cost_estimate=pl.CostEstimate(
             flops=6 * total * width * hidden_width,
             bytes_accessed=10 * total * width,
             transcendentals=0,
         ),
-    )(*h_rows, *kept, second_weight, *sums)
+    )(*h_rows, *cot_rows, *map(far, (*kept, second_weight, *sums)))
 
 
 def combine_kernel(base_ref, back_ref, slot_ref, col_ref, gates_ref, ext_ref, h_ref, part_ref, router_ref):
@@ -487,6 +510,8 @@
     cot_picked = dot(dispatch, cotangent.astype(LOW)).astype(LOW).reshape(experts, half, width)
 
     extra_width = -(-(2 + experts) // LANES) * LANES
+    qk_full = jnp.concatenate([w_query, w_key], axis=1)
+    router, gain_attn, gain_moe = lax.optimization_barrier((router, gain_attn, gain_moe, qk_full))[:3]
     extra = jnp.concatenate(
         [
             gain_attn[:, None],
@@ -496,7 +521,6 @@
         ],
         axis=1,
     )
-    qk_full = jnp.concatenate([w_query, w_key], axis=1)
     vx_full = jnp.concatenate([w_value, w_out_proj.T, extra], axis=1)
     qk_full = qk_full.reshape((1,) * bits + qk_full.shape)
     vx_full = vx_full.reshape((1,) * bits + vx_full.shape)
@@ -504,37 +528,39 @@
         vx_full = double(vx_full, order_b[step], bits)
         qk_full = double(qk_full, order_a[step], bits)
         if step == bits - 2:
-            cot_picked, qk_full, vx_full = lax.optimization_barrier((cot_picked, qk_full, vx_full))
+            rows_all = lax.all_gather(after(block_in, vx_full), "tensor", axis=0, tiled=True)
+    cot_own = trade(after(cot_picked, rows_all))
     qk_full = qk_full.reshape(width, 2 * inner)
     vx_full = vx_full.reshape(width, 2 * inner + extra_width)
-    cot_own = trade(cot_picked)
-
-    rows_all = lax.all_gather(block_in, "tensor", axis=0, tiled=True)
-    shape = jax.ShapeDtypeStruct
-    attn_part, h_one, qkv, probs, mixed, ext = call(
+
+    attn_part, ext, h_one, qkv, probs, mixed, rows_far, qk_far, vx_far = call(
         attention_kernel,
         [
-            shape((group_rows, width), FULL),
-            shape((group_rows, width), LOW),
-            shape((group_rows, 3 * inner), LOW),
-            shape((inner // HEAD_DIM, group_rows, group_rows), FULL),
-            shape((group_rows, inner), LOW),
-            shape((extra_width, width), FULL),
+            near_shape((group_rows, width), FULL),
+            near_shape((extra_width, width), FULL),
+            far_shape((group_rows, width), LOW),
+            far_shape((group_rows, 3 * inner), LOW),
+            far_shape((inner // HEAD_DIM, group_rows, group_rows), FULL),
+            far_shape((group_rows, inner), LOW),
+            far_shape(rows_all.shape, FULL),
+            far_shape(qk_full.shape, LOW),
+            far_shape(vx_full.shape, LOW),
         ],
         seq_lengths,
         rows_all,
         qk_full,
         vx_full,
+        limit=14,
         flops=8 * group_rows * width * inner + 4 * group_rows * group_rows * inner,
         smem=(0,),
     )
     residual, h_two, gates, sent = call(
         dispatch_kernel,
         [
-            shape((group_rows, width), FULL),
-            shape((group_rows, width), LOW),
-            shape((experts, group_rows), FULL),
-            shape((experts, rows_sent, LANES), LOW),
+            far_shape((group_rows, width), FULL),
+            far_shape((group_rows, width), LOW),
+            near_shape((experts, group_rows), FULL),
+            near_shape((experts, rows_sent, LANES), LOW),
         ],
         base,
         rows_all,
@@ -546,40 +572,39 @@
         smem=(0,),
     )
 
-    sent, cot_own = lax.optimization_barrier((sent, cot_own))
     cot_crossed = cross(cot_own)
     cot_own = (cot_own, swap(cot_own))
     cot_far = (cot_crossed, swap(cot_crossed))
     h_own = trade(sent)
-    h_crossed = cross(h_own)
-    h_own = (h_own, swap(h_own))
-    h_far = (h_crossed, swap(h_crossed))
+    h_crossed = cross(after(h_own, cot_crossed))
+    h_own = (after(h_own, cot_far[1]), swap(h_own))
     first_weight = expert_in[0]
     second_weight = expert_out[0]
     own_back, own_given, own_kept = expert_rows(h_own, cot_own, first_weight, second_weight, half)
+    h_crossed = after(h_crossed, own_back)
+    h_far = (h_crossed, swap(h_crossed))
     far_back, far_given, far_kept = expert_rows(h_far, cot_far, first_weight, second_weight, half)
-    far_total = cross(add_low(far_back, swap(far_given)))
+    far_sum = add_low(far_back, swap(far_given))
+    far_total = cross(far_sum)
     back = trade(add_low(own_back, swap(own_given), far_total))
 
-    far_out, far_given, *sums = expert_weights(h_far, far_kept, second_weight, (), half)
+    far_kept[0] = after(far_kept[0], far_sum)
+    far_out, far_given, *sums = expert_weights(h_far, cot_far, far_kept, second_weight, (), half)
     own_out, own_given, grad_first, grad_second = expert_weights(
-        h_own, own_kept, second_weight, sums, half
-    )
-    far_total = cross(add_low(far_out, swap(far_given)))
+        h_own, cot_own, own_kept, second_weight, sums, half
+    )
+    far_total = cross(after(add_low(far_out, swap(far_given)), far_total))
     out_rows = add_low(own_out, swap(own_given), far_total)
-    out_rows, back = lax.optimization_barrier((out_rows, back))
-    back_out = trade(out_rows).reshape(slots, width)
-
     h_part, router_part = call(
         combine_kernel,
-        [shape((group_rows, width), FULL), shape((experts, width), FULL)],
+        [near_shape((group_rows, width), FULL), near_shape((experts, width), FULL)],
         base,
-        back,
+        after(back, own_out),
         slot_row,
         slot_col,
         gates,
         ext,
-        h_two,
+        far(h_two),
         flops=2 * slots * group_rows * width,
         smem=(0,),
     )
@@ -587,26 +612,20 @@
     qk_part, vx_part, one_part, resid_grad, _, _ = call(
         backward_kernel,
         [
-            shape((width, 2 * inner), LOW),
-            shape((width, 2 * inner + extra_width), LOW),
-            shape((group_rows, width), FULL),
-            shape((group_rows, width), FULL),
-            shape((group_rows, 2 * inner), LOW),
-            shape((group_rows, inner), LOW),
+            near_shape((width, 2 * inner), LOW),
+            near_shape((width, 2 * inner + extra_width), LOW),
+            near_shape((group_rows, width), FULL),
+            near_shape((group_rows, width), FULL),
+            near_shape((group_rows, 2 * inner), LOW),
+            near_shape((group_rows, inner), LOW),
         ],
         h_part,
         swap(h_part),
-        cotangent,
-        residual,
-        rows_all,
+        *map(far, (cotangent, residual, rows_far)),
         ext,
-        qk_full,
-        vx_full,
-        h_one,
-        qkv,
-        probs,
-        mixed,
+        *map(far, (qk_far, vx_far, h_one, qkv, probs, mixed)),
         router_part,
+        limit=14,
         flops=20 * group_rows * width * inner + 12 * group_rows * group_rows * inner,
     )
 
@@ -622,8 +641,8 @@
     for step in range(bits):
         vx_sum = halve(vx_sum, order_b[bits - 1 - step], bits)
         qk_sum = halve(qk_sum, order_a[bits - 1 - step], bits)
-        if step == 1:
-            vx_sum, qk_sum, back_out = lax.optimization_barrier((vx_sum, qk_sum, back_out))
+        if step == 0:
+            back_out = trade(after(out_rows, qk_sum)).reshape(slots, width)
     qk_sum = qk_sum.reshape(width // dp_count, 2 * inner)
     vx_sum = vx_sum.reshape(width // dp_count, 2 * inner + extra_width)
 

time: 314 us -> 270 us (0.86)
  local copies, waits for them, and re-layouts: 48.9 us -> 16.8 us
  blocking collectives: 34.3 us -> 2.36 us
  Pallas kernels: 38.4 us -> 53 us
  starting transfers between devices: 47.9 us -> 53.3 us
  waiting for transfers between devices: 128 us -> 124 us
  other arithmetic: 11.6 us -> 15.2 us
    unnamed x111 -> x48, local copies, waits for them, and re-layouts: 41.1 us -> 8.93 us
    all_to_all x1 -> x0, blocking collectives: 31.9 us -> none  [trade(): lax.all_to_all(values, 'dp', split_axis=0, concat_axis=0, tiled=True, axi...]
    all_to_all x3 -> x4, waiting for transfers between devices: 0.01 us -> 26 us  [trade(): lax.all_to_all(values, 'dp', split_axis=0, concat_axis=0, tiled=True, axi...]
    ppermute x4, waiting for transfers between devices: 62.1 us -> 36.2 us  [cross(): return lax.ppermute(values, 'dp', partners(0))]
    pallas_call x4, Pallas kernels: 24.3 us -> 35.5 us  [the longest x2 19.6 us: expert_weights(): pl.pallas_call(kernel, grid=(2 * steps,), out_shape=[near_shape((experts,...]
    ppermute x8, waiting for transfers between devices: 36.9 us -> 32.7 us  [halve(): lax.ppermute(given, 'dp', partners(bit)).astype(FULL)]
    pallas_call x4, Pallas kernels: 14.2 us -> 17.5 us  [call(): pl.pallas_call(kernel, out_shape=out_shape, in_specs=[pl.BlockSpec(memory...]
    all_to_all x3 -> x4, starting transfers between devices: 17.1 us -> 19.5 us  [trade(): lax.all_to_all(values, 'dp', split_axis=0, concat_axis=0, tiled=True, axi...]
  transfers between devices with their start and end apart: 36 -> 37, of which waited for: 23 -> 23; matrix products, arithmetic and copies ran while one was open for 6% -> 8% of each run, Pallas kernels for 9% -> 17%
where the time goes in v4:
time: 270 us; the launch traced here: 269 us
  waiting for transfers between devices  124 us (46%)
  starting transfers between devices  53.3 us (20%)
  Pallas kernels  53 us (20%)
  local copies, waits for them, and re-layouts  16.8 us (6%)
  other arithmetic  15.2 us (6%)
  matrix products  3.15 us (1%)
    ppermute x4, waiting for transfers between devices, cross(): return lax.ppermute(values, 'dp', partners(0))  36.2 us
    ppermute x8, waiting for transfers between devices, halve(): lax.ppermute(given, 'dp', partners(bit)).astype(FULL)  32.7 us
    all_to_all x4, waiting for transfers between devices, trade(): lax.all_to_all(values, 'dp', split_axis=0, concat_axis=0, tiled=True, axi...  26 us
    ppermute x8, waiting for transfers between devices, double(): other = lax.ppermute(block, 'dp', partners(bit))  19.9 us
    pallas_call x2, Pallas kernels, expert_weights(): pl.pallas_call(kernel, grid=(2 * steps,), out_shape=[near_shape((experts,...  19.6 us
    all_to_all x4, starting transfers between devices, trade(): lax.all_to_all(values, 'dp', split_axis=0, concat_axis=0, tiled=True, axi...  19.5 us
    pallas_call x4, Pallas kernels, call(): pl.pallas_call(kernel, out_shape=out_shape, in_specs=[pl.BlockSpec(memory...  17.5 us
    pallas_call x2, Pallas kernels, expert_rows(): pl.pallas_call(kernel, grid=(2 * steps,), out_shape=[near_shape(h_rows[0]...  15.9 us
  transfers between devices with their start and end apart: 37, of which 23 were waited for; matrix products, arithmetic and copies ran while one was open for 8% of the time, Pallas kernels for 17%

profile of v4, /device:TPU:0, one launch (start us, length us, event | category | flops | bytes accessed | tf_op | source)
XLA Modules:
  0.0 268.6 jit_solution(13420585747610613696)
XLA Ops:
  5.4 4.1 %collective-permute-start = (bf16[1,1,1,1,48,896]{5,4,0,1,3,2:T(8,128)(2,1)S(1)}, bf16[1,1,1,1,48,896]{5,4,0,1,3,2:T(8,128)(2,1)S(1)}, u32[]{:S(2)}, u32[]{:S(2)}) collective-permute-start(bf16[1,1,1,1,48,896]{5,4,0,1,3,2:T(8,128)(2,1)S(1)} %bitcast.53), channel_id=1, source_target_pairs={{0,16},{2,18},{4,20},{6,22},{8,24},{10,26},{12,28},{14,30},{16,0},... | collective-permute-start | bytes 258056 | tf_op jit(solution)/shard_map/ppermute | solution.py:62
  10.7 6.3 %collective-permute-done.3 = bf16[1,1,1,1,48,768]{5,4,0,1,3,2:T(8,128)(2,1)S(1)} collective-permute-done((bf16[1,1,1,1,48,768]{5,4,0,1,3,2:T(8,128)(2,1)S(1)}, bf16[1,1,1,1,48,768]{5,4,0,1,3,2:T(8,128)(2,1)S(1)}, u32[]{:S(2)}, u32[]{:S(2)}) %collective-permute-start.3) | collective-permute-done | bytes 73760 | tf_op jit(solution)/shard_map/ppermute | solution.py:62
  19.3 4.6 %collective-permute-done.4 = bf16[2,1,1,1,48,768]{5,4,0,1,3,2:T(8,128)(2,1)S(1)} collective-permute-done((bf16[2,1,1,1,48,768]{5,4,0,1,3,2:T(8,128)(2,1)S(1)}, bf16[2,1,1,1,48,768]{5,4,0,1,3,2:T(8,128)(2,1)S(1)}, u32[]{:S(2)}, u32[]{:S(2)}) %collective-permute-start.4) | collective-permute-done | bytes 147488 | tf_op jit(solution)/shard_map/ppermute | solution.py:62
  32.5 4.8 %collective-permute-done.2 = bf16[2,2,1,1,48,896]{5,4,0,1,3,2:T(8,128)(2,1)S(1)} collective-permute-done((bf16[2,2,1,1,48,896]{5,4,0,1,3,2:T(8,128)(2,1)S(1)}, bf16[2,2,1,1,48,896]{5,4,0,1,3,2:T(8,128)(2,1)S(1)}, u32[]{:S(2)}, u32[]{:S(2)}) %collective-permute-start.2) | collective-permute-done | bytes 344096 | tf_op jit(solution)/shard_map/ppermute | solution.py:62
  42.6 5.3 %all-to-all-start.1 = ((bf16[8,64,768]{2,1,0:T(8,128)(2,1)}), bf16[8,64,768]{2,1,0:T(8,128)(2,1)S(1)}, u32[]{:S(2)}, u32[]{:S(2)}) async-start(bf16[8,64,768]{2,1,0:T(8,128)(2,1)} %bitcast.22), calls=%async_computation.1 | async-start | bytes 1572864 | tf_op jit(solution)/shard_map/all_to_all | solution.py:83
  52.7 5.0 %shard_map.212 = (f32[256,768]{1,0:T(8,128)S(1)}, f32[128,768]{1,0:T(8,128)S(1)}, bf16[256,768]{1,0:T(8,128)(2,1)}, bf16[256,1152]{1,0:T(8,128)(2,1)}, f32[6,256...) custom-call(s32[1,4]{1,0:T(1,128)S(1)} %copy-done.7, ...), custom_call_target="tpu_custom_call" | custom-call | flops 704643072 | bytes 6684704 | tf_op jit(solution)/shard_map/pallas_call | solution.py:114
  62.0 6.3 %all-to-all-done.1.cot_a = bf16[8,64,768]{2,1,0:T(8,128)(2,1)S(1)} async-done(((bf16[8,64,768]{2,1,0:T(8,128)(2,1)}), bf16[8,64,768]{2,1,0:T(8,128)(2,1)S(1)}, u32[]{:S(2)}, u32[]{:S(2)}) %all-to-all-start.1) | async-done | bytes 786464 | tf_op jit(solution)/shard_map/all_to_all | solution.py:83
  68.4 6.0 %all-to-all-start = ((bf16[8,400,128]{2,1,0:T(8,128)(2,1)}), bf16[8,400,128]{2,1,0:T(8,128)(2,1)S(1)}, u32[]{:S(2)}, u32[]{:S(2)}) async-start(bf16[8,400,128]{2,1,0:T(8,128)(2,1)} %get-tuple-element.67), calls=%async_computation | async-start | bytes 1638400 | tf_op jit(solution)/shard_map/all_to_all | solution.py:83
  75.9 19.7 %all-to-all-done.h_a = bf16[8,400,128]{2,1,0:T(8,128)(2,1)S(1)} async-done(((bf16[8,400,128]{2,1,0:T(8,128)(2,1)}), bf16[8,400,128]{2,1,0:T(8,128)(2,1)S(1)}, u32[]{:S(2)}, u32[]{:S(2)}) %all-to-all-start) | async-done | bytes 819232 | tf_op jit(solution)/shard_map/all_to_all | solution.py:83
  101.9 7.9 %shard_map.214 = (bf16[8,400,128]{2,1,0:T(8,128)(2,1)S(1)}, bf16[8,400,128]{2,1,0:T(8,128)(2,1)S(1)}, bf16[1024,768]{1,0:T(8,128)(2,1)}, bf16[1024,768]{1,0:T(8,128)(2,1)}, f32[1024,128]{1,0:T(8,128)}) custom-call(bf16[8,400,128]{2,1,0:T(8,128)(2,1)S(1)} %all-to-all-done.h_a, bf16[8,400,128]{2,1,0:T(8,128)(2,1)S(1)} %collective-permute-done.11.h_b, ...), custom_call_target="tpu_custom_call" | custom-call | flops 3623878656 | bytes 9437184 | tf_op jit(solution)/shard_map/pallas_call | solution.py:314
  109.8 7.0 %collective-permute-done.13.h_a = bf16[8,400,128]{2,1,0:T(8,128)(2,1)S(1)} collective-permute-done((bf16[8,400,128]{2,1,0:T(8,128)(2,1)S(1)}, bf16[8,400,128]{2,1,0:T(8,128)(2,1)S(1)}, u32[]{:S(2)}, u32[]{:S(2)}) %collective-permute-start.13) | collective-permute-done | bytes 819232 | tf_op jit(solution)/shard_map/ppermute | solution.py:89
  119.1 8.0 %shard_map.215 = (bf16[8,400,128]{2,1,0:T(8,128)(2,1)S(1)}, bf16[8,400,128]{2,1,0:T(8,128)(2,1)S(1)}, bf16[1024,768]{1,0:T(8,128)(2,1)}, bf16[1024,768]{1,0:T(8,128)(2,1)}, f32[1024,128]{1,0:T(8,128)}) custom-call(bf16[8,400,128]{2,1,0:T(8,128)(2,1)S(1)} %collective-permute-done.13.h_a, bf16[8,400,128]{2,1,0:T(8,128)(2,1)S(1)} %collective-permute-done.14.h_b, ...), custom_call_target="tpu_custom_call" | custom-call | flops 3623878656 | bytes 9437184 | tf_op jit(solution)/shard_map/pallas_call | solution.py:314
  131.3 18.8 %collective-permute-done.18 = bf16[8,400,128]{2,1,0:T(8,128)(2,1)S(1)} collective-permute-done((bf16[8,400,128]{2,1,0:T(8,128)(2,1)S(1)}, bf16[8,400,128]{2,1,0:T(8,128)(2,1)S(1)}, u32[]{:S(2)}, u32[]{:S(2)}) %collective-permute-start.18) | collective-permute-done | bytes 819232 | tf_op jit(solution)/shard_map/ppermute | solution.py:89
  151.4 3.6 %all-to-all-start.2 = ((bf16[8,400,128]{2,1,0:T(8,128)(2,1)}), bf16[8,400,128]{2,1,0:T(8,128)(2,1)S(1)}, u32[]{:S(2)}, u32[]{:S(2)}) async-start(bf16[8,400,128]{2,1,0:T(8,128)(2,1)} %add_convert_fusion), calls=%async_computation.2 | async-start | bytes 1638400 | tf_op jit(solution)/shard_map/all_to_all | solution.py:83
  158.4 9.1 %shard_map.216 = (bf16[8,64,768]{2,1,0:T(8,128)(2,1)S(1)}, bf16[8,64,768]{2,1,0:T(8,128)(2,1)}, f32[768,768]{1,0:T(8,128)}, f32[768,768]{1,0:T(8,128)}) custom-call(bf16[8,400,128]{2,1,0:T(8,128)(2,1)S(1)} %copy-done.11, bf16[8,400,128]{2,1,0:T(8,128)(2,1)S(1)} %copy-done.13, bf16[8,64,768]{2,1,0:T(8,128)(2,1)S(1)} %collective-permute-done.9.cot_a, ...), custom_call_target="tpu_custom_call" | custom-call | flops 3623878656 | bytes 7864320 | tf_op jit(solution)/shard_map/pallas_call | solution.py:358
  168.4 10.5 %shard_map.217 = (bf16[8,64,768]{2,1,0:T(8,128)(2,1)S(1)}, bf16[8,64,768]{2,1,0:T(8,128)(2,1)}, f32[768,768]{1,0:T(8,128)}, f32[768,768]{1,0:T(8,128)}) custom-call(bf16[8,400,128]{2,1,0:T(8,128)(2,1)S(1)} %all-to-all-done.h_a, bf16[8,400,128]{2,1,0:T(8,128)(2,1)S(1)} %copy-done.9, bf16[8,64,768]{2,1,0:T(8,128)(2,1)S(1)} %copy-done.2, ...), custom_call_target="tpu_custom_call" | custom-call | flops 3623878656 | bytes 7864320 | tf_op jit(solution)/shard_map/pallas_call | solution.py:358
  187.1 7.8 %shard_map.219 = (bf16[768,768]{1,0:T(8,128)(2,1)S(1)}, bf16[768,896]{1,0:T(8,128)(2,1)S(1)}, f32[256,768]{1,0:T(8,128)S(1)}, f32[256,768]{1,0:T(8,128)S(1)}, bf...) custom-call(f32[256,768]{1,0:T(8,128)S(1)} %get-tuple-element.93.part_ref, ...), custom_call_target="tpu_custom_call" | custom-call | flops 1811939328 | bytes 20054016 | tf_op jit(solution)/shard_map/pallas_call | solution.py:114
  195.7 10.4 %collective-permute-done.19 = bf16[8,64,768]{2,1,0:T(8,128)(2,1)} collective-permute-done((bf16[8,64,768]{2,1,0:T(8,128)(2,1)}, bf16[8,64,768]{2,1,0:T(8,128)(2,1)}, u32[]{:S(2)}, u32[]{:S(2)}) %collective-permute-start.19) | collective-permute-done | bytes 786464 | tf_op jit(solution)/shard_map/ppermute | solution.py:89
  211.8 6.4 %collective-permute-done.22 = bf16[2,2,2,1,48,768]{5,4,3,2,1,0:T(8,128)(2,1)S(1)} collective-permute-done((bf16[2,2,2,1,48,768]{5,4,3,2,1,0:T(8,128)(2,1)S(1)}, bf16[2,2,2,1,48,768]{5,4,3,2,1,0:T(8,128)(2,1)S(1)}, u32[]{:S(2)}, u32[]{:S(2)}) %collective-permute-start.22) | collective-permute-done | bytes 589856 | tf_op jit(solution)/shard_map/ppermute | solution.py:76
  221.3 4.6 %all-to-all-start.3 = ((bf16[8,64,768]{2,1,0:T(8,128)(2,1)}), bf16[8,64,768]{2,1,0:T(8,128)(2,1)}, u32[]{:S(2)}, u32[]{:S(2)}) async-start(bf16[8,64,768]{2,1,0:T(8,128)(2,1)} %add_convert_fusion.2), calls=%async_computation.3 | async-start | bytes 1572864 | tf_op jit(solution)/shard_map/all_to_all | solution.py:83
  225.9 13.1 %collective-permute-done.25 = bf16[2,2,1,1,48,768]{5,4,3,2,1,0:T(8,128)(2,1)} collective-permute-done((bf16[2,2,1,1,48,768]{5,4,3,2,1,0:T(8,128)(2,1)S(1)}, bf16[2,2,1,1,48,768]{5,4,3,2,1,0:T(8,128)(2,1)}, u32[]{:S(2)}, u32[]{:S(2)}) %collective-permute-start.25) | collective-permute-done | bytes 294944 | tf_op jit(solution)/shard_map/ppermute | solution.py:76
  244.2 3.9 %collective-permute-done.26 = bf16[2,1,1,1,48,768]{5,4,3,2,1,0:T(8,128)(2,1)S(1)} collective-permute-done((bf16[2,1,1,1,48,768]{5,4,3,2,1,0:T(8,128)(2,1)S(1)}, bf16[2,1,1,1,48,768]{5,4,3,2,1,0:T(8,128)(2,1)S(1)}, u32[]{:S(2)}, u32[]{:S(2)}) %collective-permute-start.26) | collective-permute-done | bytes 147488 | tf_op jit(solution)/shard_map/ppermute | solution.py:76
  253.5 3.0 %collective-permute-done.30 = bf16[2,1,1,1,48,896]{5,4,3,2,1,0:T(8,128)(2,1)S(1)} collective-permute-done((bf16[2,1,1,1,48,896]{5,4,3,2,1,0:T(8,128)(2,1)S(1)}, bf16[2,1,1,1,48,896]{5,4,3,2,1,0:T(8,128)(2,1)S(1)}, u32[]{:S(2)}, u32[]{:S(2)}) %collective-permute-start.30) | collective-permute-done | bytes 172064 | tf_op jit(solution)/shard_map/ppermute | solution.py:76
  256.6 3.4 %collective-permute-start.31 = (bf16[1,1,1,1,48,896]{5,4,3,2,1,0:T(8,128)(2,1)S(1)}, bf16[1,1,1,1,48,896]{5,4,3,2,1,0:T(8,128)(2,1)S(1)}, u32[]{:S(2)}, u32[]{:S(2)}) collective-permute-start(bf16[1,1,1,1,48,896]{5,4,3,2,1,0:T(8,128)(2,1)S(1)} %dynamic-slice_convert_fusion.5), channel_id=1, source_target_pairs={{0,16},{2,18},{4,20},{6,22},{8,24},{10,26},{12,28},{14,30},{16,0},... | collective-permute-start | bytes 258056 | tf_op jit(solution)/shard_map/ppermute | solution.py:76
  (173 shorter events, 88.1 us)
Async XLA Ops:
  5.4 12.5 %collective-permute-start = (bf16[1,1,1,1,48,896]{5,4,0,1,3,2:T(8,128)(2,1)S(1)}, bf16[1,1,1,1,48,896]{5,4,0,1,3,2:T(8,128)(2,1)S(1)}, u32[]{:S(2)}, u32[]{:S(2)}) collective-permute-start(bf16[1,1,1,1,48,896]{5,4,0,1,3,2:T(8,128)(2,1)S(1)} %bitcast.53), channel_id=1, source_target_pairs={{0,16},{2,18},{4,20},{6,22},{8,24},{10,26},{12,28},{14,30},{16,0},... | collective-permute-start | bytes 258056 | tf_op jit(solution)/shard_map/ppermute | solution.py:62
  9.5 7.5 %collective-permute-start.3 = (bf16[1,1,1,1,48,768]{5,4,0,1,3,2:T(8,128)(2,1)S(1)}, bf16[1,1,1,1,48,768]{5,4,0,1,3,2:T(8,128)(2,1)S(1)}, u32[]{:S(2)}, u32[]{:S(2)}) collective-permute-start(bf16[1,1,1,1,48,768]{5,4,0,1,3,2:T(8,128)(2,1)S(1)} %bitcast.58), channel_id=1, source_target_pairs={{0,16},{2,18},{4,20},{6,22},{8,24},{10,26},{12,28},{14,30},{16,0},... | collective-permute-start | bytes 221192 | tf_op jit(solution)/shard_map/ppermute | solution.py:62
  17.0 6.8 %collective-permute-start.4 = (bf16[2,1,1,1,48,768]{5,4,0,1,3,2:T(8,128)(2,1)S(1)}, bf16[2,1,1,1,48,768]{5,4,0,1,3,2:T(8,128)(2,1)S(1)}, u32[]{:S(2)}, u32[]{:S(2)}) collective-permute-start(bf16[2,1,1,1,48,768]{5,4,0,1,3,2:T(8,128)(2,1)S(1)} %maximum_select_fusion.10), channel_id=1, source_target_pairs={{0,8},{2,10},{4,12},{6,14},{8,0},{10,2},{12,4},{14,6},{16,24},{18,... | collective-permute-start | bytes 442376 | tf_op jit(solution)/shard_map/ppermute | solution.py:62
  17.9 8.3 %collective-permute-start.1 = (bf16[2,1,1,1,48,896]{5,4,0,1,3,2:T(8,128)(2,1)S(1)}, bf16[2,1,1,1,48,896]{5,4,0,1,3,2:T(8,128)(2,1)S(1)}, u32[]{:S(2)}, u32[]{:S(2)}) collective-permute-start(bf16[2,1,1,1,48,896]{5,4,0,1,3,2:T(8,128)(2,1)S(1)} %maximum_select_fusion.8), channel_id=1, source_target_pairs={{0,8},{2,10},{4,12},{6,14},{8,0},{10,2},{12,4},{14,6},{16,24},{18,... | collective-permute-start | bytes 516104 | tf_op jit(solution)/shard_map/ppermute | solution.py:62
  23.9 6.8 %collective-permute-start.5 = (bf16[2,2,1,1,48,768]{5,4,0,1,3,2:T(8,128)(2,1)S(1)}, bf16[2,2,1,1,48,768]{5,4,0,1,3,2:T(8,128)(2,1)S(1)}, u32[]{:S(2)}, u32[]{:S(2)}) collective-permute-start(bf16[2,2,1,1,48,768]{5,4,0,1,3,2:T(8,128)(2,1)S(1)} %maximum_select_fusion.6), channel_id=1, source_target_pairs={{0,4},{2,6},{4,0},{6,2},{8,12},{10,14},{12,8},{14,10},{16,20},{18,... | collective-permute-start | bytes 884744 | tf_op jit(solution)/shard_map/ppermute | solution.py:62
  26.2 11.1 %collective-permute-start.2 = (bf16[2,2,1,1,48,896]{5,4,0,1,3,2:T(8,128)(2,1)S(1)}, bf16[2,2,1,1,48,896]{5,4,0,1,3,2:T(8,128)(2,1)S(1)}, u32[]{:S(2)}, u32[]{:S(2)}) collective-permute-start(bf16[2,2,1,1,48,896]{5,4,0,1,3,2:T(8,128)(2,1)S(1)} %maximum_select_fusion.4), channel_id=1, source_target_pairs={{0,2},{2,0},{4,6},{6,4},{8,10},{10,8},{12,14},{14,12},{16,18},{18,... | collective-permute-start | bytes 1032200 | tf_op jit(solution)/shard_map/ppermute | solution.py:62
  30.8 17.1 %collective-permute-start.6 = (bf16[2,2,2,1,48,768]{5,4,0,1,3,2:T(8,128)(2,1)S(1)}, bf16[2,2,2,1,48,768]{5,4,0,1,3,2:T(8,128)(2,1)}, u32[]{:S(2)}, u32[]{:S(2)}) collective-permute-start(bf16[2,2,2,1,48,768]{5,4,0,1,3,2:T(8,128)(2,1)S(1)} %maximum_select_fusion.3), channel_id=1, source_target_pairs={{0,2},{2,0},{4,6},{6,4},{8,10},{10,8},{12,14},{14,12},{16,18},{18,... | collective-permute-start | bytes 1769480 | tf_op jit(solution)/shard_map/ppermute | solution.py:62
  37.4 13.0 %collective-permute-start.7 = (bf16[2,2,1,2,48,896]{5,4,0,1,3,2:T(8,128)(2,1)S(1)}, bf16[2,2,1,2,48,896]{5,4,0,1,3,2:T(8,128)(2,1)}, u32[]{:S(2)}, u32[]{:S(2)}) collective-permute-start(bf16[2,2,1,2,48,896]{5,4,0,1,3,2:T(8,128)(2,1)S(1)} %maximum_select_fusion.2), channel_id=1, source_target_pairs={{0,4},{2,6},{4,0},{6,2},{8,12},{10,14},{12,8},{14,10},{16,20},{18,... | collective-permute-start | bytes 2064392 | tf_op jit(solution)/shard_map/ppermute | solution.py:62
  42.6 25.7 %all-to-all-start.1 = ((bf16[8,64,768]{2,1,0:T(8,128)(2,1)}), bf16[8,64,768]{2,1,0:T(8,128)(2,1)S(1)}, u32[]{:S(2)}, u32[]{:S(2)}) async-start(bf16[8,64,768]{2,1,0:T(8,128)(2,1)} %bitcast.22), calls=%async_computation.1 | async-start | bytes 1572864 | tf_op jit(solution)/shard_map/all_to_all | solution.py:83
  68.4 27.2 %all-to-all-start = ((bf16[8,400,128]{2,1,0:T(8,128)(2,1)}), bf16[8,400,128]{2,1,0:T(8,128)(2,1)S(1)}, u32[]{:S(2)}, u32[]{:S(2)}) async-start(bf16[8,400,128]{2,1,0:T(8,128)(2,1)} %get-tuple-element.67), calls=%async_computation | async-start | bytes 1638400 | tf_op jit(solution)/shard_map/all_to_all | solution.py:83
  74.4 21.2 %collective-permute-start.9 = (bf16[8,64,768]{2,1,0:T(8,128)(2,1)S(1)}, bf16[8,64,768]{2,1,0:T(8,128)(2,1)S(1)}, u32[]{:S(2)}, u32[]{:S(2)}) collective-permute-start(bf16[8,64,768]{2,1,0:T(8,128)(2,1)S(1)} %all-to-all-done.1.cot_a), channel_id=1, source_target_pairs={{0,2},{2,0},{4,6},{6,4},{8,10},{10,8},{12,14},{14,12},{16,18},{18,... | collective-permute-start | bytes 2359304 | tf_op jit(solution)/shard_map/ppermute | solution.py:89
  96.1 20.7 %collective-permute-start.13 = (bf16[8,400,128]{2,1,0:T(8,128)(2,1)S(1)}, bf16[8,400,128]{2,1,0:T(8,128)(2,1)S(1)}, u32[]{:S(2)}, u32[]{:S(2)}) collective-permute-start(bf16[8,400,128]{2,1,0:T(8,128)(2,1)S(1)} %all-to-all-done.h_a), channel_id=1, source_target_pairs={{0,2},{2,0},{4,6},{6,4},{8,10},{10,8},{12,14},{14,12},{16,18},{18,... | collective-permute-start | bytes 2457608 | tf_op jit(solution)/shard_map/ppermute | solution.py:89
  129.7 20.4 %collective-permute-start.18 = (bf16[8,400,128]{2,1,0:T(8,128)(2,1)S(1)}, bf16[8,400,128]{2,1,0:T(8,128)(2,1)S(1)}, u32[]{:S(2)}, u32[]{:S(2)}) collective-permute-start(bf16[8,400,128]{2,1,0:T(8,128)(2,1)S(1)} %add_convert_fusion.1), channel_id=1, source_target_pairs={{0,2},{2,0},{4,6},{6,4},{8,10},{10,8},{12,14},{14,12},{16,18},{18,... | collective-permute-start | bytes 2457608 | tf_op jit(solution)/shard_map/ppermute | solution.py:89
  151.4 28.4 %all-to-all-start.2 = ((bf16[8,400,128]{2,1,0:T(8,128)(2,1)}), bf16[8,400,128]{2,1,0:T(8,128)(2,1)S(1)}, u32[]{:S(2)}, u32[]{:S(2)}) async-start(bf16[8,400,128]{2,1,0:T(8,128)(2,1)} %add_convert_fusion), calls=%async_computation.2 | async-start | bytes 1638400 | tf_op jit(solution)/shard_map/all_to_all | solution.py:83
  168.4 14.7 %collective-permute-start.17 = (bf16[8,64,768]{2,1,0:T(8,128)(2,1)}, bf16[8,64,768]{2,1,0:T(8,128)(2,1)}, u32[]{:S(2)}, u32[]{:S(2)}) collective-permute-start(bf16[8,64,768]{2,1,0:T(8,128)(2,1)} %get-tuple-element.87), channel_id=1, source_target_pairs={{0,1},{1,0},{2,3},{3,2},{4,5},{5,4},{6,7},{7,6},{8,9},{9,8},{10,11... | collective-permute-start | bytes 2359304 | tf_op jit(solution)/shard_map/ppermute | solution.py:48
  183.0 12.6 %collective-permute-start.16 = (bf16[8,64,768]{2,1,0:T(8,128)(2,1)}, bf16[8,64,768]{2,1,0:T(8,128)(2,1)}, u32[]{:S(2)}, u32[]{:S(2)}) collective-permute-start(bf16[8,64,768]{2,1,0:T(8,128)(2,1)} %get-tuple-element.85), channel_id=1, source_target_pairs={{0,1},{1,0},{2,3},{3,2},{4,5},{5,4},{6,7},{7,6},{8,9},{9,8},{10,11... | collective-permute-start | bytes 2359304 | tf_op jit(solution)/shard_map/ppermute | solution.py:48
  185.4 20.7 %collective-permute-start.19 = (bf16[8,64,768]{2,1,0:T(8,128)(2,1)}, bf16[8,64,768]{2,1,0:T(8,128)(2,1)}, u32[]{:S(2)}, u32[]{:S(2)}) collective-permute-start(bf16[8,64,768]{2,1,0:T(8,128)(2,1)} %add_convert_fusion.3), channel_id=1, source_target_pairs={{0,2},{2,0},{4,6},{6,4},{8,10},{10,8},{12,14},{14,12},{16,18},{18,... | collective-permute-start | bytes 2359304 | tf_op jit(solution)/shard_map/ppermute | solution.py:89
  194.9 23.2 %collective-permute-start.22 = (bf16[2,2,2,1,48,768]{5,4,3,2,1,0:T(8,128)(2,1)S(1)}, bf16[2,2,2,1,48,768]{5,4,3,2,1,0:T(8,128)(2,1)S(1)}, u32[]{:S(2)}, u32[]{:S(2)}) collective-permute-start(bf16[2,2,2,1,48,768]{5,4,3,2,1,0:T(8,128)(2,1)S(1)} %constant_dynamic-slice_fusion.2), channel_id=1, source_target_pairs={{0,2},{2,0},{4,6},{6,4},{8,10},{10,8},{12,14},{14,12},{16,18},{18,... | collective-permute-start | bytes 1769480 | tf_op jit(solution)/shard_map/ppermute | solution.py:76
  195.6 16.0 %collective-permute-start.24 = (bf16[128,768]{1,0:T(8,128)(2,1)S(1)}, bf16[128,768]{1,0:T(8,128)(2,1)S(1)}, u32[]{:S(2)}, u32[]{:S(2)}) collective-permute-start(bf16[128,768]{1,0:T(8,128)(2,1)S(1)} %dynamic-slice_convert_fusion.2), channel_id=1, source_target_pairs={{0,1},{1,0},{2,3},{3,2},{4,5},{5,4},{6,7},{7,6},{8,9},{9,8},{10,11... | collective-permute-start | bytes 589832 | tf_op jit(solution)/shard_map/ppermute | solution.py:48
  209.6 31.8 %collective-permute-start.28 = (bf16[2,2,1,2,48,896]{5,4,3,2,1,0:T(8,128)(2,1)}, bf16[2,2,1,2,48,896]{5,4,3,2,1,0:T(8,128)(2,1)}, u32[]{:S(2)}, u32[]{:S(2)}) collective-permute-start(bf16[2,2,1,2,48,896]{5,4,3,2,1,0:T(8,128)(2,1)} %constant_dynamic-slice_fusion), channel_id=1, source_target_pairs={{0,4},{2,6},{4,0},{6,2},{8,12},{10,14},{12,8},{14,10},{16,20},{18,... | collective-permute-start | bytes 2064392 | tf_op jit(solution)/shard_map/ppermute | solution.py:76
  218.3 20.7 %collective-permute-start.25 = (bf16[2,2,1,1,48,768]{5,4,3,2,1,0:T(8,128)(2,1)S(1)}, bf16[2,2,1,1,48,768]{5,4,3,2,1,0:T(8,128)(2,1)}, u32[]{:S(2)}, u32[]{:S(2)}) collective-permute-start(bf16[2,2,1,1,48,768]{5,4,3,2,1,0:T(8,128)(2,1)S(1)} %dynamic-slice_convert_fusion.1), channel_id=1, source_target_pairs={{0,4},{2,6},{4,0},{6,2},{8,12},{10,14},{12,8},{14,10},{16,20},{18,... | collective-permute-start | bytes 884744 | tf_op jit(solution)/shard_map/ppermute | solution.py:76
  221.3 42.1 %all-to-all-start.3 = ((bf16[8,64,768]{2,1,0:T(8,128)(2,1)}), bf16[8,64,768]{2,1,0:T(8,128)(2,1)}, u32[]{:S(2)}, u32[]{:S(2)}) async-start(bf16[8,64,768]{2,1,0:T(8,128)(2,1)} %add_convert_fusion.2), calls=%async_computation.3 | async-start | bytes 1572864 | tf_op jit(solution)/shard_map/all_to_all | solution.py:83
  240.1 8.1 %collective-permute-start.26 = (bf16[2,1,1,1,48,768]{5,4,3,2,1,0:T(8,128)(2,1)S(1)}, bf16[2,1,1,1,48,768]{5,4,3,2,1,0:T(8,128)(2,1)S(1)}, u32[]{:S(2)}, u32[]{:S(2)}) collective-permute-start(bf16[2,1,1,1,48,768]{5,4,3,2,1,0:T(8,128)(2,1)S(1)} %dynamic-slice_convert_fusion.4), channel_id=1, source_target_pairs={{0,8},{2,10},{4,12},{6,14},{8,0},{10,2},{12,4},{14,6},{16,24},{18,... | collective-permute-start | bytes 442376 | tf_op jit(solution)/shard_map/ppermute | solution.py:76
  242.7 7.3 %collective-permute-start.29 = (bf16[2,2,1,1,48,896]{5,4,3,2,1,0:T(8,128)(2,1)S(1)}, bf16[2,2,1,1,48,896]{5,4,3,2,1,0:T(8,128)(2,1)S(1)}, u32[]{:S(2)}, u32[]{:S(2)}) collective-permute-start(bf16[2,2,1,1,48,896]{5,4,3,2,1,0:T(8,128)(2,1)S(1)} %dynamic-slice_convert_fusion), channel_id=1, source_target_pairs={{0,2},{2,0},{4,6},{6,4},{8,10},{10,8},{12,14},{14,12},{16,18},{18,... | collective-permute-start | bytes 1032200 | tf_op jit(solution)/shard_map/ppermute | solution.py:76
  (36 other events, 219.2 us)

commit v5 on v4

--- a/solution.py
+++ b/solution.py
@@ -510,8 +510,6 @@
     cot_picked = dot(dispatch, cotangent.astype(LOW)).astype(LOW).reshape(experts, half, width)
 
     extra_width = -(-(2 + experts) // LANES) * LANES
-    qk_full = jnp.concatenate([w_query, w_key], axis=1)
-    router, gain_attn, gain_moe = lax.optimization_barrier((router, gain_attn, gain_moe, qk_full))[:3]
     extra = jnp.concatenate(
         [
             gain_attn[:, None],
@@ -521,10 +519,12 @@
         ],
         axis=1,
     )
-    vx_full = jnp.concatenate([w_value, w_out_proj.T, extra], axis=1)
-    qk_full = qk_full.reshape((1,) * bits + qk_full.shape)
-    vx_full = vx_full.reshape((1,) * bits + vx_full.shape)
-    for step in range(bits):
+    shard = jnp.concatenate([w_query, w_key, w_value, w_out_proj.T, extra], axis=1)
+    lines = [[low + 4 * high for high in range(dp_count // 4)] for low in range(4)]
+    line = lax.all_gather(shard, "dp", axis=0, tiled=True, axis_index_groups=lines)
+    line = line.reshape((2,) * (bits - 2) + (1, 1) + shard.shape)
+    qk_full, vx_full = line[..., : 2 * inner], line[..., 2 * inner :]
+    for step in range(bits - 2, bits):
         vx_full = double(vx_full, order_b[step], bits)
         qk_full = double(qk_full, order_a[step], bits)
         if step == bits - 2:
@@ -586,15 +586,14 @@
     far_back, far_given, far_kept = expert_rows(h_far, cot_far, first_weight, second_weight, half)
     far_sum = add_low(far_back, swap(far_given))
     far_total = cross(far_sum)
-    back = trade(add_low(own_back, swap(own_given), far_total))
-
     far_kept[0] = after(far_kept[0], far_sum)
     far_out, far_given, *sums = expert_weights(h_far, cot_far, far_kept, second_weight, (), half)
-    own_out, own_given, grad_first, grad_second = expert_weights(
+    back = trade(after(add_low(own_back, swap(own_given), far_total), far_out))
+    own_out, out_given, grad_first, grad_second = expert_weights(
         h_own, cot_own, own_kept, second_weight, sums, half
     )
     far_total = cross(after(add_low(far_out, swap(far_given)), far_total))
-    out_rows = add_low(own_out, swap(own_given), far_total)
+    out_given = swap(out_given)
     h_part, router_part = call(
         combine_kernel,
         [near_shape((group_rows, width), FULL), near_shape((experts, width), FULL)],
@@ -642,7 +641,8 @@
         vx_sum = halve(vx_sum, order_b[bits - 1 - step], bits)
         qk_sum = halve(qk_sum, order_a[bits - 1 - step], bits)
         if step == 0:
-            back_out = trade(after(out_rows, qk_sum)).reshape(slots, width)
+            out_rows = add_low(own_out, out_given, after(far_total, qk_sum))
+            back_out = trade(out_rows).reshape(slots, width)
     qk_sum = qk_sum.reshape(width // dp_count, 2 * inner)
     vx_sum = vx_sum.reshape(width // dp_count, 2 * inner + extra_width)
 

time: 270 us -> 251 us (0.930)
  waiting for transfers between devices: 124 us -> 103 us
  blocking collectives: 2.36 us -> 21.8 us
  starting transfers between devices: 53.3 us -> 42.2 us
  local copies, waits for them, and re-layouts: 16.8 us -> 13.5 us
    all_gather x0 -> x1, blocking collectives: none -> 19.4 us  [local(): lax.all_gather(shard, 'dp', axis=0, tiled=True, axis_index_groups=lines)]
    ppermute x4, waiting for transfers between devices: 36.2 us -> 16.8 us  [cross(): return lax.ppermute(values, 'dp', partners(0))]
    ppermute x8 -> x4, waiting for transfers between devices: 19.9 us -> 8.79 us  [double(): other = lax.ppermute(block, 'dp', partners(bit))]
    ppermute x8 -> x4, starting transfers between devices: 12.8 us -> 4.99 us  [double(): other = lax.ppermute(block, 'dp', partners(bit))]
    ppermute x8, waiting for transfers between devices: 32.7 us -> 40.1 us  [halve(): lax.ppermute(given, 'dp', partners(bit)).astype(FULL)]
    all_to_all x4, waiting for transfers between devices: 26 us -> 28.9 us  [trade(): lax.all_to_all(values, 'dp', split_axis=0, concat_axis=0, tiled=True, axi...]
    unnamed x48 -> x40, local copies, waits for them, and re-layouts: 8.93 us -> 7.29 us
  transfers between devices with their start and end apart: 37 -> 33, of which waited for: 23 -> 19; matrix products, arithmetic and copies ran while one was open for 8% -> 7% of each run, Pallas kernels for 17% -> 18%
where the time goes in v5:
time: 251 us; the launch traced here: 250 us
  waiting for transfers between devices  103 us (41%)
  Pallas kernels  51.8 us (21%)
  starting transfers between devices  42.2 us (17%)
  blocking collectives  21.8 us (9%)
  local copies, waits for them, and re-layouts  13.5 us (5%)
  other arithmetic  13.2 us (5%)
  matrix products  3.15 us (1%)
    ppermute x8, waiting for transfers between devices, halve(): lax.ppermute(given, 'dp', partners(bit)).astype(FULL)  40.1 us
    all_to_all x4, waiting for transfers between devices, trade(): lax.all_to_all(values, 'dp', split_axis=0, concat_axis=0, tiled=True, axi...  28.9 us
    all_gather x1, blocking collectives, local(): lax.all_gather(shard, 'dp', axis=0, tiled=True, axis_index_groups=lines)  19.4 us
    pallas_call x2, Pallas kernels, expert_weights(): pl.pallas_call(kernel, grid=(2 * steps,), out_shape=[near_shape((experts,...  19 us
    pallas_call x4, Pallas kernels, call(): pl.pallas_call(kernel, out_shape=out_shape, in_specs=[pl.BlockSpec(memory...  17.4 us
    all_to_all x4, starting transfers between devices, trade(): lax.all_to_all(values, 'dp', split_axis=0, concat_axis=0, tiled=True, axi...  16.9 us
    ppermute x4, waiting for transfers between devices, cross(): return lax.ppermute(values, 'dp', partners(0))  16.8 us
    pallas_call x2, Pallas kernels, expert_rows(): pl.pallas_call(kernel, grid=(2 * steps,), out_shape=[near_shape(h_rows[0]...  15.5 us
  transfers between devices with their start and end apart: 33, of which 19 were waited for; matrix products, arithmetic and copies ran while one was open for 7% of the time, Pallas kernels for 18%

profile of v5, /device:TPU:0, one launch (start us, length us, event | category | flops | bytes accessed | tf_op | source)
XLA Modules:
  0.0 250.1 jit_solution(4729480541535860439)
XLA Ops:
  3.9 19.4 %all_gather.6 = bf16[192,1664]{1,0:T(8,128)(2,1)S(1)} all-gather(bf16[48,1664]{1,0:T(8,128)(2,1)S(1)} %concatenate.59), channel_id=1, replica_groups={{0,8,16,24},{2,10,18,26},{4,12,20,28},{6,14,22,30},{1,9,17,25},{3,11,19..., dimensions={0}, use_global_device_ids=true | all-gather | bytes 798720 | tf_op jit(solution)/shard_map/all_gather | solution.py:524
  27.0 4.9 %collective-permute-done.1 = bf16[2,2,1,1,48,768]{5,4,3,2,1,0:T(8,128)(2,1)S(1)} collective-permute-done((bf16[2,2,1,1,48,768]{5,4,3,2,1,0:T(8,128)(2,1)S(1)}, bf16[2,2,1,1,48,768]{5,4,3,2,1,0:T(8,128)(2,1)S(1)}, u32[]{:S(2)}, u32[]{:S(2)}) %collective-permute-start.1) | collective-permute-done | bytes 294944 | tf_op jit(solution)/shard_map/ppermute | solution.py:62
  38.5 4.9 %all-to-all-start.1 = ((bf16[8,64,768]{2,1,0:T(8,128)(2,1)}), bf16[8,64,768]{2,1,0:T(8,128)(2,1)S(1)}, u32[]{:S(2)}, u32[]{:S(2)}) async-start(bf16[8,64,768]{2,1,0:T(8,128)(2,1)} %bitcast.11), calls=%async_computation.1 | async-start | bytes 1572864 | tf_op jit(solution)/shard_map/all_to_all | solution.py:83
  46.0 3.1 %collective-permute-done.3 = bf16[2,2,1,2,48,896]{5,4,3,2,1,0:T(8,128)(2,1)} collective-permute-done((bf16[2,2,1,2,48,896]{5,4,3,2,1,0:T(8,128)(2,1)S(1)}, bf16[2,2,1,2,48,896]{5,4,3,2,1,0:T(8,128)(2,1)}, u32[]{:S(2)}, u32[]{:S(2)}) %collective-permute-start.3) | collective-permute-done | bytes 688160 | tf_op jit(solution)/shard_map/ppermute | solution.py:62
  50.7 5.0 %shard_map.212 = (f32[256,768]{1,0:T(8,128)S(1)}, f32[128,768]{1,0:T(8,128)S(1)}, bf16[256,768]{1,0:T(8,128)(2,1)}, bf16[256,1152]{1,0:T(8,128)(2,1)}, f32[6,256...) custom-call(s32[1,4]{1,0:T(1,128)S(1)} %copy-done.6, ...), custom_call_target="tpu_custom_call" | custom-call | flops 704643072 | bytes 6684704 | tf_op jit(solution)/shard_map/pallas_call | solution.py:114
  60.1 3.8 %all-to-all-done.1.cot_a = bf16[8,64,768]{2,1,0:T(8,128)(2,1)S(1)} async-done(((bf16[8,64,768]{2,1,0:T(8,128)(2,1)}), bf16[8,64,768]{2,1,0:T(8,128)(2,1)S(1)}, u32[]{:S(2)}, u32[]{:S(2)}) %all-to-all-start.1) | async-done | bytes 786464 | tf_op jit(solution)/shard_map/all_to_all | solution.py:83
  63.8 3.8 %all-to-all-start = ((bf16[8,400,128]{2,1,0:T(8,128)(2,1)}), bf16[8,400,128]{2,1,0:T(8,128)(2,1)S(1)}, u32[]{:S(2)}, u32[]{:S(2)}) async-start(bf16[8,400,128]{2,1,0:T(8,128)(2,1)} %get-tuple-element.62), calls=%async_computation | async-start | bytes 1638400 | tf_op jit(solution)/shard_map/all_to_all | solution.py:83
  69.7 19.2 %all-to-all-done.h_a = bf16[8,400,128]{2,1,0:T(8,128)(2,1)S(1)} async-done(((bf16[8,400,128]{2,1,0:T(8,128)(2,1)}), bf16[8,400,128]{2,1,0:T(8,128)(2,1)S(1)}, u32[]{:S(2)}, u32[]{:S(2)}) %all-to-all-start) | async-done | bytes 819232 | tf_op jit(solution)/shard_map/all_to_all | solution.py:83
  95.1 7.8 %shard_map.214 = (bf16[8,400,128]{2,1,0:T(8,128)(2,1)S(1)}, bf16[8,400,128]{2,1,0:T(8,128)(2,1)S(1)}, bf16[1024,768]{1,0:T(8,128)(2,1)}, bf16[1024,768]{1,0:T(8,128)(2,1)}, f32[1024,128]{1,0:T(8,128)}) custom-call(bf16[8,400,128]{2,1,0:T(8,128)(2,1)S(1)} %all-to-all-done.h_a, bf16[8,400,128]{2,1,0:T(8,128)(2,1)S(1)} %collective-permute-done.7.h_b, ...), custom_call_target="tpu_custom_call" | custom-call | flops 3623878656 | bytes 9437184 | tf_op jit(solution)/shard_map/pallas_call | solution.py:314
  102.9 7.1 %collective-permute-done.9.h_a = bf16[8,400,128]{2,1,0:T(8,128)(2,1)S(1)} collective-permute-done((bf16[8,400,128]{2,1,0:T(8,128)(2,1)S(1)}, bf16[8,400,128]{2,1,0:T(8,128)(2,1)S(1)}, u32[]{:S(2)}, u32[]{:S(2)}) %collective-permute-start.9) | collective-permute-done | bytes 819232 | tf_op jit(solution)/shard_map/ppermute | solution.py:89
  112.3 7.7 %shard_map.215 = (bf16[8,400,128]{2,1,0:T(8,128)(2,1)S(1)}, bf16[8,400,128]{2,1,0:T(8,128)(2,1)S(1)}, bf16[1024,768]{1,0:T(8,128)(2,1)}, bf16[1024,768]{1,0:T(8,128)(2,1)}, f32[1024,128]{1,0:T(8,128)}) custom-call(bf16[8,400,128]{2,1,0:T(8,128)(2,1)S(1)} %collective-permute-done.9.h_a, bf16[8,400,128]{2,1,0:T(8,128)(2,1)S(1)} %collective-permute-done.10.h_b, ...), custom_call_target="tpu_custom_call" | custom-call | flops 3623878656 | bytes 9437184 | tf_op jit(solution)/shard_map/pallas_call | solution.py:314
  124.4 8.8 %shard_map.216 = (bf16[8,64,768]{2,1,0:T(8,128)(2,1)S(1)}, bf16[8,64,768]{2,1,0:T(8,128)(2,1)S(1)}, f32[768,768]{1,0:T(8,128)}, f32[768,768]{1,0:T(8,128)}) custom-call(bf16[8,400,128]{2,1,0:T(8,128)(2,1)S(1)} %collective-permute-done.9.h_a, bf16[8,400,128]{2,1,0:T(8,128)(2,1)S(1)} %collective-permute-done.10.h_b, ...), custom_call_target="tpu_custom_call" | custom-call | flops 3623878656 | bytes 7864320 | tf_op jit(solution)/shard_map/pallas_call | solution.py:358
  133.2 9.7 %collective-permute-done.14 = bf16[8,400,128]{2,1,0:T(8,128)(2,1)S(1)} collective-permute-done((bf16[8,400,128]{2,1,0:T(8,128)(2,1)S(1)}, bf16[8,400,128]{2,1,0:T(8,128)(2,1)S(1)}, u32[]{:S(2)}, u32[]{:S(2)}) %collective-permute-start.14) | collective-permute-done | bytes 819232 | tf_op jit(solution)/shard_map/ppermute | solution.py:89
  144.2 3.9 %all-to-all-start.2 = ((bf16[8,400,128]{2,1,0:T(8,128)(2,1)}), bf16[8,400,128]{2,1,0:T(8,128)(2,1)S(1)}, u32[]{:S(2)}, u32[]{:S(2)}) async-start(bf16[8,400,128]{2,1,0:T(8,128)(2,1)} %add_convert_fusion), calls=%async_computation.2 | async-start | bytes 1638400 | tf_op jit(solution)/shard_map/all_to_all | solution.py:83
  150.4 10.2 %shard_map.217 = (bf16[8,64,768]{2,1,0:T(8,128)(2,1)S(1)}, bf16[8,64,768]{2,1,0:T(8,128)(2,1)S(1)}, f32[768,768]{1,0:T(8,128)}, f32[768,768]{1,0:T(8,128)}) custom-call(bf16[8,400,128]{2,1,0:T(8,128)(2,1)S(1)} %all-to-all-done.h_a, bf16[8,400,128]{2,1,0:T(8,128)(2,1)S(1)} %copy-done.8, bf16[8,64,768]{2,1,0:T(8,128)(2,1)S(1)} %copy-done.2, ...), custom_call_target="tpu_custom_call" | custom-call | flops 3623878656 | bytes 7864320 | tf_op jit(solution)/shard_map/pallas_call | solution.py:358
  162.4 5.9 %all-to-all-done.2.back_ref = bf16[8,400,128]{2,1,0:T(8,128)(2,1)S(1)} async-done(((bf16[8,400,128]{2,1,0:T(8,128)(2,1)}), bf16[8,400,128]{2,1,0:T(8,128)(2,1)S(1)}, u32[]{:S(2)}, u32[]{:S(2)}) %all-to-all-start.2) | async-done | bytes 819232 | tf_op jit(solution)/shard_map/all_to_all | solution.py:83
  168.4 2.6 %shard_map.218 = (f32[256,768]{1,0:T(8,128)S(1)}, f32[8,768]{1,0:T(8,128)S(1)}) custom-call(s32[1]{0:T(128)} %bitcast.base_ref, bf16[8,400,128]{2,1,0:T(8,128)(2,1)S(1)} %all-to-all-done.2.back_ref, bf16[8,256]{1,0:T(8,128)(2,1)S(1)} %copy.67.slot_ref, bf16[256,8]{1,0:T(8,128)(2,1)S(1)} %fusion.col_ref, f32[8,256]{1,0:T(8,128)S(1)} %get-tuple-element.87.gates_ref, ...), custom_call_target="tpu_custom_call" | custom-call | flops 201326592 | bytes 3244040 | tf_op jit(solution)/shard_map/pallas_call | solution.py:114
  175.1 7.8 %shard_map.219 = (bf16[768,768]{1,0:T(8,128)(2,1)S(1)}, bf16[768,896]{1,0:T(8,128)(2,1)S(1)}, f32[256,768]{1,0:T(8,128)S(1)}, f32[256,768]{1,0:T(8,128)S(1)}, bf...) custom-call(f32[256,768]{1,0:T(8,128)S(1)} %get-tuple-element.89.part_ref, ...), custom_call_target="tpu_custom_call" | custom-call | flops 1811939328 | bytes 20054016 | tf_op jit(solution)/shard_map/pallas_call | solution.py:114
  186.9 18.6 %collective-permute-done.18 = bf16[2,2,2,1,48,768]{5,4,3,2,1,0:T(8,128)(2,1)S(1)} collective-permute-done((bf16[2,2,2,1,48,768]{5,4,3,2,1,0:T(8,128)(2,1)S(1)}, bf16[2,2,2,1,48,768]{5,4,3,2,1,0:T(8,128)(2,1)S(1)}, u32[]{:S(2)}, u32[]{:S(2)}) %collective-permute-start.18) | collective-permute-done | bytes 589856 | tf_op jit(solution)/shard_map/ppermute | solution.py:76
  208.4 4.2 %all-to-all-start.3 = ((bf16[8,64,768]{2,1,0:T(8,128)(2,1)}), bf16[8,64,768]{2,1,0:T(8,128)(2,1)}, u32[]{:S(2)}, u32[]{:S(2)}) async-start(bf16[8,64,768]{2,1,0:T(8,128)(2,1)} %add_convert_fusion.2), calls=%async_computation.3 | async-start | bytes 1572864 | tf_op jit(solution)/shard_map/all_to_all | solution.py:83
  218.7 9.2 %collective-permute-done.22 = bf16[2,1,1,1,48,768]{5,4,3,2,1,0:T(8,128)(2,1)S(1)} collective-permute-done((bf16[2,1,1,1,48,768]{5,4,3,2,1,0:T(8,128)(2,1)S(1)}, bf16[2,1,1,1,48,768]{5,4,3,2,1,0:T(8,128)(2,1)S(1)}, u32[]{:S(2)}, u32[]{:S(2)}) %collective-permute-start.22) | collective-permute-done | bytes 147488 | tf_op jit(solution)/shard_map/ppermute | solution.py:76
  228.0 4.8 %collective-permute-start.23 = (bf16[1,1,1,1,48,768]{5,4,3,2,1,0:T(8,128)(2,1)S(1)}, bf16[1,1,1,1,48,768]{5,4,3,2,1,0:T(8,128)(2,1)S(1)}, u32[]{:S(2)}, u32[]{:S(2)}) collective-permute-start(bf16[1,1,1,1,48,768]{5,4,3,2,1,0:T(8,128)(2,1)S(1)} %dynamic-slice_convert_fusion.6), channel_id=1, source_target_pairs={{0,16},{2,18},{4,20},{6,22},{8,24},{10,26},{12,28},{14,30},{16,0},... | collective-permute-start | bytes 221192 | tf_op jit(solution)/shard_map/ppermute | solution.py:76
  233.0 2.9 %collective-permute-done.23 = bf16[1,1,1,1,48,768]{5,4,3,2,1,0:T(8,128)(2,1)S(1)} collective-permute-done((bf16[1,1,1,1,48,768]{5,4,3,2,1,0:T(8,128)(2,1)S(1)}, bf16[1,1,1,1,48,768]{5,4,3,2,1,0:T(8,128)(2,1)S(1)}, u32[]{:S(2)}, u32[]{:S(2)}) %collective-permute-start.23) | collective-permute-done | bytes 73760 | tf_op jit(solution)/shard_map/ppermute | solution.py:76
  239.2 5.6 %collective-permute-done.27 = bf16[1,1,1,1,48,896]{5,4,3,2,1,0:T(8,128)(2,1)S(1)} collective-permute-done((bf16[1,1,1,1,48,896]{5,4,3,2,1,0:T(8,128)(2,1)S(1)}, bf16[1,1,1,1,48,896]{5,4,3,2,1,0:T(8,128)(2,1)S(1)}, u32[]{:S(2)}, u32[]{:S(2)}) %collective-permute-start.27) | collective-permute-done | bytes 86048 | tf_op jit(solution)/shard_map/ppermute | solution.py:76
  (148 shorter events, 68.1 us)
Async XLA Ops:
  23.3 9.8 %collective-permute-start = (bf16[2,2,1,1,48,896]{5,4,3,2,1,0:T(8,128)(2,1)S(1)}, bf16[2,2,1,1,48,896]{5,4,3,2,1,0:T(8,128)(2,1)S(1)}, u32[]{:S(2)}, u32[]{:S(2)}) collective-permute-start(bf16[2,2,1,1,48,896]{5,4,3,2,1,0:T(8,128)(2,1)S(1)} %slice.44), channel_id=1, source_target_pairs={{0,2},{2,0},{4,6},{6,4},{8,10},{10,8},{12,14},{14,12},{16,18},{18,... | collective-permute-start | bytes 1032200 | tf_op jit(solution)/shard_map/ppermute | solution.py:62
  24.9 7.1 %collective-permute-start.1 = (bf16[2,2,1,1,48,768]{5,4,3,2,1,0:T(8,128)(2,1)S(1)}, bf16[2,2,1,1,48,768]{5,4,3,2,1,0:T(8,128)(2,1)S(1)}, u32[]{:S(2)}, u32[]{:S(2)}) collective-permute-start(bf16[2,2,1,1,48,768]{5,4,3,2,1,0:T(8,128)(2,1)S(1)} %slice.45), channel_id=1, source_target_pairs={{0,4},{2,6},{4,0},{6,2},{8,12},{10,14},{12,8},{14,10},{16,20},{18,... | collective-permute-start | bytes 884744 | tf_op jit(solution)/shard_map/ppermute | solution.py:62
  32.8 11.3 %collective-permute-start.2 = (bf16[2,2,2,1,48,768]{5,4,3,2,1,0:T(8,128)(2,1)}, bf16[2,2,2,1,48,768]{5,4,3,2,1,0:T(8,128)(2,1)}, u32[]{:S(2)}, u32[]{:S(2)}) collective-permute-start(bf16[2,2,2,1,48,768]{5,4,3,2,1,0:T(8,128)(2,1)} %maximum_select_fusion.3), channel_id=1, source_target_pairs={{0,2},{2,0},{4,6},{6,4},{8,10},{10,8},{12,14},{14,12},{16,18},{18,... | collective-permute-start | bytes 1769480 | tf_op jit(solution)/shard_map/ppermute | solution.py:62
  33.2 16.0 %collective-permute-start.3 = (bf16[2,2,1,2,48,896]{5,4,3,2,1,0:T(8,128)(2,1)S(1)}, bf16[2,2,1,2,48,896]{5,4,3,2,1,0:T(8,128)(2,1)}, u32[]{:S(2)}, u32[]{:S(2)}) collective-permute-start(bf16[2,2,1,2,48,896]{5,4,3,2,1,0:T(8,128)(2,1)S(1)} %maximum_select_fusion.2), channel_id=1, source_target_pairs={{0,4},{2,6},{4,0},{6,2},{8,12},{10,14},{12,8},{14,10},{16,20},{18,... | collective-permute-start | bytes 2064392 | tf_op jit(solution)/shard_map/ppermute | solution.py:62
  38.5 25.4 %all-to-all-start.1 = ((bf16[8,64,768]{2,1,0:T(8,128)(2,1)}), bf16[8,64,768]{2,1,0:T(8,128)(2,1)S(1)}, u32[]{:S(2)}, u32[]{:S(2)}) async-start(bf16[8,64,768]{2,1,0:T(8,128)(2,1)} %bitcast.11), calls=%async_computation.1 | async-start | bytes 1572864 | tf_op jit(solution)/shard_map/all_to_all | solution.py:83
  63.8 25.0 %all-to-all-start = ((bf16[8,400,128]{2,1,0:T(8,128)(2,1)}), bf16[8,400,128]{2,1,0:T(8,128)(2,1)S(1)}, u32[]{:S(2)}, u32[]{:S(2)}) async-start(bf16[8,400,128]{2,1,0:T(8,128)(2,1)} %get-tuple-element.62), calls=%async_computation | async-start | bytes 1638400 | tf_op jit(solution)/shard_map/all_to_all | solution.py:83
  67.7 21.2 %collective-permute-start.5 = (bf16[8,64,768]{2,1,0:T(8,128)(2,1)S(1)}, bf16[8,64,768]{2,1,0:T(8,128)(2,1)S(1)}, u32[]{:S(2)}, u32[]{:S(2)}) collective-permute-start(bf16[8,64,768]{2,1,0:T(8,128)(2,1)S(1)} %all-to-all-done.1.cot_a), channel_id=1, source_target_pairs={{0,2},{2,0},{4,6},{6,4},{8,10},{10,8},{12,14},{14,12},{16,18},{18,... | collective-permute-start | bytes 2359304 | tf_op jit(solution)/shard_map/ppermute | solution.py:89
  88.8 4.6 %collective-permute-start.7 = (bf16[8,400,128]{2,1,0:T(8,128)(2,1)S(1)}, bf16[8,400,128]{2,1,0:T(8,128)(2,1)S(1)}, u32[]{:S(2)}, u32[]{:S(2)}) collective-permute-start(bf16[8,400,128]{2,1,0:T(8,128)(2,1)S(1)} %all-to-all-done.h_a), channel_id=1, source_target_pairs={{0,1},{1,0},{2,3},{3,2},{4,5},{5,4},{6,7},{7,6},{8,9},{9,8},{10,11... | collective-permute-start | bytes 2457608 | tf_op jit(solution)/shard_map/ppermute | solution.py:48
  89.3 20.7 %collective-permute-start.9 = (bf16[8,400,128]{2,1,0:T(8,128)(2,1)S(1)}, bf16[8,400,128]{2,1,0:T(8,128)(2,1)S(1)}, u32[]{:S(2)}, u32[]{:S(2)}) collective-permute-start(bf16[8,400,128]{2,1,0:T(8,128)(2,1)S(1)} %all-to-all-done.h_a), channel_id=1, source_target_pairs={{0,2},{2,0},{4,6},{6,4},{8,10},{10,8},{12,14},{14,12},{16,18},{18,... | collective-permute-start | bytes 2457608 | tf_op jit(solution)/shard_map/ppermute | solution.py:89
  120.2 13.0 %collective-permute-start.16 = (bf16[8,400,128]{2,1,0:T(8,128)(2,1)S(1)}, bf16[8,400,128]{2,1,0:T(8,128)(2,1)S(1)}, u32[]{:S(2)}, u32[]{:S(2)}) collective-permute-start(bf16[8,400,128]{2,1,0:T(8,128)(2,1)S(1)} %get-tuple-element.84), channel_id=1, source_target_pairs={{0,1},{1,0},{2,3},{3,2},{4,5},{5,4},{6,7},{7,6},{8,9},{9,8},{10,11... | collective-permute-start | bytes 2457608 | tf_op jit(solution)/shard_map/ppermute | solution.py:48
  122.6 20.4 %collective-permute-start.14 = (bf16[8,400,128]{2,1,0:T(8,128)(2,1)S(1)}, bf16[8,400,128]{2,1,0:T(8,128)(2,1)S(1)}, u32[]{:S(2)}, u32[]{:S(2)}) collective-permute-start(bf16[8,400,128]{2,1,0:T(8,128)(2,1)S(1)} %add_convert_fusion.1), channel_id=1, source_target_pairs={{0,2},{2,0},{4,6},{6,4},{8,10},{10,8},{12,14},{14,12},{16,18},{18,... | collective-permute-start | bytes 2457608 | tf_op jit(solution)/shard_map/ppermute | solution.py:89
  144.2 24.2 %all-to-all-start.2 = ((bf16[8,400,128]{2,1,0:T(8,128)(2,1)}), bf16[8,400,128]{2,1,0:T(8,128)(2,1)S(1)}, u32[]{:S(2)}, u32[]{:S(2)}) async-start(bf16[8,400,128]{2,1,0:T(8,128)(2,1)} %add_convert_fusion), calls=%async_computation.2 | async-start | bytes 1638400 | tf_op jit(solution)/shard_map/all_to_all | solution.py:83
  148.1 23.7 %collective-permute-start.13 = (bf16[8,64,768]{2,1,0:T(8,128)(2,1)}, bf16[8,64,768]{2,1,0:T(8,128)(2,1)}, u32[]{:S(2)}, u32[]{:S(2)}) collective-permute-start(bf16[8,64,768]{2,1,0:T(8,128)(2,1)} %copy-done.10), channel_id=1, source_target_pairs={{0,1},{1,0},{2,3},{3,2},{4,5},{5,4},{6,7},{7,6},{8,9},{9,8},{10,11... | collective-permute-start | bytes 2359304 | tf_op jit(solution)/shard_map/ppermute | solution.py:48
  171.2 36.0 %collective-permute-start.12 = (bf16[8,64,768]{2,1,0:T(8,128)(2,1)}, bf16[8,64,768]{2,1,0:T(8,128)(2,1)S(1)}, u32[]{:S(2)}, u32[]{:S(2)}) collective-permute-start(bf16[8,64,768]{2,1,0:T(8,128)(2,1)} %copy-done.9), channel_id=1, source_target_pairs={{0,1},{1,0},{2,3},{3,2},{4,5},{5,4},{6,7},{7,6},{8,9},{9,8},{10,11... | collective-permute-start | bytes 2359304 | tf_op jit(solution)/shard_map/ppermute | solution.py:48
  173.3 33.9 %collective-permute-start.15 = (bf16[8,64,768]{2,1,0:T(8,128)(2,1)S(1)}, bf16[8,64,768]{2,1,0:T(8,128)(2,1)S(1)}, u32[]{:S(2)}, u32[]{:S(2)}) collective-permute-start(bf16[8,64,768]{2,1,0:T(8,128)(2,1)S(1)} %add_convert_fusion.3), channel_id=1, source_target_pairs={{0,2},{2,0},{4,6},{6,4},{8,10},{10,8},{12,14},{14,12},{16,18},{18,... | collective-permute-start | bytes 2359304 | tf_op jit(solution)/shard_map/ppermute | solution.py:89
  184.0 31.7 %collective-permute-start.24 = (bf16[2,2,1,2,48,896]{5,4,3,2,1,0:T(8,128)(2,1)}, bf16[2,2,1,2,48,896]{5,4,3,2,1,0:T(8,128)(2,1)}, u32[]{:S(2)}, u32[]{:S(2)}) collective-permute-start(bf16[2,2,1,2,48,896]{5,4,3,2,1,0:T(8,128)(2,1)} %constant_dynamic-slice_fusion), channel_id=1, source_target_pairs={{0,4},{2,6},{4,0},{6,2},{8,12},{10,14},{12,8},{14,10},{16,20},{18,... | collective-permute-start | bytes 2064392 | tf_op jit(solution)/shard_map/ppermute | solution.py:76
  185.4 20.1 %collective-permute-start.18 = (bf16[2,2,2,1,48,768]{5,4,3,2,1,0:T(8,128)(2,1)S(1)}, bf16[2,2,2,1,48,768]{5,4,3,2,1,0:T(8,128)(2,1)S(1)}, u32[]{:S(2)}, u32[]{:S(2)}) collective-permute-start(bf16[2,2,2,1,48,768]{5,4,3,2,1,0:T(8,128)(2,1)S(1)} %constant_dynamic-slice_fusion.2), channel_id=1, source_target_pairs={{0,2},{2,0},{4,6},{6,4},{8,10},{10,8},{12,14},{14,12},{16,18},{18,... | collective-permute-start | bytes 1769480 | tf_op jit(solution)/shard_map/ppermute | solution.py:76
  205.7 8.3 %collective-permute-start.21 = (bf16[2,2,1,1,48,768]{5,4,3,2,1,0:T(8,128)(2,1)S(1)}, bf16[2,2,1,1,48,768]{5,4,3,2,1,0:T(8,128)(2,1)}, u32[]{:S(2)}, u32[]{:S(2)}) collective-permute-start(bf16[2,2,1,1,48,768]{5,4,3,2,1,0:T(8,128)(2,1)S(1)} %dynamic-slice_convert_fusion.1), channel_id=1, source_target_pairs={{0,4},{2,6},{4,0},{6,2},{8,12},{10,14},{12,8},{14,10},{16,20},{18,... | collective-permute-start | bytes 884744 | tf_op jit(solution)/shard_map/ppermute | solution.py:76
  208.4 36.6 %all-to-all-start.3 = ((bf16[8,64,768]{2,1,0:T(8,128)(2,1)}), bf16[8,64,768]{2,1,0:T(8,128)(2,1)}, u32[]{:S(2)}, u32[]{:S(2)}) async-start(bf16[8,64,768]{2,1,0:T(8,128)(2,1)} %add_convert_fusion.2), calls=%async_computation.3 | async-start | bytes 1572864 | tf_op jit(solution)/shard_map/all_to_all | solution.py:83
  215.0 12.9 %collective-permute-start.22 = (bf16[2,1,1,1,48,768]{5,4,3,2,1,0:T(8,128)(2,1)S(1)}, bf16[2,1,1,1,48,768]{5,4,3,2,1,0:T(8,128)(2,1)S(1)}, u32[]{:S(2)}, u32[]{:S(2)}) collective-permute-start(bf16[2,1,1,1,48,768]{5,4,3,2,1,0:T(8,128)(2,1)S(1)} %dynamic-slice_convert_fusion.4), channel_id=1, source_target_pairs={{0,8},{2,10},{4,12},{6,14},{8,0},{10,2},{12,4},{14,6},{16,24},{18,... | collective-permute-start | bytes 442376 | tf_op jit(solution)/shard_map/ppermute | solution.py:76
  216.9 15.9 %collective-permute-start.25 = (bf16[2,2,1,1,48,896]{5,4,3,2,1,0:T(8,128)(2,1)S(1)}, bf16[2,2,1,1,48,896]{5,4,3,2,1,0:T(8,128)(2,1)S(1)}, u32[]{:S(2)}, u32[]{:S(2)}) collective-permute-start(bf16[2,2,1,1,48,896]{5,4,3,2,1,0:T(8,128)(2,1)S(1)} %dynamic-slice_convert_fusion), channel_id=1, source_target_pairs={{0,2},{2,0},{4,6},{6,4},{8,10},{10,8},{12,14},{14,12},{16,18},{18,... | collective-permute-start | bytes 1032200 | tf_op jit(solution)/shard_map/ppermute | solution.py:76
  228.0 7.9 %collective-permute-start.23 = (bf16[1,1,1,1,48,768]{5,4,3,2,1,0:T(8,128)(2,1)S(1)}, bf16[1,1,1,1,48,768]{5,4,3,2,1,0:T(8,128)(2,1)S(1)}, u32[]{:S(2)}, u32[]{:S(2)}) collective-permute-start(bf16[1,1,1,1,48,768]{5,4,3,2,1,0:T(8,128)(2,1)S(1)} %dynamic-slice_convert_fusion.6), channel_id=1, source_target_pairs={{0,16},{2,18},{4,20},{6,22},{8,24},{10,26},{12,28},{14,30},{16,0},... | collective-permute-start | bytes 221192 | tf_op jit(solution)/shard_map/ppermute | solution.py:76
  232.9 5.5 %collective-permute-start.26 = (bf16[2,1,1,1,48,896]{5,4,3,2,1,0:T(8,128)(2,1)S(1)}, bf16[2,1,1,1,48,896]{5,4,3,2,1,0:T(8,128)(2,1)S(1)}, u32[]{:S(2)}, u32[]{:S(2)}) collective-permute-start(bf16[2,1,1,1,48,896]{5,4,3,2,1,0:T(8,128)(2,1)S(1)} %dynamic-slice_convert_fusion.3), channel_id=1, source_target_pairs={{0,8},{2,10},{4,12},{6,14},{8,0},{10,2},{12,4},{14,6},{16,24},{18,... | collective-permute-start | bytes 516104 | tf_op jit(solution)/shard_map/ppermute | solution.py:76
  238.4 6.4 %collective-permute-start.27 = (bf16[1,1,1,1,48,896]{5,4,3,2,1,0:T(8,128)(2,1)S(1)}, bf16[1,1,1,1,48,896]{5,4,3,2,1,0:T(8,128)(2,1)S(1)}, u32[]{:S(2)}, u32[]{:S(2)}) collective-permute-start(bf16[1,1,1,1,48,896]{5,4,3,2,1,0:T(8,128)(2,1)S(1)} %dynamic-slice_convert_fusion.5), channel_id=1, source_target_pairs={{0,16},{2,18},{4,20},{6,22},{8,24},{10,26},{12,28},{14,30},{16,0},... | collective-permute-start | bytes 258056 | tf_op jit(solution)/shard_map/ppermute | solution.py:76
  (28 other events, 184.9 us)

commit v6 on v5

--- a/solution.py
+++ b/solution.py
@@ -588,17 +588,20 @@
     far_total = cross(far_sum)
     far_kept[0] = after(far_kept[0], far_sum)
     far_out, far_given, *sums = expert_weights(h_far, cot_far, far_kept, second_weight, (), half)
-    back = trade(after(add_low(own_back, swap(own_given), far_total), far_out))
+    back_sum = after(add_low(own_back, swap(own_given), far_total), far_out)
+    back = trade(back_sum)
+    out_far = add_low(far_out, swap(far_given))
+    own_kept[0] = after(own_kept[0], out_far, back_sum)
     own_out, out_given, grad_first, grad_second = expert_weights(
         h_own, cot_own, own_kept, second_weight, sums, half
     )
-    far_total = cross(after(add_low(far_out, swap(far_given)), far_total))
+    out_far = cross(after(out_far, far_total))
     out_given = swap(out_given)
     h_part, router_part = call(
         combine_kernel,
         [near_shape((group_rows, width), FULL), near_shape((experts, width), FULL)],
         base,
-        after(back, own_out),
+        after(back, own_out, out_far),
         slot_row,
         slot_col,
         gates,
@@ -641,7 +644,7 @@
         vx_sum = halve(vx_sum, order_b[bits - 1 - step], bits)
         qk_sum = halve(qk_sum, order_a[bits - 1 - step], bits)
         if step == 0:
-            out_rows = add_low(own_out, out_given, after(far_total, qk_sum))
+            out_rows = add_low(own_out, out_given, after(out_far, one_other))
             back_out = trade(out_rows).reshape(slots, width)
     qk_sum = qk_sum.reshape(width // dp_count, 2 * inner)
     vx_sum = vx_sum.reshape(width // dp_count, 2 * inner + extra_width)

time: 251 us -> 254 us (1.012)
  waiting for transfers between devices: 103 us -> 113 us
  local copies, waits for them, and re-layouts: 13.5 us -> 9.65 us
    all_to_all x4, waiting for transfers between devices: 28.9 us -> 38.6 us  [trade(): lax.all_to_all(values, 'dp', split_axis=0, concat_axis=0, tiled=True, axi...]
    ppermute x8, waiting for transfers between devices: 40.1 us -> 34.1 us  [halve(): lax.ppermute(given, 'dp', partners(bit)).astype(FULL)]
    ppermute x4, waiting for transfers between devices: 16.8 us -> 22.7 us  [cross(): return lax.ppermute(values, 'dp', partners(0))]
    unnamed x40 -> x30, local copies, waits for them, and re-layouts: 7.29 us -> 4.32 us
  transfers between devices with their start and end apart: 33 -> 33, of which waited for: 19 -> 21; matrix products, arithmetic and copies ran while one was open for 7% -> 6% of each run, Pallas kernels for 18% -> 14%
where the time goes in v6:
time: 254 us; the launch traced here: 253 us
  waiting for transfers between devices  113 us (44%)
  Pallas kernels  51.9 us (20%)
  starting transfers between devices  40.7 us (16%)
  blocking collectives  21.8 us (9%)
  other arithmetic  11.1 us (4%)
  local copies, waits for them, and re-layouts  9.65 us (4%)
  matrix products  3.09 us (1%)
    all_to_all x4, waiting for transfers between devices, trade(): lax.all_to_all(values, 'dp', split_axis=0, concat_axis=0, tiled=True, axi...  38.6 us
    ppermute x8, waiting for transfers between devices, halve(): lax.ppermute(given, 'dp', partners(bit)).astype(FULL)  34.1 us
    ppermute x4, waiting for transfers between devices, cross(): return lax.ppermute(values, 'dp', partners(0))  22.7 us
    all_gather x1, blocking collectives, local(): lax.all_gather(shard, 'dp', axis=0, tiled=True, axis_index_groups=lines)  19.4 us
    pallas_call x2, Pallas kernels, expert_weights(): pl.pallas_call(kernel, grid=(2 * steps,), out_shape=[near_shape((experts,...  19 us
    all_to_all x4, starting transfers between devices, trade(): lax.all_to_all(values, 'dp', split_axis=0, concat_axis=0, tiled=True, axi...  18 us
    pallas_call x4, Pallas kernels, call(): pl.pallas_call(kernel, out_shape=out_shape, in_specs=[pl.BlockSpec(memory...  17.4 us
    pallas_call x2, Pallas kernels, expert_rows(): pl.pallas_call(kernel, grid=(2 * steps,), out_shape=[near_shape(h_rows[0]...  15.5 us
  transfers between devices with their start and end apart: 33, of which 21 were waited for; matrix products, arithmetic and copies ran while one was open for 6% of the time, Pallas kernels for 14%

profile of v6, /device:TPU:0, one launch (start us, length us, event | category | flops | bytes accessed | tf_op | source)
XLA Modules:
  0.0 252.7 jit_solution(12376669744848725949)
XLA Ops:
  3.9 19.4 %all_gather.6 = bf16[192,1664]{1,0:T(8,128)(2,1)S(1)} all-gather(bf16[48,1664]{1,0:T(8,128)(2,1)S(1)} %concatenate.59), channel_id=1, replica_groups={{0,8,16,24},{2,10,18,26},{4,12,20,28},{6,14,22,30},{1,9,17,25},{3,11,19..., dimensions={0}, use_global_device_ids=true | all-gather | bytes 798720 | tf_op jit(solution)/shard_map/all_gather | solution.py:524
  27.0 4.9 %collective-permute-done.1 = bf16[2,2,1,1,48,768]{5,4,3,2,1,0:T(8,128)(2,1)S(1)} collective-permute-done((bf16[2,2,1,1,48,768]{5,4,3,2,1,0:T(8,128)(2,1)S(1)}, bf16[2,2,1,1,48,768]{5,4,3,2,1,0:T(8,128)(2,1)S(1)}, u32[]{:S(2)}, u32[]{:S(2)}) %collective-permute-start.1) | collective-permute-done | bytes 294944 | tf_op jit(solution)/shard_map/ppermute | solution.py:62
  38.5 4.9 %all-to-all-start.1 = ((bf16[8,64,768]{2,1,0:T(8,128)(2,1)}), bf16[8,64,768]{2,1,0:T(8,128)(2,1)S(1)}, u32[]{:S(2)}, u32[]{:S(2)}) async-start(bf16[8,64,768]{2,1,0:T(8,128)(2,1)} %bitcast.11), calls=%async_computation.1 | async-start | bytes 1572864 | tf_op jit(solution)/shard_map/all_to_all | solution.py:83
  50.8 5.0 %shard_map.212 = (f32[256,768]{1,0:T(8,128)S(1)}, f32[128,768]{1,0:T(8,128)S(1)}, bf16[256,768]{1,0:T(8,128)(2,1)}, bf16[256,1152]{1,0:T(8,128)(2,1)}, f32[6,256...) custom-call(s32[1,4]{1,0:T(1,128)S(1)} %copy-done.3, ...), custom_call_target="tpu_custom_call" | custom-call | flops 704643072 | bytes 6684704 | tf_op jit(solution)/shard_map/pallas_call | solution.py:114
  60.1 3.7 %all-to-all-done.1.cot_a = bf16[8,64,768]{2,1,0:T(8,128)(2,1)S(1)} async-done(((bf16[8,64,768]{2,1,0:T(8,128)(2,1)}), bf16[8,64,768]{2,1,0:T(8,128)(2,1)S(1)}, u32[]{:S(2)}, u32[]{:S(2)}) %all-to-all-start.1) | async-done | bytes 786464 | tf_op jit(solution)/shard_map/all_to_all | solution.py:83
  63.8 3.9 %all-to-all-start = ((bf16[8,400,128]{2,1,0:T(8,128)(2,1)}), bf16[8,400,128]{2,1,0:T(8,128)(2,1)S(1)}, u32[]{:S(2)}, u32[]{:S(2)}) async-start(bf16[8,400,128]{2,1,0:T(8,128)(2,1)} %get-tuple-element.63), calls=%async_computation | async-start | bytes 1638400 | tf_op jit(solution)/shard_map/all_to_all | solution.py:83
  69.7 19.2 %all-to-all-done.h_a = bf16[8,400,128]{2,1,0:T(8,128)(2,1)S(1)} async-done(((bf16[8,400,128]{2,1,0:T(8,128)(2,1)}), bf16[8,400,128]{2,1,0:T(8,128)(2,1)S(1)}, u32[]{:S(2)}, u32[]{:S(2)}) %all-to-all-start) | async-done | bytes 819232 | tf_op jit(solution)/shard_map/all_to_all | solution.py:83
  95.2 7.8 %shard_map.214 = (bf16[8,400,128]{2,1,0:T(8,128)(2,1)S(1)}, bf16[8,400,128]{2,1,0:T(8,128)(2,1)S(1)}, bf16[1024,768]{1,0:T(8,128)(2,1)}, bf16[1024,768]{1,0:T(8,128)(2,1)}, f32[1024,128]{1,0:T(8,128)}) custom-call(bf16[8,400,128]{2,1,0:T(8,128)(2,1)S(1)} %all-to-all-done.h_a, bf16[8,400,128]{2,1,0:T(8,128)(2,1)S(1)} %collective-permute-done.7.h_b, ...), custom_call_target="tpu_custom_call" | custom-call | flops 3623878656 | bytes 9437184 | tf_op jit(solution)/shard_map/pallas_call | solution.py:314
  103.0 7.1 %collective-permute-done.9.h_a = bf16[8,400,128]{2,1,0:T(8,128)(2,1)S(1)} collective-permute-done((bf16[8,400,128]{2,1,0:T(8,128)(2,1)S(1)}, bf16[8,400,128]{2,1,0:T(8,128)(2,1)S(1)}, u32[]{:S(2)}, u32[]{:S(2)}) %collective-permute-start.9) | collective-permute-done | bytes 819232 | tf_op jit(solution)/shard_map/ppermute | solution.py:89
  112.4 7.7 %shard_map.215 = (bf16[8,400,128]{2,1,0:T(8,128)(2,1)S(1)}, bf16[8,400,128]{2,1,0:T(8,128)(2,1)S(1)}, bf16[1024,768]{1,0:T(8,128)(2,1)}, bf16[1024,768]{1,0:T(8,128)(2,1)}, f32[1024,128]{1,0:T(8,128)}) custom-call(bf16[8,400,128]{2,1,0:T(8,128)(2,1)S(1)} %collective-permute-done.9.h_a, bf16[8,400,128]{2,1,0:T(8,128)(2,1)S(1)} %collective-permute-done.10.h_b, ...), custom_call_target="tpu_custom_call" | custom-call | flops 3623878656 | bytes 9437184 | tf_op jit(solution)/shard_map/pallas_call | solution.py:314
  124.4 8.8 %shard_map.216 = (bf16[8,64,768]{2,1,0:T(8,128)(2,1)S(1)}, bf16[8,64,768]{2,1,0:T(8,128)(2,1)}, f32[768,768]{1,0:T(8,128)}, f32[768,768]{1,0:T(8,128)}) custom-call(bf16[8,400,128]{2,1,0:T(8,128)(2,1)S(1)} %collective-permute-done.9.h_a, bf16[8,400,128]{2,1,0:T(8,128)(2,1)S(1)} %collective-permute-done.10.h_b, bf16[8,64,768]{2,1,0:T(8,128)(2,1)S(1)} %copy-done.9, ...), custom_call_target="tpu_custom_call" | custom-call | flops 3623878656 | bytes 7864320 | tf_op jit(solution)/shard_map/pallas_call | solution.py:358
  133.3 9.8 %collective-permute-done.14 = bf16[8,400,128]{2,1,0:T(8,128)(2,1)S(1)} collective-permute-done((bf16[8,400,128]{2,1,0:T(8,128)(2,1)S(1)}, bf16[8,400,128]{2,1,0:T(8,128)(2,1)S(1)}, u32[]{:S(2)}, u32[]{:S(2)}) %collective-permute-start.14) | collective-permute-done | bytes 819232 | tf_op jit(solution)/shard_map/ppermute | solution.py:89
  144.3 3.8 %all-to-all-start.2 = ((bf16[8,400,128]{2,1,0:T(8,128)(2,1)}), bf16[8,400,128]{2,1,0:T(8,128)(2,1)S(1)}, u32[]{:S(2)}, u32[]{:S(2)}) async-start(bf16[8,400,128]{2,1,0:T(8,128)(2,1)} %add_convert_fusion), calls=%async_computation.2 | async-start | bytes 1638400 | tf_op jit(solution)/shard_map/all_to_all | solution.py:83
  152.4 10.2 %shard_map.217 = (bf16[8,64,768]{2,1,0:T(8,128)(2,1)S(1)}, bf16[8,64,768]{2,1,0:T(8,128)(2,1)S(1)}, f32[768,768]{1,0:T(8,128)}, f32[768,768]{1,0:T(8,128)}) custom-call(bf16[8,400,128]{2,1,0:T(8,128)(2,1)S(1)} %all-to-all-done.h_a, bf16[8,400,128]{2,1,0:T(8,128)(2,1)S(1)} %copy-done.5, bf16[8,64,768]{2,1,0:T(8,128)(2,1)S(1)} %copy-done.2, ...), custom_call_target="tpu_custom_call" | custom-call | flops 3623878656 | bytes 7864320 | tf_op jit(solution)/shard_map/pallas_call | solution.py:358
  162.5 5.8 %collective-permute-done.16 = bf16[8,64,768]{2,1,0:T(8,128)(2,1)S(1)} collective-permute-done((bf16[8,64,768]{2,1,0:T(8,128)(2,1)S(1)}, bf16[8,64,768]{2,1,0:T(8,128)(2,1)S(1)}, u32[]{:S(2)}, u32[]{:S(2)}) %collective-permute-start.16) | collective-permute-done | bytes 786464 | tf_op jit(solution)/shard_map/ppermute | solution.py:89
  169.6 5.4 %all-to-all-start.3 = ((bf16[8,64,768]{2,1,0:T(8,128)(2,1)}), bf16[8,64,768]{2,1,0:T(8,128)(2,1)}, u32[]{:S(2)}, u32[]{:S(2)}) async-start(bf16[8,64,768]{2,1,0:T(8,128)(2,1)} %add_convert_fusion.2), calls=%async_computation.3 | async-start | bytes 1572864 | tf_op jit(solution)/shard_map/all_to_all | solution.py:83
  177.8 15.7 %all-to-all-done.3 = bf16[8,64,768]{2,1,0:T(8,128)(2,1)} async-done(((bf16[8,64,768]{2,1,0:T(8,128)(2,1)}), bf16[8,64,768]{2,1,0:T(8,128)(2,1)}, u32[]{:S(2)}, u32[]{:S(2)}) %all-to-all-start.3) | async-done | bytes 786464 | tf_op jit(solution)/shard_map/all_to_all | solution.py:83
  195.2 7.8 %shard_map.219 = (bf16[768,768]{1,0:T(8,128)(2,1)S(1)}, bf16[768,896]{1,0:T(8,128)(2,1)S(1)}, f32[256,768]{1,0:T(8,128)S(1)}, f32[256,768]{1,0:T(8,128)S(1)}, bf...) custom-call(f32[256,768]{1,0:T(8,128)S(1)} %get-tuple-element.91.part_ref, ...), custom_call_target="tpu_custom_call" | custom-call | flops 1811939328 | bytes 20054016 | tf_op jit(solution)/shard_map/pallas_call | solution.py:114
  207.1 8.9 %collective-permute-done.20 = bf16[2,2,2,1,48,768]{5,4,3,2,1,0:T(8,128)(2,1)S(1)} collective-permute-done((bf16[2,2,2,1,48,768]{5,4,3,2,1,0:T(8,128)(2,1)S(1)}, bf16[2,2,2,1,48,768]{5,4,3,2,1,0:T(8,128)(2,1)S(1)}, u32[]{:S(2)}, u32[]{:S(2)}) %collective-permute-start.20) | collective-permute-done | bytes 589856 | tf_op jit(solution)/shard_map/ppermute | solution.py:76
  219.2 10.0 %collective-permute-done.21 = bf16[2,2,1,1,48,768]{5,4,3,2,1,0:T(8,128)(2,1)S(1)} collective-permute-done((bf16[2,2,1,1,48,768]{5,4,3,2,1,0:T(8,128)(2,1)S(1)}, bf16[2,2,1,1,48,768]{5,4,3,2,1,0:T(8,128)(2,1)S(1)}, u32[]{:S(2)}, u32[]{:S(2)}) %collective-permute-start.21) | collective-permute-done | bytes 294944 | tf_op jit(solution)/shard_map/ppermute | solution.py:76
  230.3 4.3 %collective-permute-done.22 = bf16[2,1,1,1,48,768]{5,4,3,2,1,0:T(8,128)(2,1)S(1)} collective-permute-done((bf16[2,1,1,1,48,768]{5,4,3,2,1,0:T(8,128)(2,1)S(1)}, bf16[2,1,1,1,48,768]{5,4,3,2,1,0:T(8,128)(2,1)S(1)}, u32[]{:S(2)}, u32[]{:S(2)}) %collective-permute-start.22) | collective-permute-done | bytes 147488 | tf_op jit(solution)/shard_map/ppermute | solution.py:76
  235.0 3.9 %collective-permute-done.25 = bf16[2,2,1,1,48,896]{5,4,3,2,1,0:T(8,128)(2,1)S(1)} collective-permute-done((bf16[2,2,1,1,48,896]{5,4,3,2,1,0:T(8,128)(2,1)S(1)}, bf16[2,2,1,1,48,896]{5,4,3,2,1,0:T(8,128)(2,1)S(1)}, u32[]{:S(2)}, u32[]{:S(2)}) %collective-permute-start.25) | collective-permute-done | bytes 344096 | tf_op jit(solution)/shard_map/ppermute | solution.py:76
  240.8 3.7 %collective-permute-done.26 = bf16[2,1,1,1,48,896]{5,4,3,2,1,0:T(8,128)(2,1)S(1)} collective-permute-done((bf16[2,1,1,1,48,896]{5,4,3,2,1,0:T(8,128)(2,1)S(1)}, bf16[2,1,1,1,48,896]{5,4,3,2,1,0:T(8,128)(2,1)S(1)}, u32[]{:S(2)}, u32[]{:S(2)}) %collective-permute-start.26) | collective-permute-done | bytes 172064 | tf_op jit(solution)/shard_map/ppermute | solution.py:76
  246.6 3.4 %collective-permute-done.27 = bf16[1,1,1,1,48,896]{5,4,3,2,1,0:T(8,128)(2,1)S(1)} collective-permute-done((bf16[1,1,1,1,48,896]{5,4,3,2,1,0:T(8,128)(2,1)S(1)}, bf16[1,1,1,1,48,896]{5,4,3,2,1,0:T(8,128)(2,1)S(1)}, u32[]{:S(2)}, u32[]{:S(2)}) %collective-permute-start.27) | collective-permute-done | bytes 86048 | tf_op jit(solution)/shard_map/ppermute | solution.py:76
  (138 shorter events, 66.7 us)
Async XLA Ops:
  23.3 9.8 %collective-permute-start = (bf16[2,2,1,1,48,896]{5,4,3,2,1,0:T(8,128)(2,1)S(1)}, bf16[2,2,1,1,48,896]{5,4,3,2,1,0:T(8,128)(2,1)S(1)}, u32[]{:S(2)}, u32[]{:S(2)}) collective-permute-start(bf16[2,2,1,1,48,896]{5,4,3,2,1,0:T(8,128)(2,1)S(1)} %slice.44), channel_id=1, source_target_pairs={{0,2},{2,0},{4,6},{6,4},{8,10},{10,8},{12,14},{14,12},{16,18},{18,... | collective-permute-start | bytes 1032200 | tf_op jit(solution)/shard_map/ppermute | solution.py:62
  24.9 7.1 %collective-permute-start.1 = (bf16[2,2,1,1,48,768]{5,4,3,2,1,0:T(8,128)(2,1)S(1)}, bf16[2,2,1,1,48,768]{5,4,3,2,1,0:T(8,128)(2,1)S(1)}, u32[]{:S(2)}, u32[]{:S(2)}) collective-permute-start(bf16[2,2,1,1,48,768]{5,4,3,2,1,0:T(8,128)(2,1)S(1)} %slice.45), channel_id=1, source_target_pairs={{0,4},{2,6},{4,0},{6,2},{8,12},{10,14},{12,8},{14,10},{16,20},{18,... | collective-permute-start | bytes 884744 | tf_op jit(solution)/shard_map/ppermute | solution.py:62
  32.8 11.3 %collective-permute-start.2 = (bf16[2,2,2,1,48,768]{5,4,3,2,1,0:T(8,128)(2,1)}, bf16[2,2,2,1,48,768]{5,4,3,2,1,0:T(8,128)(2,1)}, u32[]{:S(2)}, u32[]{:S(2)}) collective-permute-start(bf16[2,2,2,1,48,768]{5,4,3,2,1,0:T(8,128)(2,1)} %maximum_select_fusion.3), channel_id=1, source_target_pairs={{0,2},{2,0},{4,6},{6,4},{8,10},{10,8},{12,14},{14,12},{16,18},{18,... | collective-permute-start | bytes 1769480 | tf_op jit(solution)/shard_map/ppermute | solution.py:62
  33.2 16.0 %collective-permute-start.3 = (bf16[2,2,1,2,48,896]{5,4,3,2,1,0:T(8,128)(2,1)S(1)}, bf16[2,2,1,2,48,896]{5,4,3,2,1,0:T(8,128)(2,1)}, u32[]{:S(2)}, u32[]{:S(2)}) collective-permute-start(bf16[2,2,1,2,48,896]{5,4,3,2,1,0:T(8,128)(2,1)S(1)} %maximum_select_fusion.2), channel_id=1, source_target_pairs={{0,4},{2,6},{4,0},{6,2},{8,12},{10,14},{12,8},{14,10},{16,20},{18,... | collective-permute-start | bytes 2064392 | tf_op jit(solution)/shard_map/ppermute | solution.py:62
  38.5 25.4 %all-to-all-start.1 = ((bf16[8,64,768]{2,1,0:T(8,128)(2,1)}), bf16[8,64,768]{2,1,0:T(8,128)(2,1)S(1)}, u32[]{:S(2)}, u32[]{:S(2)}) async-start(bf16[8,64,768]{2,1,0:T(8,128)(2,1)} %bitcast.11), calls=%async_computation.1 | async-start | bytes 1572864 | tf_op jit(solution)/shard_map/all_to_all | solution.py:83
  63.8 25.1 %all-to-all-start = ((bf16[8,400,128]{2,1,0:T(8,128)(2,1)}), bf16[8,400,128]{2,1,0:T(8,128)(2,1)S(1)}, u32[]{:S(2)}, u32[]{:S(2)}) async-start(bf16[8,400,128]{2,1,0:T(8,128)(2,1)} %get-tuple-element.63), calls=%async_computation | async-start | bytes 1638400 | tf_op jit(solution)/shard_map/all_to_all | solution.py:83
  67.8 21.2 %collective-permute-start.5 = (bf16[8,64,768]{2,1,0:T(8,128)(2,1)S(1)}, bf16[8,64,768]{2,1,0:T(8,128)(2,1)S(1)}, u32[]{:S(2)}, u32[]{:S(2)}) collective-permute-start(bf16[8,64,768]{2,1,0:T(8,128)(2,1)S(1)} %all-to-all-done.1.cot_a), channel_id=1, source_target_pairs={{0,2},{2,0},{4,6},{6,4},{8,10},{10,8},{12,14},{14,12},{16,18},{18,... | collective-permute-start | bytes 2359304 | tf_op jit(solution)/shard_map/ppermute | solution.py:89
  89.5 20.6 %collective-permute-start.9 = (bf16[8,400,128]{2,1,0:T(8,128)(2,1)S(1)}, bf16[8,400,128]{2,1,0:T(8,128)(2,1)S(1)}, u32[]{:S(2)}, u32[]{:S(2)}) collective-permute-start(bf16[8,400,128]{2,1,0:T(8,128)(2,1)S(1)} %all-to-all-done.h_a), channel_id=1, source_target_pairs={{0,2},{2,0},{4,6},{6,4},{8,10},{10,8},{12,14},{14,12},{16,18},{18,... | collective-permute-start | bytes 2457608 | tf_op jit(solution)/shard_map/ppermute | solution.py:89
  120.3 13.0 %collective-permute-start.13 = (bf16[8,400,128]{2,1,0:T(8,128)(2,1)S(1)}, bf16[8,400,128]{2,1,0:T(8,128)(2,1)S(1)}, u32[]{:S(2)}, u32[]{:S(2)}) collective-permute-start(bf16[8,400,128]{2,1,0:T(8,128)(2,1)S(1)} %get-tuple-element.78), channel_id=1, source_target_pairs={{0,1},{1,0},{2,3},{3,2},{4,5},{5,4},{6,7},{7,6},{8,9},{9,8},{10,11... | collective-permute-start | bytes 2457608 | tf_op jit(solution)/shard_map/ppermute | solution.py:48
  122.7 20.4 %collective-permute-start.14 = (bf16[8,400,128]{2,1,0:T(8,128)(2,1)S(1)}, bf16[8,400,128]{2,1,0:T(8,128)(2,1)S(1)}, u32[]{:S(2)}, u32[]{:S(2)}) collective-permute-start(bf16[8,400,128]{2,1,0:T(8,128)(2,1)S(1)} %add_convert_fusion.1), channel_id=1, source_target_pairs={{0,2},{2,0},{4,6},{6,4},{8,10},{10,8},{12,14},{14,12},{16,18},{18,... | collective-permute-start | bytes 2457608 | tf_op jit(solution)/shard_map/ppermute | solution.py:89
  133.3 14.8 %collective-permute-start.12 = (bf16[8,64,768]{2,1,0:T(8,128)(2,1)}, bf16[8,64,768]{2,1,0:T(8,128)(2,1)}, u32[]{:S(2)}, u32[]{:S(2)}) collective-permute-start(bf16[8,64,768]{2,1,0:T(8,128)(2,1)} %get-tuple-element.77), channel_id=1, source_target_pairs={{0,1},{1,0},{2,3},{3,2},{4,5},{5,4},{6,7},{7,6},{8,9},{9,8},{10,11... | collective-permute-start | bytes 2359304 | tf_op jit(solution)/shard_map/ppermute | solution.py:48
  144.3 25.3 %all-to-all-start.2 = ((bf16[8,400,128]{2,1,0:T(8,128)(2,1)}), bf16[8,400,128]{2,1,0:T(8,128)(2,1)S(1)}, u32[]{:S(2)}, u32[]{:S(2)}) async-start(bf16[8,400,128]{2,1,0:T(8,128)(2,1)} %add_convert_fusion), calls=%async_computation.2 | async-start | bytes 1638400 | tf_op jit(solution)/shard_map/all_to_all | solution.py:83
  149.5 18.8 %collective-permute-start.16 = (bf16[8,64,768]{2,1,0:T(8,128)(2,1)S(1)}, bf16[8,64,768]{2,1,0:T(8,128)(2,1)S(1)}, u32[]{:S(2)}, u32[]{:S(2)}) collective-permute-start(bf16[8,64,768]{2,1,0:T(8,128)(2,1)S(1)} %add_convert_fusion.3), channel_id=1, source_target_pairs={{0,2},{2,0},{4,6},{6,4},{8,10},{10,8},{12,14},{14,12},{16,18},{18,... | collective-permute-start | bytes 2359304 | tf_op jit(solution)/shard_map/ppermute | solution.py:89
  162.5 5.8 %collective-permute-start.15 = (bf16[8,64,768]{2,1,0:T(8,128)(2,1)S(1)}, bf16[8,64,768]{2,1,0:T(8,128)(2,1)S(1)}, u32[]{:S(2)}, u32[]{:S(2)}) collective-permute-start(bf16[8,64,768]{2,1,0:T(8,128)(2,1)S(1)} %get-tuple-element.86), channel_id=1, source_target_pairs={{0,1},{1,0},{2,3},{3,2},{4,5},{5,4},{6,7},{7,6},{8,9},{9,8},{10,11... | collective-permute-start | bytes 2359304 | tf_op jit(solution)/shard_map/ppermute | solution.py:48
  169.6 23.9 %all-to-all-start.3 = ((bf16[8,64,768]{2,1,0:T(8,128)(2,1)}), bf16[8,64,768]{2,1,0:T(8,128)(2,1)}, u32[]{:S(2)}, u32[]{:S(2)}) async-start(bf16[8,64,768]{2,1,0:T(8,128)(2,1)} %add_convert_fusion.2), calls=%async_computation.3 | async-start | bytes 1572864 | tf_op jit(solution)/shard_map/all_to_all | solution.py:83
  177.6 17.6 %collective-permute-start.17 = (f32[256,768]{1,0:T(8,128)S(1)}, f32[256,768]{1,0:T(8,128)S(1)}, u32[]{:S(2)}, u32[]{:S(2)}) collective-permute-start(f32[256,768]{1,0:T(8,128)S(1)} %get-tuple-element.91.part_ref), channel_id=1, source_target_pairs={{0,1},{1,0},{2,3},{3,2},{4,5},{5,4},{6,7},{7,6},{8,9},{9,8},{10,11... | collective-permute-start | bytes 2359304 | tf_op jit(solution)/shard_map/ppermute | solution.py:48
  203.0 13.0 %collective-permute-start.20 = (bf16[2,2,2,1,48,768]{5,4,3,2,1,0:T(8,128)(2,1)S(1)}, bf16[2,2,2,1,48,768]{5,4,3,2,1,0:T(8,128)(2,1)S(1)}, u32[]{:S(2)}, u32[]{:S(2)}) collective-permute-start(bf16[2,2,2,1,48,768]{5,4,3,2,1,0:T(8,128)(2,1)S(1)} %constant_dynamic-slice_fusion.1), channel_id=1, source_target_pairs={{0,2},{2,0},{4,6},{6,4},{8,10},{10,8},{12,14},{14,12},{16,18},{18,... | collective-permute-start | bytes 1769480 | tf_op jit(solution)/shard_map/ppermute | solution.py:76
  204.9 13.5 %collective-permute-start.19 = (f32[128,768]{1,0:T(8,128)S(1)}, f32[128,768]{1,0:T(8,128)S(1)}, u32[]{:S(2)}, u32[]{:S(2)}) collective-permute-start(f32[128,768]{1,0:T(8,128)S(1)} %constant_dynamic-slice_fusion.2), channel_id=1, source_target_pairs={{0,1},{1,0},{2,3},{3,2},{4,5},{5,4},{6,7},{7,6},{8,9},{9,8},{10,11... | collective-permute-start | bytes 1179656 | tf_op jit(solution)/shard_map/ppermute | solution.py:48
  205.5 24.2 %collective-permute-start.24 = (bf16[2,2,1,2,48,896]{5,4,3,2,1,0:T(8,128)(2,1)S(1)}, bf16[2,2,1,2,48,896]{5,4,3,2,1,0:T(8,128)(2,1)S(1)}, u32[]{:S(2)}, u32[]{:S(2)}) collective-permute-start(bf16[2,2,1,2,48,896]{5,4,3,2,1,0:T(8,128)(2,1)S(1)} %constant_dynamic-slice_fusion), channel_id=1, source_target_pairs={{0,4},{2,6},{4,0},{6,2},{8,12},{10,14},{12,8},{14,10},{16,20},{18,... | collective-permute-start | bytes 2064392 | tf_op jit(solution)/shard_map/ppermute | solution.py:76
  216.2 13.1 %collective-permute-start.21 = (bf16[2,2,1,1,48,768]{5,4,3,2,1,0:T(8,128)(2,1)S(1)}, bf16[2,2,1,1,48,768]{5,4,3,2,1,0:T(8,128)(2,1)S(1)}, u32[]{:S(2)}, u32[]{:S(2)}) collective-permute-start(bf16[2,2,1,1,48,768]{5,4,3,2,1,0:T(8,128)(2,1)S(1)} %dynamic-slice_convert_fusion.1), channel_id=1, source_target_pairs={{0,4},{2,6},{4,0},{6,2},{8,12},{10,14},{12,8},{14,10},{16,20},{18,... | collective-permute-start | bytes 884744 | tf_op jit(solution)/shard_map/ppermute | solution.py:76
  229.9 9.0 %collective-permute-start.25 = (bf16[2,2,1,1,48,896]{5,4,3,2,1,0:T(8,128)(2,1)S(1)}, bf16[2,2,1,1,48,896]{5,4,3,2,1,0:T(8,128)(2,1)S(1)}, u32[]{:S(2)}, u32[]{:S(2)}) collective-permute-start(bf16[2,2,1,1,48,896]{5,4,3,2,1,0:T(8,128)(2,1)S(1)} %dynamic-slice_convert_fusion), channel_id=1, source_target_pairs={{0,2},{2,0},{4,6},{6,4},{8,10},{10,8},{12,14},{14,12},{16,18},{18,... | collective-permute-start | bytes 1032200 | tf_op jit(solution)/shard_map/ppermute | solution.py:76
  234.6 6.1 %collective-permute-start.23 = (bf16[1,1,1,1,48,768]{5,4,3,2,1,0:T(8,128)(2,1)S(1)}, bf16[1,1,1,1,48,768]{5,4,3,2,1,0:T(8,128)(2,1)S(1)}, u32[]{:S(2)}, u32[]{:S(2)}) collective-permute-start(bf16[1,1,1,1,48,768]{5,4,3,2,1,0:T(8,128)(2,1)S(1)} %dynamic-slice_convert_fusion.6), channel_id=1, source_target_pairs={{0,16},{2,18},{4,20},{6,22},{8,24},{10,26},{12,28},{14,30},{16,0},... | collective-permute-start | bytes 221192 | tf_op jit(solution)/shard_map/ppermute | solution.py:76
  239.0 5.5 %collective-permute-start.26 = (bf16[2,1,1,1,48,896]{5,4,3,2,1,0:T(8,128)(2,1)S(1)}, bf16[2,1,1,1,48,896]{5,4,3,2,1,0:T(8,128)(2,1)S(1)}, u32[]{:S(2)}, u32[]{:S(2)}) collective-permute-start(bf16[2,1,1,1,48,896]{5,4,3,2,1,0:T(8,128)(2,1)S(1)} %dynamic-slice_convert_fusion.3), channel_id=1, source_target_pairs={{0,8},{2,10},{4,12},{6,14},{8,0},{10,2},{12,4},{14,6},{16,24},{18,... | collective-permute-start | bytes 516104 | tf_op jit(solution)/shard_map/ppermute | solution.py:76
  244.5 5.4 %collective-permute-start.27 = (bf16[1,1,1,1,48,896]{5,4,3,2,1,0:T(8,128)(2,1)S(1)}, bf16[1,1,1,1,48,896]{5,4,3,2,1,0:T(8,128)(2,1)S(1)}, u32[]{:S(2)}, u32[]{:S(2)}) collective-permute-start(bf16[1,1,1,1,48,896]{5,4,3,2,1,0:T(8,128)(2,1)S(1)} %dynamic-slice_convert_fusion.5), channel_id=1, source_target_pairs={{0,16},{2,18},{4,20},{6,22},{8,24},{10,26},{12,28},{14,30},{16,0},... | collective-permute-start | bytes 258056 | tf_op jit(solution)/shard_map/ppermute | solution.py:76
  (23 other events, 156.9 us)

commit v7 on v6

--- a/solution.py
+++ b/solution.py
@@ -597,6 +597,8 @@
     )
     out_far = cross(after(out_far, far_total))
     out_given = swap(out_given)
+    back_out = trade(add_low(own_out, out_given, out_far)).reshape(slots, width)
+
     h_part, router_part = call(
         combine_kernel,
         [near_shape((group_rows, width), FULL), near_shape((experts, width), FULL)],
@@ -643,9 +645,8 @@
     for step in range(bits):
         vx_sum = halve(vx_sum, order_b[bits - 1 - step], bits)
         qk_sum = halve(qk_sum, order_a[bits - 1 - step], bits)
-        if step == 0:
-            out_rows = add_low(own_out, out_given, after(out_far, one_other))
-            back_out = trade(out_rows).reshape(slots, width)
+        if step == 1:
+            back_out = after(back_out, vx_sum, qk_sum)
     qk_sum = qk_sum.reshape(width // dp_count, 2 * inner)
     vx_sum = vx_sum.reshape(width // dp_count, 2 * inner + extra_width)
 

time: 254 us -> 239 us (0.941)
  waiting for transfers between devices: 113 us -> 88.5 us
  starting transfers between devices: 40.7 us -> 46.9 us
  other arithmetic: 11.1 us -> 14.4 us
    all_to_all x4, waiting for transfers between devices: 38.6 us -> 22.9 us  [trade(): lax.all_to_all(values, 'dp', split_axis=0, concat_axis=0, tiled=True, axi...]
    ppermute x8, waiting for transfers between devices: 34.1 us -> 25.6 us  [halve(): lax.ppermute(given, 'dp', partners(bit)).astype(FULL)]
    ppermute x8, starting transfers between devices: 8.82 us -> 15.6 us  [halve(): lax.ppermute(given, 'dp', partners(bit)).astype(FULL)]
    unnamed x30 -> x34, local copies, waits for them, and re-layouts: 4.32 us -> 5.25 us
  transfers between devices with their start and end apart: 33 -> 33, of which waited for: 21 -> 20; matrix products, arithmetic and copies ran while one was open for 6% -> 9% of each run, Pallas kernels for 14% -> 19%
where the time goes in v7:
time: 239 us; the launch traced here: 238 us
  waiting for transfers between devices  88.5 us (37%)
  Pallas kernels  52.1 us (22%)
  starting transfers between devices  46.9 us (20%)
  blocking collectives  21.8 us (9%)
  other arithmetic  14.4 us (6%)
  local copies, waits for them, and re-layouts  12 us (5%)
    ppermute x8, waiting for transfers between devices, halve(): lax.ppermute(given, 'dp', partners(bit)).astype(FULL)  25.6 us
    all_to_all x4, waiting for transfers between devices, trade(): lax.all_to_all(values, 'dp', split_axis=0, concat_axis=0, tiled=True, axi...  22.9 us
    ppermute x4, waiting for transfers between devices, cross(): return lax.ppermute(values, 'dp', partners(0))  21.8 us
    all_gather x1, blocking collectives, local(): lax.all_gather(shard, 'dp', axis=0, tiled=True, axis_index_groups=lines)  19.4 us
    pallas_call x2, Pallas kernels, expert_weights(): pl.pallas_call(kernel, grid=(2 * steps,), out_shape=[near_shape((experts,...  19.3 us
    all_to_all x4, starting transfers between devices, trade(): lax.all_to_all(values, 'dp', split_axis=0, concat_axis=0, tiled=True, axi...  18.1 us
    pallas_call x4, Pallas kernels, call(): pl.pallas_call(kernel, out_shape=out_shape, in_specs=[pl.BlockSpec(memory...  17.4 us
    ppermute x8, starting transfers between devices, halve(): lax.ppermute(given, 'dp', partners(bit)).astype(FULL)  15.6 us
  transfers between devices with their start and end apart: 33, of which 20 were waited for; matrix products, arithmetic and copies ran while one was open for 9% of the time, Pallas kernels for 19%

profile of v7, /device:TPU:0, one launch (start us, length us, event | category | flops | bytes accessed | tf_op | source)
XLA Modules:
  0.0 238.5 jit_solution(14992453007480721589)
XLA Ops:
  3.9 19.4 %all_gather.6 = bf16[192,1664]{1,0:T(8,128)(2,1)S(1)} all-gather(bf16[48,1664]{1,0:T(8,128)(2,1)S(1)} %concatenate.59), channel_id=1, replica_groups={{0,8,16,24},{2,10,18,26},{4,12,20,28},{6,14,22,30},{1,9,17,25},{3,11,19..., dimensions={0}, use_global_device_ids=true | all-gather | bytes 798720 | tf_op jit(solution)/shard_map/all_gather | solution.py:524
  27.2 4.8 %collective-permute-done.1 = bf16[2,2,1,1,48,768]{5,4,3,2,1,0:T(8,128)(2,1)S(1)} collective-permute-done((bf16[2,2,1,1,48,768]{5,4,3,2,1,0:T(8,128)(2,1)S(1)}, bf16[2,2,1,1,48,768]{5,4,3,2,1,0:T(8,128)(2,1)S(1)}, u32[]{:S(2)}, u32[]{:S(2)}) %collective-permute-start.1) | collective-permute-done | bytes 294944 | tf_op jit(solution)/shard_map/ppermute | solution.py:62
  38.4 4.9 %all-to-all-start.1 = ((bf16[8,64,768]{2,1,0:T(8,128)(2,1)}), bf16[8,64,768]{2,1,0:T(8,128)(2,1)S(1)}, u32[]{:S(2)}, u32[]{:S(2)}) async-start(bf16[8,64,768]{2,1,0:T(8,128)(2,1)} %bitcast.11), calls=%async_computation.1 | async-start | bytes 1572864 | tf_op jit(solution)/shard_map/all_to_all | solution.py:83
  46.0 3.2 %collective-permute-done.3 = bf16[2,2,1,2,48,896]{5,4,3,2,1,0:T(8,128)(2,1)} collective-permute-done((bf16[2,2,1,2,48,896]{5,4,3,2,1,0:T(8,128)(2,1)S(1)}, bf16[2,2,1,2,48,896]{5,4,3,2,1,0:T(8,128)(2,1)}, u32[]{:S(2)}, u32[]{:S(2)}) %collective-permute-start.3) | collective-permute-done | bytes 688160 | tf_op jit(solution)/shard_map/ppermute | solution.py:62
  50.8 5.0 %shard_map.212 = (f32[256,768]{1,0:T(8,128)S(1)}, f32[128,768]{1,0:T(8,128)S(1)}, bf16[256,768]{1,0:T(8,128)(2,1)}, bf16[256,1152]{1,0:T(8,128)(2,1)}, f32[6,256...) custom-call(s32[1,4]{1,0:T(1,128)S(1)} %copy-done.5, ...), custom_call_target="tpu_custom_call" | custom-call | flops 704643072 | bytes 6684704 | tf_op jit(solution)/shard_map/pallas_call | solution.py:114
  60.2 3.6 %all-to-all-done.1.cot_a = bf16[8,64,768]{2,1,0:T(8,128)(2,1)S(1)} async-done(((bf16[8,64,768]{2,1,0:T(8,128)(2,1)}), bf16[8,64,768]{2,1,0:T(8,128)(2,1)S(1)}, u32[]{:S(2)}, u32[]{:S(2)}) %all-to-all-start.1) | async-done | bytes 786464 | tf_op jit(solution)/shard_map/all_to_all | solution.py:83
  63.8 4.0 %all-to-all-start = ((bf16[8,400,128]{2,1,0:T(8,128)(2,1)}), bf16[8,400,128]{2,1,0:T(8,128)(2,1)S(1)}, u32[]{:S(2)}, u32[]{:S(2)}) async-start(bf16[8,400,128]{2,1,0:T(8,128)(2,1)} %get-tuple-element.63), calls=%async_computation | async-start | bytes 1638400 | tf_op jit(solution)/shard_map/all_to_all | solution.py:83
  69.6 19.3 %all-to-all-done.h_a = bf16[8,400,128]{2,1,0:T(8,128)(2,1)S(1)} async-done(((bf16[8,400,128]{2,1,0:T(8,128)(2,1)}), bf16[8,400,128]{2,1,0:T(8,128)(2,1)S(1)}, u32[]{:S(2)}, u32[]{:S(2)}) %all-to-all-start) | async-done | bytes 819232 | tf_op jit(solution)/shard_map/all_to_all | solution.py:83
  95.2 7.8 %shard_map.214 = (bf16[8,400,128]{2,1,0:T(8,128)(2,1)S(1)}, bf16[8,400,128]{2,1,0:T(8,128)(2,1)S(1)}, bf16[1024,768]{1,0:T(8,128)(2,1)}, bf16[1024,768]{1,0:T(8,128)(2,1)}, f32[1024,128]{1,0:T(8,128)}) custom-call(bf16[8,400,128]{2,1,0:T(8,128)(2,1)S(1)} %all-to-all-done.h_a, bf16[8,400,128]{2,1,0:T(8,128)(2,1)S(1)} %collective-permute-done.7.h_b, ...), custom_call_target="tpu_custom_call" | custom-call | flops 3623878656 | bytes 9437184 | tf_op jit(solution)/shard_map/pallas_call | solution.py:314
  103.0 7.1 %collective-permute-done.9.h_a = bf16[8,400,128]{2,1,0:T(8,128)(2,1)S(1)} collective-permute-done((bf16[8,400,128]{2,1,0:T(8,128)(2,1)S(1)}, bf16[8,400,128]{2,1,0:T(8,128)(2,1)S(1)}, u32[]{:S(2)}, u32[]{:S(2)}) %collective-permute-start.9) | collective-permute-done | bytes 819232 | tf_op jit(solution)/shard_map/ppermute | solution.py:89
  112.4 7.7 %shard_map.215 = (bf16[8,400,128]{2,1,0:T(8,128)(2,1)S(1)}, bf16[8,400,128]{2,1,0:T(8,128)(2,1)S(1)}, bf16[1024,768]{1,0:T(8,128)(2,1)}, bf16[1024,768]{1,0:T(8,128)(2,1)}, f32[1024,128]{1,0:T(8,128)}) custom-call(bf16[8,400,128]{2,1,0:T(8,128)(2,1)S(1)} %collective-permute-done.9.h_a, bf16[8,400,128]{2,1,0:T(8,128)(2,1)S(1)} %collective-permute-done.10.h_b, ...), custom_call_target="tpu_custom_call" | custom-call | flops 3623878656 | bytes 9437184 | tf_op jit(solution)/shard_map/pallas_call | solution.py:314
  124.3 8.9 %shard_map.216 = (bf16[8,64,768]{2,1,0:T(8,128)(2,1)S(1)}, bf16[8,64,768]{2,1,0:T(8,128)(2,1)}, f32[768,768]{1,0:T(8,128)}, f32[768,768]{1,0:T(8,128)}) custom-call(bf16[8,400,128]{2,1,0:T(8,128)(2,1)S(1)} %collective-permute-done.9.h_a, bf16[8,400,128]{2,1,0:T(8,128)(2,1)S(1)} %collective-permute-done.10.h_b, bf16[8,64,768]{2,1,0:T(8,128)(2,1)S(1)} %copy-done.11, ...), custom_call_target="tpu_custom_call" | custom-call | flops 3623878656 | bytes 7864320 | tf_op jit(solution)/shard_map/pallas_call | solution.py:358
  133.2 9.9 %collective-permute-done.14 = bf16[8,400,128]{2,1,0:T(8,128)(2,1)S(1)} collective-permute-done((bf16[8,400,128]{2,1,0:T(8,128)(2,1)S(1)}, bf16[8,400,128]{2,1,0:T(8,128)(2,1)S(1)}, u32[]{:S(2)}, u32[]{:S(2)}) %collective-permute-start.14) | collective-permute-done | bytes 819232 | tf_op jit(solution)/shard_map/ppermute | solution.py:89
  144.3 3.8 %all-to-all-start.3 = ((bf16[8,400,128]{2,1,0:T(8,128)(2,1)}), bf16[8,400,128]{2,1,0:T(8,128)(2,1)S(1)}, u32[]{:S(2)}, u32[]{:S(2)}) async-start(bf16[8,400,128]{2,1,0:T(8,128)(2,1)} %add_convert_fusion), calls=%async_computation.3 | async-start | bytes 1638400 | tf_op jit(solution)/shard_map/all_to_all | solution.py:83
  152.3 10.4 %shard_map.217 = (bf16[8,64,768]{2,1,0:T(8,128)(2,1)S(1)}, bf16[8,64,768]{2,1,0:T(8,128)(2,1)}, f32[768,768]{1,0:T(8,128)}, f32[768,768]{1,0:T(8,128)}) custom-call(bf16[8,400,128]{2,1,0:T(8,128)(2,1)S(1)} %all-to-all-done.h_a, bf16[8,400,128]{2,1,0:T(8,128)(2,1)S(1)} %copy-done.7, bf16[8,64,768]{2,1,0:T(8,128)(2,1)S(1)} %copy-done.2, ...), custom_call_target="tpu_custom_call" | custom-call | flops 3623878656 | bytes 7864320 | tf_op jit(solution)/shard_map/pallas_call | solution.py:358
  163.6 4.8 %collective-permute-done.16 = bf16[8,64,768]{2,1,0:T(8,128)(2,1)} collective-permute-done((bf16[8,64,768]{2,1,0:T(8,128)(2,1)S(1)}, bf16[8,64,768]{2,1,0:T(8,128)(2,1)}, u32[]{:S(2)}, u32[]{:S(2)}) %collective-permute-start.16) | collective-permute-done | bytes 786464 | tf_op jit(solution)/shard_map/ppermute | solution.py:89
  171.3 2.6 %add_convert_fusion.2 = bf16[8,64,768]{2,1,0:T(8,128)(2,1)} fusion(bf16[8,64,768]{2,1,0:T(8,128)(2,1)} %collective-permute-done.16, bf16[8,64,768]{2,1,0:T(8,128)(2,1)} %collective-permute-done.15, bf16[8,64,768]{2,1,0:T(8,128)(2,1)S(1)} %copy-done.4), kind=kLoop, calls=%fused_computation.2 | loop fusion | flops 2359296 | bytes 3145728 | tf_op jit(solution)/shard_map/convert_element_type | solution.py:97
  173.9 5.4 %all-to-all-start.2 = ((bf16[8,64,768]{2,1,0:T(8,128)(2,1)}), bf16[8,64,768]{2,1,0:T(8,128)(2,1)S(1)}, u32[]{:S(2)}, u32[]{:S(2)}) async-start(bf16[8,64,768]{2,1,0:T(8,128)(2,1)} %add_convert_fusion.2), calls=%async_computation.2 | async-start | bytes 1572864 | tf_op jit(solution)/shard_map/all_to_all | solution.py:83
  179.3 7.8 %shard_map.219 = (bf16[768,768]{1,0:T(8,128)(2,1)S(1)}, bf16[768,896]{1,0:T(8,128)(2,1)S(1)}, f32[256,768]{1,0:T(8,128)S(1)}, f32[256,768]{1,0:T(8,128)S(1)}, bf...) custom-call(f32[256,768]{1,0:T(8,128)S(1)} %get-tuple-element.91.part_ref, ...), custom_call_target="tpu_custom_call" | custom-call | flops 1811939328 | bytes 20054016 | tf_op jit(solution)/shard_map/pallas_call | solution.py:114
  192.2 12.8 %collective-permute-done.20 = bf16[2,2,2,1,48,768]{5,4,3,2,1,0:T(8,128)(2,1)S(1)} collective-permute-done((bf16[2,2,2,1,48,768]{5,4,3,2,1,0:T(8,128)(2,1)S(1)}, bf16[2,2,2,1,48,768]{5,4,3,2,1,0:T(8,128)(2,1)S(1)}, u32[]{:S(2)}, u32[]{:S(2)}) %collective-permute-start.20) | collective-permute-done | bytes 589856 | tf_op jit(solution)/shard_map/ppermute | solution.py:76
  209.8 4.3 %collective-permute-done.21 = bf16[2,2,1,1,48,768]{5,4,3,2,1,0:T(8,128)(2,1)S(1)} collective-permute-done((bf16[2,2,1,1,48,768]{5,4,3,2,1,0:T(8,128)(2,1)S(1)}, bf16[2,2,1,1,48,768]{5,4,3,2,1,0:T(8,128)(2,1)S(1)}, u32[]{:S(2)}, u32[]{:S(2)}) %collective-permute-start.21) | collective-permute-done | bytes 294944 | tf_op jit(solution)/shard_map/ppermute | solution.py:76
  214.2 3.2 %collective-permute-start.24 = (bf16[2,1,1,1,48,768]{5,4,3,2,1,0:T(8,128)(2,1)S(1)}, bf16[2,1,1,1,48,768]{5,4,3,2,1,0:T(8,128)(2,1)S(1)}, u32[]{:S(2)}, u32[]{:S(2)}) collective-permute-start(bf16[2,1,1,1,48,768]{5,4,3,2,1,0:T(8,128)(2,1)S(1)} %dynamic-slice_convert_fusion.4), channel_id=1, source_target_pairs={{0,8},{2,10},{4,12},{6,14},{8,0},{10,2},{12,4},{14,6},{16,24},{18,... | collective-permute-start | bytes 442376 | tf_op jit(solution)/shard_map/ppermute | solution.py:76
  218.6 3.2 %collective-permute-start.26 = (bf16[2,1,1,1,48,896]{5,4,3,2,1,0:T(8,128)(2,1)}, bf16[2,1,1,1,48,896]{5,4,3,2,1,0:T(8,128)(2,1)}, u32[]{:S(2)}, u32[]{:S(2)}) collective-permute-start(bf16[2,1,1,1,48,896]{5,4,3,2,1,0:T(8,128)(2,1)} %dynamic-slice_convert_fusion.3), channel_id=1, source_target_pairs={{0,8},{2,10},{4,12},{6,14},{8,0},{10,2},{12,4},{14,6},{16,24},{18,... | collective-permute-start | bytes 516104 | tf_op jit(solution)/shard_map/ppermute | solution.py:76
  224.3 3.2 %collective-permute-done.25 = bf16[1,1,1,1,48,768]{5,4,3,2,1,0:T(8,128)(2,1)} collective-permute-done((bf16[1,1,1,1,48,768]{5,4,3,2,1,0:T(8,128)(2,1)S(1)}, bf16[1,1,1,1,48,768]{5,4,3,2,1,0:T(8,128)(2,1)}, u32[]{:S(2)}, u32[]{:S(2)}) %collective-permute-start.25) | collective-permute-done | bytes 73760 | tf_op jit(solution)/shard_map/ppermute | solution.py:76
  (142 shorter events, 70.4 us)
Async XLA Ops:
  23.3 9.8 %collective-permute-start = (bf16[2,2,1,1,48,896]{5,4,3,2,1,0:T(8,128)(2,1)S(1)}, bf16[2,2,1,1,48,896]{5,4,3,2,1,0:T(8,128)(2,1)S(1)}, u32[]{:S(2)}, u32[]{:S(2)}) collective-permute-start(bf16[2,2,1,1,48,896]{5,4,3,2,1,0:T(8,128)(2,1)S(1)} %slice.44), channel_id=1, source_target_pairs={{0,2},{2,0},{4,6},{6,4},{8,10},{10,8},{12,14},{14,12},{16,18},{18,... | collective-permute-start | bytes 1032200 | tf_op jit(solution)/shard_map/ppermute | solution.py:62
  24.9 7.1 %collective-permute-start.1 = (bf16[2,2,1,1,48,768]{5,4,3,2,1,0:T(8,128)(2,1)S(1)}, bf16[2,2,1,1,48,768]{5,4,3,2,1,0:T(8,128)(2,1)S(1)}, u32[]{:S(2)}, u32[]{:S(2)}) collective-permute-start(bf16[2,2,1,1,48,768]{5,4,3,2,1,0:T(8,128)(2,1)S(1)} %slice.45), channel_id=1, source_target_pairs={{0,4},{2,6},{4,0},{6,2},{8,12},{10,14},{12,8},{14,10},{16,20},{18,... | collective-permute-start | bytes 884744 | tf_op jit(solution)/shard_map/ppermute | solution.py:62
  32.8 11.3 %collective-permute-start.2 = (bf16[2,2,2,1,48,768]{5,4,3,2,1,0:T(8,128)(2,1)}, bf16[2,2,2,1,48,768]{5,4,3,2,1,0:T(8,128)(2,1)}, u32[]{:S(2)}, u32[]{:S(2)}) collective-permute-start(bf16[2,2,2,1,48,768]{5,4,3,2,1,0:T(8,128)(2,1)} %maximum_select_fusion.3), channel_id=1, source_target_pairs={{0,2},{2,0},{4,6},{6,4},{8,10},{10,8},{12,14},{14,12},{16,18},{18,... | collective-permute-start | bytes 1769480 | tf_op jit(solution)/shard_map/ppermute | solution.py:62
  33.2 16.1 %collective-permute-start.3 = (bf16[2,2,1,2,48,896]{5,4,3,2,1,0:T(8,128)(2,1)S(1)}, bf16[2,2,1,2,48,896]{5,4,3,2,1,0:T(8,128)(2,1)}, u32[]{:S(2)}, u32[]{:S(2)}) collective-permute-start(bf16[2,2,1,2,48,896]{5,4,3,2,1,0:T(8,128)(2,1)S(1)} %maximum_select_fusion.2), channel_id=1, source_target_pairs={{0,4},{2,6},{4,0},{6,2},{8,12},{10,14},{12,8},{14,10},{16,20},{18,... | collective-permute-start | bytes 2064392 | tf_op jit(solution)/shard_map/ppermute | solution.py:62
  38.4 25.4 %all-to-all-start.1 = ((bf16[8,64,768]{2,1,0:T(8,128)(2,1)}), bf16[8,64,768]{2,1,0:T(8,128)(2,1)S(1)}, u32[]{:S(2)}, u32[]{:S(2)}) async-start(bf16[8,64,768]{2,1,0:T(8,128)(2,1)} %bitcast.11), calls=%async_computation.1 | async-start | bytes 1572864 | tf_op jit(solution)/shard_map/all_to_all | solution.py:83
  63.8 25.2 %all-to-all-start = ((bf16[8,400,128]{2,1,0:T(8,128)(2,1)}), bf16[8,400,128]{2,1,0:T(8,128)(2,1)S(1)}, u32[]{:S(2)}, u32[]{:S(2)}) async-start(bf16[8,400,128]{2,1,0:T(8,128)(2,1)} %get-tuple-element.63), calls=%async_computation | async-start | bytes 1638400 | tf_op jit(solution)/shard_map/all_to_all | solution.py:83
  67.8 21.2 %collective-permute-start.5 = (bf16[8,64,768]{2,1,0:T(8,128)(2,1)S(1)}, bf16[8,64,768]{2,1,0:T(8,128)(2,1)S(1)}, u32[]{:S(2)}, u32[]{:S(2)}) collective-permute-start(bf16[8,64,768]{2,1,0:T(8,128)(2,1)S(1)} %all-to-all-done.1.cot_a), channel_id=1, source_target_pairs={{0,2},{2,0},{4,6},{6,4},{8,10},{10,8},{12,14},{14,12},{16,18},{18,... | collective-permute-start | bytes 2359304 | tf_op jit(solution)/shard_map/ppermute | solution.py:89
  89.5 20.6 %collective-permute-start.9 = (bf16[8,400,128]{2,1,0:T(8,128)(2,1)S(1)}, bf16[8,400,128]{2,1,0:T(8,128)(2,1)S(1)}, u32[]{:S(2)}, u32[]{:S(2)}) collective-permute-start(bf16[8,400,128]{2,1,0:T(8,128)(2,1)S(1)} %all-to-all-done.h_a), channel_id=1, source_target_pairs={{0,2},{2,0},{4,6},{6,4},{8,10},{10,8},{12,14},{14,12},{16,18},{18,... | collective-permute-start | bytes 2457608 | tf_op jit(solution)/shard_map/ppermute | solution.py:89
  120.3 12.9 %collective-permute-start.13 = (bf16[8,400,128]{2,1,0:T(8,128)(2,1)S(1)}, bf16[8,400,128]{2,1,0:T(8,128)(2,1)S(1)}, u32[]{:S(2)}, u32[]{:S(2)}) collective-permute-start(bf16[8,400,128]{2,1,0:T(8,128)(2,1)S(1)} %get-tuple-element.78), channel_id=1, source_target_pairs={{0,1},{1,0},{2,3},{3,2},{4,5},{5,4},{6,7},{7,6},{8,9},{9,8},{10,11... | collective-permute-start | bytes 2457608 | tf_op jit(solution)/shard_map/ppermute | solution.py:48
  122.7 20.4 %collective-permute-start.14 = (bf16[8,400,128]{2,1,0:T(8,128)(2,1)S(1)}, bf16[8,400,128]{2,1,0:T(8,128)(2,1)S(1)}, u32[]{:S(2)}, u32[]{:S(2)}) collective-permute-start(bf16[8,400,128]{2,1,0:T(8,128)(2,1)S(1)} %add_convert_fusion.1), channel_id=1, source_target_pairs={{0,2},{2,0},{4,6},{6,4},{8,10},{10,8},{12,14},{14,12},{16,18},{18,... | collective-permute-start | bytes 2457608 | tf_op jit(solution)/shard_map/ppermute | solution.py:89
  133.2 14.9 %collective-permute-start.12 = (bf16[8,64,768]{2,1,0:T(8,128)(2,1)}, bf16[8,64,768]{2,1,0:T(8,128)(2,1)}, u32[]{:S(2)}, u32[]{:S(2)}) collective-permute-start(bf16[8,64,768]{2,1,0:T(8,128)(2,1)} %get-tuple-element.77), channel_id=1, source_target_pairs={{0,1},{1,0},{2,3},{3,2},{4,5},{5,4},{6,7},{7,6},{8,9},{9,8},{10,11... | collective-permute-start | bytes 2359304 | tf_op jit(solution)/shard_map/ppermute | solution.py:48
  144.3 24.2 %all-to-all-start.3 = ((bf16[8,400,128]{2,1,0:T(8,128)(2,1)}), bf16[8,400,128]{2,1,0:T(8,128)(2,1)S(1)}, u32[]{:S(2)}, u32[]{:S(2)}) async-start(bf16[8,400,128]{2,1,0:T(8,128)(2,1)} %add_convert_fusion), calls=%async_computation.3 | async-start | bytes 1638400 | tf_op jit(solution)/shard_map/all_to_all | solution.py:83
  149.5 18.9 %collective-permute-start.16 = (bf16[8,64,768]{2,1,0:T(8,128)(2,1)S(1)}, bf16[8,64,768]{2,1,0:T(8,128)(2,1)}, u32[]{:S(2)}, u32[]{:S(2)}) collective-permute-start(bf16[8,64,768]{2,1,0:T(8,128)(2,1)S(1)} %add_convert_fusion.3), channel_id=1, source_target_pairs={{0,2},{2,0},{4,6},{6,4},{8,10},{10,8},{12,14},{14,12},{16,18},{18,... | collective-permute-start | bytes 2359304 | tf_op jit(solution)/shard_map/ppermute | solution.py:89
  163.6 7.6 %collective-permute-start.15 = (bf16[8,64,768]{2,1,0:T(8,128)(2,1)}, bf16[8,64,768]{2,1,0:T(8,128)(2,1)}, u32[]{:S(2)}, u32[]{:S(2)}) collective-permute-start(bf16[8,64,768]{2,1,0:T(8,128)(2,1)} %get-tuple-element.86), channel_id=1, source_target_pairs={{0,1},{1,0},{2,3},{3,2},{4,5},{5,4},{6,7},{7,6},{8,9},{9,8},{10,11... | collective-permute-start | bytes 2359304 | tf_op jit(solution)/shard_map/ppermute | solution.py:48
  171.0 8.3 %collective-permute-start.17 = (f32[256,768]{1,0:T(8,128)S(1)}, f32[256,768]{1,0:T(8,128)S(1)}, u32[]{:S(2)}, u32[]{:S(2)}) collective-permute-start(f32[256,768]{1,0:T(8,128)S(1)} %get-tuple-element.91.part_ref), channel_id=1, source_target_pairs={{0,1},{1,0},{2,3},{3,2},{4,5},{5,4},{6,7},{7,6},{8,9},{9,8},{10,11... | collective-permute-start | bytes 2359304 | tf_op jit(solution)/shard_map/ppermute | solution.py:48
  173.9 49.3 %all-to-all-start.2 = ((bf16[8,64,768]{2,1,0:T(8,128)(2,1)}), bf16[8,64,768]{2,1,0:T(8,128)(2,1)S(1)}, u32[]{:S(2)}, u32[]{:S(2)}) async-start(bf16[8,64,768]{2,1,0:T(8,128)(2,1)} %add_convert_fusion.2), calls=%async_computation.2 | async-start | bytes 1572864 | tf_op jit(solution)/shard_map/all_to_all | solution.py:83
  187.5 20.5 %collective-permute-start.18 = (bf16[2,2,1,2,48,896]{5,4,3,2,1,0:T(8,128)(2,1)S(1)}, bf16[2,2,1,2,48,896]{5,4,3,2,1,0:T(8,128)(2,1)S(1)}, u32[]{:S(2)}, u32[]{:S(2)}) collective-permute-start(bf16[2,2,1,2,48,896]{5,4,3,2,1,0:T(8,128)(2,1)S(1)} %constant_dynamic-slice_fusion.2), channel_id=1, source_target_pairs={{0,4},{2,6},{4,0},{6,2},{8,12},{10,14},{12,8},{14,10},{16,20},{18,... | collective-permute-start | bytes 2064392 | tf_op jit(solution)/shard_map/ppermute | solution.py:76
  189.4 15.5 %collective-permute-start.20 = (bf16[2,2,2,1,48,768]{5,4,3,2,1,0:T(8,128)(2,1)S(1)}, bf16[2,2,2,1,48,768]{5,4,3,2,1,0:T(8,128)(2,1)S(1)}, u32[]{:S(2)}, u32[]{:S(2)}) collective-permute-start(bf16[2,2,2,1,48,768]{5,4,3,2,1,0:T(8,128)(2,1)S(1)} %constant_dynamic-slice_fusion.1), channel_id=1, source_target_pairs={{0,2},{2,0},{4,6},{6,4},{8,10},{10,8},{12,14},{14,12},{16,18},{18,... | collective-permute-start | bytes 1769480 | tf_op jit(solution)/shard_map/ppermute | solution.py:76
  205.1 8.9 %collective-permute-start.21 = (bf16[2,2,1,1,48,768]{5,4,3,2,1,0:T(8,128)(2,1)S(1)}, bf16[2,2,1,1,48,768]{5,4,3,2,1,0:T(8,128)(2,1)S(1)}, u32[]{:S(2)}, u32[]{:S(2)}) collective-permute-start(bf16[2,2,1,1,48,768]{5,4,3,2,1,0:T(8,128)(2,1)S(1)} %dynamic-slice_convert_fusion.1), channel_id=1, source_target_pairs={{0,4},{2,6},{4,0},{6,2},{8,12},{10,14},{12,8},{14,10},{16,20},{18,... | collective-permute-start | bytes 884744 | tf_op jit(solution)/shard_map/ppermute | solution.py:76
  208.2 9.7 %collective-permute-start.19 = (bf16[2,2,1,1,48,896]{5,4,3,2,1,0:T(8,128)(2,1)S(1)}, bf16[2,2,1,1,48,896]{5,4,3,2,1,0:T(8,128)(2,1)S(1)}, u32[]{:S(2)}, u32[]{:S(2)}) collective-permute-start(bf16[2,2,1,1,48,896]{5,4,3,2,1,0:T(8,128)(2,1)S(1)} %dynamic-slice_convert_fusion), channel_id=1, source_target_pairs={{0,2},{2,0},{4,6},{6,4},{8,10},{10,8},{12,14},{14,12},{16,18},{18,... | collective-permute-start | bytes 1032200 | tf_op jit(solution)/shard_map/ppermute | solution.py:76
  214.2 7.7 %collective-permute-start.24 = (bf16[2,1,1,1,48,768]{5,4,3,2,1,0:T(8,128)(2,1)S(1)}, bf16[2,1,1,1,48,768]{5,4,3,2,1,0:T(8,128)(2,1)S(1)}, u32[]{:S(2)}, u32[]{:S(2)}) collective-permute-start(bf16[2,1,1,1,48,768]{5,4,3,2,1,0:T(8,128)(2,1)S(1)} %dynamic-slice_convert_fusion.4), channel_id=1, source_target_pairs={{0,8},{2,10},{4,12},{6,14},{8,0},{10,2},{12,4},{14,6},{16,24},{18,... | collective-permute-start | bytes 442376 | tf_op jit(solution)/shard_map/ppermute | solution.py:76
  218.6 9.8 %collective-permute-start.26 = (bf16[2,1,1,1,48,896]{5,4,3,2,1,0:T(8,128)(2,1)}, bf16[2,1,1,1,48,896]{5,4,3,2,1,0:T(8,128)(2,1)}, u32[]{:S(2)}, u32[]{:S(2)}) collective-permute-start(bf16[2,1,1,1,48,896]{5,4,3,2,1,0:T(8,128)(2,1)} %dynamic-slice_convert_fusion.3), channel_id=1, source_target_pairs={{0,8},{2,10},{4,12},{6,14},{8,0},{10,2},{12,4},{14,6},{16,24},{18,... | collective-permute-start | bytes 516104 | tf_op jit(solution)/shard_map/ppermute | solution.py:76
  221.9 5.6 %collective-permute-start.25 = (bf16[1,1,1,1,48,768]{5,4,3,2,1,0:T(8,128)(2,1)S(1)}, bf16[1,1,1,1,48,768]{5,4,3,2,1,0:T(8,128)(2,1)}, u32[]{:S(2)}, u32[]{:S(2)}) collective-permute-start(bf16[1,1,1,1,48,768]{5,4,3,2,1,0:T(8,128)(2,1)S(1)} %dynamic-slice_convert_fusion.6), channel_id=1, source_target_pairs={{0,16},{2,18},{4,20},{6,22},{8,24},{10,26},{12,28},{14,30},{16,0},... | collective-permute-start | bytes 221192 | tf_op jit(solution)/shard_map/ppermute | solution.py:76
  224.3 13.3 %collective-permute-start.22 = (f32[128,768]{1,0:T(8,128)}, f32[128,768]{1,0:T(8,128)S(1)}, u32[]{:S(2)}, u32[]{:S(2)}) collective-permute-start(f32[128,768]{1,0:T(8,128)} %constant_dynamic-slice_fusion), channel_id=1, source_target_pairs={{0,1},{1,0},{2,3},{3,2},{4,5},{5,4},{6,7},{7,6},{8,9},{9,8},{10,11... | collective-permute-start | bytes 1179656 | tf_op jit(solution)/shard_map/ppermute | solution.py:48
  (25 other events, 178.8 us)

commit v8 on v7

--- a/solution.py
+++ b/solution.py
@@ -240,7 +240,7 @@
     return (gate * cot_ref[...].reshape(sources * half, width).astype(FULL)).astype(LOW)
 
 
-def expert_step(half, h_ref, cot_ref, first_ref, second_ref, back_ref, hid_ref, pre_ref, gate_ref):
+def expert_core(half, h_ref, cot_ref, first_ref, second_ref):
     sources = h_ref.shape[0]
     blocks = (h_ref.shape[1] - EXTRA_ROWS) // half
     count, shift = sources * half, half.bit_length() - 1
@@ -251,7 +251,6 @@
     on_lane = iota((count, LANES), 1) == (iota((count, LANES), 0) & (half - 1))
     gate_lanes = dot(two_rows.astype(LOW), extra)
     gate = jnp.sum(jnp.where(on_lane, gate_lanes, 0.0), axis=1, keepdims=True)
-    gate_ref[...] = jnp.broadcast_to(gate, (count, LANES))
     arrived = gated_cot(gate, cot_ref)
     incoming = rows_of(h_ref, half)
     pre = dot(incoming, first_ref[...])
@@ -260,11 +259,18 @@
     bend = jnp.tanh(GELU_SCALE * pre * (1.0 + GELU_CUBE * square))
     rise = 0.5 * (1.0 + bend)
     hidden = (pre * rise).astype(LOW)
-    hid_ref[...] = hidden
     slope = rise + (0.5 * GELU_SCALE) * pre * (1.0 - bend * bend) * (1.0 + 3.0 * GELU_CUBE * square)
+    grad_pre = (grad_hidden * slope).astype(LOW)
+    return incoming, gate, arrived, hidden, grad_hidden, grad_pre
+
+
+def expert_step(half, h_ref, cot_ref, first_ref, second_ref, back_ref):
+    sources = h_ref.shape[0]
+    blocks = (h_ref.shape[1] - EXTRA_ROWS) // half
+    count, shift = sources * half, half.bit_length() - 1
+    on_lane = iota((count, LANES), 1) == (iota((count, LANES), 0) & (half - 1))
+    _, _, _, hidden, grad_hidden, grad_pre = expert_core(half, h_ref, cot_ref, first_ref, second_ref)
     gated = jnp.sum(hidden.astype(FULL) * grad_hidden, axis=1, keepdims=True)
-    grad_pre = (grad_hidden * slope).astype(LOW)
-    pre_ref[...] = grad_pre
     grad_rows = contract_cols(grad_pre, first_ref[...]).astype(LOW).reshape(sources, half, blocks * LANES)
     for block in range(blocks):
         back_ref[:, block * half : (block + 1) * half, :] = grad_rows[
@@ -300,44 +306,38 @@
     experts, rows_sent, _ = h_rows[0].shape
     width, hidden_width = first_weight.shape
     sources = min(experts, 256 // half)
-    count, steps = sources * half, experts // sources
-    total = 2 * experts * half
-
-    def kernel(h_a, h_b, cot_a, cot_b, first_ref, second_ref, back_a, back_b, *kept):
+    steps, total = experts // sources, 2 * experts * half
+
+    def kernel(h_a, h_b, cot_a, cot_b, first_ref, second_ref, back_a, back_b):
         in_halves(
             steps,
-            lambda: expert_step(half, h_a, cot_a, first_ref, second_ref, back_a, *kept),
-            lambda: expert_step(half, h_b, cot_b, first_ref, second_ref, back_b, *kept),
+            lambda: expert_step(half, h_a, cot_a, first_ref, second_ref, back_a),
+            lambda: expert_step(half, h_b, cot_b, first_ref, second_ref, back_b),
         )
 
-    lanes = ((hidden_width, LOW), (hidden_width, LOW), (LANES, FULL))
-    back_a, back_b, *kept = pl.pallas_call(
+    return pl.pallas_call(
         kernel,
         grid=(2 * steps,),
-        out_shape=[near_shape(h_rows[0].shape, LOW)] * 2
-        + [far_shape((total, n), kind) for n, kind in lanes],
+        out_shape=[near_shape(h_rows[0].shape, LOW)] * 2,
         in_specs=part_specs(sources, steps, [(rows_sent, LANES), (half, width)])
         + [whole(first_weight), whole(second_weight)],
-        out_specs=part_specs(sources, steps, [(rows_sent, LANES)])
-        + [pl.BlockSpec((count, n), lambda i: (i, 0)) for n, _ in lanes],
+        out_specs=part_specs(sources, steps, [(rows_sent, LANES)]),
         compiler_params=pltpu.CompilerParams(vmem_limit_bytes=16 * MIB),
         cost_estimate=pl.CostEstimate(
             flops=6 * total * width * hidden_width,
-            bytes_accessed=12 * total * width,
+            bytes_accessed=8 * total * width,
             transcendentals=total * hidden_width,
         ),
     )(*h_rows, *cot_rows, far(first_weight), far(second_weight))
-    return back_a, back_b, kept
-
-
-def expert_weights(h_rows, cot_rows, kept, second_weight, sums, half):
+
+
+def expert_weights(h_rows, cot_rows, first_weight, second_weight, sums, half):
     experts, rows_sent, _ = h_rows[0].shape
     hidden_width, width = second_weight.shape
     sources = min(experts, 256 // half)
-    count, steps = sources * half, experts // sources
-    total = 2 * experts * half
-
-    def kernel(h_a, h_b, cot_a, cot_b, hid_ref, pre_ref, gate_ref, second_ref, *refs):
+    steps, total = experts // sources, 2 * experts * half
+
+    def kernel(h_a, h_b, cot_a, cot_b, first_ref, second_ref, *refs):
         out_a, out_b, grad_first, grad_second = refs[-4:]
 
         @pl.when(pl.program_id(0) == 0)
@@ -346,11 +346,13 @@
                 grad[...] = refs[at][...] if sums else jnp.zeros(grad.shape, FULL)
 
         def step(h_ref, cot_ref, out_ref):
-            hidden, gate = hid_ref[...], gate_ref[:, 0:1]
+            incoming, gate, arrived, hidden, _, grad_pre = expert_core(
+                half, h_ref, cot_ref, first_ref, second_ref
+            )
             produced = dot(hidden, second_ref[...])
             out_ref[...] = (gate * produced).astype(LOW).reshape(out_ref.shape)
-            grad_first[...] += contract_rows(rows_of(h_ref, half), pre_ref[...])
-            grad_second[...] += contract_rows(hidden, gated_cot(gate, cot_ref))
+            grad_first[...] += contract_rows(incoming, grad_pre)
+            grad_second[...] += contract_rows(hidden, arrived)
 
         in_halves(steps, lambda: step(h_a, cot_a, out_a), lambda: step(h_b, cot_b, out_b))
 
@@ -360,16 +362,15 @@
         grid=(2 * steps,),
         out_shape=[near_shape((experts, half, width), LOW)] * 2 + grads,
         in_specs=part_specs(sources, steps, [(rows_sent, LANES), (half, width)])
-        + [pl.BlockSpec((count, x.shape[1]), lambda i: (i, 0)) for x in kept]
-        + [whole(x) for x in (second_weight, *sums)],
+        + [whole(x) for x in (first_weight, second_weight, *sums)],
         out_specs=part_specs(sources, steps, [(half, width)]) + [whole(x) for x in grads],
-        compiler_params=pltpu.CompilerParams(vmem_limit_bytes=24 * MIB),
+        compiler_params=pltpu.CompilerParams(vmem_limit_bytes=28 * MIB),
         cost_estimate=pl.CostEstimate(
-            flops=6 * total * width * hidden_width,
+            flops=10 * total * width * hidden_width,
             bytes_accessed=10 * total * width,
-            transcendentals=0,
+            transcendentals=total * hidden_width,
         ),
-    )(*h_rows, *cot_rows, *map(far, (*kept, second_weight, *sums)))
+    )(*h_rows, *cot_rows, *map(far, (first_weight, second_weight, *sums)))
 
 
 def combine_kernel(base_ref, back_ref, slot_ref, col_ref, gates_ref, ext_ref, h_ref, part_ref, router_ref):
@@ -507,7 +508,6 @@
     in_slot = slot_row[:, None, :] == slot_ids[None, :, None]
     dispatch = in_slot.astype(LOW).reshape(slots, group_rows)
     base = base.reshape(1).astype(jnp.int32)
-    cot_picked = dot(dispatch, cotangent.astype(LOW)).astype(LOW).reshape(experts, half, width)
 
     extra_width = -(-(2 + experts) // LANES) * LANES
     extra = jnp.concatenate(
@@ -528,8 +528,9 @@
         vx_full = double(vx_full, order_b[step], bits)
         qk_full = double(qk_full, order_a[step], bits)
         if step == bits - 2:
-            rows_all = lax.all_gather(after(block_in, vx_full), "tensor", axis=0, tiled=True)
-    cot_own = trade(after(cot_picked, rows_all))
+            cot_low = after(cotangent, vx_full).astype(LOW)
+    cot_own = trade(dot(dispatch, cot_low).astype(LOW).reshape(experts, half, width))
+    rows_all = lax.all_gather(block_in, "tensor", axis=0, tiled=True)
     qk_full = qk_full.reshape(width, 2 * inner)
     vx_full = vx_full.reshape(width, 2 * inner + extra_width)
 
@@ -580,20 +581,20 @@
     h_own = (after(h_own, cot_far[1]), swap(h_own))
     first_weight = expert_in[0]
     second_weight = expert_out[0]
-    own_back, own_given, own_kept = expert_rows(h_own, cot_own, first_weight, second_weight, half)
+    own_back, own_given = expert_rows(h_own, cot_own, first_weight, second_weight, half)
     h_crossed = after(h_crossed, own_back)
     h_far = (h_crossed, swap(h_crossed))
-    far_back, far_given, far_kept = expert_rows(h_far, cot_far, first_weight, second_weight, half)
+    far_back, far_given = expert_rows(h_far, cot_far, first_weight, second_weight, half)
     far_sum = add_low(far_back, swap(far_given))
     far_total = cross(far_sum)
-    far_kept[0] = after(far_kept[0], far_sum)
-    far_out, far_given, *sums = expert_weights(h_far, cot_far, far_kept, second_weight, (), half)
+    held = after(first_weight, far_sum)
+    far_out, far_given, *sums = expert_weights(h_far, cot_far, held, second_weight, (), half)
     back_sum = after(add_low(own_back, swap(own_given), far_total), far_out)
     back = trade(back_sum)
     out_far = add_low(far_out, swap(far_given))
-    own_kept[0] = after(own_kept[0], out_far, back_sum)
+    held = after(first_weight, out_far, back_sum)
     own_out, out_given, grad_first, grad_second = expert_weights(
-        h_own, cot_own, own_kept, second_weight, sums, half
+        h_own, cot_own, held, second_weight, sums, half
     )
     out_far = cross(after(out_far, far_total))
     out_given = swap(out_given)

time: 239 us -> 243 us (1.017)
  Pallas kernels: 52.1 us -> 56.3 us
  waiting for transfers between devices: 88.5 us -> 91.8 us
    ppermute x8, waiting for transfers between devices: 25.6 us -> 32.8 us  [halve(): lax.ppermute(given, 'dp', partners(bit)).astype(FULL)]
    pallas_call x2, Pallas kernels: 19.3 us -> 24.8 us  [expert_weights(): pl.pallas_call(kernel, grid=(2 * steps,), out_shape=[near_shape((experts,...]
    ppermute x8, starting transfers between devices: 15.6 us -> 12 us  [halve(): lax.ppermute(given, 'dp', partners(bit)).astype(FULL)]
    all_to_all x4, waiting for transfers between devices: 22.9 us -> 19.7 us  [trade(): lax.all_to_all(values, 'dp', split_axis=0, concat_axis=0, tiled=True, axi...]
    all_to_all x4, starting transfers between devices: 18.1 us -> 20.8 us  [trade(): lax.all_to_all(values, 'dp', split_axis=0, concat_axis=0, tiled=True, axi...]
    unnamed x34 -> x30, local copies, waits for them, and re-layouts: 5.25 us -> 3.26 us
  transfers between devices with their start and end apart: 33 -> 33, of which waited for: 20 -> 20; matrix products, arithmetic and copies ran while one was open for 9% -> 8% of each run, Pallas kernels for 19% -> 20%
where the time goes in v8:
time: 243 us; the launch traced here: 242 us
  waiting for transfers between devices  91.8 us (38%)
  Pallas kernels  56.3 us (23%)
  starting transfers between devices  45 us (19%)
  blocking collectives  21.8 us (9%)
  other arithmetic  14 us (6%)
  local copies, waits for them, and re-layouts  9.94 us (4%)
    ppermute x8, waiting for transfers between devices, halve(): lax.ppermute(given, 'dp', partners(bit)).astype(FULL)  32.8 us
    pallas_call x2, Pallas kernels, expert_weights(): pl.pallas_call(kernel, grid=(2 * steps,), out_shape=[near_shape((experts,...  24.8 us
    all_to_all x4, starting transfers between devices, trade(): lax.all_to_all(values, 'dp', split_axis=0, concat_axis=0, tiled=True, axi...  20.8 us
    ppermute x4, waiting for transfers between devices, cross(): return lax.ppermute(values, 'dp', partners(0))  20.5 us
    all_to_all x4, waiting for transfers between devices, trade(): lax.all_to_all(values, 'dp', split_axis=0, concat_axis=0, tiled=True, axi...  19.7 us
    all_gather x1, blocking collectives, local(): lax.all_gather(shard, 'dp', axis=0, tiled=True, axis_index_groups=lines)  19.4 us
    pallas_call x4, Pallas kernels, call(): pl.pallas_call(kernel, out_shape=out_shape, in_specs=[pl.BlockSpec(memory...  17.4 us
    pallas_call x2, Pallas kernels, expert_rows(): pl.pallas_call(kernel, grid=(2 * steps,), out_shape=[near_shape(h_rows[0]...  14.1 us
  transfers between devices with their start and end apart: 33, of which 20 were waited for; matrix products, arithmetic and copies ran while one was open for 8% of the time, Pallas kernels for 20%

profile of v8, /device:TPU:0, one launch (start us, length us, event | category | flops | bytes accessed | tf_op | source)
XLA Modules:
  0.0 241.8 jit_solution(4848330251328121010)
XLA Ops:
  3.9 19.4 %all_gather.7 = bf16[192,1664]{1,0:T(8,128)(2,1)S(1)} all-gather(bf16[48,1664]{1,0:T(8,128)(2,1)S(1)} %concatenate.59), channel_id=1, replica_groups={{0,8,16,24},{2,10,18,26},{4,12,20,28},{6,14,22,30},{1,9,17,25},{3,11,19..., dimensions={0}, use_global_device_ids=true | all-gather | bytes 798720 | tf_op jit(solution)/shard_map/all_gather | solution.py:524
  26.8 3.2 %collective-permute-done = bf16[2,2,1,1,48,768]{5,4,3,2,1,0:T(8,128)(2,1)S(1)} collective-permute-done((bf16[2,2,1,1,48,768]{5,4,3,2,1,0:T(8,128)(2,1)S(1)}, bf16[2,2,1,1,48,768]{5,4,3,2,1,0:T(8,128)(2,1)S(1)}, u32[]{:S(2)}, u32[]{:S(2)}) %collective-permute-start) | collective-permute-done | bytes 294944 | tf_op jit(solution)/shard_map/ppermute | solution.py:62
  36.5 6.6 %all-to-all-start.1 = ((bf16[8,64,768]{2,1,0:T(8,128)(2,1)}), bf16[8,64,768]{2,1,0:T(8,128)(2,1)S(1)}, u32[]{:S(2)}, u32[]{:S(2)}) async-start(bf16[8,64,768]{2,1,0:T(8,128)(2,1)} %bitcast.11), calls=%async_computation.1 | async-start | bytes 1572864 | tf_op jit(solution)/shard_map/all_to_all | solution.py:83
  47.6 4.6 %collective-permute-done.3 = bf16[2,2,1,2,48,896]{5,4,3,2,1,0:T(8,128)(2,1)} collective-permute-done((bf16[2,2,1,2,48,896]{5,4,3,2,1,0:T(8,128)(2,1)S(1)}, bf16[2,2,1,2,48,896]{5,4,3,2,1,0:T(8,128)(2,1)}, u32[]{:S(2)}, u32[]{:S(2)}) %collective-permute-start.3) | collective-permute-done | bytes 688160 | tf_op jit(solution)/shard_map/ppermute | solution.py:62
  53.8 5.0 %shard_map.212 = (f32[256,768]{1,0:T(8,128)S(1)}, f32[128,768]{1,0:T(8,128)S(1)}, bf16[256,768]{1,0:T(8,128)(2,1)}, bf16[256,1152]{1,0:T(8,128)(2,1)}, f32[6,256...) custom-call(s32[1,4]{1,0:T(1,128)S(1)} %copy-done.3, ...), custom_call_target="tpu_custom_call" | custom-call | flops 704643072 | bytes 6684704 | tf_op jit(solution)/shard_map/pallas_call | solution.py:114
  63.2 5.0 %all-to-all-start = ((bf16[8,400,128]{2,1,0:T(8,128)(2,1)}), bf16[8,400,128]{2,1,0:T(8,128)(2,1)S(1)}, u32[]{:S(2)}, u32[]{:S(2)}) async-start(bf16[8,400,128]{2,1,0:T(8,128)(2,1)} %get-tuple-element.55), calls=%async_computation | async-start | bytes 1638400 | tf_op jit(solution)/shard_map/all_to_all | solution.py:83
  69.6 19.7 %all-to-all-done.h_a = bf16[8,400,128]{2,1,0:T(8,128)(2,1)S(1)} async-done(((bf16[8,400,128]{2,1,0:T(8,128)(2,1)}), bf16[8,400,128]{2,1,0:T(8,128)(2,1)S(1)}, u32[]{:S(2)}, u32[]{:S(2)}) %all-to-all-start) | async-done | bytes 819232 | tf_op jit(solution)/shard_map/all_to_all | solution.py:83
  93.9 7.3 %shard_map.214 = (bf16[8,400,128]{2,1,0:T(8,128)(2,1)S(1)}, bf16[8,400,128]{2,1,0:T(8,128)(2,1)S(1)}) custom-call(bf16[8,400,128]{2,1,0:T(8,128)(2,1)S(1)} %all-to-all-done.h_a, bf16[8,400,128]{2,1,0:T(8,128)(2,1)S(1)} %collective-permute-done.7.h_b, bf16[8,64,768]{2,1,0:T(8,128)(2,1)S(1)} %all-to-all-done.1.cot_a, ...), custom_call_target="tpu_custom_call" | custom-call | flops 3623878656 | bytes 6291456 | tf_op jit(solution)/shard_map/pallas_call | solution.py:318
  101.3 10.1 %collective-permute-done.9.h_a = bf16[8,400,128]{2,1,0:T(8,128)(2,1)S(1)} collective-permute-done((bf16[8,400,128]{2,1,0:T(8,128)(2,1)S(1)}, bf16[8,400,128]{2,1,0:T(8,128)(2,1)S(1)}, u32[]{:S(2)}, u32[]{:S(2)}) %collective-permute-start.9) | collective-permute-done | bytes 819232 | tf_op jit(solution)/shard_map/ppermute | solution.py:89
  113.7 6.7 %shard_map.215 = (bf16[8,400,128]{2,1,0:T(8,128)(2,1)S(1)}, bf16[8,400,128]{2,1,0:T(8,128)(2,1)S(1)}) custom-call(bf16[8,400,128]{2,1,0:T(8,128)(2,1)S(1)} %collective-permute-done.9.h_a, bf16[8,400,128]{2,1,0:T(8,128)(2,1)S(1)} %collective-permute-done.10.h_b, bf16[8,64,768]{2,1,0:T(8,128)(2,1)S(1)} %copy-done.9, ...), custom_call_target="tpu_custom_call" | custom-call | flops 3623878656 | bytes 6291456 | tf_op jit(solution)/shard_map/pallas_call | solution.py:318
  124.6 11.7 %shard_map.216 = (bf16[8,64,768]{2,1,0:T(8,128)(2,1)S(1)}, bf16[8,64,768]{2,1,0:T(8,128)(2,1)}, f32[768,768]{1,0:T(8,128)}, f32[768,768]{1,0:T(8,128)}) custom-call(bf16[8,400,128]{2,1,0:T(8,128)(2,1)S(1)} %collective-permute-done.9.h_a, bf16[8,400,128]{2,1,0:T(8,128)(2,1)S(1)} %collective-permute-done.10.h_b, bf16[8,64,768]{2,1,0:T(8,128)(2,1)S(1)} %copy-done.9, ...), custom_call_target="tpu_custom_call" | custom-call | flops 6039797760 | bytes 7864320 | tf_op jit(solution)/shard_map/pallas_call | solution.py:360
  136.3 7.1 %collective-permute-done.14 = bf16[8,400,128]{2,1,0:T(8,128)(2,1)S(1)} collective-permute-done((bf16[8,400,128]{2,1,0:T(8,128)(2,1)S(1)}, bf16[8,400,128]{2,1,0:T(8,128)(2,1)S(1)}, u32[]{:S(2)}, u32[]{:S(2)}) %collective-permute-start.14) | collective-permute-done | bytes 819232 | tf_op jit(solution)/shard_map/ppermute | solution.py:89
  144.6 3.8 %all-to-all-start.3 = ((bf16[8,400,128]{2,1,0:T(8,128)(2,1)}), bf16[8,400,128]{2,1,0:T(8,128)(2,1)S(1)}, u32[]{:S(2)}, u32[]{:S(2)}) async-start(bf16[8,400,128]{2,1,0:T(8,128)(2,1)} %add_convert_fusion), calls=%async_computation.3 | async-start | bytes 1638400 | tf_op jit(solution)/shard_map/all_to_all | solution.py:83
  151.7 13.2 %shard_map.217 = (bf16[8,64,768]{2,1,0:T(8,128)(2,1)S(1)}, bf16[8,64,768]{2,1,0:T(8,128)(2,1)}, f32[768,768]{1,0:T(8,128)}, f32[768,768]{1,0:T(8,128)}) custom-call(bf16[8,400,128]{2,1,0:T(8,128)(2,1)S(1)} %all-to-all-done.h_a, bf16[8,400,128]{2,1,0:T(8,128)(2,1)S(1)} %copy-done.5, bf16[8,64,768]{2,1,0:T(8,128)(2,1)S(1)} %all-to-all-done.1.cot_a, ...), custom_call_target="tpu_custom_call" | custom-call | flops 6039797760 | bytes 7864320 | tf_op jit(solution)/shard_map/pallas_call | solution.py:360
  165.7 3.3 %collective-permute-done.16 = bf16[8,64,768]{2,1,0:T(8,128)(2,1)} collective-permute-done((bf16[8,64,768]{2,1,0:T(8,128)(2,1)S(1)}, bf16[8,64,768]{2,1,0:T(8,128)(2,1)}, u32[]{:S(2)}, u32[]{:S(2)}) %collective-permute-start.16) | collective-permute-done | bytes 786464 | tf_op jit(solution)/shard_map/ppermute | solution.py:89
  174.4 5.4 %all-to-all-start.2 = ((bf16[8,64,768]{2,1,0:T(8,128)(2,1)}), bf16[8,64,768]{2,1,0:T(8,128)(2,1)S(1)}, u32[]{:S(2)}, u32[]{:S(2)}) async-start(bf16[8,64,768]{2,1,0:T(8,128)(2,1)} %add_convert_fusion.2), calls=%async_computation.2 | async-start | bytes 1572864 | tf_op jit(solution)/shard_map/all_to_all | solution.py:83
  179.9 7.8 %shard_map.219 = (bf16[768,768]{1,0:T(8,128)(2,1)S(1)}, bf16[768,896]{1,0:T(8,128)(2,1)S(1)}, f32[256,768]{1,0:T(8,128)S(1)}, f32[256,768]{1,0:T(8,128)S(1)}, bf...) custom-call(f32[256,768]{1,0:T(8,128)S(1)} %get-tuple-element.77.part_ref, ...), custom_call_target="tpu_custom_call" | custom-call | flops 1811939328 | bytes 20054016 | tf_op jit(solution)/shard_map/pallas_call | solution.py:114
  192.6 12.9 %collective-permute-done.20 = bf16[2,2,2,1,48,768]{5,4,3,2,1,0:T(8,128)(2,1)S(1)} collective-permute-done((bf16[2,2,2,1,48,768]{5,4,3,2,1,0:T(8,128)(2,1)S(1)}, bf16[2,2,2,1,48,768]{5,4,3,2,1,0:T(8,128)(2,1)S(1)}, u32[]{:S(2)}, u32[]{:S(2)}) %collective-permute-start.20) | collective-permute-done | bytes 589856 | tf_op jit(solution)/shard_map/ppermute | solution.py:76
  210.2 4.3 %collective-permute-done.21 = bf16[2,2,1,1,48,768]{5,4,3,2,1,0:T(8,128)(2,1)S(1)} collective-permute-done((bf16[2,2,1,1,48,768]{5,4,3,2,1,0:T(8,128)(2,1)S(1)}, bf16[2,2,1,1,48,768]{5,4,3,2,1,0:T(8,128)(2,1)S(1)}, u32[]{:S(2)}, u32[]{:S(2)}) %collective-permute-start.21) | collective-permute-done | bytes 294944 | tf_op jit(solution)/shard_map/ppermute | solution.py:76
  215.3 3.1 %collective-permute-start.24 = (bf16[2,1,1,1,48,768]{5,4,3,2,1,0:T(8,128)(2,1)}, bf16[2,1,1,1,48,768]{5,4,3,2,1,0:T(8,128)(2,1)S(1)}, u32[]{:S(2)}, u32[]{:S(2)}) collective-permute-start(bf16[2,1,1,1,48,768]{5,4,3,2,1,0:T(8,128)(2,1)} %dynamic-slice_convert_fusion.4), channel_id=1, source_target_pairs={{0,8},{2,10},{4,12},{6,14},{8,0},{10,2},{12,4},{14,6},{16,24},{18,... | collective-permute-start | bytes 442376 | tf_op jit(solution)/shard_map/ppermute | solution.py:76
  219.7 2.9 %collective-permute-done.24 = bf16[2,1,1,1,48,768]{5,4,3,2,1,0:T(8,128)(2,1)S(1)} collective-permute-done((bf16[2,1,1,1,48,768]{5,4,3,2,1,0:T(8,128)(2,1)}, bf16[2,1,1,1,48,768]{5,4,3,2,1,0:T(8,128)(2,1)S(1)}, u32[]{:S(2)}, u32[]{:S(2)}) %collective-permute-start.24) | collective-permute-done | bytes 147488 | tf_op jit(solution)/shard_map/ppermute | solution.py:76
  224.8 3.5 %collective-permute-done.25 = bf16[1,1,1,1,48,768]{5,4,3,2,1,0:T(8,128)(2,1)S(1)} collective-permute-done((bf16[1,1,1,1,48,768]{5,4,3,2,1,0:T(8,128)(2,1)S(1)}, bf16[1,1,1,1,48,768]{5,4,3,2,1,0:T(8,128)(2,1)S(1)}, u32[]{:S(2)}, u32[]{:S(2)}) %collective-permute-start.25) | collective-permute-done | bytes 73760 | tf_op jit(solution)/shard_map/ppermute | solution.py:76
  228.3 2.7 %collective-permute-done.26 = bf16[2,1,1,1,48,896]{5,4,3,2,1,0:T(8,128)(2,1)S(1)} collective-permute-done((bf16[2,1,1,1,48,896]{5,4,3,2,1,0:T(8,128)(2,1)S(1)}, bf16[2,1,1,1,48,896]{5,4,3,2,1,0:T(8,128)(2,1)S(1)}, u32[]{:S(2)}, u32[]{:S(2)}) %collective-permute-start.26) | collective-permute-done | bytes 172064 | tf_op jit(solution)/shard_map/ppermute | solution.py:76
  233.2 4.0 %collective-permute-done.27 = bf16[1,1,1,1,48,896]{5,4,3,2,1,0:T(8,128)(2,1)S(1)} collective-permute-done((bf16[1,1,1,1,48,896]{5,4,3,2,1,0:T(8,128)(2,1)S(1)}, bf16[1,1,1,1,48,896]{5,4,3,2,1,0:T(8,128)(2,1)S(1)}, u32[]{:S(2)}, u32[]{:S(2)}) %collective-permute-start.27) | collective-permute-done | bytes 86048 | tf_op jit(solution)/shard_map/ppermute | solution.py:76
  (138 shorter events, 67.3 us)
Async XLA Ops:
  23.3 6.8 %collective-permute-start = (bf16[2,2,1,1,48,768]{5,4,3,2,1,0:T(8,128)(2,1)S(1)}, bf16[2,2,1,1,48,768]{5,4,3,2,1,0:T(8,128)(2,1)S(1)}, u32[]{:S(2)}, u32[]{:S(2)}) collective-permute-start(bf16[2,2,1,1,48,768]{5,4,3,2,1,0:T(8,128)(2,1)S(1)} %slice.44), channel_id=1, source_target_pairs={{0,4},{2,6},{4,0},{6,2},{8,12},{10,14},{12,8},{14,10},{16,20},{18,... | collective-permute-start | bytes 884744 | tf_op jit(solution)/shard_map/ppermute | solution.py:62
  24.9 9.8 %collective-permute-start.2 = (bf16[2,2,1,1,48,896]{5,4,3,2,1,0:T(8,128)(2,1)S(1)}, bf16[2,2,1,1,48,896]{5,4,3,2,1,0:T(8,128)(2,1)S(1)}, u32[]{:S(2)}, u32[]{:S(2)}) collective-permute-start(bf16[2,2,1,1,48,896]{5,4,3,2,1,0:T(8,128)(2,1)S(1)} %slice.45), channel_id=1, source_target_pairs={{0,2},{2,0},{4,6},{6,4},{8,10},{10,8},{12,14},{14,12},{16,18},{18,... | collective-permute-start | bytes 1032200 | tf_op jit(solution)/shard_map/ppermute | solution.py:62
  31.0 14.5 %collective-permute-start.1 = (bf16[2,2,2,1,48,768]{5,4,3,2,1,0:T(8,128)(2,1)}, bf16[2,2,2,1,48,768]{5,4,3,2,1,0:T(8,128)(2,1)}, u32[]{:S(2)}, u32[]{:S(2)}) collective-permute-start(bf16[2,2,2,1,48,768]{5,4,3,2,1,0:T(8,128)(2,1)} %maximum_select_fusion.3), channel_id=1, source_target_pairs={{0,2},{2,0},{4,6},{6,4},{8,10},{10,8},{12,14},{14,12},{16,18},{18,... | collective-permute-start | bytes 1769480 | tf_op jit(solution)/shard_map/ppermute | solution.py:62
  34.8 17.4 %collective-permute-start.3 = (bf16[2,2,1,2,48,896]{5,4,3,2,1,0:T(8,128)(2,1)S(1)}, bf16[2,2,1,2,48,896]{5,4,3,2,1,0:T(8,128)(2,1)}, u32[]{:S(2)}, u32[]{:S(2)}) collective-permute-start(bf16[2,2,1,2,48,896]{5,4,3,2,1,0:T(8,128)(2,1)S(1)} %maximum_select_fusion.2), channel_id=1, source_target_pairs={{0,4},{2,6},{4,0},{6,2},{8,12},{10,14},{12,8},{14,10},{16,20},{18,... | collective-permute-start | bytes 2064392 | tf_op jit(solution)/shard_map/ppermute | solution.py:62
  36.5 26.7 %all-to-all-start.1 = ((bf16[8,64,768]{2,1,0:T(8,128)(2,1)}), bf16[8,64,768]{2,1,0:T(8,128)(2,1)S(1)}, u32[]{:S(2)}, u32[]{:S(2)}) async-start(bf16[8,64,768]{2,1,0:T(8,128)(2,1)} %bitcast.11), calls=%async_computation.1 | async-start | bytes 1572864 | tf_op jit(solution)/shard_map/all_to_all | solution.py:83
  63.2 26.2 %all-to-all-start = ((bf16[8,400,128]{2,1,0:T(8,128)(2,1)}), bf16[8,400,128]{2,1,0:T(8,128)(2,1)S(1)}, u32[]{:S(2)}, u32[]{:S(2)}) async-start(bf16[8,400,128]{2,1,0:T(8,128)(2,1)} %get-tuple-element.55), calls=%async_computation | async-start | bytes 1638400 | tf_op jit(solution)/shard_map/all_to_all | solution.py:83
  68.2 21.2 %collective-permute-start.5 = (bf16[8,64,768]{2,1,0:T(8,128)(2,1)S(1)}, bf16[8,64,768]{2,1,0:T(8,128)(2,1)S(1)}, u32[]{:S(2)}, u32[]{:S(2)}) collective-permute-start(bf16[8,64,768]{2,1,0:T(8,128)(2,1)S(1)} %all-to-all-done.1.cot_a), channel_id=1, source_target_pairs={{0,2},{2,0},{4,6},{6,4},{8,10},{10,8},{12,14},{14,12},{16,18},{18,... | collective-permute-start | bytes 2359304 | tf_op jit(solution)/shard_map/ppermute | solution.py:89
  90.7 20.7 %collective-permute-start.9 = (bf16[8,400,128]{2,1,0:T(8,128)(2,1)S(1)}, bf16[8,400,128]{2,1,0:T(8,128)(2,1)S(1)}, u32[]{:S(2)}, u32[]{:S(2)}) collective-permute-start(bf16[8,400,128]{2,1,0:T(8,128)(2,1)S(1)} %all-to-all-done.h_a), channel_id=1, source_target_pairs={{0,2},{2,0},{4,6},{6,4},{8,10},{10,8},{12,14},{14,12},{16,18},{18,... | collective-permute-start | bytes 2457608 | tf_op jit(solution)/shard_map/ppermute | solution.py:89
  120.6 15.6 %collective-permute-start.13 = (bf16[8,400,128]{2,1,0:T(8,128)(2,1)S(1)}, bf16[8,400,128]{2,1,0:T(8,128)(2,1)S(1)}, u32[]{:S(2)}, u32[]{:S(2)}) collective-permute-start(bf16[8,400,128]{2,1,0:T(8,128)(2,1)S(1)} %get-tuple-element.66), channel_id=1, source_target_pairs={{0,1},{1,0},{2,3},{3,2},{4,5},{5,4},{6,7},{7,6},{8,9},{9,8},{10,11... | collective-permute-start | bytes 2457608 | tf_op jit(solution)/shard_map/ppermute | solution.py:48
  123.1 20.4 %collective-permute-start.14 = (bf16[8,400,128]{2,1,0:T(8,128)(2,1)S(1)}, bf16[8,400,128]{2,1,0:T(8,128)(2,1)S(1)}, u32[]{:S(2)}, u32[]{:S(2)}) collective-permute-start(bf16[8,400,128]{2,1,0:T(8,128)(2,1)S(1)} %add_convert_fusion.1), channel_id=1, source_target_pairs={{0,2},{2,0},{4,6},{6,4},{8,10},{10,8},{12,14},{14,12},{16,18},{18,... | collective-permute-start | bytes 2457608 | tf_op jit(solution)/shard_map/ppermute | solution.py:89
  136.3 12.2 %collective-permute-start.12 = (bf16[8,64,768]{2,1,0:T(8,128)(2,1)}, bf16[8,64,768]{2,1,0:T(8,128)(2,1)}, u32[]{:S(2)}, u32[]{:S(2)}) collective-permute-start(bf16[8,64,768]{2,1,0:T(8,128)(2,1)} %get-tuple-element.65), channel_id=1, source_target_pairs={{0,1},{1,0},{2,3},{3,2},{4,5},{5,4},{6,7},{7,6},{8,9},{9,8},{10,11... | collective-permute-start | bytes 2359304 | tf_op jit(solution)/shard_map/ppermute | solution.py:48
  144.6 24.4 %all-to-all-start.3 = ((bf16[8,400,128]{2,1,0:T(8,128)(2,1)}), bf16[8,400,128]{2,1,0:T(8,128)(2,1)S(1)}, u32[]{:S(2)}, u32[]{:S(2)}) async-start(bf16[8,400,128]{2,1,0:T(8,128)(2,1)} %add_convert_fusion), calls=%async_computation.3 | async-start | bytes 1638400 | tf_op jit(solution)/shard_map/all_to_all | solution.py:83
  150.1 18.9 %collective-permute-start.16 = (bf16[8,64,768]{2,1,0:T(8,128)(2,1)S(1)}, bf16[8,64,768]{2,1,0:T(8,128)(2,1)}, u32[]{:S(2)}, u32[]{:S(2)}) collective-permute-start(bf16[8,64,768]{2,1,0:T(8,128)(2,1)S(1)} %add_convert_fusion.3), channel_id=1, source_target_pairs={{0,2},{2,0},{4,6},{6,4},{8,10},{10,8},{12,14},{14,12},{16,18},{18,... | collective-permute-start | bytes 2359304 | tf_op jit(solution)/shard_map/ppermute | solution.py:89
  165.7 6.1 %collective-permute-start.15 = (bf16[8,64,768]{2,1,0:T(8,128)(2,1)}, bf16[8,64,768]{2,1,0:T(8,128)(2,1)}, u32[]{:S(2)}, u32[]{:S(2)}) collective-permute-start(bf16[8,64,768]{2,1,0:T(8,128)(2,1)} %get-tuple-element.72), channel_id=1, source_target_pairs={{0,1},{1,0},{2,3},{3,2},{4,5},{5,4},{6,7},{7,6},{8,9},{9,8},{10,11... | collective-permute-start | bytes 2359304 | tf_op jit(solution)/shard_map/ppermute | solution.py:48
  171.6 8.2 %collective-permute-start.17 = (f32[256,768]{1,0:T(8,128)S(1)}, f32[256,768]{1,0:T(8,128)S(1)}, u32[]{:S(2)}, u32[]{:S(2)}) collective-permute-start(f32[256,768]{1,0:T(8,128)S(1)} %get-tuple-element.77.part_ref), channel_id=1, source_target_pairs={{0,1},{1,0},{2,3},{3,2},{4,5},{5,4},{6,7},{7,6},{8,9},{9,8},{10,11... | collective-permute-start | bytes 2359304 | tf_op jit(solution)/shard_map/ppermute | solution.py:48
  174.4 44.1 %all-to-all-start.2 = ((bf16[8,64,768]{2,1,0:T(8,128)(2,1)}), bf16[8,64,768]{2,1,0:T(8,128)(2,1)S(1)}, u32[]{:S(2)}, u32[]{:S(2)}) async-start(bf16[8,64,768]{2,1,0:T(8,128)(2,1)} %add_convert_fusion.2), calls=%async_computation.2 | async-start | bytes 1572864 | tf_op jit(solution)/shard_map/all_to_all | solution.py:83
  188.0 20.5 %collective-permute-start.18 = (bf16[2,2,1,2,48,896]{5,4,3,2,1,0:T(8,128)(2,1)S(1)}, bf16[2,2,1,2,48,896]{5,4,3,2,1,0:T(8,128)(2,1)S(1)}, u32[]{:S(2)}, u32[]{:S(2)}) collective-permute-start(bf16[2,2,1,2,48,896]{5,4,3,2,1,0:T(8,128)(2,1)S(1)} %constant_dynamic-slice_fusion.2), channel_id=1, source_target_pairs={{0,4},{2,6},{4,0},{6,2},{8,12},{10,14},{12,8},{14,10},{16,20},{18,... | collective-permute-start | bytes 2064392 | tf_op jit(solution)/shard_map/ppermute | solution.py:76
  190.0 15.5 %collective-permute-start.20 = (bf16[2,2,2,1,48,768]{5,4,3,2,1,0:T(8,128)(2,1)S(1)}, bf16[2,2,2,1,48,768]{5,4,3,2,1,0:T(8,128)(2,1)S(1)}, u32[]{:S(2)}, u32[]{:S(2)}) collective-permute-start(bf16[2,2,2,1,48,768]{5,4,3,2,1,0:T(8,128)(2,1)S(1)} %constant_dynamic-slice_fusion.1), channel_id=1, source_target_pairs={{0,2},{2,0},{4,6},{6,4},{8,10},{10,8},{12,14},{14,12},{16,18},{18,... | collective-permute-start | bytes 1769480 | tf_op jit(solution)/shard_map/ppermute | solution.py:76
  205.6 8.9 %collective-permute-start.21 = (bf16[2,2,1,1,48,768]{5,4,3,2,1,0:T(8,128)(2,1)S(1)}, bf16[2,2,1,1,48,768]{5,4,3,2,1,0:T(8,128)(2,1)S(1)}, u32[]{:S(2)}, u32[]{:S(2)}) collective-permute-start(bf16[2,2,1,1,48,768]{5,4,3,2,1,0:T(8,128)(2,1)S(1)} %dynamic-slice_convert_fusion.1), channel_id=1, source_target_pairs={{0,4},{2,6},{4,0},{6,2},{8,12},{10,14},{12,8},{14,10},{16,20},{18,... | collective-permute-start | bytes 884744 | tf_op jit(solution)/shard_map/ppermute | solution.py:76
  208.7 9.7 %collective-permute-start.19 = (bf16[2,2,1,1,48,896]{5,4,3,2,1,0:T(8,128)(2,1)S(1)}, bf16[2,2,1,1,48,896]{5,4,3,2,1,0:T(8,128)(2,1)S(1)}, u32[]{:S(2)}, u32[]{:S(2)}) collective-permute-start(bf16[2,2,1,1,48,896]{5,4,3,2,1,0:T(8,128)(2,1)S(1)} %dynamic-slice_convert_fusion), channel_id=1, source_target_pairs={{0,2},{2,0},{4,6},{6,4},{8,10},{10,8},{12,14},{14,12},{16,18},{18,... | collective-permute-start | bytes 1032200 | tf_op jit(solution)/shard_map/ppermute | solution.py:76
  215.3 7.3 %collective-permute-start.24 = (bf16[2,1,1,1,48,768]{5,4,3,2,1,0:T(8,128)(2,1)}, bf16[2,1,1,1,48,768]{5,4,3,2,1,0:T(8,128)(2,1)S(1)}, u32[]{:S(2)}, u32[]{:S(2)}) collective-permute-start(bf16[2,1,1,1,48,768]{5,4,3,2,1,0:T(8,128)(2,1)} %dynamic-slice_convert_fusion.4), channel_id=1, source_target_pairs={{0,8},{2,10},{4,12},{6,14},{8,0},{10,2},{12,4},{14,6},{16,24},{18,... | collective-permute-start | bytes 442376 | tf_op jit(solution)/shard_map/ppermute | solution.py:76
  219.7 20.2 %collective-permute-start.22 = (f32[128,768]{1,0:T(8,128)}, f32[128,768]{1,0:T(8,128)}, u32[]{:S(2)}, u32[]{:S(2)}) collective-permute-start(f32[128,768]{1,0:T(8,128)} %constant_dynamic-slice_fusion), channel_id=1, source_target_pairs={{0,1},{1,0},{2,3},{3,2},{4,5},{5,4},{6,7},{7,6},{8,9},{9,8},{10,11... | collective-permute-start | bytes 1179656 | tf_op jit(solution)/shard_map/ppermute | solution.py:48
  224.5 6.5 %collective-permute-start.26 = (bf16[2,1,1,1,48,896]{5,4,3,2,1,0:T(8,128)(2,1)S(1)}, bf16[2,1,1,1,48,896]{5,4,3,2,1,0:T(8,128)(2,1)S(1)}, u32[]{:S(2)}, u32[]{:S(2)}) collective-permute-start(bf16[2,1,1,1,48,896]{5,4,3,2,1,0:T(8,128)(2,1)S(1)} %dynamic-slice_convert_fusion.3), channel_id=1, source_target_pairs={{0,8},{2,10},{4,12},{6,14},{8,0},{10,2},{12,4},{14,6},{16,24},{18,... | collective-permute-start | bytes 516104 | tf_op jit(solution)/shard_map/ppermute | solution.py:76
  231.1 6.1 %collective-permute-start.27 = (bf16[1,1,1,1,48,896]{5,4,3,2,1,0:T(8,128)(2,1)S(1)}, bf16[1,1,1,1,48,896]{5,4,3,2,1,0:T(8,128)(2,1)S(1)}, u32[]{:S(2)}, u32[]{:S(2)}) collective-permute-start(bf16[1,1,1,1,48,896]{5,4,3,2,1,0:T(8,128)(2,1)S(1)} %dynamic-slice_convert_fusion.5), channel_id=1, source_target_pairs={{0,16},{2,18},{4,20},{6,22},{8,24},{10,26},{12,28},{14,30},{16,0},... | collective-permute-start | bytes 258056 | tf_op jit(solution)/shard_map/ppermute | solution.py:76
  (23 other events, 151.7 us)

commit v9 on v7

--- a/solution.py
+++ b/solution.py
@@ -136,16 +136,16 @@
     len_ref, rows_ref, qk_ref, vx_ref, attn_ref, ext_ref, h_ref, qkv_ref, probs_ref, mixed_ref, rows_out, qk_out, vx_out
 ):
     group_rows = rows_ref.shape[0]
-    inner = qk_ref.shape[1] // 2
+    inner = vx_ref.shape[1] // 2
     rows = rows_ref[...]
     rows_out[...] = rows
     qk_out[...] = qk_ref[...]
     vx_out[...] = vx_ref[...]
-    ext = vx_ref[:, 2 * inner :].astype(FULL).T
+    ext = qk_ref[:, 2 * inner :].astype(FULL).T
     ext_ref[...] = ext
     h_one = (rows * inverse_rms(rows) * ext[0:1, :]).astype(LOW)
     h_ref[...] = h_one
-    qkv_ref[:, : 2 * inner] = dot(h_one, qk_ref[...]).astype(LOW)
+    qkv_ref[:, : 2 * inner] = dot(h_one, qk_ref[:, : 2 * inner]).astype(LOW)
     qkv_ref[:, 2 * inner :] = dot(h_one, vx_ref[:, :inner]).astype(LOW)
     down, across = iota((group_rows, group_rows), 0), iota((group_rows, group_rows), 1)
     allowed = down >= across
@@ -169,7 +169,7 @@
             probs_ref[2 * pair + sub] = probs
             outs.append(dot(probs.astype(LOW), value_rows))
         mixed_ref[:, at : at + LANES] = jnp.where(low_lanes, outs[0], outs[1]).astype(LOW)
-    attn_ref[...] = contract_cols(mixed_ref[...], vx_ref[:, inner : 2 * inner])
+    attn_ref[...] = contract_cols(mixed_ref[...], vx_ref[:, inner:])
 
 
 def slot_tables(slot_row, base, half):
@@ -415,7 +415,7 @@
     mixed_ref, router_ref, qk_out, vx_out, one_ref, rgrad_ref, qkg_ref, vg_ref,
 ):
     group_rows = rows_ref.shape[0]
-    inner = qk_ref.shape[1] // 2
+    inner = vx_ref.shape[1] // 2
     h_grad = part_ref[...] + other_ref[...]
     residual = resid_ref[...]
     inv_two = inverse_rms(residual)
@@ -427,8 +427,8 @@
     )
     rgrad_ref[...] = resid_grad
     attn_grad = resid_grad.astype(LOW)
-    vx_out[:, inner : 2 * inner] = contract_rows(attn_grad, mixed_ref[...]).astype(LOW)
-    mixed_grad = dot(attn_grad, vx_ref[:, inner : 2 * inner]).astype(LOW)
+    vx_out[:, inner:] = contract_rows(attn_grad, mixed_ref[...]).astype(LOW)
+    mixed_grad = dot(attn_grad, vx_ref[:, inner:]).astype(LOW)
     low_lanes = iota((group_rows, LANES), 1) < HEAD_DIM
     for pair in range(inner // LANES):
         at = pair * LANES
@@ -457,16 +457,16 @@
         ).astype(LOW)
         vg_ref[:, at : at + LANES] = jnp.where(low_lanes, grads[0][2], grads[1][2]).astype(LOW)
     h_one = h_ref[...]
-    qk_out[...] = contract_rows(h_one, qkg_ref[...]).astype(LOW)
+    qk_out[:, : 2 * inner] = contract_rows(h_one, qkg_ref[...]).astype(LOW)
     vx_out[:, :inner] = contract_rows(h_one, vg_ref[...]).astype(LOW)
-    one_grad = contract_cols(qkg_ref[...], qk_ref[...]) + contract_cols(vg_ref[...], vx_ref[:, :inner])
+    one_grad = contract_cols(qkg_ref[...], qk_ref[:, : 2 * inner]) + contract_cols(vg_ref[...], vx_ref[:, :inner])
     one_ref[...] = one_grad
     rows = rows_ref[...]
     gain_one_row = jnp.sum(one_grad * (rows * inverse_rms(rows)), axis=0, keepdims=True)
     router_rows = router_ref[...]
     sub = iota(router_rows.shape, 0)
     extra = jnp.where(sub == 0, gain_one_row, jnp.where(sub == 1, gain_two_row, router_rows))
-    vx_out[:, 2 * inner :] = extra.T.astype(LOW)
+    qk_out[:, 2 * inner :] = extra.T.astype(LOW)
 
 
 def local(
@@ -519,19 +519,20 @@
         ],
         axis=1,
     )
-    shard = jnp.concatenate([w_query, w_key, w_value, w_out_proj.T, extra], axis=1)
+    shard = jnp.concatenate([w_query, w_key, extra, w_value, w_out_proj.T], axis=1)
     lines = [[low + 4 * high for high in range(dp_count // 4)] for low in range(4)]
     line = lax.all_gather(shard, "dp", axis=0, tiled=True, axis_index_groups=lines)
     line = line.reshape((2,) * (bits - 2) + (1, 1) + shard.shape)
-    qk_full, vx_full = line[..., : 2 * inner], line[..., 2 * inner :]
+    held = 2 * inner + extra_width
+    qk_full, vx_full = line[..., :held], line[..., held:]
     for step in range(bits - 2, bits):
         vx_full = double(vx_full, order_b[step], bits)
         qk_full = double(qk_full, order_a[step], bits)
         if step == bits - 2:
             rows_all = lax.all_gather(after(block_in, vx_full), "tensor", axis=0, tiled=True)
     cot_own = trade(after(cot_picked, rows_all))
-    qk_full = qk_full.reshape(width, 2 * inner)
-    vx_full = vx_full.reshape(width, 2 * inner + extra_width)
+    qk_full = qk_full.reshape(width, 2 * inner + extra_width)
+    vx_full = vx_full.reshape(width, 2 * inner)
 
     attn_part, ext, h_one, qkv, probs, mixed, rows_far, qk_far, vx_far = call(
         attention_kernel,
@@ -616,8 +617,8 @@
     qk_part, vx_part, one_part, resid_grad, _, _ = call(
         backward_kernel,
         [
+            near_shape((width, 2 * inner + extra_width), LOW),
             near_shape((width, 2 * inner), LOW),
-            near_shape((width, 2 * inner + extra_width), LOW),
             near_shape((group_rows, width), FULL),
             near_shape((group_rows, width), FULL),
             near_shape((group_rows, 2 * inner), LOW),
@@ -640,15 +641,15 @@
         return lax.dynamic_slice_in_dim(values, start, tok_rows, 0)
 
     one_other = swap(rows_at(one_part, other_start).astype(LOW)).astype(FULL)
-    qk_sum = qk_part.reshape((2,) * bits + (width // dp_count, 2 * inner))
-    vx_sum = vx_part.reshape((2,) * bits + (width // dp_count, 2 * inner + extra_width))
+    qk_sum = qk_part.reshape((2,) * bits + (width // dp_count, 2 * inner + extra_width))
+    vx_sum = vx_part.reshape((2,) * bits + (width // dp_count, 2 * inner))
     for step in range(bits):
         vx_sum = halve(vx_sum, order_b[bits - 1 - step], bits)
         qk_sum = halve(qk_sum, order_a[bits - 1 - step], bits)
         if step == 1:
             back_out = after(back_out, vx_sum, qk_sum)
-    qk_sum = qk_sum.reshape(width // dp_count, 2 * inner)
-    vx_sum = vx_sum.reshape(width // dp_count, 2 * inner + extra_width)
+    qk_sum = qk_sum.reshape(width // dp_count, 2 * inner + extra_width)
+    vx_sum = vx_sum.reshape(width // dp_count, 2 * inner)
 
     out_part = contract_rows(dispatch, back_out)
     block_out = rows_at(residual, own_start) + (
@@ -660,7 +661,7 @@
     grad_in = rows_at(resid_grad, own_start) + inv_own * (
         scaled_one - normed_own * jnp.mean(scaled_one * normed_own, axis=1, keepdims=True)
     )
-    extra_sum = vx_sum[:, 2 * inner :]
+    extra_sum = qk_sum[:, 2 * inner :]
     extra_sum = extra_sum + swap(extra_sum)
     share = extra_sum.shape[0] // 2
     extra_own = lax.dynamic_slice_in_dim(extra_sum, core * share, share, 0)
@@ -668,9 +669,9 @@
         block_out,
         grad_in,
         qk_sum[:, :inner],
-        qk_sum[:, inner:],
+        qk_sum[:, inner : 2 * inner],
         vx_sum[:, :inner],
-        vx_sum[:, inner : 2 * inner].T,
+        vx_sum[:, inner:].T,
         extra_own[:, 2 : 2 + experts],
         extra_own[:, 0],
         extra_own[:, 1],

time: 239 us -> 241 us (level)
    all_to_all x4, waiting for transfers between devices: 22.9 us -> 26.3 us  [trade(): lax.all_to_all(values, 'dp', split_axis=0, concat_axis=0, tiled=True, axi...]
    ppermute x4, waiting for transfers between devices: 8.79 us -> 5.44 us  [double(): other = lax.ppermute(block, 'dp', partners(bit))]
  transfers between devices with their start and end apart: 33 -> 33, of which waited for: 20 -> 18; matrix products, arithmetic and copies ran while one was open for 9% -> 8% of each run, Pallas kernels for 19% -> 18%
where the time goes in v9:
time: 241 us; the launch traced here: 239 us
  waiting for transfers between devices  87.9 us (36%)
  Pallas kernels  51.9 us (22%)
  starting transfers between devices  48.3 us (20%)
  blocking collectives  21.8 us (9%)
  other arithmetic  14.4 us (6%)
  local copies, waits for them, and re-layouts  12 us (5%)
    all_to_all x4, waiting for transfers between devices, trade(): lax.all_to_all(values, 'dp', split_axis=0, concat_axis=0, tiled=True, axi...  26.3 us
    ppermute x8, waiting for transfers between devices, halve(): lax.ppermute(given, 'dp', partners(bit)).astype(FULL)  25.5 us
    ppermute x4, waiting for transfers between devices, cross(): return lax.ppermute(values, 'dp', partners(0))  21.7 us
    all_gather x1, blocking collectives, local(): lax.all_gather(shard, 'dp', axis=0, tiled=True, axis_index_groups=lines)  19.4 us
    pallas_call x2, Pallas kernels, expert_weights(): pl.pallas_call(kernel, grid=(2 * steps,), out_shape=[near_shape((experts,...  19.3 us
    all_to_all x4, starting transfers between devices, trade(): lax.all_to_all(values, 'dp', split_axis=0, concat_axis=0, tiled=True, axi...  19 us
    pallas_call x4, Pallas kernels, call(): pl.pallas_call(kernel, out_shape=out_shape, in_specs=[pl.BlockSpec(memory...  17.1 us
    pallas_call x2, Pallas kernels, expert_rows(): pl.pallas_call(kernel, grid=(2 * steps,), out_shape=[near_shape(h_rows[0]...  15.5 us
  transfers between devices with their start and end apart: 33, of which 18 were waited for; matrix products, arithmetic and copies ran while one was open for 8% of the time, Pallas kernels for 18%

profile of v9, /device:TPU:0, one launch (start us, length us, event | category | flops | bytes accessed | tf_op | source)
XLA Modules:
  0.0 239.1 jit_solution(10465374252822220632)
XLA Ops:
  3.9 19.4 %all_gather.6 = bf16[192,1664]{1,0:T(8,128)(2,1)S(1)} all-gather(bf16[48,1664]{1,0:T(8,128)(2,1)S(1)} %concatenate.59), channel_id=1, replica_groups={{0,8,16,24},{2,10,18,26},{4,12,20,28},{6,14,22,30},{1,9,17,25},{3,11,19..., dimensions={0}, use_global_device_ids=true | all-gather | bytes 798720 | tf_op jit(solution)/shard_map/all_gather | solution.py:524
  27.2 2.9 %collective-permute-done = bf16[2,2,1,1,48,768]{5,4,3,2,1,0:T(8,128)(2,1)S(1)} collective-permute-done((bf16[2,2,1,1,48,768]{5,4,3,2,1,0:T(8,128)(2,1)S(1)}, bf16[2,2,1,1,48,768]{5,4,3,2,1,0:T(8,128)(2,1)S(1)}, u32[]{:S(2)}, u32[]{:S(2)}) %collective-permute-start) | collective-permute-done | bytes 294944 | tf_op jit(solution)/shard_map/ppermute | solution.py:62
  38.4 6.1 %all-to-all-start.1 = ((bf16[8,64,768]{2,1,0:T(8,128)(2,1)}), bf16[8,64,768]{2,1,0:T(8,128)(2,1)S(1)}, u32[]{:S(2)}, u32[]{:S(2)}) async-start(bf16[8,64,768]{2,1,0:T(8,128)(2,1)} %bitcast.11), calls=%async_computation.1 | async-start | bytes 1572864 | tf_op jit(solution)/shard_map/all_to_all | solution.py:83
  48.4 4.7 %shard_map.212 = (f32[256,768]{1,0:T(8,128)S(1)}, f32[128,768]{1,0:T(8,128)S(1)}, bf16[256,768]{1,0:T(8,128)(2,1)}, bf16[256,1152]{1,0:T(8,128)(2,1)}, f32[6,256...) custom-call(s32[1,4]{1,0:T(1,128)S(1)} %copy-done.5, ...), custom_call_target="tpu_custom_call" | custom-call | flops 704643072 | bytes 6684704 | tf_op jit(solution)/shard_map/pallas_call | solution.py:114
  57.5 7.4 %all-to-all-done.1.cot_a = bf16[8,64,768]{2,1,0:T(8,128)(2,1)S(1)} async-done(((bf16[8,64,768]{2,1,0:T(8,128)(2,1)}), bf16[8,64,768]{2,1,0:T(8,128)(2,1)S(1)}, u32[]{:S(2)}, u32[]{:S(2)}) %all-to-all-start.1) | async-done | bytes 786464 | tf_op jit(solution)/shard_map/all_to_all | solution.py:83
  65.0 3.7 %all-to-all-start = ((bf16[8,400,128]{2,1,0:T(8,128)(2,1)}), bf16[8,400,128]{2,1,0:T(8,128)(2,1)S(1)}, u32[]{:S(2)}, u32[]{:S(2)}) async-start(bf16[8,400,128]{2,1,0:T(8,128)(2,1)} %get-tuple-element.63), calls=%async_computation | async-start | bytes 1638400 | tf_op jit(solution)/shard_map/all_to_all | solution.py:83
  70.8 18.9 %all-to-all-done.h_a = bf16[8,400,128]{2,1,0:T(8,128)(2,1)S(1)} async-done(((bf16[8,400,128]{2,1,0:T(8,128)(2,1)}), bf16[8,400,128]{2,1,0:T(8,128)(2,1)S(1)}, u32[]{:S(2)}, u32[]{:S(2)}) %all-to-all-start) | async-done | bytes 819232 | tf_op jit(solution)/shard_map/all_to_all | solution.py:83
  96.0 7.8 %shard_map.214 = (bf16[8,400,128]{2,1,0:T(8,128)(2,1)S(1)}, bf16[8,400,128]{2,1,0:T(8,128)(2,1)S(1)}, bf16[1024,768]{1,0:T(8,128)(2,1)}, bf16[1024,768]{1,0:T(8,128)(2,1)}, f32[1024,128]{1,0:T(8,128)}) custom-call(bf16[8,400,128]{2,1,0:T(8,128)(2,1)S(1)} %all-to-all-done.h_a, bf16[8,400,128]{2,1,0:T(8,128)(2,1)S(1)} %collective-permute-done.7.h_b, ...), custom_call_target="tpu_custom_call" | custom-call | flops 3623878656 | bytes 9437184 | tf_op jit(solution)/shard_map/pallas_call | solution.py:314
  103.8 7.4 %collective-permute-done.9.h_a = bf16[8,400,128]{2,1,0:T(8,128)(2,1)S(1)} collective-permute-done((bf16[8,400,128]{2,1,0:T(8,128)(2,1)S(1)}, bf16[8,400,128]{2,1,0:T(8,128)(2,1)S(1)}, u32[]{:S(2)}, u32[]{:S(2)}) %collective-permute-start.9) | collective-permute-done | bytes 819232 | tf_op jit(solution)/shard_map/ppermute | solution.py:89
  113.4 7.7 %shard_map.215 = (bf16[8,400,128]{2,1,0:T(8,128)(2,1)S(1)}, bf16[8,400,128]{2,1,0:T(8,128)(2,1)S(1)}, bf16[1024,768]{1,0:T(8,128)(2,1)}, bf16[1024,768]{1,0:T(8,128)(2,1)}, f32[1024,128]{1,0:T(8,128)}) custom-call(bf16[8,400,128]{2,1,0:T(8,128)(2,1)S(1)} %collective-permute-done.9.h_a, bf16[8,400,128]{2,1,0:T(8,128)(2,1)S(1)} %collective-permute-done.10.h_b, ...), custom_call_target="tpu_custom_call" | custom-call | flops 3623878656 | bytes 9437184 | tf_op jit(solution)/shard_map/pallas_call | solution.py:314
  125.5 8.9 %shard_map.216 = (bf16[8,64,768]{2,1,0:T(8,128)(2,1)S(1)}, bf16[8,64,768]{2,1,0:T(8,128)(2,1)}, f32[768,768]{1,0:T(8,128)}, f32[768,768]{1,0:T(8,128)}) custom-call(bf16[8,400,128]{2,1,0:T(8,128)(2,1)S(1)} %collective-permute-done.9.h_a, bf16[8,400,128]{2,1,0:T(8,128)(2,1)S(1)} %collective-permute-done.10.h_b, bf16[8,64,768]{2,1,0:T(8,128)(2,1)S(1)} %copy-done.11, ...), custom_call_target="tpu_custom_call" | custom-call | flops 3623878656 | bytes 7864320 | tf_op jit(solution)/shard_map/pallas_call | solution.py:358
  134.4 9.7 %collective-permute-done.14 = bf16[8,400,128]{2,1,0:T(8,128)(2,1)S(1)} collective-permute-done((bf16[8,400,128]{2,1,0:T(8,128)(2,1)S(1)}, bf16[8,400,128]{2,1,0:T(8,128)(2,1)S(1)}, u32[]{:S(2)}, u32[]{:S(2)}) %collective-permute-start.14) | collective-permute-done | bytes 819232 | tf_op jit(solution)/shard_map/ppermute | solution.py:89
  145.3 3.8 %all-to-all-start.3 = ((bf16[8,400,128]{2,1,0:T(8,128)(2,1)}), bf16[8,400,128]{2,1,0:T(8,128)(2,1)S(1)}, u32[]{:S(2)}, u32[]{:S(2)}) async-start(bf16[8,400,128]{2,1,0:T(8,128)(2,1)} %add_convert_fusion), calls=%async_computation.3 | async-start | bytes 1638400 | tf_op jit(solution)/shard_map/all_to_all | solution.py:83
  153.5 10.4 %shard_map.217 = (bf16[8,64,768]{2,1,0:T(8,128)(2,1)S(1)}, bf16[8,64,768]{2,1,0:T(8,128)(2,1)}, f32[768,768]{1,0:T(8,128)}, f32[768,768]{1,0:T(8,128)}) custom-call(bf16[8,400,128]{2,1,0:T(8,128)(2,1)S(1)} %all-to-all-done.h_a, bf16[8,400,128]{2,1,0:T(8,128)(2,1)S(1)} %copy-done.7, bf16[8,64,768]{2,1,0:T(8,128)(2,1)S(1)} %copy-done.2, ...), custom_call_target="tpu_custom_call" | custom-call | flops 3623878656 | bytes 7864320 | tf_op jit(solution)/shard_map/pallas_call | solution.py:358
  164.8 4.6 %collective-permute-done.16 = bf16[8,64,768]{2,1,0:T(8,128)(2,1)} collective-permute-done((bf16[8,64,768]{2,1,0:T(8,128)(2,1)S(1)}, bf16[8,64,768]{2,1,0:T(8,128)(2,1)}, u32[]{:S(2)}, u32[]{:S(2)}) %collective-permute-start.16) | collective-permute-done | bytes 786464 | tf_op jit(solution)/shard_map/ppermute | solution.py:89
  169.5 2.5 %shard_map.218 = (f32[256,768]{1,0:T(8,128)S(1)}, f32[8,768]{1,0:T(8,128)S(1)}) custom-call(s32[1]{0:T(128)} %bitcast.base_ref, bf16[8,400,128]{2,1,0:T(8,128)(2,1)S(1)} %all-to-all-done.3.back_ref, bf16[8,256]{1,0:T(8,128)(2,1)S(1)} %copy.67.slot_ref, bf16[256,8]{1,0:T(8,128)(2,1)S(1)} %fusion.col_ref, f32[8,256]{1,0:T(8,128)S(1)} %get-tuple-element.89.gates_ref, ...), custom_call_target="tpu_custom_call" | custom-call | flops 201326592 | bytes 3244040 | tf_op jit(solution)/shard_map/pallas_call | solution.py:114
  172.3 2.6 %add_convert_fusion.2 = bf16[8,64,768]{2,1,0:T(8,128)(2,1)} fusion(bf16[8,64,768]{2,1,0:T(8,128)(2,1)} %collective-permute-done.16, bf16[8,64,768]{2,1,0:T(8,128)(2,1)} %collective-permute-done.15, bf16[8,64,768]{2,1,0:T(8,128)(2,1)S(1)} %copy-done.4), kind=kLoop, calls=%fused_computation.2 | loop fusion | flops 2359296 | bytes 3145728 | tf_op jit(solution)/shard_map/convert_element_type | solution.py:97
  174.9 5.4 %all-to-all-start.2 = ((bf16[8,64,768]{2,1,0:T(8,128)(2,1)}), bf16[8,64,768]{2,1,0:T(8,128)(2,1)S(1)}, u32[]{:S(2)}, u32[]{:S(2)}) async-start(bf16[8,64,768]{2,1,0:T(8,128)(2,1)} %add_convert_fusion.2), calls=%async_computation.2 | async-start | bytes 1572864 | tf_op jit(solution)/shard_map/all_to_all | solution.py:83
  180.3 7.8 %shard_map.219 = (bf16[768,896]{1,0:T(8,128)(2,1)S(1)}, bf16[768,768]{1,0:T(8,128)(2,1)S(1)}, f32[256,768]{1,0:T(8,128)S(1)}, f32[256,768]{1,0:T(8,128)S(1)}, bf...) custom-call(f32[256,768]{1,0:T(8,128)S(1)} %get-tuple-element.91.part_ref, ...), custom_call_target="tpu_custom_call" | custom-call | flops 1811939328 | bytes 20054016 | tf_op jit(solution)/shard_map/pallas_call | solution.py:114
  193.3 14.7 %collective-permute-done.18 = bf16[2,2,1,2,48,768]{5,4,3,2,1,0:T(8,128)(2,1)S(1)} collective-permute-done((bf16[2,2,1,2,48,768]{5,4,3,2,1,0:T(8,128)(2,1)S(1)}, bf16[2,2,1,2,48,768]{5,4,3,2,1,0:T(8,128)(2,1)S(1)}, u32[]{:S(2)}, u32[]{:S(2)}) %collective-permute-start.18) | collective-permute-done | bytes 589856 | tf_op jit(solution)/shard_map/ppermute | solution.py:76
  209.7 7.1 %collective-permute-done.19 = bf16[2,2,1,1,48,768]{5,4,3,2,1,0:T(8,128)(2,1)S(1)} collective-permute-done((bf16[2,2,1,1,48,768]{5,4,3,2,1,0:T(8,128)(2,1)S(1)}, bf16[2,2,1,1,48,768]{5,4,3,2,1,0:T(8,128)(2,1)S(1)}, u32[]{:S(2)}, u32[]{:S(2)}) %collective-permute-start.19) | collective-permute-done | bytes 294944 | tf_op jit(solution)/shard_map/ppermute | solution.py:76
  219.9 2.6 %collective-permute-start.24 = (bf16[2,1,1,1,48,896]{5,4,3,2,1,0:T(8,128)(2,1)}, bf16[2,1,1,1,48,896]{5,4,3,2,1,0:T(8,128)(2,1)}, u32[]{:S(2)}, u32[]{:S(2)}) collective-permute-start(bf16[2,1,1,1,48,896]{5,4,3,2,1,0:T(8,128)(2,1)} %dynamic-slice_convert_fusion.3), channel_id=1, source_target_pairs={{0,8},{2,10},{4,12},{6,14},{8,0},{10,2},{12,4},{14,6},{16,24},{18,... | collective-permute-start | bytes 516104 | tf_op jit(solution)/shard_map/ppermute | solution.py:76
  222.6 2.9 %collective-permute-start.27 = (bf16[1,1,1,1,48,768]{5,4,3,2,1,0:T(8,128)(2,1)S(1)}, bf16[1,1,1,1,48,768]{5,4,3,2,1,0:T(8,128)(2,1)}, u32[]{:S(2)}, u32[]{:S(2)}) collective-permute-start(bf16[1,1,1,1,48,768]{5,4,3,2,1,0:T(8,128)(2,1)S(1)} %dynamic-slice_convert_fusion.6), channel_id=1, source_target_pairs={{0,16},{2,18},{4,20},{6,22},{8,24},{10,26},{12,28},{14,30},{16,0},... | collective-permute-start | bytes 221192 | tf_op jit(solution)/shard_map/ppermute | solution.py:76
  230.1 2.7 %collective-permute-start.25 = (bf16[1,1,1,1,48,896]{5,4,3,2,1,0:T(8,128)(2,1)S(1)}, bf16[1,1,1,1,48,896]{5,4,3,2,1,0:T(8,128)(2,1)S(1)}, u32[]{:S(2)}, u32[]{:S(2)}) collective-permute-start(bf16[1,1,1,1,48,896]{5,4,3,2,1,0:T(8,128)(2,1)S(1)} %dynamic-slice_convert_fusion.5), channel_id=1, source_target_pairs={{0,16},{2,18},{4,20},{6,22},{8,24},{10,26},{12,28},{14,30},{16,0},... | collective-permute-start | bytes 258056 | tf_op jit(solution)/shard_map/ppermute | solution.py:76
  (142 shorter events, 66.4 us)
Async XLA Ops:
  23.3 6.8 %collective-permute-start = (bf16[2,2,1,1,48,768]{5,4,3,2,1,0:T(8,128)(2,1)S(1)}, bf16[2,2,1,1,48,768]{5,4,3,2,1,0:T(8,128)(2,1)S(1)}, u32[]{:S(2)}, u32[]{:S(2)}) collective-permute-start(bf16[2,2,1,1,48,768]{5,4,3,2,1,0:T(8,128)(2,1)S(1)} %slice.44), channel_id=1, source_target_pairs={{0,2},{2,0},{4,6},{6,4},{8,10},{10,8},{12,14},{14,12},{16,18},{18,... | collective-permute-start | bytes 884744 | tf_op jit(solution)/shard_map/ppermute | solution.py:62
  24.9 9.7 %collective-permute-start.1 = (bf16[2,2,1,1,48,896]{5,4,3,2,1,0:T(8,128)(2,1)S(1)}, bf16[2,2,1,1,48,896]{5,4,3,2,1,0:T(8,128)(2,1)S(1)}, u32[]{:S(2)}, u32[]{:S(2)}) collective-permute-start(bf16[2,2,1,1,48,896]{5,4,3,2,1,0:T(8,128)(2,1)S(1)} %slice.45), channel_id=1, source_target_pairs={{0,4},{2,6},{4,0},{6,2},{8,12},{10,14},{12,8},{14,10},{16,20},{18,... | collective-permute-start | bytes 1032200 | tf_op jit(solution)/shard_map/ppermute | solution.py:62
  31.0 14.0 %collective-permute-start.3 = (bf16[2,2,1,2,48,768]{5,4,3,2,1,0:T(8,128)(2,1)}, bf16[2,2,1,2,48,768]{5,4,3,2,1,0:T(8,128)(2,1)}, u32[]{:S(2)}, u32[]{:S(2)}) collective-permute-start(bf16[2,2,1,2,48,768]{5,4,3,2,1,0:T(8,128)(2,1)} %maximum_select_fusion.3), channel_id=1, source_target_pairs={{0,4},{2,6},{4,0},{6,2},{8,12},{10,14},{12,8},{14,10},{16,20},{18,... | collective-permute-start | bytes 1769480 | tf_op jit(solution)/shard_map/ppermute | solution.py:62
  34.7 12.2 %collective-permute-start.2 = (bf16[2,2,2,1,48,896]{5,4,3,2,1,0:T(8,128)(2,1)S(1)}, bf16[2,2,2,1,48,896]{5,4,3,2,1,0:T(8,128)(2,1)}, u32[]{:S(2)}, u32[]{:S(2)}) collective-permute-start(bf16[2,2,2,1,48,896]{5,4,3,2,1,0:T(8,128)(2,1)S(1)} %maximum_select_fusion.2), channel_id=1, source_target_pairs={{0,2},{2,0},{4,6},{6,4},{8,10},{10,8},{12,14},{14,12},{16,18},{18,... | collective-permute-start | bytes 2064392 | tf_op jit(solution)/shard_map/ppermute | solution.py:62
  38.4 26.6 %all-to-all-start.1 = ((bf16[8,64,768]{2,1,0:T(8,128)(2,1)}), bf16[8,64,768]{2,1,0:T(8,128)(2,1)S(1)}, u32[]{:S(2)}, u32[]{:S(2)}) async-start(bf16[8,64,768]{2,1,0:T(8,128)(2,1)} %bitcast.11), calls=%async_computation.1 | async-start | bytes 1572864 | tf_op jit(solution)/shard_map/all_to_all | solution.py:83
  65.0 24.7 %all-to-all-start = ((bf16[8,400,128]{2,1,0:T(8,128)(2,1)}), bf16[8,400,128]{2,1,0:T(8,128)(2,1)S(1)}, u32[]{:S(2)}, u32[]{:S(2)}) async-start(bf16[8,400,128]{2,1,0:T(8,128)(2,1)} %get-tuple-element.63), calls=%async_computation | async-start | bytes 1638400 | tf_op jit(solution)/shard_map/all_to_all | solution.py:83
  68.7 21.0 %collective-permute-start.5 = (bf16[8,64,768]{2,1,0:T(8,128)(2,1)S(1)}, bf16[8,64,768]{2,1,0:T(8,128)(2,1)S(1)}, u32[]{:S(2)}, u32[]{:S(2)}) collective-permute-start(bf16[8,64,768]{2,1,0:T(8,128)(2,1)S(1)} %all-to-all-done.1.cot_a), channel_id=1, source_target_pairs={{0,2},{2,0},{4,6},{6,4},{8,10},{10,8},{12,14},{14,12},{16,18},{18,... | collective-permute-start | bytes 2359304 | tf_op jit(solution)/shard_map/ppermute | solution.py:89
  90.3 20.8 %collective-permute-start.9 = (bf16[8,400,128]{2,1,0:T(8,128)(2,1)S(1)}, bf16[8,400,128]{2,1,0:T(8,128)(2,1)S(1)}, u32[]{:S(2)}, u32[]{:S(2)}) collective-permute-start(bf16[8,400,128]{2,1,0:T(8,128)(2,1)S(1)} %all-to-all-done.h_a), channel_id=1, source_target_pairs={{0,2},{2,0},{4,6},{6,4},{8,10},{10,8},{12,14},{14,12},{16,18},{18,... | collective-permute-start | bytes 2457608 | tf_op jit(solution)/shard_map/ppermute | solution.py:89
  121.3 13.1 %collective-permute-start.13 = (bf16[8,400,128]{2,1,0:T(8,128)(2,1)S(1)}, bf16[8,400,128]{2,1,0:T(8,128)(2,1)S(1)}, u32[]{:S(2)}, u32[]{:S(2)}) collective-permute-start(bf16[8,400,128]{2,1,0:T(8,128)(2,1)S(1)} %get-tuple-element.78), channel_id=1, source_target_pairs={{0,1},{1,0},{2,3},{3,2},{4,5},{5,4},{6,7},{7,6},{8,9},{9,8},{10,11... | collective-permute-start | bytes 2457608 | tf_op jit(solution)/shard_map/ppermute | solution.py:48
  123.7 20.4 %collective-permute-start.14 = (bf16[8,400,128]{2,1,0:T(8,128)(2,1)S(1)}, bf16[8,400,128]{2,1,0:T(8,128)(2,1)S(1)}, u32[]{:S(2)}, u32[]{:S(2)}) collective-permute-start(bf16[8,400,128]{2,1,0:T(8,128)(2,1)S(1)} %add_convert_fusion.1), channel_id=1, source_target_pairs={{0,2},{2,0},{4,6},{6,4},{8,10},{10,8},{12,14},{14,12},{16,18},{18,... | collective-permute-start | bytes 2457608 | tf_op jit(solution)/shard_map/ppermute | solution.py:89
  134.4 14.7 %collective-permute-start.12 = (bf16[8,64,768]{2,1,0:T(8,128)(2,1)}, bf16[8,64,768]{2,1,0:T(8,128)(2,1)}, u32[]{:S(2)}, u32[]{:S(2)}) collective-permute-start(bf16[8,64,768]{2,1,0:T(8,128)(2,1)} %get-tuple-element.77), channel_id=1, source_target_pairs={{0,1},{1,0},{2,3},{3,2},{4,5},{5,4},{6,7},{7,6},{8,9},{9,8},{10,11... | collective-permute-start | bytes 2359304 | tf_op jit(solution)/shard_map/ppermute | solution.py:48
  145.3 24.2 %all-to-all-start.3 = ((bf16[8,400,128]{2,1,0:T(8,128)(2,1)}), bf16[8,400,128]{2,1,0:T(8,128)(2,1)S(1)}, u32[]{:S(2)}, u32[]{:S(2)}) async-start(bf16[8,400,128]{2,1,0:T(8,128)(2,1)} %add_convert_fusion), calls=%async_computation.3 | async-start | bytes 1638400 | tf_op jit(solution)/shard_map/all_to_all | solution.py:83
  150.5 18.9 %collective-permute-start.16 = (bf16[8,64,768]{2,1,0:T(8,128)(2,1)S(1)}, bf16[8,64,768]{2,1,0:T(8,128)(2,1)}, u32[]{:S(2)}, u32[]{:S(2)}) collective-permute-start(bf16[8,64,768]{2,1,0:T(8,128)(2,1)S(1)} %add_convert_fusion.3), channel_id=1, source_target_pairs={{0,2},{2,0},{4,6},{6,4},{8,10},{10,8},{12,14},{14,12},{16,18},{18,... | collective-permute-start | bytes 2359304 | tf_op jit(solution)/shard_map/ppermute | solution.py:89
  164.8 7.5 %collective-permute-start.15 = (bf16[8,64,768]{2,1,0:T(8,128)(2,1)}, bf16[8,64,768]{2,1,0:T(8,128)(2,1)}, u32[]{:S(2)}, u32[]{:S(2)}) collective-permute-start(bf16[8,64,768]{2,1,0:T(8,128)(2,1)} %get-tuple-element.86), channel_id=1, source_target_pairs={{0,1},{1,0},{2,3},{3,2},{4,5},{5,4},{6,7},{7,6},{8,9},{9,8},{10,11... | collective-permute-start | bytes 2359304 | tf_op jit(solution)/shard_map/ppermute | solution.py:48
  172.0 8.3 %collective-permute-start.17 = (f32[256,768]{1,0:T(8,128)S(1)}, f32[256,768]{1,0:T(8,128)S(1)}, u32[]{:S(2)}, u32[]{:S(2)}) collective-permute-start(f32[256,768]{1,0:T(8,128)S(1)} %get-tuple-element.91.part_ref), channel_id=1, source_target_pairs={{0,1},{1,0},{2,3},{3,2},{4,5},{5,4},{6,7},{7,6},{8,9},{9,8},{10,11... | collective-permute-start | bytes 2359304 | tf_op jit(solution)/shard_map/ppermute | solution.py:48
  174.9 50.6 %all-to-all-start.2 = ((bf16[8,64,768]{2,1,0:T(8,128)(2,1)}), bf16[8,64,768]{2,1,0:T(8,128)(2,1)S(1)}, u32[]{:S(2)}, u32[]{:S(2)}) async-start(bf16[8,64,768]{2,1,0:T(8,128)(2,1)} %add_convert_fusion.2), calls=%async_computation.2 | async-start | bytes 1572864 | tf_op jit(solution)/shard_map/all_to_all | solution.py:83
  188.5 20.3 %collective-permute-start.20 = (bf16[2,2,2,1,48,896]{5,4,3,2,1,0:T(8,128)(2,1)S(1)}, bf16[2,2,2,1,48,896]{5,4,3,2,1,0:T(8,128)(2,1)S(1)}, u32[]{:S(2)}, u32[]{:S(2)}) collective-permute-start(bf16[2,2,2,1,48,896]{5,4,3,2,1,0:T(8,128)(2,1)S(1)} %constant_dynamic-slice_fusion.1), channel_id=1, source_target_pairs={{0,2},{2,0},{4,6},{6,4},{8,10},{10,8},{12,14},{14,12},{16,18},{18,... | collective-permute-start | bytes 2064392 | tf_op jit(solution)/shard_map/ppermute | solution.py:76
  190.3 17.7 %collective-permute-start.18 = (bf16[2,2,1,2,48,768]{5,4,3,2,1,0:T(8,128)(2,1)S(1)}, bf16[2,2,1,2,48,768]{5,4,3,2,1,0:T(8,128)(2,1)S(1)}, u32[]{:S(2)}, u32[]{:S(2)}) collective-permute-start(bf16[2,2,1,2,48,768]{5,4,3,2,1,0:T(8,128)(2,1)S(1)} %constant_dynamic-slice_fusion.2), channel_id=1, source_target_pairs={{0,4},{2,6},{4,0},{6,2},{8,12},{10,14},{12,8},{14,10},{16,20},{18,... | collective-permute-start | bytes 1769480 | tf_op jit(solution)/shard_map/ppermute | solution.py:76
  208.2 8.6 %collective-permute-start.19 = (bf16[2,2,1,1,48,768]{5,4,3,2,1,0:T(8,128)(2,1)S(1)}, bf16[2,2,1,1,48,768]{5,4,3,2,1,0:T(8,128)(2,1)S(1)}, u32[]{:S(2)}, u32[]{:S(2)}) collective-permute-start(bf16[2,2,1,1,48,768]{5,4,3,2,1,0:T(8,128)(2,1)S(1)} %dynamic-slice_convert_fusion.1), channel_id=1, source_target_pairs={{0,2},{2,0},{4,6},{6,4},{8,10},{10,8},{12,14},{14,12},{16,18},{18,... | collective-permute-start | bytes 884744 | tf_op jit(solution)/shard_map/ppermute | solution.py:76
  208.9 10.2 %collective-permute-start.21 = (bf16[2,2,1,1,48,896]{5,4,3,2,1,0:T(8,128)(2,1)S(1)}, bf16[2,2,1,1,48,896]{5,4,3,2,1,0:T(8,128)(2,1)S(1)}, u32[]{:S(2)}, u32[]{:S(2)}) collective-permute-start(bf16[2,2,1,1,48,896]{5,4,3,2,1,0:T(8,128)(2,1)S(1)} %dynamic-slice_convert_fusion), channel_id=1, source_target_pairs={{0,4},{2,6},{4,0},{6,2},{8,12},{10,14},{12,8},{14,10},{16,20},{18,... | collective-permute-start | bytes 1032200 | tf_op jit(solution)/shard_map/ppermute | solution.py:76
  216.9 5.6 %collective-permute-start.26 = (bf16[2,1,1,1,48,768]{5,4,3,2,1,0:T(8,128)(2,1)S(1)}, bf16[2,1,1,1,48,768]{5,4,3,2,1,0:T(8,128)(2,1)S(1)}, u32[]{:S(2)}, u32[]{:S(2)}) collective-permute-start(bf16[2,1,1,1,48,768]{5,4,3,2,1,0:T(8,128)(2,1)S(1)} %dynamic-slice_convert_fusion.4), channel_id=1, source_target_pairs={{0,8},{2,10},{4,12},{6,14},{8,0},{10,2},{12,4},{14,6},{16,24},{18,... | collective-permute-start | bytes 442376 | tf_op jit(solution)/shard_map/ppermute | solution.py:76
  219.9 9.2 %collective-permute-start.24 = (bf16[2,1,1,1,48,896]{5,4,3,2,1,0:T(8,128)(2,1)}, bf16[2,1,1,1,48,896]{5,4,3,2,1,0:T(8,128)(2,1)}, u32[]{:S(2)}, u32[]{:S(2)}) collective-permute-start(bf16[2,1,1,1,48,896]{5,4,3,2,1,0:T(8,128)(2,1)} %dynamic-slice_convert_fusion.3), channel_id=1, source_target_pairs={{0,8},{2,10},{4,12},{6,14},{8,0},{10,2},{12,4},{14,6},{16,24},{18,... | collective-permute-start | bytes 516104 | tf_op jit(solution)/shard_map/ppermute | solution.py:76
  222.6 5.6 %collective-permute-start.27 = (bf16[1,1,1,1,48,768]{5,4,3,2,1,0:T(8,128)(2,1)S(1)}, bf16[1,1,1,1,48,768]{5,4,3,2,1,0:T(8,128)(2,1)}, u32[]{:S(2)}, u32[]{:S(2)}) collective-permute-start(bf16[1,1,1,1,48,768]{5,4,3,2,1,0:T(8,128)(2,1)S(1)} %dynamic-slice_convert_fusion.6), channel_id=1, source_target_pairs={{0,16},{2,18},{4,20},{6,22},{8,24},{10,26},{12,28},{14,30},{16,0},... | collective-permute-start | bytes 221192 | tf_op jit(solution)/shard_map/ppermute | solution.py:76
  226.6 11.6 %collective-permute-start.22 = (f32[128,768]{1,0:T(8,128)}, f32[128,768]{1,0:T(8,128)S(1)}, u32[]{:S(2)}, u32[]{:S(2)}) collective-permute-start(f32[128,768]{1,0:T(8,128)} %constant_dynamic-slice_fusion), channel_id=1, source_target_pairs={{0,1},{1,0},{2,3},{3,2},{4,5},{5,4},{6,7},{7,6},{8,9},{9,8},{10,11... | collective-permute-start | bytes 1179656 | tf_op jit(solution)/shard_map/ppermute | solution.py:48
  (25 other events, 176.2 us)
